TPU v7x, 512 devices: a whole 4x8x8 slice. The times are simulated.
512 devices in a mesh: ep: 64 (over x, z, core), tp: 8 (over y).
Axes of the slice: x: 4, y: 8, z: 8, core: 2. Of those that a mesh axis runs over, the one named last changes fastest.
Arguments:
- hidden: bfloat16 [1024, 3584], P('ep'), may hold values from -12 to 12
- norm_gain: bfloat16 [3584], replicated, may hold values from 0.099609375 to 1.8984375
- queries: bfloat16 [1024, 64, 576], P(('ep', 'tp')), may hold values from -96 to 96
- latent_cache: bfloat16 [1024, 384, 576], P(('ep', 'tp')), may hold values from -6 to 6
- lengths: int32 [1024], P(('ep', 'tp')), may hold values from 2 to 384, as said below
- expert_ids: int32 [1024, 8], P('ep'), may hold values from 0 to 63, all different within a row; in each aligned block of 16 rows (0 to 15, 16 to 31, ...) at most 4 rows name the same one
- router: bfloat16 [64, 3584], P('ep'), may hold values from -0.09375 to 0.09375
- w_gate: bfloat16 [64, 3584, 1024], P('ep', None, 'tp'), may hold values from -0.09375 to 0.09375
- w_up: bfloat16 [64, 3584, 1024], P('ep', None, 'tp'), may hold values from -0.09375 to 0.09375
- w_down: bfloat16 [64, 1024, 3584], P('ep', 'tp'), may hold values from -0.1875 to 0.1875
- w_uv: bfloat16 [64, 512, 128], P('tp'), may hold values from -0.5 to 0.5
- w_out: bfloat16 [8192, 3584], P('tp', 'ep'), may hold values from -0.125 to 0.125
Outputs:
- layer_out: bfloat16 [1024, 3584], P('ep', 'tp')
Inputs may be any that keep to these rules, and one draw needn't show every extreme that they name: `expert_ids`: each row names 8 different experts. Among the 16 rows of one index of ep (aligned blocks of rows), no expert is named by more than 4 rows, a bound that some block reaches. `lengths`: some row holds all 384 positions in every draw.
All inputs are finite; a program needn't handle non-finite values.
Results may differ from a plain program's by a relative error of at most 0.009.
Values may be sent and summed in bfloat16 or wider, within the bound.
No kernel may reach another device: no remote copies, remote signals or barrier semaphores. Data moves between devices by JAX's collectives and lax.ppermute only.
A program may use at most 64 MiB of HBM per device.

v0:
```python
import jax
import jax.numpy as jnp
from jax import lax
from jax.sharding import PartitionSpec as P

ROUTE_SCALE = 2.5
EPSILON = 1e-06
SCORE_SCALE = 192.0 ** (-0.5)


def normalize(hidden, norm_gain):
    values = hidden.astype(jnp.float32)
    factor = lax.rsqrt(jnp.mean(values * values, axis=-1, keepdims=True) + EPSILON)
    return (values * factor * norm_gain.astype(jnp.float32)).astype(jnp.bfloat16)


def attend(queries, latent_cache, lengths, latent_width):
    scores = (
        jnp.einsum("rhc,rpc->rhp", queries, latent_cache, preferred_element_type=jnp.float32)
        * SCORE_SCALE
    )
    positions = jnp.arange(latent_cache.shape[1], dtype=jnp.int32)
    visible = positions[None, None, :] < lengths[:, None, None]
    scores = jnp.where(visible, scores, -1e30)
    row_peak = jnp.max(scores, axis=-1, keepdims=True)
    raised = jnp.exp(scores - row_peak)
    soft_weights = (raised / jnp.sum(raised, axis=-1, keepdims=True)).astype(jnp.bfloat16)
    context = jnp.einsum(
        "rhp,rpl->rhl",
        soft_weights,
        latent_cache[:, :, :latent_width],
        preferred_element_type=jnp.float32,
    )
    return context.astype(jnp.bfloat16)


def expert_terms(rows_in, w_gate, w_up, w_down, router):
    gate_act = jnp.einsum("bcd,df->bcf", rows_in, w_gate[0], preferred_element_type=jnp.float32)
    lifted = jnp.einsum("bcd,df->bcf", rows_in, w_up[0], preferred_element_type=jnp.float32)
    inner_act = (jax.nn.silu(gate_act) * lifted).astype(jnp.bfloat16)
    partial_value = jnp.einsum(
        "bcf,fd->bcd", inner_act, w_down[0], preferred_element_type=jnp.float32
    )
    logits = jnp.einsum("bcd,d->bc", rows_in, router[0], preferred_element_type=jnp.float32)
    partial_value = partial_value.astype(jnp.bfloat16)
    score_vals = jax.nn.sigmoid(logits).astype(jnp.bfloat16)
    return (partial_value, score_vals)


def on_device(
    hidden,
    norm_gain,
    queries,
    latent_cache,
    lengths,
    expert_ids,
    router,
    w_gate,
    w_up,
    w_down,
    w_uv,
    w_out,
):
    rows_here = hidden.shape[0]
    model_width = hidden.shape[1]
    top_k = expert_ids.shape[1]
    ep_size = lax.axis_size("ep")
    tp_size = lax.axis_size("tp")
    capacity = max(2, 2 * rows_here * top_k // ep_size)
    feature_width = model_width // tp_size
    normalized = normalize(hidden, norm_gain)
    context = attend(queries, latent_cache, lengths, w_uv.shape[1])
    regrouped = lax.all_to_all(context, "tp", split_axis=1, concat_axis=0, tiled=True)
    head_values = jnp.einsum("rhl,hlv->rhv", regrouped, w_uv, preferred_element_type=jnp.float32)
    flat_values = head_values.astype(jnp.bfloat16).reshape(rows_here, -1)
    attn_cols = jnp.dot(
        lax.all_gather(flat_values, "ep", axis=0, tiled=True),
        w_out,
        preferred_element_type=jnp.float32,
    )
    attn_cols = attn_cols.astype(jnp.bfloat16).reshape(ep_size, rows_here, -1)
    flat_ids = expert_ids.reshape(-1)
    expert_range = jnp.arange(ep_size, dtype=jnp.int32)
    onehot = (flat_ids[:, None] == expert_range[None, :]).astype(jnp.int32)
    running = jnp.cumsum(onehot, axis=0) - 1
    slot_index = jnp.sum(onehot * running, axis=1)
    targets = flat_ids * capacity + slot_index
    slot_range = jnp.arange(ep_size * capacity, dtype=jnp.int32)
    placing = jnp.any(
        targets.reshape(rows_here, top_k)[None, :, :] == slot_range[:, None, None], axis=2
    )
    send_rows = jnp.dot(
        placing.astype(jnp.bfloat16), normalized, preferred_element_type=jnp.float32
    )
    send_rows = send_rows.astype(jnp.bfloat16).reshape(ep_size, capacity, model_width)
    partial_value, score_vals = expert_terms(
        lax.all_to_all(send_rows, "ep", split_axis=0, concat_axis=0, tiled=True),
        w_gate,
        w_up,
        w_down,
        router,
    )
    back_parts, back_scores, attn_back = (
        lax.all_to_all(partial_value, "ep", split_axis=0, concat_axis=0, tiled=True),
        lax.all_to_all(score_vals, "ep", split_axis=0, concat_axis=0, tiled=True),
        lax.all_to_all(attn_cols, "ep", split_axis=0, concat_axis=0, tiled=True),
    )
    flat_parts = back_parts.reshape(ep_size * capacity, -1)
    picked = jnp.take(flat_parts, targets, axis=0).reshape(rows_here, top_k, -1)
    picked_scores = (
        jnp.take(back_scores.reshape(-1), targets).reshape(rows_here, top_k).astype(jnp.float32)
    )
    weights = ROUTE_SCALE * picked_scores / jnp.sum(picked_scores, axis=1, keepdims=True)
    expert_sum = jnp.einsum(
        "rk,rkd->rd", weights, picked.astype(jnp.float32), preferred_element_type=jnp.float32
    )
    attn_rows = (
        jnp.transpose(attn_back, (1, 0, 2)).reshape(rows_here, model_width).astype(jnp.float32)
    )
    merged = lax.psum_scatter(attn_rows + expert_sum, "tp", scatter_dimension=1, tiled=True)
    own_features = lax.dynamic_slice_in_dim(
        hidden, lax.axis_index("tp") * feature_width, feature_width, 1
    )
    return (own_features.astype(jnp.float32) + merged).astype(jnp.bfloat16)


def solution(mesh):
    return jax.shard_map(
        on_device,
        mesh=mesh,
        in_specs=(
            P("ep", None),
            P(),
            P(("ep", "tp"), None, None),
            P(("ep", "tp"), None, None),
            P(("ep", "tp")),
            P("ep", None),
            P("ep", None),
            P("ep", None, "tp"),
            P("ep", None, "tp"),
            P("ep", "tp", None),
            P("tp", None, None),
            P("tp", "ep"),
        ),
        out_specs=P("ep", "tp"),
        check_vma=False,
    )
```

profile of v0, /device:TPU:1, one launch (start us, length us, event | category | flops | bytes accessed | tf_op | source)
XLA Modules:
  0.0 256.2 jit_solution(16269727993837356739)
XLA Ops:
  7.4 1.6 fusion.9
  9.1 1.5 convolution_convert_fusion.2
  11.4 7.7 %all-to-all-start = ((bf16[2,64,512]{2,0,1:T(2,128)(2,1)}), bf16[2,64,512]{2,0,1:T(2,128)(2,1)S(1)}, u32[]{:S(2)}, u32[]{:S(2)}) async-start(bf16[2,64,512]{2,0,1:T(2,128)(2,1)} %copy.52), calls=%async_computation | async-start | bytes 262144 | tf_op jit(solution)/shard_map/all_to_all | solution.py:73
  20.8 1.5 reshape.109
  22.3 4.8 %all-to-all-done = bf16[2,64,512]{2,0,1:T(2,128)(2,1)S(1)} async-done(((bf16[2,64,512]{2,0,1:T(2,128)(2,1)}), bf16[2,64,512]{2,0,1:T(2,128)(2,1)S(1)}, u32[]{:S(2)}, u32[]{:S(2)}) %all-to-all-start) | async-done | bytes 131104 | tf_op jit(solution)/shard_map/all_to_all | solution.py:73
  27.1 15.3 %all-to-all-start.2 = ((bf16[64,4,3584]{2,1,0:T(4,128)(2,1)}), bf16[64,4,3584]{2,1,0:T(4,128)(2,1)S(1)}, u32[]{:S(2)}, u32[]{:S(2)}) async-start(bf16[64,4,3584]{2,1,0:T(4,128)(2,1)} %reshape.109), calls=%async_computation.2 | async-start | bytes 3670016 | tf_op jit(solution)/shard_map/all_to_all | solution.py:97
  43.6 45.5 %all-to-all-done.2 = bf16[64,4,3584]{2,1,0:T(4,128)(2,1)S(1)} async-done(((bf16[64,4,3584]{2,1,0:T(4,128)(2,1)}), bf16[64,4,3584]{2,1,0:T(4,128)(2,1)S(1)}, u32[]{:S(2)}, u32[]{:S(2)}) %all-to-all-start.2) | async-done | bytes 1835040 | tf_op jit(solution)/shard_map/all_to_all | solution.py:97
  90.7 6.1 %all-to-all-start.3 = ((bf16[64,1,4]{2,1,0:T(2,128)(2,1)}), bf16[64,1,4]{2,1,0:T(2,128)(2,1)S(1)}, u32[]{:S(2)}, u32[]{:S(2)}) async-start(bf16[64,1,4]{2,1,0:T(2,128)(2,1)} %copy.59), calls=%async_computation.3 | async-start | bytes 65536 | tf_op jit(solution)/shard_map/all_to_all | solution.py:105
  96.8 1.8 fusion.5
  98.6 30.6 %all-gather.2.cloned.1.call-done = bf16[1024,1024]{1,0:T(8,128)(2,1)} async-done(((bf16[16,1024]{1,0:T(8,128)(2,1)}), bf16[1024,1024]{1,0:T(8,128)(2,1)}) %all-gather.2.cloned.1.call-update) | async-done | bytes 2097168 | tf_op jit(solution)/shard_map/all_gather | solution.py:77
  129.2 2.3 convolution_convert_fusion.3
  132.7 6.5 %all-to-all-start.1 = ((bf16[64,2,448]{2,1,0:T(2,128)(2,1)}), bf16[64,2,448]{2,1,0:T(2,128)(2,1)S(1)}, u32[]{:S(2)}, u32[]{:S(2)}) async-start(bf16[64,2,448]{2,1,0:T(2,128)(2,1)} %reshape.140), calls=%async_computation.1 | async-start | bytes 262144 | tf_op jit(solution)/shard_map/all_to_all | solution.py:106
  139.3 3.9 %convolution_convert_fusion = bf16[64,4,3584]{2,0,1:T(8,128)(2,1)} fusion(bf16[64,4,3584]{2,1,0:T(4,128)(2,1)S(1)} %all-to-all-done.2, bf16[1,128,3584]{2,1,0:T(8,128)(2,1)} %param.21, bf16[1,3584,128]{2,1,0:T(8,128)(2,1)} %param.20, f32[64,4,128]{2,0,1:T(8,128)S(1)} %fusion.5), kind=kOutput, calls=%fused_computation.3 | convolution fusion | flops 470876160 | bytes 5636096 | tf_op jit(solution)/shard_map/bcf,fd->bcd/dot_general | solution.py:41
  143.1 4.2 %copy.62 = bf16[64,4,3584]{2,1,0:T(4,128)(2,1)} copy(bf16[64,4,3584]{2,0,1:T(8,128)(2,1)} %convolution_convert_fusion) | data formatting | bytes 3670016 | tf_op jit(solution)/shard_map/convert_element_type | solution.py:45
  147.3 2.3 all-to-all-done.1
  149.6 8.3 %all-to-all-start.4 = ((bf16[64,4,3584]{2,1,0:T(4,128)(2,1)}), bf16[64,4,3584]{2,1,0:T(4,128)(2,1)}, u32[]{:S(2)}, u32[]{:S(2)}) async-start(bf16[64,4,3584]{2,1,0:T(4,128)(2,1)} %copy.62), calls=%async_computation.4 | async-start | bytes 3670016 | tf_op jit(solution)/shard_map/all_to_all | solution.py:104
  158.5 1.2 gather_fusion
  160.8 42.5 %all-to-all-done.4 = bf16[64,4,3584]{2,1,0:T(4,128)(2,1)} async-done(((bf16[64,4,3584]{2,1,0:T(4,128)(2,1)}), bf16[64,4,3584]{2,1,0:T(4,128)(2,1)}, u32[]{:S(2)}, u32[]{:S(2)}) %all-to-all-start.4) | async-done | bytes 1835040 | tf_op jit(solution)/shard_map/all_to_all | solution.py:104
  203.3 2.9 %reshape.111 = bf16[256,3584]{1,0:T(8,128)(2,1)S(1)} reshape(bf16[64,4,3584]{2,1,0:T(4,128)(2,1)} %all-to-all-done.4) | data formatting | bytes 3670016 | tf_op jit(solution)/shard_map/reshape | solution.py:108
  206.2 2.1 gather_fusion.1
  208.3 1.6 fusion.19
  210.0 1.8 copy.66
  211.8 35.8 %reduce-scatter.4.cloned.1.call-done = f32[448,16]{1,0:T(8,128)} async-done(((f32[3584,16]{1,0:T(8,128)}), f32[448,16]{1,0:T(8,128)}) %reduce-scatter.4.cloned.1.call-update) | async-done | bytes 28688
  247.6 1.0 copy.67
  (59 shorter events, 9.6 us)
Async XLA Ops:
  6.5 36.2 %copy-start = (bf16[8,512,128]{2,1,0:T(8,128)(2,1)S(1)}, bf16[8,512,128]{2,1,0:T(8,128)(2,1)}, u32[]{:S(2)}) copy-start(bf16[8,512,128]{2,1,0:T(8,128)(2,1)} %param.22) | copy-start | bytes 3145732
  7.4 11.7 %copy-start.4 = (s32[16,8]{0,1:T(8,128)S(1)}, s32[16,8]{0,1:T(8,128)}, u32[]{:S(2)}) copy-start(s32[16,8]{0,1:T(8,128)} %param.17) | copy-start | bytes 1540
  7.4 12.6 %copy-start.3 = (bf16[3584]{0:T(1024)(128)(2,1)S(1)}, bf16[3584]{0:T(1024)(128)(2,1)}, u32[]{:S(2)}) copy-start(bf16[3584]{0:T(1024)(128)(2,1)} %param.13) | copy-start | bytes 21508
  7.4 12.6 %copy-start.1 = (bf16[16,3584]{1,0:T(8,128)(2,1)S(1)}, bf16[16,3584]{1,0:T(8,128)(2,1)}, u32[]{:S(2)}) copy-start(bf16[16,3584]{1,0:T(8,128)(2,1)} %param.12) | copy-start | bytes 344068
  11.4 15.7 %all-to-all-start = ((bf16[2,64,512]{2,0,1:T(2,128)(2,1)}), bf16[2,64,512]{2,0,1:T(2,128)(2,1)S(1)}, u32[]{:S(2)}, u32[]{:S(2)}) async-start(bf16[2,64,512]{2,0,1:T(2,128)(2,1)} %copy.52), calls=%async_computation | async-start | bytes 262144 | tf_op jit(solution)/shard_map/all_to_all | solution.py:73
  19.7 2.6 %copy-start.5 = (s32[128]{0:T(128)}, s32[128]{0:T(128)S(1)}, u32[]{:S(2)}) copy-start(s32[128]{0:T(128)S(1)} %select_reduce_fusion) | copy-start | bytes 1540
  27.1 62.0 %all-to-all-start.2 = ((bf16[64,4,3584]{2,1,0:T(4,128)(2,1)}), bf16[64,4,3584]{2,1,0:T(4,128)(2,1)S(1)}, u32[]{:S(2)}, u32[]{:S(2)}) async-start(bf16[64,4,3584]{2,1,0:T(4,128)(2,1)} %reshape.109), calls=%async_computation.2 | async-start | bytes 3670016 | tf_op jit(solution)/shard_map/all_to_all | solution.py:97
  42.5 46.6 %copy-start.7 = (bf16[1,3584]{1,0:T(2,128)(2,1)S(1)}, bf16[1,3584]{1,0:T(2,128)(2,1)}, u32[]{:S(2)}) copy-start(bf16[1,3584]{1,0:T(2,128)(2,1)} %param.18) | copy-start | bytes 21508
  42.5 86.7 %all-gather.2.cloned.1.call-start = ((), (), s32[]{:S(2)}) async-start(), calls=%async_computation.6 | async-start | bytes 2129920 | tf_op jit(solution)/shard_map/all_gather | solution.py:77
  89.9 39.3 %copy-start.2 = (bf16[1024,56]{0,1:T(8,128)(2,1)S(1)}, bf16[1024,56]{0,1:T(8,128)(2,1)}, u32[]{:S(2)}) copy-start(bf16[1024,56]{0,1:T(8,128)(2,1)} %param.23) | copy-start | bytes 344068
  90.7 42.0 %all-to-all-start.3 = ((bf16[64,1,4]{2,1,0:T(2,128)(2,1)}), bf16[64,1,4]{2,1,0:T(2,128)(2,1)S(1)}, u32[]{:S(2)}, u32[]{:S(2)}) async-start(bf16[64,1,4]{2,1,0:T(2,128)(2,1)} %copy.59), calls=%async_computation.3 | async-start | bytes 65536 | tf_op jit(solution)/shard_map/all_to_all | solution.py:105
  132.7 16.9 %all-to-all-start.1 = ((bf16[64,2,448]{2,1,0:T(2,128)(2,1)}), bf16[64,2,448]{2,1,0:T(2,128)(2,1)S(1)}, u32[]{:S(2)}, u32[]{:S(2)}) async-start(bf16[64,2,448]{2,1,0:T(2,128)(2,1)} %reshape.140), calls=%async_computation.1 | async-start | bytes 262144 | tf_op jit(solution)/shard_map/all_to_all | solution.py:106
  147.3 11.0 %copy-start.6 = (s32[128]{0:T(128)S(1)}, s32[128]{0:T(128)}, u32[]{:S(2)}) copy-start(s32[128]{0:T(128)} %copy-done.5) | copy-start | bytes 1540
  149.6 53.7 %all-to-all-start.4 = ((bf16[64,4,3584]{2,1,0:T(4,128)(2,1)}), bf16[64,4,3584]{2,1,0:T(4,128)(2,1)}, u32[]{:S(2)}, u32[]{:S(2)}) async-start(bf16[64,4,3584]{2,1,0:T(4,128)(2,1)} %copy.62), calls=%async_computation.4 | async-start | bytes 3670016 | tf_op jit(solution)/shard_map/all_to_all | solution.py:104
  158.0 89.7 %reduce-scatter.4.cloned.1.call-start = ((), (), s32[]{:S(2)}) async-start(), calls=%async_computation.7 | async-start | bytes 2064384
Sparse Core Ops, SparseCore 0:
  46.7 82.4 all-gather.1
  211.9 35.6 reduce-scatter.3
where the time goes:
time: 261 us; the launch traced here: 256 us
  waiting for transfers between devices  162 us (62%)
  starting transfers between devices  44.2 us (17%)
  local copies, waits for them, and re-layouts  19.4 us (7%)
  matrix products  14.5 us (6%)
  between operations  13.7 us (5%)
  other arithmetic  2.82 us (1%)
    all_to_all x1, waiting for transfers between devices, on_device(): lax.all_to_all(send_rows, 'ep', split_axis=0, concat_axis=0, tiled=True)  45.5 us
    all_to_all x1, waiting for transfers between devices, on_device(): lax.all_to_all(partial_value, 'ep', split_axis=0, concat_axis=0, tiled=True)  42.5 us
    unnamed x3, waiting for transfers between devices  35.8 us
    all_gather x1, waiting for transfers between devices, on_device(): lax.all_gather(flat_values, 'ep', axis=0, tiled=True)  30.6 us
    all_to_all x1, starting transfers between devices, on_device(): lax.all_to_all(send_rows, 'ep', split_axis=0, concat_axis=0, tiled=True)  15.3 us
    all_to_all x1, starting transfers between devices, on_device(): lax.all_to_all(partial_value, 'ep', split_axis=0, concat_axis=0, tiled=True)  8.32 us
    all_to_all x1, starting transfers between devices, on_device(): lax.all_to_all(context, 'tp', split_axis=1, concat_axis=0, tiled=True)  7.65 us
    all_to_all x1, starting transfers between devices, on_device(): lax.all_to_all(attn_cols, 'ep', split_axis=0, concat_axis=0, tiled=True)  6.54 us
  transfers between devices with their start and end apart: 7, of which 6 were waited for; matrix products, arithmetic and copies ran while one was open for 8% of the time, Pallas kernels for 0%

commit v1 on v0

v1 whole, which is shorter than its diff:
```python
import jax
import jax.numpy as jnp
from jax import lax
from jax.experimental import pallas as pl
from jax.experimental.pallas import tpu as pltpu
from jax.sharding import Mesh, PartitionSpec as P

ROUTE_SCALE = 2.5
EPSILON = 1e-06
SCORE_SCALE = 192.0 ** (-0.5)
SLOTS = 4
EP = ("x", "z", "c")
XC = ("x", "c")
NT = (((1,), (1,)), ((), ()))
TN = (((0,), (0,)), ((), ()))
F32 = jnp.float32
BF16 = jnp.bfloat16


def kernel_call(body, outs, *args, smem=(), flops=0):
    in_specs = [
        pl.BlockSpec(memory_space=pltpu.SMEM if i in smem else pltpu.VMEM)
        for i in range(len(args))
    ]
    vmem = pl.BlockSpec(memory_space=pltpu.VMEM)
    nbytes = sum(a.size * a.dtype.itemsize for a in args)
    return pl.pallas_call(
        body,
        out_shape=tuple(jax.ShapeDtypeStruct(s, d) for s, d in outs),
        in_specs=in_specs,
        out_specs=tuple(vmem for _ in outs),
        compiler_params=pltpu.CompilerParams(vmem_limit_bytes=40 << 20),
        cost_estimate=pl.CostEstimate(flops=flops, bytes_accessed=nbytes, transcendentals=0),
    )(*args)


def prepare(hidden_ref, gain_ref, ids_ref, send_ref, place_ref):
    values = hidden_ref[...].astype(F32)
    factor = lax.rsqrt(jnp.mean(values * values, axis=-1, keepdims=True) + EPSILON)
    normalized = (values * factor * gain_ref[...].astype(F32)).astype(BF16)
    slots, rows = place_ref.shape
    slot = lax.broadcasted_iota(jnp.int32, (slots, rows), 0)
    named = jnp.zeros((slots, rows), jnp.bool_)
    for k in range(ids_ref.shape[0]):
        named = named | (ids_ref[k : k + 1, :] == slot // SLOTS)
    named = named.astype(F32)
    earlier = lax.broadcasted_iota(jnp.int32, (rows, rows), 0) < lax.broadcasted_iota(
        jnp.int32, (rows, rows), 1
    )
    rank = jnp.dot(
        named.astype(BF16), earlier.astype(F32).astype(BF16), preferred_element_type=F32
    )
    place = jnp.where(rank == (slot % SLOTS).astype(F32), named, 0.0)
    place_ref[...] = place
    send_ref[...] = jnp.dot(
        place.astype(BF16), normalized, preferred_element_type=F32
    ).astype(BF16)


def attend(lengths_ref, queries_ref, cache_ref, context_ref):
    rows, heads, _ = queries_ref.shape
    latent = context_ref.shape[2]
    groups = context_ref.shape[0]
    found = []
    for r in range(rows):
        keys = cache_ref[r]
        scores = jnp.dot(queries_ref[r], keys, preferred_element_type=F32) * SCORE_SCALE
        positions = lax.broadcasted_iota(jnp.int32, scores.shape, 1)
        scores = jnp.where(positions < lengths_ref[r], scores, -1e30)
        raised = jnp.exp(scores - jnp.max(scores, axis=-1, keepdims=True))
        soft = (raised / jnp.sum(raised, axis=-1, keepdims=True)).astype(BF16)
        context = lax.dot_general(soft, keys[:latent], NT, preferred_element_type=F32)
        found.append(context.reshape(groups, heads // groups, latent))
    context_ref[...] = jnp.concatenate(found, axis=1).astype(BF16)


def lift_heads(context_ref, w_uv_ref, values_ref):
    copies, rows, _ = values_ref.shape
    heads, latent, width = w_uv_ref.shape
    context = context_ref[...].reshape(rows * heads, latent)
    token = lax.broadcasted_iota(jnp.int32, (rows, rows * heads), 0)
    entry = lax.broadcasted_iota(jnp.int32, (rows, rows * heads), 1)
    for h in range(heads):
        lifted = jnp.dot(context, w_uv_ref[h], preferred_element_type=F32).astype(BF16)
        pick = (entry == token * heads + h).astype(F32).astype(BF16)
        mine = jnp.dot(pick, lifted, preferred_element_type=F32).astype(BF16)
        for copy in range(copies):
            values_ref[copy, :, h * width : (h + 1) * width] = mine


def project(values_ref, w_out_ref, parts_ref):
    blocks, rows, depth = values_ref.shape
    slices = parts_ref.shape[1]
    cols = w_out_ref.shape[0] * 2 // slices
    values = values_ref[...].reshape(blocks * rows, depth)
    for s in range(slices // 2):
        part = lax.dot_general(
            values, w_out_ref[s * cols : (s + 1) * cols, :], NT, preferred_element_type=F32
        )
        part = part.astype(BF16).reshape(blocks, rows, cols)
        parts_ref[:, 2 * s, :, :cols] = part
        parts_ref[:, 2 * s + 1, :, :cols] = part


def lift_experts(rows_ref, w_gate_ref, w_up_ref, router_ref, inner_ref, score_ref):
    rows = rows_ref[...]
    gate = jnp.dot(rows, w_gate_ref[...], preferred_element_type=F32)
    lifted = jnp.dot(rows, w_up_ref[...], preferred_element_type=F32)
    column = jnp.broadcast_to(router_ref[...], (128, rows.shape[1]))
    logits = lax.dot_general(rows, column, NT, preferred_element_type=F32)
    inner = (gate / (1.0 + jnp.exp(-gate)) * lifted).astype(BF16)
    for copy in range(inner_ref.shape[0]):
        inner_ref[copy] = inner
    score_ref[...] = (1.0 / (1.0 + jnp.exp(-logits))).astype(BF16)


def lower_experts(inner_ref, w_down_ref, score_ref, back_ref):
    blocks, slots, _ = inner_ref.shape
    width = w_down_ref.shape[2]
    total = jnp.zeros((slots, width), F32)
    for j in range(blocks):
        total += jnp.dot(inner_ref[j], w_down_ref[j], preferred_element_type=F32)
    back_ref[:, :width] = total.astype(BF16)
    back_ref[:, width:] = score_ref[:, : back_ref.shape[1] - width]


def combine(back_ref, place_ref, attn_ref, own_ref, out_ref):
    width = out_ref.shape[1]
    score = back_ref[:, width : width + 1].astype(F32)
    share = place_ref[...] * score
    share = ROUTE_SCALE * share / jnp.sum(share, axis=0, keepdims=True)
    upper = share.astype(BF16)
    lower = (share - upper.astype(F32)).astype(BF16)
    parts = back_ref[:, :width]
    merged = attn_ref[...] + (
        lax.dot_general(upper, parts, TN, preferred_element_type=F32)
        + lax.dot_general(lower, parts, TN, preferred_element_type=F32)
    )
    out_ref[...] = (own_ref[...].astype(F32) + merged).astype(BF16)


def on_device(
    hidden,
    norm_gain,
    queries,
    latent_cache,
    lengths,
    expert_ids,
    router,
    w_gate,
    w_up,
    w_down,
    w_uv,
    w_out,
):
    rows, model_width = hidden.shape
    ep_size = lax.axis_size(EP)
    tp_size = lax.axis_size("y")
    xc_size = lax.axis_size(XC)
    z_size = lax.axis_size("z")
    slots = ep_size * SLOTS
    width = model_width // tp_size
    hidden_units = w_gate.shape[2]
    latent = w_uv.shape[1]
    heads = w_uv.shape[0]
    out_cols, depth = w_out.shape[1], w_out.shape[0]
    tp = lax.axis_index("y")

    send, place = kernel_call(
        prepare,
        [((slots, model_width), BF16), ((slots, rows), F32)],
        hidden,
        norm_gain.reshape(1, model_width),
        expert_ids.T,
    )
    named_rows = lax.all_to_all(
        send.reshape(ep_size, SLOTS, model_width), EP, 0, 0, tiled=True
    ).reshape(slots, model_width)

    (context,) = kernel_call(
        attend,
        [((tp_size, 2 * heads, latent), BF16)],
        lengths,
        queries,
        jnp.swapaxes(latent_cache, 1, 2),
        smem=(0,),
    )
    context = lax.all_to_all(context, "y", 0, 0, tiled=True)

    out_weights = jnp.broadcast_to(w_out.T[None], (xc_size, out_cols, depth))
    out_weights = lax.all_to_all(out_weights, XC, 0, 0, tiled=True)
    out_weights = out_weights.reshape(xc_size * out_cols, depth)
    down = w_down[0].reshape(hidden_units, tp_size, width).transpose(1, 0, 2)
    down = lax.all_to_all(down, "y", 0, 0, tiled=True)

    (values,) = kernel_call(
        lift_heads, [((z_size, rows, heads * w_uv.shape[2]), BF16)], context, w_uv
    )
    values = lax.all_to_all(values, "z", 0, 0, tiled=True)
    (attn_parts,) = kernel_call(
        project, [((z_size, tp_size, rows, 128), BF16)], values, out_weights
    )
    attn_parts = lax.all_to_all(
        attn_parts.reshape(z_size * tp_size, rows, 128), ("z", "y"), 0, 0, tiled=True
    ).reshape(z_size, tp_size, rows, 128)
    half = z_size // 2
    attn_parts = lax.dynamic_slice_in_dim(attn_parts, (tp % 2) * half, half, 0)
    attn_rows = jnp.sum(attn_parts.astype(F32), axis=1)[:, :, : 2 * out_cols]
    attn_rows = attn_rows.transpose(1, 0, 2).reshape(rows, width)

    inner, score = kernel_call(
        lift_experts,
        [((tp_size, slots, hidden_units), BF16), ((slots, 128), BF16)],
        named_rows,
        w_gate[0],
        w_up[0],
        router,
    )
    inner = lax.all_to_all(inner, "y", 0, 0, tiled=True)
    padded = -(-(width + 1) // 128) * 128
    (back,) = kernel_call(
        lower_experts, [((slots, padded), BF16)], inner, down, score
    )
    back = lax.all_to_all(
        back.reshape(ep_size, SLOTS, padded), EP, 0, 0, tiled=True
    ).reshape(slots, padded)
    own = lax.dynamic_slice_in_dim(hidden, tp * width, width, 1)
    (out,) = kernel_call(combine, [((rows, width), BF16)], back, place, attn_rows, own)
    return out


def solution(mesh):
    split = Mesh(mesh.devices.reshape(4, 8, 2, 8), ("x", "z", "c", "y"))
    return jax.shard_map(
        on_device,
        mesh=split,
        in_specs=(
            P(EP, None),
            P(),
            P(EP + ("y",), None, None),
            P(EP + ("y",), None, None),
            P(EP + ("y",)),
            P(EP, None),
            P(EP, None),
            P(EP, None, "y"),
            P(EP, None, "y"),
            P(EP, "y", None),
            P("y", None, None),
            P("y", EP),
        ),
        out_specs=P(EP, "y"),
        check_vma=False,
    )
```

time: 261 us -> 206 us (0.79); the launches traced: 256 us -> 205 us
  waiting for transfers between devices: 162 us -> 107 us
  blocking collectives: 0 us -> 34.6 us
  matrix products: 14.5 us -> 0 us
  between operations: 13.7 us -> 0.19 us
  Pallas kernels: 0 us -> 8.9 us
  starting transfers between devices: 44.2 us -> 38 us
  other arithmetic: 2.82 us -> 0.02 us
  local copies, waits for them, and re-layouts: 19.4 us -> 16.7 us
    unnamed x3 -> x0, waiting for transfers between devices: 35.8 us -> none
    all_to_all x0 -> x2, blocking collectives: none -> 34.6 us  [the longest x1 19.2 us: on_device(): values = lax.all_to_all(values, 'z', 0, 0, tiled=True)]
    all_gather x1 -> x0, waiting for transfers between devices: 30.6 us -> none  [on_device(): lax.all_gather(flat_values, 'ep', axis=0, tiled=True)]
    dot_general x9 -> x0, matrix products: 14.5 us -> none  [the longest x1 3.88 us: expert_terms(): jnp.einsum('bcf,fd->bcd', inner_act, w_down[0], preferred_element_type=jn...]
    all_to_all x5 -> x6, waiting for transfers between devices: 95.1 us -> 107 us  [the longest x1 43.3 us: on_device(): lax.all_to_all(send.reshape(ep_size, SLOTS, model_width), EP, 0, 0, tiled...]
    pallas_call x0 -> x7, Pallas kernels: none -> 8.9 us  [kernel_call(): pl.pallas_call(body, out_shape=tuple((jax.ShapeDtypeStruct(s, d) for s, d...]
    all_to_all x5 -> x6, starting transfers between devices: 43.9 us -> 38 us  [the longest x1 8.85 us: on_device(): lax.all_to_all(attn_parts.reshape(z_size * tp_size, rows, 128), ('z', 'y'...]
    convert_element_type x5 -> x0, local copies, waits for them, and re-layouts: 5.58 us -> none  [the longest x1 4.17 us: expert_terms(): partial_value = partial_value.astype(jnp.bfloat16)]
  transfers between devices with their start and end apart: 7 -> 6, of which waited for: 6 -> 6; matrix products, arithmetic and copies ran while one was open for 8% -> 4% of each run, Pallas kernels for 0% -> 2%
where the time goes in v1:
time: 206 us; the launch traced here: 205 us
  waiting for transfers between devices  107 us (52%)
  starting transfers between devices  38 us (18%)
  blocking collectives  34.6 us (17%)
  local copies, waits for them, and re-layouts  16.7 us (8%)
  Pallas kernels  8.9 us (4%)
    all_to_all x1, waiting for transfers between devices, on_device(): lax.all_to_all(send.reshape(ep_size, SLOTS, model_width), EP, 0, 0, tiled...  43.3 us
    all_to_all x1, blocking collectives, on_device(): values = lax.all_to_all(values, 'z', 0, 0, tiled=True)  19.2 us
    all_to_all x1, waiting for transfers between devices, on_device(): down = lax.all_to_all(down, 'y', 0, 0, tiled=True)  16.4 us
    all_to_all x1, blocking collectives, on_device(): context = lax.all_to_all(context, 'y', 0, 0, tiled=True)  15.4 us
    all_to_all x1, waiting for transfers between devices, on_device(): inner = lax.all_to_all(inner, 'y', 0, 0, tiled=True)  13.8 us
    all_to_all x1, waiting for transfers between devices, on_device(): lax.all_to_all(back.reshape(ep_size, SLOTS, padded), EP, 0, 0, tiled=True)  11.8 us
    all_to_all x1, waiting for transfers between devices, on_device(): out_weights = lax.all_to_all(out_weights, XC, 0, 0, tiled=True)  11.4 us
    all_to_all x1, waiting for transfers between devices, on_device(): lax.all_to_all(attn_parts.reshape(z_size * tp_size, rows, 128), ('z', 'y'...  10 us
  transfers between devices with their start and end apart: 6, of which 6 were waited for; matrix products, arithmetic and copies ran while one was open for 4% of the time, Pallas kernels for 2%

profile of v1, /device:TPU:1, one launch (start us, length us, event | category | flops | bytes accessed | tf_op | source)
XLA Modules:
  0.0 205.0 jit_solution(9447733488595919464)
XLA Ops:
  0.0 1.3 copy-done.3
  2.8 1.5 shard_map.121
  4.4 15.4 %all_to_all.40.context_ref = bf16[8,16,512]{2,1,0:T(8,128)(2,1)S(1)} all-to-all(bf16[8,16,512]{2,1,0:T(8,128)(2,1)S(1)} %shard_map.121), channel_id=1, replica_groups=mesh['x'=4,'z'=8,'c'=2,'y'=8] {'y'}, dimensions={0} | all-to-all | bytes 262144 | tf_op jit(solution)/shard_map/all_to_all | solution.py:188
  19.7 1.5 shard_map.122
  21.2 19.2 %all_to_all.41.values_ref = bf16[8,16,1024]{2,1,0:T(8,128)(2,1)S(1)} all-to-all(bf16[8,16,1024]{2,1,0:T(8,128)(2,1)S(1)} %shard_map.122), channel_id=1, replica_groups=mesh['x'=4,'z'=8,'c'=2,'y'=8] {'z'}, dimensions={0} | all-to-all | bytes 524288 | tf_op jit(solution)/shard_map/all_to_all | solution.py:199
  41.5 7.9 %all-to-all-start.6 = ((bf16[8,56,1024]{2,1,0:T(8,128)(2,1)}), bf16[8,56,1024]{2,1,0:T(8,128)(2,1)S(1)}, u32[]{:S(2)}, u32[]{:S(2)}) async-start(bf16[8,56,1024]{2,1,0:T(8,128)(2,1)} %broadcast_in_dim.2), calls=%async_computation.6 | async-start | bytes 1835008 | tf_op jit(solution)/shard_map/all_to_all | solution.py:191
  50.2 1.5 reshape.29
  51.8 11.4 %all-to-all-done.6 = bf16[8,56,1024]{2,1,0:T(8,128)(2,1)S(1)} async-done(((bf16[8,56,1024]{2,1,0:T(8,128)(2,1)}), bf16[8,56,1024]{2,1,0:T(8,128)(2,1)S(1)}, u32[]{:S(2)}, u32[]{:S(2)}) %all-to-all-start.6) | async-done | bytes 917536 | tf_op jit(solution)/shard_map/all_to_all | solution.py:191
  63.1 5.0 %all-to-all-start = ((bf16[64,4,3584]{2,1,0:T(4,128)(2,1)}), bf16[64,4,3584]{2,1,0:T(4,128)(2,1)S(1)}, u32[]{:S(2)}, u32[]{:S(2)}) async-start(bf16[64,4,3584]{2,1,0:T(4,128)(2,1)} %reshape.29), calls=%async_computation | async-start | bytes 3670016 | tf_op jit(solution)/shard_map/all_to_all | solution.py:176
  68.1 2.2 %copy.15 = bf16[1,128,3584]{1,2,0:T(8,128)(2,1)} copy(bf16[1,128,3584]{2,1,0:T(8,128)(2,1)} %param.21) | data formatting | bytes 1835008 | tf_op args[9]
  70.3 43.3 %all-to-all-done = bf16[64,4,3584]{2,1,0:T(4,128)(2,1)S(1)} async-done(((bf16[64,4,3584]{2,1,0:T(4,128)(2,1)}), bf16[64,4,3584]{2,1,0:T(4,128)(2,1)S(1)}, u32[]{:S(2)}, u32[]{:S(2)}) %all-to-all-start) | async-done | bytes 1835040 | tf_op jit(solution)/shard_map/all_to_all | solution.py:176
  113.6 1.3 copy-done.9
  114.9 4.2 %all-to-all-start.2 = ((bf16[8,128,448]{1,2,0:T(8,128)(2,1)}), bf16[8,128,448]{1,2,0:T(8,128)(2,1)}, u32[]{:S(2)}, u32[]{:S(2)}) async-start(bf16[8,128,448]{1,2,0:T(8,128)(2,1)} %bitcast.18), calls=%async_computation.2 | async-start | bytes 1835008 | tf_op jit(solution)/shard_map/all_to_all | solution.py:194
  119.1 2.9 %reshape.30.rows_ref = bf16[256,3584]{1,0:T(8,128)(2,1)S(1)} reshape(bf16[64,4,3584]{2,1,0:T(4,128)(2,1)} %copy-done.9) | data formatting | bytes 3670016 | tf_op jit(solution)/shard_map/reshape | solution.py:178
  123.3 1.2 copy-done.2
  124.5 2.4 %shard_map.119 = (bf16[8,256,128]{2,1,0:T(8,128)(2,1)}, bf16[256,128]{1,0:T(8,128)(2,1)S(1)}) custom-call(bf16[256,3584]{1,0:T(8,128)(2,1)S(1)} %reshape.30.rows_ref, bf16[3584,128]{1,0:T(8,128)(2,1)S(1)} %bitcast.14, bf16[3584,128]{1,0:T(8,128)(2,1)S(1)} %bitcast.15, bf16[1,3584]{1,0:T(2,128)(2,1)S(1)} %copy-done.6), custom_call_target="tpu_custom_call" | custom-call | bytes 3677184 | tf_op jit(solution)/shard_map/pallas_call | solution.py:27
  126.9 16.4 %all-to-all-done.2 = bf16[8,128,448]{1,2,0:T(8,128)(2,1)} async-done(((bf16[8,128,448]{1,2,0:T(8,128)(2,1)}), bf16[8,128,448]{1,2,0:T(8,128)(2,1)}, u32[]{:S(2)}, u32[]{:S(2)}) %all-to-all-start.2) | async-done | bytes 917536 | tf_op jit(solution)/shard_map/all_to_all | solution.py:194
  143.2 3.6 %all-to-all-start.1 = ((bf16[8,256,128]{2,1,0:T(8,128)(2,1)}), bf16[8,256,128]{2,1,0:T(8,128)(2,1)S(1)}, u32[]{:S(2)}, u32[]{:S(2)}) async-start(bf16[8,256,128]{2,1,0:T(8,128)(2,1)} %get-tuple-element.10), calls=%async_computation.1 | async-start | bytes 1048576 | tf_op jit(solution)/shard_map/all_to_all | solution.py:219
  148.0 13.8 %all-to-all-done.1.inner_ref = bf16[8,256,128]{2,1,0:T(8,128)(2,1)S(1)} async-done(((bf16[8,256,128]{2,1,0:T(8,128)(2,1)}), bf16[8,256,128]{2,1,0:T(8,128)(2,1)S(1)}, u32[]{:S(2)}, u32[]{:S(2)}) %all-to-all-start.1) | async-done | bytes 524320 | tf_op jit(solution)/shard_map/all_to_all | solution.py:219
  161.8 8.8 %all-to-all-start.7 = ((bf16[64,16,128]{2,1,0:T(8,128)(2,1)}), bf16[64,16,128]{2,1,0:T(8,128)(2,1)S(1)}, u32[]{:S(2)}, u32[]{:S(2)}) async-start(bf16[64,16,128]{2,1,0:T(8,128)(2,1)} %bitcast.8), calls=%async_computation.7 | async-start | bytes 524288 | tf_op jit(solution)/shard_map/all_to_all | solution.py:203
  170.6 1.5 copy.16.w_down_ref
  173.6 10.0 %all-to-all-done.7 = bf16[64,16,128]{2,1,0:T(8,128)(2,1)S(1)} async-done(((bf16[64,16,128]{2,1,0:T(8,128)(2,1)}), bf16[64,16,128]{2,1,0:T(8,128)(2,1)S(1)}, u32[]{:S(2)}, u32[]{:S(2)}) %all-to-all-start.7) | async-done | bytes 262176 | tf_op jit(solution)/shard_map/all_to_all | solution.py:203
  183.6 8.4 %all-to-all-start.3 = ((bf16[64,4,512]{2,1,0:T(4,128)(2,1)}), bf16[64,4,512]{2,1,0:T(4,128)(2,1)S(1)}, u32[]{:S(2)}, u32[]{:S(2)}) async-start(bf16[64,4,512]{2,1,0:T(4,128)(2,1)} %reshape.31), calls=%async_computation.3 | async-start | bytes 524288 | tf_op jit(solution)/shard_map/all_to_all | solution.py:224
  192.2 11.8 %all-to-all-done.3 = bf16[64,4,512]{2,1,0:T(4,128)(2,1)S(1)} async-done(((bf16[64,4,512]{2,1,0:T(4,128)(2,1)}), bf16[64,4,512]{2,1,0:T(4,128)(2,1)S(1)}, u32[]{:S(2)}, u32[]{:S(2)}) %all-to-all-start.3) | async-done | bytes 262176 | tf_op jit(solution)/shard_map/all_to_all | solution.py:224
  (34 shorter events, 8.4 us)
Async XLA Ops:
  0.0 19.7 %copy-start = (bf16[8,512,128]{2,1,0:T(8,128)(2,1)S(1)}, bf16[8,512,128]{2,1,0:T(8,128)(2,1)}, u32[]{:S(2)}) copy-start(bf16[8,512,128]{2,1,0:T(8,128)(2,1)} %w_uv_ref.1) | copy-start | bytes 3145732
  0.0 1.3 copy-start.3
  1.3 0.9 copy-start.4
  2.2 0.7 copy-start.8
  2.8 37.6 %copy-start.10 = (bf16[1024,56]{0,1:T(8,128)(2,1)S(1)}, bf16[1024,56]{0,1:T(8,128)(2,1)}, u32[]{:S(2)}) copy-start(bf16[1024,56]{0,1:T(8,128)(2,1)} %param.23) | copy-start | bytes 344068
  21.2 28.2 %copy-start.11 = (bf16[3584]{0:T(1024)(128)(2,1)S(1)}, bf16[3584]{0:T(1024)(128)(2,1)}, u32[]{:S(2)}) copy-start(bf16[3584]{0:T(1024)(128)(2,1)} %param.13) | copy-start | bytes 21508
  21.2 28.2 %copy-start.5 = (bf16[16,3584]{1,0:T(8,128)(2,1)S(1)}, bf16[16,3584]{1,0:T(8,128)(2,1)}, u32[]{:S(2)}) copy-start(bf16[16,3584]{1,0:T(8,128)(2,1)} %hidden_ref.1) | copy-start | bytes 344068
  21.2 28.2 %copy-start.7 = (s32[16,8]{0,1:T(8,128)S(1)}, s32[16,8]{0,1:T(8,128)}, u32[]{:S(2)}) copy-start(s32[16,8]{0,1:T(8,128)} %param.17) | copy-start | bytes 1540
  41.5 21.6 %all-to-all-start.6 = ((bf16[8,56,1024]{2,1,0:T(8,128)(2,1)}), bf16[8,56,1024]{2,1,0:T(8,128)(2,1)S(1)}, u32[]{:S(2)}, u32[]{:S(2)}) async-start(bf16[8,56,1024]{2,1,0:T(8,128)(2,1)} %broadcast_in_dim.2), calls=%async_computation.6 | async-start | bytes 1835008 | tf_op jit(solution)/shard_map/all_to_all | solution.py:191
  63.1 50.5 %all-to-all-start = ((bf16[64,4,3584]{2,1,0:T(4,128)(2,1)}), bf16[64,4,3584]{2,1,0:T(4,128)(2,1)S(1)}, u32[]{:S(2)}, u32[]{:S(2)}) async-start(bf16[64,4,3584]{2,1,0:T(4,128)(2,1)} %reshape.29), calls=%async_computation | async-start | bytes 3670016 | tf_op jit(solution)/shard_map/all_to_all | solution.py:176
  113.6 1.3 copy-start.9
  114.9 28.3 %all-to-all-start.2 = ((bf16[8,128,448]{1,2,0:T(8,128)(2,1)}), bf16[8,128,448]{1,2,0:T(8,128)(2,1)}, u32[]{:S(2)}, u32[]{:S(2)}) async-start(bf16[8,128,448]{1,2,0:T(8,128)(2,1)} %bitcast.18), calls=%async_computation.2 | async-start | bytes 1835008 | tf_op jit(solution)/shard_map/all_to_all | solution.py:194
  119.1 3.0 %copy-start.6 = (bf16[1,3584]{1,0:T(2,128)(2,1)S(1)}, bf16[1,3584]{1,0:T(2,128)(2,1)}, u32[]{:S(2)}) copy-start(bf16[1,3584]{1,0:T(2,128)(2,1)} %router_ref.1) | copy-start | bytes 21508
  122.1 1.2 copy-start.1
  123.3 1.2 copy-start.2
  143.2 18.5 %all-to-all-start.1 = ((bf16[8,256,128]{2,1,0:T(8,128)(2,1)}), bf16[8,256,128]{2,1,0:T(8,128)(2,1)S(1)}, u32[]{:S(2)}, u32[]{:S(2)}) async-start(bf16[8,256,128]{2,1,0:T(8,128)(2,1)} %get-tuple-element.10), calls=%async_computation.1 | async-start | bytes 1048576 | tf_op jit(solution)/shard_map/all_to_all | solution.py:219
  161.8 21.8 %all-to-all-start.7 = ((bf16[64,16,128]{2,1,0:T(8,128)(2,1)}), bf16[64,16,128]{2,1,0:T(8,128)(2,1)S(1)}, u32[]{:S(2)}, u32[]{:S(2)}) async-start(bf16[64,16,128]{2,1,0:T(8,128)(2,1)} %bitcast.8), calls=%async_computation.7 | async-start | bytes 524288 | tf_op jit(solution)/shard_map/all_to_all | solution.py:203
  183.6 20.4 %all-to-all-start.3 = ((bf16[64,4,512]{2,1,0:T(4,128)(2,1)}), bf16[64,4,512]{2,1,0:T(4,128)(2,1)S(1)}, u32[]{:S(2)}, u32[]{:S(2)}) async-start(bf16[64,4,512]{2,1,0:T(4,128)(2,1)} %reshape.31), calls=%async_computation.3 | async-start | bytes 524288 | tf_op jit(solution)/shard_map/all_to_all | solution.py:224

commit v2 on v1

v2 whole, which is shorter than its diff:
```python
import jax
import jax.numpy as jnp
from jax import lax
from jax.experimental import pallas as pl
from jax.experimental.pallas import tpu as pltpu
from jax.sharding import Mesh, PartitionSpec as P

ROUTE_SCALE = 2.5
EPSILON = 1e-06
SCORE_SCALE = 192.0 ** (-0.5)
SLOTS = 4
EP = ("x", "zh", "zl", "c")
TP, X, ZH, ZL, CORE = range(5)
PADDED = 512
ATTN = 224
NT = (((1,), (1,)), ((), ()))
TN = (((0,), (0,)), ((), ()))
F32 = jnp.float32
BF16 = jnp.bfloat16


def kernel_call(body, outs, *args, smem=(), flops=0):
    in_specs = [
        pl.BlockSpec(memory_space=pltpu.SMEM if i in smem else pltpu.VMEM)
        for i in range(len(args))
    ]
    vmem = pl.BlockSpec(memory_space=pltpu.VMEM)
    nbytes = sum(a.size * a.dtype.itemsize for a in args)
    return pl.pallas_call(
        body,
        out_shape=tuple(jax.ShapeDtypeStruct(s, d) for s, d in outs),
        in_specs=in_specs,
        out_specs=tuple(vmem for _ in outs),
        compiler_params=pltpu.CompilerParams(vmem_limit_bytes=40 << 20),
        cost_estimate=pl.CostEstimate(flops=flops, bytes_accessed=nbytes, transcendentals=0),
    )(*args)


def prepare(hidden_ref, gain_ref, ids_ref, send_ref, place_ref):
    values = hidden_ref[...].astype(F32)
    factor = lax.rsqrt(jnp.mean(values * values, axis=-1, keepdims=True) + EPSILON)
    normalized = (values * factor * gain_ref[...].astype(F32)).astype(BF16)
    slots, rows = place_ref.shape
    slot = lax.broadcasted_iota(jnp.int32, (slots, rows), 0)
    named = jnp.zeros((slots, rows), jnp.bool_)
    for k in range(ids_ref.shape[0]):
        named = named | (ids_ref[k : k + 1, :] == slot // SLOTS)
    named = named.astype(F32)
    earlier = lax.broadcasted_iota(jnp.int32, (rows, rows), 0) < lax.broadcasted_iota(
        jnp.int32, (rows, rows), 1
    )
    rank = jnp.dot(
        named.astype(BF16), earlier.astype(F32).astype(BF16), preferred_element_type=F32
    )
    place = jnp.where(rank == (slot % SLOTS).astype(F32), named, 0.0)
    place_ref[...] = place
    send_ref[...] = jnp.dot(
        place.astype(BF16), normalized, preferred_element_type=F32
    ).astype(BF16)


def attend(place_ref, lengths_ref, queries_ref, cache_ref, context_ref):
    rows, heads, _ = queries_ref.shape
    groups, _, latent = context_ref.shape
    found = []
    for r in range(rows):
        keys = cache_ref[r]
        scores = jnp.dot(queries_ref[r], keys, preferred_element_type=F32) * SCORE_SCALE
        positions = lax.broadcasted_iota(jnp.int32, scores.shape, 1)
        scores = jnp.where(positions < lengths_ref[r], scores, -1e30)
        raised = jnp.exp(scores - jnp.max(scores, axis=-1, keepdims=True))
        soft = (raised / jnp.sum(raised, axis=-1, keepdims=True)).astype(BF16)
        context = lax.dot_general(soft, keys[:latent], NT, preferred_element_type=F32)
        found.append(context.reshape(groups, heads // groups, latent))
    found = jnp.concatenate(found, axis=1).astype(BF16)
    for g in range(groups):
        context_ref[(g - place_ref[TP] + groups) % groups] = found[g]


def lift_heads(place_ref, *refs):
    *parts, w_uv_ref, values_ref = refs
    heads, _, width = w_uv_ref.shape
    rows = values_ref.shape[0]
    share = rows // len(parts)
    context = jnp.concatenate([part[...] for part in parts], axis=0)
    token = lax.broadcasted_iota(jnp.int32, (rows, rows * heads), 0)
    entry = lax.broadcasted_iota(jnp.int32, (rows, rows * heads), 1)
    source = (place_ref[TP] - entry // (share * heads) + len(parts)) % len(parts)
    named = source * share + entry // heads % share
    for h in range(heads):
        lifted = jnp.dot(context, w_uv_ref[h], preferred_element_type=F32).astype(BF16)
        pick = ((token == named) & (entry % heads == h)).astype(F32).astype(BF16)
        mine = jnp.dot(pick, lifted, preferred_element_type=F32).astype(BF16)
        values_ref[:, h * width : (h + 1) * width] = mine


def project(place_ref, *refs):
    *parts, out_ref = refs
    values = [part[...] for part in parts[:4]]
    depth = values[0].shape[2]
    values = jnp.concatenate([part.reshape(-1, depth) for part in values], axis=0)
    for k in range(4):
        for j in range(2):
            weights = parts[4 + k][j]
            part = lax.dot_general(values, weights, NT, preferred_element_type=F32)
            x = (place_ref[X] - k + 4) % 4
            half = (place_ref[ZH] + j) % 2
            out_ref[x * 2 + half] = jnp.concatenate(
                [part, jnp.zeros((part.shape[0], 128 - part.shape[1]), F32)], axis=1
            ).astype(BF16)


def lift_experts(rows_ref, w_gate_ref, w_up_ref, router_ref, attn_ref, inner_ref, score_ref):
    rows = rows_ref[...]
    slots = rows.shape[0]
    gate = jnp.dot(rows, w_gate_ref[...], preferred_element_type=F32)
    lifted = jnp.dot(rows, w_up_ref[...], preferred_element_type=F32)
    column = jnp.broadcast_to(router_ref[...], (128, rows.shape[1]))
    logits = lax.dot_general(rows, column, NT, preferred_element_type=F32)
    inner = (gate / (1.0 + jnp.exp(-gate)) * lifted).astype(BF16)
    for copy in range(inner_ref.shape[0]):
        inner_ref[copy, :slots] = inner
        inner_ref[copy, slots:] = attn_ref[copy]
    score_ref[...] = (1.0 / (1.0 + jnp.exp(-logits))).astype(BF16)


def one_hot(condition):
    return condition.astype(F32).astype(BF16)


def iotas(*shape):
    return lax.broadcasted_iota(jnp.int32, shape, 0), lax.broadcasted_iota(jnp.int32, shape, 1)


def lower_experts(place_ref, *refs):
    inner_ref, *parts, score_ref, back_ref = refs
    sources, _, _ = inner_ref.shape
    slots, _ = back_ref.shape
    width = parts[0].shape[1]
    total = jnp.zeros((slots, width), F32)
    for k in range(sources):
        source = (place_ref[TP] - k + sources) % sources
        total += jnp.dot(inner_ref[source, :slots], parts[k][...], preferred_element_type=F32)
    back_ref[:, :width] = total.astype(BF16)
    back_ref[:, width:PADDED] = score_ref[:, : PADDED - width]
    attn = jnp.zeros((inner_ref.shape[1] - slots, 128), F32)
    for k in range(sources):
        attn += inner_ref[k, slots:].astype(F32)
    attn = attn.astype(BF16)
    tokens = attn.shape[0]
    cols = ATTN // 4
    row, entry = iotas(tokens // 4, tokens)
    zl, core = row // 8, row // 4 % 2
    held = ((place_ref[ZL] - zl + 4) % 4) * 2 + (place_ref[CORE] - core + 2) % 2
    lane_in, lane_out = iotas(128, ATTN)
    packed = jnp.zeros((tokens // 4, ATTN), F32)
    for q in range(4):
        pick = one_hot(entry == held * 16 + row % 4 * 4 + q)
        mine = jnp.dot(pick, attn, preferred_element_type=F32).astype(BF16)
        spread = one_hot((lane_out == lane_in + q * cols) & (lane_in < cols))
        packed += jnp.dot(mine, spread, preferred_element_type=F32)
    packed = packed.astype(BF16)
    for copy in range(slots * 4 // tokens):
        back_ref[copy * tokens // 4 : (copy + 1) * tokens // 4, PADDED:] = packed


def combine(place_ref, back_ref, slot_ref, own_ref, out_ref):
    rows, width = out_ref.shape
    score = back_ref[:, width : width + 1].astype(F32)
    share = slot_ref[...] * score
    share = ROUTE_SCALE * share / jnp.sum(share, axis=0, keepdims=True)
    upper = share.astype(BF16)
    lower = (share - upper.astype(F32)).astype(BF16)
    parts = back_ref[:, :width]
    merged = lax.dot_general(upper, parts, TN, preferred_element_type=F32) + lax.dot_general(
        lower, parts, TN, preferred_element_type=F32
    )
    first = pl.multiple_of((place_ref[X] * 2 + place_ref[ZH]) * 32, 32)
    packed = back_ref[pl.ds(first, 32), PADDED:]
    cols = ATTN // 4
    lane_in, lane_out = iotas(ATTN, width)
    row, lane = iotas(32, width)
    token, entry = iotas(rows, 32)
    for q in range(4):
        spread = one_hot((lane_out % cols + q * cols == lane_in))
        mine = jnp.dot(packed, spread, preferred_element_type=F32)
        mine = jnp.where(lane // cols == row // 4, mine, 0.0).astype(BF16)
        pick = one_hot(token == entry % 4 * 4 + q)
        merged += jnp.dot(pick, mine, preferred_element_type=F32)
    out_ref[...] = (own_ref[...].astype(F32) + merged).astype(BF16)


def shift(value, axis, k):
    size = lax.axis_size(axis)
    return lax.ppermute(value, axis, [(i, (i + k) % size) for i in range(size)])


def spread(blocks, axis):
    return [blocks[0]] + [shift(blocks[k], axis, k) for k in range(1, lax.axis_size(axis))]


def gather(value, first, second):
    pair = jnp.stack([value, shift(value, first, 1)])
    return [pair] + [shift(pair, second, k) for k in range(1, lax.axis_size(second))]


def on_device(
    hidden,
    norm_gain,
    queries,
    latent_cache,
    lengths,
    expert_ids,
    router,
    w_gate,
    w_up,
    w_down,
    w_uv,
    w_out,
):
    rows, model_width = hidden.shape
    ep_size = lax.axis_size(EP)
    tp_size = lax.axis_size("y")
    slots = ep_size * SLOTS
    width = model_width // tp_size
    hidden_units = w_gate.shape[2]
    heads, latent, value_width = w_uv.shape
    out_cols, depth = w_out.shape[1], w_out.shape[0]
    here = jnp.stack([lax.axis_index(a) for a in ("y", "x", "zh", "zl", "c")]).astype(jnp.int32)
    tp = here[0]

    send, place = kernel_call(
        prepare,
        [((slots, model_width), BF16), ((slots, rows), F32)],
        hidden,
        norm_gain.reshape(1, model_width),
        expert_ids.T,
    )
    named_rows = lax.all_to_all(
        send.reshape(ep_size, SLOTS, model_width), EP, 0, 0, tiled=True
    ).reshape(slots, model_width)

    (context,) = kernel_call(
        attend,
        [((tp_size, 2 * heads, latent), BF16)],
        here,
        lengths,
        queries,
        jnp.swapaxes(latent_cache, 1, 2),
        smem=(0, 1),
    )
    context = spread(context, "y")
    (values,) = kernel_call(
        lift_heads, [((rows, depth), BF16)], here, *context, w_uv, smem=(0,)
    )
    values = gather(values, "c", "zl")
    out_weights = gather(w_out.T, "zh", "x")
    (attn_parts,) = kernel_call(
        project, [((tp_size, rows * 8, 128), BF16)], here, *values, *out_weights, smem=(0,)
    )

    down = w_down[0].reshape(hidden_units, tp_size, width).transpose(1, 0, 2)
    down = [lax.dynamic_index_in_dim(down, (tp + k) % tp_size, 0, False) for k in range(tp_size)]
    down = spread(down, "y")

    inner, score = kernel_call(
        lift_experts,
        [((tp_size, slots + rows * 8, hidden_units), BF16), ((slots, 128), BF16)],
        named_rows,
        w_gate[0],
        w_up[0],
        router,
        attn_parts,
    )
    inner = lax.all_to_all(inner, "y", 0, 0, tiled=True)
    (back,) = kernel_call(
        lower_experts,
        [((slots, PADDED + ATTN), BF16)],
        here,
        inner,
        *down,
        score,
        smem=(0,),
    )
    back = lax.all_to_all(
        back.reshape(ep_size, SLOTS, PADDED + ATTN), EP, 0, 0, tiled=True
    ).reshape(slots, PADDED + ATTN)
    own = lax.dynamic_slice_in_dim(hidden, tp * width, width, 1)
    (out,) = kernel_call(
        combine, [((rows, width), BF16)], here, back, place, own, smem=(0,)
    )
    return out


def solution(mesh):
    split = Mesh(mesh.devices.reshape(4, 2, 4, 2, 8), ("x", "zh", "zl", "c", "y"))
    return jax.shard_map(
        on_device,
        mesh=split,
        in_specs=(
            P(EP, None),
            P(),
            P(EP + ("y",), None, None),
            P(EP + ("y",), None, None),
            P(EP + ("y",)),
            P(EP, None),
            P(EP, None),
            P(EP, None, "y"),
            P(EP, None, "y"),
            P(EP, "y", None),
            P("y", None, None),
            P("y", EP),
        ),
        out_specs=P(EP, "y"),
        check_vma=False,
    )
```

time: 206 us -> 180 us (0.87)
  starting transfers between devices: 38 us -> 121 us
  waiting for transfers between devices: 107 us -> 32.7 us
  blocking collectives: 34.6 us -> 0 us
  local copies, waits for them, and re-layouts: 16.7 us -> 13.7 us
    ppermute x0 -> x22, starting transfers between devices: none -> 87 us  [shift(): return lax.ppermute(value, axis, [(i, (i + k) % size) for i in range(size)])]
    all_to_all x1, waiting for transfers between devices: 43.3 us -> 0.01 us  [on_device(): lax.all_to_all(send.reshape(ep_size, SLOTS, model_width), EP, 0, 0, tiled...]
    all_to_all x4 -> x1, waiting for transfers between devices: 49.5 us -> 13.8 us  [on_device(): lax.all_to_all(back.reshape(ep_size, SLOTS, PADDED + ATTN), EP, 0, 0, til...]
    all_to_all x2 -> x0, blocking collectives: 34.6 us -> none  [the longest x1 19.2 us: on_device(): values = lax.all_to_all(values, 'z', 0, 0, tiled=True)]
    ppermute x0 -> x22, waiting for transfers between devices: none -> 18.9 us  [shift(): return lax.ppermute(value, axis, [(i, (i + k) % size) for i in range(size)])]
    all_to_all x4 -> x1, starting transfers between devices: 29.4 us -> 11.9 us  [on_device(): lax.all_to_all(back.reshape(ep_size, SLOTS, PADDED + ATTN), EP, 0, 0, til...]
    all_to_all x1, waiting for transfers between devices: 13.8 us -> 0.01 us  [on_device(): inner = lax.all_to_all(inner, 'y', 0, 0, tiled=True)]
    all_to_all x1, starting transfers between devices: 4.99 us -> 15.1 us  [on_device(): lax.all_to_all(send.reshape(ep_size, SLOTS, model_width), EP, 0, 0, tiled...]
  transfers between devices with their start and end apart: 6 -> 25, of which waited for: 6 -> 8; matrix products, arithmetic and copies ran while one was open for 4% -> 1% of each run, Pallas kernels for 2% -> 3%
where the time goes in v2:
time: 180 us; the launch traced here: 179 us
  starting transfers between devices  121 us (67%)
  waiting for transfers between devices  32.7 us (18%)
  local copies, waits for them, and re-layouts  13.7 us (8%)
  Pallas kernels  10.6 us (6%)
    ppermute x22, starting transfers between devices, shift(): return lax.ppermute(value, axis, [(i, (i + k) % size) for i in range(size)])  87 us
    ppermute x22, waiting for transfers between devices, shift(): return lax.ppermute(value, axis, [(i, (i + k) % size) for i in range(size)])  18.9 us
    all_to_all x1, starting transfers between devices, on_device(): lax.all_to_all(send.reshape(ep_size, SLOTS, model_width), EP, 0, 0, tiled...  15.1 us
    all_to_all x1, waiting for transfers between devices, on_device(): lax.all_to_all(back.reshape(ep_size, SLOTS, PADDED + ATTN), EP, 0, 0, til...  13.8 us
    all_to_all x1, starting transfers between devices, on_device(): lax.all_to_all(back.reshape(ep_size, SLOTS, PADDED + ATTN), EP, 0, 0, til...  11.9 us
    pallas_call x7, Pallas kernels, kernel_call(): pl.pallas_call(body, out_shape=tuple((jax.ShapeDtypeStruct(s, d) for s, d...  10.6 us
    all_to_all x1, starting transfers between devices, on_device(): inner = lax.all_to_all(inner, 'y', 0, 0, tiled=True)  6.95 us
    unnamed x33, local copies, waits for them, and re-layouts  5.57 us
  transfers between devices with their start and end apart: 25, of which 8 were waited for; matrix products, arithmetic and copies ran while one was open for 1% of the time, Pallas kernels for 3%

profile of v2, /device:TPU:1, one launch (start us, length us, event | category | flops | bytes accessed | tf_op | source)
XLA Modules:
  0.0 178.6 jit_solution(15106258530251116813)
XLA Ops:
  5.2 15.1 %all-to-all-start = ((bf16[64,4,3584]{2,1,0:T(4,128)(2,1)}), bf16[64,4,3584]{2,1,0:T(4,128)(2,1)}, u32[]{:S(2)}, u32[]{:S(2)}) async-start(bf16[64,4,3584]{2,1,0:T(4,128)(2,1)} %reshape.32), calls=%async_computation | async-start | bytes 3670016 | tf_op jit(solution)/shard_map/all_to_all | solution.py:239
  20.4 7.2 %collective-permute-start.11 = (bf16[56,1024]{1,0:T(8,128)(2,1)S(1)}, bf16[56,1024]{1,0:T(8,128)(2,1)S(1)}, u32[]{:S(2)}, u32[]{:S(2)}) collective-permute-start(bf16[56,1024]{1,0:T(8,128)(2,1)S(1)} %bitcast.54), channel_id=1, source_target_pairs={{0,64},{64,0},{1,65},{65,1},{2,66},{66,2},{3,67},{67,3},{4,68},{68... | collective-permute-start | bytes 344072 | tf_op jit(solution)/shard_map/ppermute | solution.py:195
  29.2 3.2 %collective-permute-start = (bf16[16,512]{1,0:T(8,128)(2,1)S(1)}, bf16[16,512]{1,0:T(8,128)(2,1)S(1)}, u32[]{:S(2)}, u32[]{:S(2)}) collective-permute-start(bf16[16,512]{1,0:T(8,128)(2,1)S(1)} %get-tuple-element.27), channel_id=1, source_target_pairs={{0,1},{1,2},{2,3},{3,4},{4,5},{5,6},{6,7},{7,0},{8,9},{9,10},{10,1... | collective-permute-start | bytes 49160 | tf_op jit(solution)/shard_map/ppermute | solution.py:195
  32.5 4.2 %collective-permute-start.1 = (bf16[16,512]{1,0:T(8,128)(2,1)S(1)}, bf16[16,512]{1,0:T(8,128)(2,1)S(1)}, u32[]{:S(2)}, u32[]{:S(2)}) collective-permute-start(bf16[16,512]{1,0:T(8,128)(2,1)S(1)} %get-tuple-element.26), channel_id=1, source_target_pairs={{0,2},{1,3},{2,4},{3,5},{4,6},{5,7},{6,0},{7,1},{8,10},{9,11},{10,... | collective-permute-start | bytes 49160 | tf_op jit(solution)/shard_map/ppermute | solution.py:195
  36.7 4.6 %collective-permute-start.2 = (bf16[16,512]{1,0:T(8,128)(2,1)S(1)}, bf16[16,512]{1,0:T(8,128)(2,1)S(1)}, u32[]{:S(2)}, u32[]{:S(2)}) collective-permute-start(bf16[16,512]{1,0:T(8,128)(2,1)S(1)} %get-tuple-element.25), channel_id=1, source_target_pairs={{0,3},{1,4},{2,5},{3,6},{4,7},{5,0},{6,1},{7,2},{8,11},{9,12},{10,... | collective-permute-start | bytes 49160 | tf_op jit(solution)/shard_map/ppermute | solution.py:195
  41.3 3.5 %collective-permute-start.3 = (bf16[16,512]{1,0:T(8,128)(2,1)S(1)}, bf16[16,512]{1,0:T(8,128)(2,1)S(1)}, u32[]{:S(2)}, u32[]{:S(2)}) collective-permute-start(bf16[16,512]{1,0:T(8,128)(2,1)S(1)} %get-tuple-element.24), channel_id=1, source_target_pairs={{0,4},{1,5},{2,6},{3,7},{4,0},{5,1},{6,2},{7,3},{8,12},{9,13},{10,... | collective-permute-start | bytes 49160 | tf_op jit(solution)/shard_map/ppermute | solution.py:195
  44.9 4.9 %collective-permute-start.4 = (bf16[16,512]{1,0:T(8,128)(2,1)S(1)}, bf16[16,512]{1,0:T(8,128)(2,1)S(1)}, u32[]{:S(2)}, u32[]{:S(2)}) collective-permute-start(bf16[16,512]{1,0:T(8,128)(2,1)S(1)} %get-tuple-element.23), channel_id=1, source_target_pairs={{0,5},{1,6},{2,7},{3,0},{4,1},{5,2},{6,3},{7,4},{8,13},{9,14},{10,... | collective-permute-start | bytes 49160 | tf_op jit(solution)/shard_map/ppermute | solution.py:195
  49.8 5.0 %collective-permute-start.5 = (bf16[16,512]{1,0:T(8,128)(2,1)S(1)}, bf16[16,512]{1,0:T(8,128)(2,1)S(1)}, u32[]{:S(2)}, u32[]{:S(2)}) collective-permute-start(bf16[16,512]{1,0:T(8,128)(2,1)S(1)} %get-tuple-element.22), channel_id=1, source_target_pairs={{0,6},{1,7},{2,0},{3,1},{4,2},{5,3},{6,4},{7,5},{8,14},{9,15},{10,... | collective-permute-start | bytes 49160 | tf_op jit(solution)/shard_map/ppermute | solution.py:195
  61.6 5.0 %collective-permute-start.7 = (bf16[16,1024]{1,0:T(8,128)(2,1)S(1)}, bf16[16,1024]{1,0:T(8,128)(2,1)S(1)}, u32[]{:S(2)}, u32[]{:S(2)}) collective-permute-start(bf16[16,1024]{1,0:T(8,128)(2,1)S(1)} %shard_map.120), channel_id=1, source_target_pairs={{0,8},{8,0},{1,9},{9,1},{2,10},{10,2},{3,11},{11,3},{4,12},{12,4},... | collective-permute-start | bytes 98312 | tf_op jit(solution)/shard_map/ppermute | solution.py:195
  66.6 4.0 %collective-permute-done.11 = bf16[56,1024]{1,0:T(8,128)(2,1)S(1)} collective-permute-done((bf16[56,1024]{1,0:T(8,128)(2,1)S(1)}, bf16[56,1024]{1,0:T(8,128)(2,1)S(1)}, u32[]{:S(2)}, u32[]{:S(2)}) %collective-permute-start.11) | collective-permute-done | bytes 114720 | tf_op jit(solution)/shard_map/ppermute | solution.py:195
  75.6 3.5 %collective-permute-start.14 = (bf16[2,56,1024]{2,1,0:T(8,128)(2,1)S(1)}, bf16[2,56,1024]{2,1,0:T(8,128)(2,1)S(1)}, u32[]{:S(2)}, u32[]{:S(2)}) collective-permute-start(bf16[2,56,1024]{2,1,0:T(8,128)(2,1)S(1)} %pad_maximum_fusion.refs_4_), channel_id=1, source_target_pairs={{0,384},{128,0},{256,128},{384,256},{1,385},{129,1},{257,129},{385... | collective-permute-start | bytes 688136 | tf_op jit(solution)/shard_map/ppermute | solution.py:195
  79.1 4.3 %collective-permute-start.8 = (bf16[2,16,1024]{2,1,0:T(8,128)(2,1)S(1)}, bf16[2,16,1024]{2,1,0:T(8,128)(2,1)S(1)}, u32[]{:S(2)}, u32[]{:S(2)}) collective-permute-start(bf16[2,16,1024]{2,1,0:T(8,128)(2,1)S(1)} %pad_maximum_fusion.1.refs_0_), channel_id=1, source_target_pairs={{0,16},{16,32},{32,48},{48,0},{1,17},{17,33},{33,49},{49,1},{2,18}... | collective-permute-start | bytes 196616 | tf_op jit(solution)/shard_map/ppermute | solution.py:195
  86.0 3.5 %collective-permute-start.10 = (bf16[2,16,1024]{2,1,0:T(8,128)(2,1)S(1)}, bf16[2,16,1024]{2,1,0:T(8,128)(2,1)S(1)}, u32[]{:S(2)}, u32[]{:S(2)}) collective-permute-start(bf16[2,16,1024]{2,1,0:T(8,128)(2,1)S(1)} %pad_maximum_fusion.1.refs_0_), channel_id=1, source_target_pairs={{0,48},{16,0},{32,16},{48,32},{1,49},{17,1},{33,17},{49,33},{2,50}... | collective-permute-start | bytes 196616 | tf_op jit(solution)/shard_map/ppermute | solution.py:195
  99.9 7.0 %all-to-all-start.1 = ((bf16[8,384,128]{2,1,0:T(8,128)(2,1)}), bf16[8,384,128]{2,1,0:T(8,128)(2,1)S(1)}, u32[]{:S(2)}, u32[]{:S(2)}) async-start(bf16[8,384,128]{2,1,0:T(8,128)(2,1)} %copy-done.4), calls=%async_computation.1 | async-start | bytes 1572864 | tf_op jit(solution)/shard_map/all_to_all | solution.py:275
  107.8 3.4 %collective-permute-start.15 = (bf16[128,448]{1,0:T(8,128)(2,1)S(1)}, bf16[128,448]{1,0:T(8,128)(2,1)S(1)}, u32[]{:S(2)}, u32[]{:S(2)}) collective-permute-start(bf16[128,448]{1,0:T(8,128)(2,1)S(1)} %bitcast.53), channel_id=1, source_target_pairs={{0,1},{1,2},{2,3},{3,4},{4,5},{5,6},{6,7},{7,0},{8,9},{9,10},{10,1... | collective-permute-start | bytes 344072 | tf_op jit(solution)/shard_map/ppermute | solution.py:195
  111.3 4.0 %collective-permute-start.16 = (bf16[128,448]{1,0:T(8,128)(2,1)S(1)}, bf16[128,448]{1,0:T(8,128)(2,1)S(1)}, u32[]{:S(2)}, u32[]{:S(2)}) collective-permute-start(bf16[128,448]{1,0:T(8,128)(2,1)S(1)} %bitcast.51), channel_id=1, source_target_pairs={{0,2},{1,3},{2,4},{3,5},{4,6},{5,7},{6,0},{7,1},{8,10},{9,11},{10,... | collective-permute-start | bytes 344072 | tf_op jit(solution)/shard_map/ppermute | solution.py:195
  115.4 4.3 %collective-permute-start.17 = (bf16[128,448]{1,0:T(8,128)(2,1)S(1)}, bf16[128,448]{1,0:T(8,128)(2,1)S(1)}, u32[]{:S(2)}, u32[]{:S(2)}) collective-permute-start(bf16[128,448]{1,0:T(8,128)(2,1)S(1)} %bitcast.47), channel_id=1, source_target_pairs={{0,3},{1,4},{2,5},{3,6},{4,7},{5,0},{6,1},{7,2},{8,11},{9,12},{10,... | collective-permute-start | bytes 344072 | tf_op jit(solution)/shard_map/ppermute | solution.py:195
  119.8 4.0 %collective-permute-start.18 = (bf16[128,448]{1,0:T(8,128)(2,1)S(1)}, bf16[128,448]{1,0:T(8,128)(2,1)S(1)}, u32[]{:S(2)}, u32[]{:S(2)}) collective-permute-start(bf16[128,448]{1,0:T(8,128)(2,1)S(1)} %bitcast.48), channel_id=1, source_target_pairs={{0,4},{1,5},{2,6},{3,7},{4,0},{5,1},{6,2},{7,3},{8,12},{9,13},{10,... | collective-permute-start | bytes 344072 | tf_op jit(solution)/shard_map/ppermute | solution.py:195
  123.9 4.3 %collective-permute-start.19 = (bf16[128,448]{1,0:T(8,128)(2,1)S(1)}, bf16[128,448]{1,0:T(8,128)(2,1)S(1)}, u32[]{:S(2)}, u32[]{:S(2)}) collective-permute-start(bf16[128,448]{1,0:T(8,128)(2,1)S(1)} %bitcast.49), channel_id=1, source_target_pairs={{0,5},{1,6},{2,7},{3,0},{4,1},{5,2},{6,3},{7,4},{8,13},{9,14},{10,... | collective-permute-start | bytes 344072 | tf_op jit(solution)/shard_map/ppermute | solution.py:195
  128.5 5.2 %collective-permute-start.20 = (bf16[128,448]{1,0:T(8,128)(2,1)S(1)}, bf16[128,448]{1,0:T(8,128)(2,1)S(1)}, u32[]{:S(2)}, u32[]{:S(2)}) collective-permute-start(bf16[128,448]{1,0:T(8,128)(2,1)S(1)} %bitcast.52), channel_id=1, source_target_pairs={{0,6},{1,7},{2,0},{3,1},{4,2},{5,3},{6,4},{7,5},{8,14},{9,15},{10,... | collective-permute-start | bytes 344072 | tf_op jit(solution)/shard_map/ppermute | solution.py:195
  133.7 3.1 %collective-permute-start.21 = (bf16[128,448]{1,0:T(8,128)(2,1)S(1)}, bf16[128,448]{1,0:T(8,128)(2,1)S(1)}, u32[]{:S(2)}, u32[]{:S(2)}) collective-permute-start(bf16[128,448]{1,0:T(8,128)(2,1)S(1)} %bitcast.50), channel_id=1, source_target_pairs={{0,7},{1,0},{2,1},{3,2},{4,3},{5,4},{6,5},{7,6},{8,15},{9,8},{10,9... | collective-permute-start | bytes 344072 | tf_op jit(solution)/shard_map/ppermute | solution.py:195
  138.5 9.1 %collective-permute-done.18.refs_5_ = bf16[128,448]{1,0:T(8,128)(2,1)S(1)} collective-permute-done((bf16[128,448]{1,0:T(8,128)(2,1)S(1)}, bf16[128,448]{1,0:T(8,128)(2,1)S(1)}, u32[]{:S(2)}, u32[]{:S(2)}) %collective-permute-start.18) | collective-permute-done | bytes 114720 | tf_op jit(solution)/shard_map/ppermute | solution.py:195
  149.8 11.9 %all-to-all-start.2 = ((bf16[64,4,736]{2,1,0:T(4,128)(2,1)}), bf16[64,4,736]{2,1,0:T(4,128)(2,1)S(1)}, u32[]{:S(2)}, u32[]{:S(2)}) async-start(bf16[64,4,736]{2,1,0:T(4,128)(2,1)} %reshape.34), calls=%async_computation.2 | async-start | bytes 786432 | tf_op jit(solution)/shard_map/all_to_all | solution.py:285
  162.6 13.8 %all-to-all-done.2 = bf16[64,4,736]{2,1,0:T(4,128)(2,1)S(1)} async-done(((bf16[64,4,736]{2,1,0:T(4,128)(2,1)}), bf16[64,4,736]{2,1,0:T(4,128)(2,1)S(1)}, u32[]{:S(2)}, u32[]{:S(2)}) %all-to-all-start.2) | async-done | bytes 376864 | tf_op jit(solution)/shard_map/all_to_all | solution.py:285
  (85 shorter events, 39.9 us)
Async XLA Ops:
  5.2 87.3 %all-to-all-start = ((bf16[64,4,3584]{2,1,0:T(4,128)(2,1)}), bf16[64,4,3584]{2,1,0:T(4,128)(2,1)}, u32[]{:S(2)}, u32[]{:S(2)}) async-start(bf16[64,4,3584]{2,1,0:T(4,128)(2,1)} %reshape.32), calls=%async_computation | async-start | bytes 3670016 | tf_op jit(solution)/shard_map/all_to_all | solution.py:239
  20.4 50.3 %collective-permute-start.11 = (bf16[56,1024]{1,0:T(8,128)(2,1)S(1)}, bf16[56,1024]{1,0:T(8,128)(2,1)S(1)}, u32[]{:S(2)}, u32[]{:S(2)}) collective-permute-start(bf16[56,1024]{1,0:T(8,128)(2,1)S(1)} %bitcast.54), channel_id=1, source_target_pairs={{0,64},{64,0},{1,65},{65,1},{2,66},{66,2},{3,67},{67,3},{4,68},{68... | collective-permute-start | bytes 344072 | tf_op jit(solution)/shard_map/ppermute | solution.py:195
  29.2 15.6 %collective-permute-start = (bf16[16,512]{1,0:T(8,128)(2,1)S(1)}, bf16[16,512]{1,0:T(8,128)(2,1)S(1)}, u32[]{:S(2)}, u32[]{:S(2)}) collective-permute-start(bf16[16,512]{1,0:T(8,128)(2,1)S(1)} %get-tuple-element.27), channel_id=1, source_target_pairs={{0,1},{1,2},{2,3},{3,4},{4,5},{5,6},{6,7},{7,0},{8,9},{9,10},{10,1... | collective-permute-start | bytes 49160 | tf_op jit(solution)/shard_map/ppermute | solution.py:195
  32.5 17.3 %collective-permute-start.1 = (bf16[16,512]{1,0:T(8,128)(2,1)S(1)}, bf16[16,512]{1,0:T(8,128)(2,1)S(1)}, u32[]{:S(2)}, u32[]{:S(2)}) collective-permute-start(bf16[16,512]{1,0:T(8,128)(2,1)S(1)} %get-tuple-element.26), channel_id=1, source_target_pairs={{0,2},{1,3},{2,4},{3,5},{4,6},{5,7},{6,0},{7,1},{8,10},{9,11},{10,... | collective-permute-start | bytes 49160 | tf_op jit(solution)/shard_map/ppermute | solution.py:195
  36.7 18.1 %collective-permute-start.2 = (bf16[16,512]{1,0:T(8,128)(2,1)S(1)}, bf16[16,512]{1,0:T(8,128)(2,1)S(1)}, u32[]{:S(2)}, u32[]{:S(2)}) collective-permute-start(bf16[16,512]{1,0:T(8,128)(2,1)S(1)} %get-tuple-element.25), channel_id=1, source_target_pairs={{0,3},{1,4},{2,5},{3,6},{4,7},{5,0},{6,1},{7,2},{8,11},{9,12},{10,... | collective-permute-start | bytes 49160 | tf_op jit(solution)/shard_map/ppermute | solution.py:195
  41.3 16.4 %collective-permute-start.3 = (bf16[16,512]{1,0:T(8,128)(2,1)S(1)}, bf16[16,512]{1,0:T(8,128)(2,1)S(1)}, u32[]{:S(2)}, u32[]{:S(2)}) collective-permute-start(bf16[16,512]{1,0:T(8,128)(2,1)S(1)} %get-tuple-element.24), channel_id=1, source_target_pairs={{0,4},{1,5},{2,6},{3,7},{4,0},{5,1},{6,2},{7,3},{8,12},{9,13},{10,... | collective-permute-start | bytes 49160 | tf_op jit(solution)/shard_map/ppermute | solution.py:195
  44.9 12.9 %collective-permute-start.4 = (bf16[16,512]{1,0:T(8,128)(2,1)S(1)}, bf16[16,512]{1,0:T(8,128)(2,1)S(1)}, u32[]{:S(2)}, u32[]{:S(2)}) collective-permute-start(bf16[16,512]{1,0:T(8,128)(2,1)S(1)} %get-tuple-element.23), channel_id=1, source_target_pairs={{0,5},{1,6},{2,7},{3,0},{4,1},{5,2},{6,3},{7,4},{8,13},{9,14},{10,... | collective-permute-start | bytes 49160 | tf_op jit(solution)/shard_map/ppermute | solution.py:195
  49.8 8.0 %collective-permute-start.5 = (bf16[16,512]{1,0:T(8,128)(2,1)S(1)}, bf16[16,512]{1,0:T(8,128)(2,1)S(1)}, u32[]{:S(2)}, u32[]{:S(2)}) collective-permute-start(bf16[16,512]{1,0:T(8,128)(2,1)S(1)} %get-tuple-element.22), channel_id=1, source_target_pairs={{0,6},{1,7},{2,0},{3,1},{4,2},{5,3},{6,4},{7,5},{8,14},{9,15},{10,... | collective-permute-start | bytes 49160 | tf_op jit(solution)/shard_map/ppermute | solution.py:195
  61.6 17.5 %collective-permute-start.7 = (bf16[16,1024]{1,0:T(8,128)(2,1)S(1)}, bf16[16,1024]{1,0:T(8,128)(2,1)S(1)}, u32[]{:S(2)}, u32[]{:S(2)}) collective-permute-start(bf16[16,1024]{1,0:T(8,128)(2,1)S(1)} %shard_map.120), channel_id=1, source_target_pairs={{0,8},{8,0},{1,9},{9,1},{2,10},{10,2},{3,11},{11,3},{4,12},{12,4},... | collective-permute-start | bytes 98312 | tf_op jit(solution)/shard_map/ppermute | solution.py:195
  70.7 20.6 %collective-permute-start.12 = (bf16[2,56,1024]{2,1,0:T(8,128)(2,1)S(1)}, bf16[2,56,1024]{2,1,0:T(8,128)(2,1)S(1)}, u32[]{:S(2)}, u32[]{:S(2)}) collective-permute-start(bf16[2,56,1024]{2,1,0:T(8,128)(2,1)S(1)} %pad_maximum_fusion.refs_4_), channel_id=1, source_target_pairs={{0,128},{128,256},{256,384},{384,0},{1,129},{129,257},{257,385},{3... | collective-permute-start | bytes 688136 | tf_op jit(solution)/shard_map/ppermute | solution.py:195
  72.6 18.7 %collective-permute-start.13 = (bf16[2,56,1024]{2,1,0:T(8,128)(2,1)S(1)}, bf16[2,56,1024]{2,1,0:T(8,128)(2,1)S(1)}, u32[]{:S(2)}, u32[]{:S(2)}) collective-permute-start(bf16[2,56,1024]{2,1,0:T(8,128)(2,1)S(1)} %pad_maximum_fusion.refs_4_), channel_id=1, source_target_pairs={{0,256},{128,384},{256,0},{384,128},{1,257},{129,385},{257,1},{385... | collective-permute-start | bytes 688136 | tf_op jit(solution)/shard_map/ppermute | solution.py:195
  75.6 15.7 %collective-permute-start.14 = (bf16[2,56,1024]{2,1,0:T(8,128)(2,1)S(1)}, bf16[2,56,1024]{2,1,0:T(8,128)(2,1)S(1)}, u32[]{:S(2)}, u32[]{:S(2)}) collective-permute-start(bf16[2,56,1024]{2,1,0:T(8,128)(2,1)S(1)} %pad_maximum_fusion.refs_4_), channel_id=1, source_target_pairs={{0,384},{128,0},{256,128},{384,256},{1,385},{129,1},{257,129},{385... | collective-permute-start | bytes 688136 | tf_op jit(solution)/shard_map/ppermute | solution.py:195
  79.1 6.8 %collective-permute-start.8 = (bf16[2,16,1024]{2,1,0:T(8,128)(2,1)S(1)}, bf16[2,16,1024]{2,1,0:T(8,128)(2,1)S(1)}, u32[]{:S(2)}, u32[]{:S(2)}) collective-permute-start(bf16[2,16,1024]{2,1,0:T(8,128)(2,1)S(1)} %pad_maximum_fusion.1.refs_0_), channel_id=1, source_target_pairs={{0,16},{16,32},{32,48},{48,0},{1,17},{17,33},{33,49},{49,1},{2,18}... | collective-permute-start | bytes 196616 | tf_op jit(solution)/shard_map/ppermute | solution.py:195
  83.5 6.4 %collective-permute-start.9 = (bf16[2,16,1024]{2,1,0:T(8,128)(2,1)S(1)}, bf16[2,16,1024]{2,1,0:T(8,128)(2,1)S(1)}, u32[]{:S(2)}, u32[]{:S(2)}) collective-permute-start(bf16[2,16,1024]{2,1,0:T(8,128)(2,1)S(1)} %pad_maximum_fusion.1.refs_0_), channel_id=1, source_target_pairs={{0,32},{16,48},{32,0},{48,16},{1,33},{17,49},{33,1},{49,17},{2,34}... | collective-permute-start | bytes 196616 | tf_op jit(solution)/shard_map/ppermute | solution.py:195
  86.0 5.3 %collective-permute-start.10 = (bf16[2,16,1024]{2,1,0:T(8,128)(2,1)S(1)}, bf16[2,16,1024]{2,1,0:T(8,128)(2,1)S(1)}, u32[]{:S(2)}, u32[]{:S(2)}) collective-permute-start(bf16[2,16,1024]{2,1,0:T(8,128)(2,1)S(1)} %pad_maximum_fusion.1.refs_0_), channel_id=1, source_target_pairs={{0,48},{16,0},{32,16},{48,32},{1,49},{17,1},{33,17},{49,33},{2,50}... | collective-permute-start | bytes 196616 | tf_op jit(solution)/shard_map/ppermute | solution.py:195
  99.9 47.6 %all-to-all-start.1 = ((bf16[8,384,128]{2,1,0:T(8,128)(2,1)}), bf16[8,384,128]{2,1,0:T(8,128)(2,1)S(1)}, u32[]{:S(2)}, u32[]{:S(2)}) async-start(bf16[8,384,128]{2,1,0:T(8,128)(2,1)} %copy-done.4), calls=%async_computation.1 | async-start | bytes 1572864 | tf_op jit(solution)/shard_map/all_to_all | solution.py:275
  107.8 20.7 %collective-permute-start.15 = (bf16[128,448]{1,0:T(8,128)(2,1)S(1)}, bf16[128,448]{1,0:T(8,128)(2,1)S(1)}, u32[]{:S(2)}, u32[]{:S(2)}) collective-permute-start(bf16[128,448]{1,0:T(8,128)(2,1)S(1)} %bitcast.53), channel_id=1, source_target_pairs={{0,1},{1,2},{2,3},{3,4},{4,5},{5,6},{6,7},{7,0},{8,9},{9,10},{10,1... | collective-permute-start | bytes 344072 | tf_op jit(solution)/shard_map/ppermute | solution.py:195
  111.3 22.5 %collective-permute-start.16 = (bf16[128,448]{1,0:T(8,128)(2,1)S(1)}, bf16[128,448]{1,0:T(8,128)(2,1)S(1)}, u32[]{:S(2)}, u32[]{:S(2)}) collective-permute-start(bf16[128,448]{1,0:T(8,128)(2,1)S(1)} %bitcast.51), channel_id=1, source_target_pairs={{0,2},{1,3},{2,4},{3,5},{4,6},{5,7},{6,0},{7,1},{8,10},{9,11},{10,... | collective-permute-start | bytes 344072 | tf_op jit(solution)/shard_map/ppermute | solution.py:195
  115.4 23.1 %collective-permute-start.17 = (bf16[128,448]{1,0:T(8,128)(2,1)S(1)}, bf16[128,448]{1,0:T(8,128)(2,1)S(1)}, u32[]{:S(2)}, u32[]{:S(2)}) collective-permute-start(bf16[128,448]{1,0:T(8,128)(2,1)S(1)} %bitcast.47), channel_id=1, source_target_pairs={{0,3},{1,4},{2,5},{3,6},{4,7},{5,0},{6,1},{7,2},{8,11},{9,12},{10,... | collective-permute-start | bytes 344072 | tf_op jit(solution)/shard_map/ppermute | solution.py:195
  119.8 27.8 %collective-permute-start.18 = (bf16[128,448]{1,0:T(8,128)(2,1)S(1)}, bf16[128,448]{1,0:T(8,128)(2,1)S(1)}, u32[]{:S(2)}, u32[]{:S(2)}) collective-permute-start(bf16[128,448]{1,0:T(8,128)(2,1)S(1)} %bitcast.48), channel_id=1, source_target_pairs={{0,4},{1,5},{2,6},{3,7},{4,0},{5,1},{6,2},{7,3},{8,12},{9,13},{10,... | collective-permute-start | bytes 344072 | tf_op jit(solution)/shard_map/ppermute | solution.py:195
  123.9 23.6 %collective-permute-start.19 = (bf16[128,448]{1,0:T(8,128)(2,1)S(1)}, bf16[128,448]{1,0:T(8,128)(2,1)S(1)}, u32[]{:S(2)}, u32[]{:S(2)}) collective-permute-start(bf16[128,448]{1,0:T(8,128)(2,1)S(1)} %bitcast.49), channel_id=1, source_target_pairs={{0,5},{1,6},{2,7},{3,0},{4,1},{5,2},{6,3},{7,4},{8,13},{9,14},{10,... | collective-permute-start | bytes 344072 | tf_op jit(solution)/shard_map/ppermute | solution.py:195
  128.5 19.1 %collective-permute-start.20 = (bf16[128,448]{1,0:T(8,128)(2,1)S(1)}, bf16[128,448]{1,0:T(8,128)(2,1)S(1)}, u32[]{:S(2)}, u32[]{:S(2)}) collective-permute-start(bf16[128,448]{1,0:T(8,128)(2,1)S(1)} %bitcast.52), channel_id=1, source_target_pairs={{0,6},{1,7},{2,0},{3,1},{4,2},{5,3},{6,4},{7,5},{8,14},{9,15},{10,... | collective-permute-start | bytes 344072 | tf_op jit(solution)/shard_map/ppermute | solution.py:195
  133.7 13.8 %collective-permute-start.21 = (bf16[128,448]{1,0:T(8,128)(2,1)S(1)}, bf16[128,448]{1,0:T(8,128)(2,1)S(1)}, u32[]{:S(2)}, u32[]{:S(2)}) collective-permute-start(bf16[128,448]{1,0:T(8,128)(2,1)S(1)} %bitcast.50), channel_id=1, source_target_pairs={{0,7},{1,0},{2,1},{3,2},{4,3},{5,4},{6,5},{7,6},{8,15},{9,8},{10,9... | collective-permute-start | bytes 344072 | tf_op jit(solution)/shard_map/ppermute | solution.py:195
  149.8 26.5 %all-to-all-start.2 = ((bf16[64,4,736]{2,1,0:T(4,128)(2,1)}), bf16[64,4,736]{2,1,0:T(4,128)(2,1)S(1)}, u32[]{:S(2)}, u32[]{:S(2)}) async-start(bf16[64,4,736]{2,1,0:T(4,128)(2,1)} %reshape.34), calls=%async_computation.2 | async-start | bytes 786432 | tf_op jit(solution)/shard_map/all_to_all | solution.py:285
  (17 other events, 229.0 us)

commit v3 on v2

--- a/solution.py
+++ b/solution.py
@@ -19,11 +19,14 @@
 BF16 = jnp.bfloat16
 
 
-def kernel_call(body, outs, *args, smem=(), flops=0):
+def kernel_call(body, outs, *args, smem=(), after=(), flops=0):
     in_specs = [
         pl.BlockSpec(memory_space=pltpu.SMEM if i in smem else pltpu.VMEM)
         for i in range(len(args))
-    ]
+    ] + [pl.BlockSpec(memory_space=pl.ANY) for _ in after]
+    if after:
+        inner, count = body, len(args)
+        body = lambda *refs: inner(*refs[:count], *refs[count + len(after) :])
     vmem = pl.BlockSpec(memory_space=pltpu.VMEM)
     nbytes = sum(a.size * a.dtype.itemsize for a in args)
     return pl.pallas_call(
@@ -33,7 +36,15 @@
         out_specs=tuple(vmem for _ in outs),
         compiler_params=pltpu.CompilerParams(vmem_limit_bytes=40 << 20),
         cost_estimate=pl.CostEstimate(flops=flops, bytes_accessed=nbytes, transcendentals=0),
-    )(*args)
+    )(*args, *after)
+
+
+def one_hot(condition):
+    return condition.astype(F32).astype(BF16)
+
+
+def iotas(*shape):
+    return lax.broadcasted_iota(jnp.int32, shape, 0), lax.broadcasted_iota(jnp.int32, shape, 1)
 
 
 def prepare(hidden_ref, gain_ref, ids_ref, send_ref, place_ref):
@@ -59,7 +70,7 @@
     ).astype(BF16)
 
 
-def attend(place_ref, lengths_ref, queries_ref, cache_ref, context_ref):
+def attend(lengths_ref, queries_ref, cache_ref, context_ref):
     rows, heads, _ = queries_ref.shape
     groups, _, latent = context_ref.shape
     found = []
@@ -72,26 +83,31 @@
         soft = (raised / jnp.sum(raised, axis=-1, keepdims=True)).astype(BF16)
         context = lax.dot_general(soft, keys[:latent], NT, preferred_element_type=F32)
         found.append(context.reshape(groups, heads // groups, latent))
-    found = jnp.concatenate(found, axis=1).astype(BF16)
-    for g in range(groups):
-        context_ref[(g - place_ref[TP] + groups) % groups] = found[g]
-
-
-def lift_heads(place_ref, *refs):
-    *parts, w_uv_ref, values_ref = refs
-    heads, _, width = w_uv_ref.shape
+    context_ref[...] = jnp.concatenate(found, axis=1).astype(BF16)
+
+
+def lift_heads(place_ref, context_ref, w_uv_ref, values_ref):
+    heads, latent, width = w_uv_ref.shape
     rows = values_ref.shape[0]
-    share = rows // len(parts)
-    context = jnp.concatenate([part[...] for part in parts], axis=0)
-    token = lax.broadcasted_iota(jnp.int32, (rows, rows * heads), 0)
-    entry = lax.broadcasted_iota(jnp.int32, (rows, rows * heads), 1)
-    source = (place_ref[TP] - entry // (share * heads) + len(parts)) % len(parts)
-    named = source * share + entry // heads % share
+    sources = context_ref.shape[0]
+    context = jnp.concatenate([context_ref[k, place_ref[TP]] for k in range(sources)], axis=0)
+    token, entry = iotas(rows, rows * heads)
     for h in range(heads):
         lifted = jnp.dot(context, w_uv_ref[h], preferred_element_type=F32).astype(BF16)
-        pick = ((token == named) & (entry % heads == h)).astype(F32).astype(BF16)
+        pick = one_hot(entry == token * heads + h)
         mine = jnp.dot(pick, lifted, preferred_element_type=F32).astype(BF16)
         values_ref[:, h * width : (h + 1) * width] = mine
+
+
+def split_down(place_ref, w_down_ref, keep_ref, send_ref):
+    pairs, _, width = keep_ref.shape
+    even = place_ref[TP] % 2 == 0
+    for p in range(pairs):
+        first = w_down_ref[:, 2 * p * width : (2 * p + 1) * width]
+        second = w_down_ref[:, (2 * p + 1) * width : (2 * p + 2) * width]
+        k = (p - place_ref[TP] // 2 + pairs) % pairs
+        keep_ref[k] = jnp.where(even, first, second)
+        send_ref[k] = jnp.where(even, second, first)
 
 
 def project(place_ref, *refs):
@@ -124,23 +140,19 @@
     score_ref[...] = (1.0 / (1.0 + jnp.exp(-logits))).astype(BF16)
 
 
-def one_hot(condition):
-    return condition.astype(F32).astype(BF16)
-
-
-def iotas(*shape):
-    return lax.broadcasted_iota(jnp.int32, shape, 0), lax.broadcasted_iota(jnp.int32, shape, 1)
-
-
 def lower_experts(place_ref, *refs):
     inner_ref, *parts, score_ref, back_ref = refs
     sources, _, _ = inner_ref.shape
     slots, _ = back_ref.shape
-    width = parts[0].shape[1]
+    width = parts[0].shape[2]
     total = jnp.zeros((slots, width), F32)
-    for k in range(sources):
-        source = (place_ref[TP] - k + sources) % sources
-        total += jnp.dot(inner_ref[source, :slots], parts[k][...], preferred_element_type=F32)
+    for k in range(len(parts)):
+        pair = (place_ref[TP] // 2 - k + len(parts)) % len(parts)
+        for j in range(2):
+            source = pair * 2 + (place_ref[TP] + j) % 2
+            total += jnp.dot(
+                inner_ref[source, :slots], parts[k][j], preferred_element_type=F32
+            )
     back_ref[:, :width] = total.astype(BF16)
     back_ref[:, width:PADDED] = score_ref[:, : PADDED - width]
     attn = jnp.zeros((inner_ref.shape[1] - slots, 128), F32)
@@ -195,13 +207,12 @@
     return lax.ppermute(value, axis, [(i, (i + k) % size) for i in range(size)])
 
 
-def spread(blocks, axis):
-    return [blocks[0]] + [shift(blocks[k], axis, k) for k in range(1, lax.axis_size(axis))]
-
-
-def gather(value, first, second):
-    pair = jnp.stack([value, shift(value, first, 1)])
-    return [pair] + [shift(pair, second, k) for k in range(1, lax.axis_size(second))]
+def pair_up(value, axis):
+    return jnp.stack([value, shift(value, axis, 1)])
+
+
+def gather(value, axis):
+    return [value] + [shift(value, axis, k) for k in range(1, lax.axis_size(axis))]
 
 
 def on_device(
@@ -229,39 +240,55 @@
     here = jnp.stack([lax.axis_index(a) for a in ("y", "x", "zh", "zl", "c")]).astype(jnp.int32)
     tp = here[0]
 
+    (context,) = kernel_call(
+        attend,
+        [((tp_size, 2 * heads, latent), BF16)],
+        lengths,
+        queries,
+        jnp.swapaxes(latent_cache, 1, 2),
+        smem=(0,),
+    )
+    contexts = lax.all_gather(context, "y", axis=0)
+    out_pair = pair_up(w_out.T, "zh")
+
     send, place = kernel_call(
         prepare,
         [((slots, model_width), BF16), ((slots, rows), F32)],
         hidden,
         norm_gain.reshape(1, model_width),
         expert_ids.T,
+        after=(context,),
     )
     named_rows = lax.all_to_all(
         send.reshape(ep_size, SLOTS, model_width), EP, 0, 0, tiled=True
     ).reshape(slots, model_width)
 
-    (context,) = kernel_call(
-        attend,
-        [((tp_size, 2 * heads, latent), BF16)],
+    out_weights = gather(out_pair, "x")
+    keep, pass_on = kernel_call(
+        split_down,
+        [((tp_size // 2, hidden_units, width), BF16)] * 2,
         here,
-        lengths,
-        queries,
-        jnp.swapaxes(latent_cache, 1, 2),
-        smem=(0, 1),
-    )
-    context = spread(context, "y")
+        w_down[0],
+        smem=(0,),
+        after=(send,),
+    )
+    arrived = lax.ppermute(pass_on, "y", [(i, i ^ 1) for i in range(tp_size)])
+    down = [jnp.stack([keep[k], arrived[k]]) for k in range(tp_size // 2)]
+    down = [down[0]] + [shift(down[k], "y", 2 * k) for k in range(1, tp_size // 2)]
     (values,) = kernel_call(
-        lift_heads, [((rows, depth), BF16)], here, *context, w_uv, smem=(0,)
-    )
-    values = gather(values, "c", "zl")
-    out_weights = gather(w_out.T, "zh", "x")
+        lift_heads,
+        [((rows, depth), BF16)],
+        here,
+        contexts,
+        w_uv,
+        smem=(0,),
+        after=(arrived,),
+        flops=30_000_000_000,
+    )
+    values = gather(pair_up(values, "c"), "zl")
     (attn_parts,) = kernel_call(
         project, [((tp_size, rows * 8, 128), BF16)], here, *values, *out_weights, smem=(0,)
     )
-
-    down = w_down[0].reshape(hidden_units, tp_size, width).transpose(1, 0, 2)
-    down = [lax.dynamic_index_in_dim(down, (tp + k) % tp_size, 0, False) for k in range(tp_size)]
-    down = spread(down, "y")
 
     inner, score = kernel_call(
         lift_experts,

time: 180 us -> 204 us (1.13)
  waiting for transfers between devices: 32.7 us -> 84.8 us
  starting transfers between devices: 121 us -> 74.5 us
  between operations: 0.61 us -> 13.8 us
  local copies, waits for them, and re-layouts: 13.7 us -> 17 us
    ppermute x22 -> x11, waiting for transfers between devices: 18.9 us -> 70.9 us  [shift(): return lax.ppermute(value, axis, [(i, (i + k) % size) for i in range(size)])]
    ppermute x22 -> x11, starting transfers between devices: 87 us -> 43 us  [shift(): return lax.ppermute(value, axis, [(i, (i + k) % size) for i in range(size)])]
    all_to_all x1, starting transfers between devices: 11.9 us -> 6.84 us  [on_device(): lax.all_to_all(back.reshape(ep_size, SLOTS, PADDED + ATTN), EP, 0, 0, til...]
    unnamed x33 -> x34, local copies, waits for them, and re-layouts: 5.57 us -> 9.83 us
    ppermute x0 -> x1, starting transfers between devices: none -> 3.19 us  [on_device(): arrived = lax.ppermute(pass_on, 'y', [(i, i ^ 1) for i in range(tp_size)])]
    pallas_call x7 -> x8, Pallas kernels: 10.6 us -> 12.4 us  [kernel_call(): pl.pallas_call(body, out_shape=tuple((jax.ShapeDtypeStruct(s, d) for s, d...]
  transfers between devices with their start and end apart: 25 -> 16, of which waited for: 8 -> 7; matrix products, arithmetic and copies ran while one was open for 1% -> 2% of each run, Pallas kernels for 3% -> 3%
where the time goes in v3:
time: 204 us; the launch traced here: 203 us
  waiting for transfers between devices  84.8 us (42%)
  starting transfers between devices  74.5 us (37%)
  local copies, waits for them, and re-layouts  17 us (8%)
  between operations  13.8 us (7%)
  Pallas kernels  12.4 us (6%)
    ppermute x11, waiting for transfers between devices, shift(): return lax.ppermute(value, axis, [(i, (i + k) % size) for i in range(size)])  70.9 us
    ppermute x11, starting transfers between devices, shift(): return lax.ppermute(value, axis, [(i, (i + k) % size) for i in range(size)])  43 us
    all_to_all x1, starting transfers between devices, on_device(): lax.all_to_all(send.reshape(ep_size, SLOTS, model_width), EP, 0, 0, tiled...  15.1 us
    all_to_all x1, waiting for transfers between devices, on_device(): lax.all_to_all(back.reshape(ep_size, SLOTS, PADDED + ATTN), EP, 0, 0, til...  13.8 us
    pallas_call x8, Pallas kernels, kernel_call(): pl.pallas_call(body, out_shape=tuple((jax.ShapeDtypeStruct(s, d) for s, d...  12.4 us
    unnamed x34, local copies, waits for them, and re-layouts  9.83 us
    all_to_all x1, starting transfers between devices, on_device(): lax.all_to_all(back.reshape(ep_size, SLOTS, PADDED + ATTN), EP, 0, 0, til...  6.84 us
    all_to_all x1, starting transfers between devices, on_device(): inner = lax.all_to_all(inner, 'y', 0, 0, tiled=True)  6.32 us
  transfers between devices with their start and end apart: 16, of which 7 were waited for; matrix products, arithmetic and copies ran while one was open for 2% of the time, Pallas kernels for 3%

profile of v3, /device:TPU:1, one launch (start us, length us, event | category | flops | bytes accessed | tf_op | source)
XLA Modules:
  0.0 202.6 jit_solution(13494750518781423029)
XLA Ops:
  9.3 2.2 %shard_map.118.refs_3_ = bf16[8,16,512]{2,1,0:T(8,128)(2,1)} custom-call(s32[2]{0:T(128)S(1)} %copy-done.13, bf16[2,64,576]{2,1,0:T(8,128)(2,1)S(1)} %copy-done.9, bf16[2,576,384]{2,1,0:T(8,128)(2,1)S(1)} %bitcast.20), custom_call_target="tpu_custom_call" | custom-call | bytes 1032200 | tf_op jit(solution)/shard_map/pallas_call | solution.py:32
  16.1 15.1 %all-to-all-start = ((bf16[64,4,3584]{2,1,0:T(4,128)(2,1)}), bf16[64,4,3584]{2,1,0:T(4,128)(2,1)}, u32[]{:S(2)}, u32[]{:S(2)}) async-start(bf16[64,4,3584]{2,1,0:T(4,128)(2,1)} %reshape.16), calls=%async_computation | async-start | bytes 3670016 | tf_op jit(solution)/shard_map/all_to_all | solution.py:262
  33.3 3.2 %collective-permute-start = (bf16[4,128,448]{2,1,0:T(8,128)(2,1)S(1)}, bf16[4,128,448]{2,1,0:T(8,128)(2,1)S(1)}, u32[]{:S(2)}, u32[]{:S(2)}) collective-permute-start(bf16[4,128,448]{2,1,0:T(8,128)(2,1)S(1)} %get-tuple-element.12), channel_id=1, source_target_pairs={{0,1},{1,0},{2,3},{3,2},{4,5},{5,4},{6,7},{7,6},{8,9},{9,8},{10,11... | collective-permute-start | bytes 1376264 | tf_op jit(solution)/shard_map/ppermute | solution.py:275
  36.5 7.2 %collective-permute-start.5 = (bf16[56,1024]{1,0:T(8,128)(2,1)S(1)}, bf16[56,1024]{1,0:T(8,128)(2,1)S(1)}, u32[]{:S(2)}, u32[]{:S(2)}) collective-permute-start(bf16[56,1024]{1,0:T(8,128)(2,1)S(1)} %bitcast.24), channel_id=1, source_target_pairs={{0,64},{64,0},{1,65},{65,1},{2,66},{66,2},{3,67},{67,3},{4,68},{68... | collective-permute-start | bytes 344072 | tf_op jit(solution)/shard_map/ppermute | solution.py:207
  43.7 37.8 %collective-permute-done.5 = bf16[56,1024]{1,0:T(8,128)(2,1)S(1)} collective-permute-done((bf16[56,1024]{1,0:T(8,128)(2,1)S(1)}, bf16[56,1024]{1,0:T(8,128)(2,1)S(1)}, u32[]{:S(2)}, u32[]{:S(2)}) %collective-permute-start.5) | collective-permute-done | bytes 114720 | tf_op jit(solution)/shard_map/ppermute | solution.py:207
  81.5 1.9 collective-permute-start.6
  83.4 3.0 %collective-permute-start.7 = (bf16[2,56,1024]{2,1,0:T(8,128)(2,1)S(1)}, bf16[2,56,1024]{2,1,0:T(8,128)(2,1)S(1)}, u32[]{:S(2)}, u32[]{:S(2)}) collective-permute-start(bf16[2,56,1024]{2,1,0:T(8,128)(2,1)S(1)} %pad_maximum_fusion.4.refs_4_), channel_id=1, source_target_pairs={{0,256},{128,384},{256,0},{384,128},{1,257},{129,385},{257,1},{385... | collective-permute-start | bytes 688136 | tf_op jit(solution)/shard_map/ppermute | solution.py:207
  86.4 3.5 %collective-permute-start.8 = (bf16[2,56,1024]{2,1,0:T(8,128)(2,1)S(1)}, bf16[2,56,1024]{2,1,0:T(8,128)(2,1)S(1)}, u32[]{:S(2)}, u32[]{:S(2)}) collective-permute-start(bf16[2,56,1024]{2,1,0:T(8,128)(2,1)S(1)} %pad_maximum_fusion.4.refs_4_), channel_id=1, source_target_pairs={{0,384},{128,0},{256,128},{384,256},{1,385},{129,1},{257,129},{385... | collective-permute-start | bytes 688136 | tf_op jit(solution)/shard_map/ppermute | solution.py:207
  92.6 2.0 shard_map.121
  94.6 4.2 %collective-permute-start.1 = (bf16[16,1024]{1,0:T(8,128)(2,1)S(1)}, bf16[16,1024]{1,0:T(8,128)(2,1)S(1)}, u32[]{:S(2)}, u32[]{:S(2)}) collective-permute-start(bf16[16,1024]{1,0:T(8,128)(2,1)S(1)} %shard_map.121), channel_id=1, source_target_pairs={{0,8},{8,0},{1,9},{9,1},{2,10},{10,2},{3,11},{11,3},{4,12},{12,4},... | collective-permute-start | bytes 98312 | tf_op jit(solution)/shard_map/ppermute | solution.py:207
  99.7 3.5 %collective-permute-start.2 = (bf16[2,16,1024]{2,1,0:T(8,128)(2,1)S(1)}, bf16[2,16,1024]{2,1,0:T(8,128)(2,1)S(1)}, u32[]{:S(2)}, u32[]{:S(2)}) collective-permute-start(bf16[2,16,1024]{2,1,0:T(8,128)(2,1)S(1)} %pad_maximum_fusion.5.refs_0_), channel_id=1, source_target_pairs={{0,16},{16,32},{32,48},{48,0},{1,17},{17,33},{33,49},{49,1},{2,18}... | collective-permute-start | bytes 196616 | tf_op jit(solution)/shard_map/ppermute | solution.py:207
  103.2 1.9 collective-permute-start.3
  105.2 4.3 %collective-permute-start.4 = (bf16[2,16,1024]{2,1,0:T(8,128)(2,1)S(1)}, bf16[2,16,1024]{2,1,0:T(8,128)(2,1)S(1)}, u32[]{:S(2)}, u32[]{:S(2)}) collective-permute-start(bf16[2,16,1024]{2,1,0:T(8,128)(2,1)S(1)} %pad_maximum_fusion.5.refs_0_), channel_id=1, source_target_pairs={{0,48},{16,0},{32,16},{48,32},{1,49},{17,1},{33,17},{49,33},{2,50}... | collective-permute-start | bytes 196616 | tf_op jit(solution)/shard_map/ppermute | solution.py:207
  109.5 1.6 collective-permute-done.3.refs_2_
  113.4 3.0 %reshape.17.rows_ref = bf16[256,3584]{1,0:T(8,128)(2,1)S(1)} reshape(bf16[64,4,3584]{2,1,0:T(4,128)(2,1)} %all-to-all-done) | data formatting | bytes 3670016 | tf_op jit(solution)/shard_map/reshape | solution.py:264
  120.2 6.3 %all-to-all-start.1 = ((bf16[8,384,128]{2,1,0:T(8,128)(2,1)}), bf16[8,384,128]{2,1,0:T(8,128)(2,1)S(1)}, u32[]{:S(2)}, u32[]{:S(2)}) async-start(bf16[8,384,128]{2,1,0:T(8,128)(2,1)} %copy-done.4), calls=%async_computation.1 | async-start | bytes 1572864 | tf_op jit(solution)/shard_map/all_to_all | solution.py:302
  126.6 7.3 %collective-permute-start.10 = (bf16[2,128,448]{2,1,0:T(8,128)(2,1)S(1)}, bf16[2,128,448]{2,1,0:T(8,128)(2,1)S(1)}, u32[]{:S(2)}, u32[]{:S(2)}) collective-permute-start(bf16[2,128,448]{2,1,0:T(8,128)(2,1)S(1)} %pad_maximum_fusion.2), channel_id=1, source_target_pairs={{0,4},{1,5},{2,6},{3,7},{4,0},{5,1},{6,2},{7,3},{8,12},{9,13},{10,... | collective-permute-start | bytes 688136 | tf_op jit(solution)/shard_map/ppermute | solution.py:207
  133.9 2.2 %collective-permute-start.11 = (bf16[2,128,448]{2,1,0:T(8,128)(2,1)S(1)}, bf16[2,128,448]{2,1,0:T(8,128)(2,1)S(1)}, u32[]{:S(2)}, u32[]{:S(2)}) collective-permute-start(bf16[2,128,448]{2,1,0:T(8,128)(2,1)S(1)} %pad_maximum_fusion.3), channel_id=1, source_target_pairs={{0,6},{1,7},{2,0},{3,1},{4,2},{5,3},{6,4},{7,5},{8,14},{9,15},{10,... | collective-permute-start | bytes 688136 | tf_op jit(solution)/shard_map/ppermute | solution.py:207
  136.2 4.0 %collective-permute-start.9 = (bf16[2,128,448]{2,1,0:T(8,128)(2,1)S(1)}, bf16[2,128,448]{2,1,0:T(8,128)(2,1)S(1)}, u32[]{:S(2)}, u32[]{:S(2)}) collective-permute-start(bf16[2,128,448]{2,1,0:T(8,128)(2,1)S(1)} %pad_maximum_fusion.1), channel_id=1, source_target_pairs={{0,2},{1,3},{2,4},{3,5},{4,6},{5,7},{6,0},{7,1},{8,10},{9,11},{10,... | collective-permute-start | bytes 688136 | tf_op jit(solution)/shard_map/ppermute | solution.py:207
  140.2 24.6 %collective-permute-done.10.refs_3_ = bf16[2,128,448]{2,1,0:T(8,128)(2,1)S(1)} collective-permute-done((bf16[2,128,448]{2,1,0:T(8,128)(2,1)S(1)}, bf16[2,128,448]{2,1,0:T(8,128)(2,1)S(1)}, u32[]{:S(2)}, u32[]{:S(2)}) %collective-permute-start.10) | collective-permute-done | bytes 229408 | tf_op jit(solution)/shard_map/ppermute | solution.py:207
  164.8 5.0 %collective-permute-done.9.refs_2_ = bf16[2,128,448]{2,1,0:T(8,128)(2,1)S(1)} collective-permute-done((bf16[2,128,448]{2,1,0:T(8,128)(2,1)S(1)}, bf16[2,128,448]{2,1,0:T(8,128)(2,1)S(1)}, u32[]{:S(2)}, u32[]{:S(2)}) %collective-permute-start.9) | collective-permute-done | bytes 229408 | tf_op jit(solution)/shard_map/ppermute | solution.py:207
  172.0 6.8 %all-to-all-start.2 = ((bf16[64,4,736]{2,1,0:T(4,128)(2,1)}), bf16[64,4,736]{2,1,0:T(4,128)(2,1)S(1)}, u32[]{:S(2)}, u32[]{:S(2)}) async-start(bf16[64,4,736]{2,1,0:T(4,128)(2,1)} %reshape.18), calls=%async_computation.2 | async-start | bytes 786432 | tf_op jit(solution)/shard_map/all_to_all | solution.py:312
  179.7 13.8 %all-to-all-done.2 = bf16[64,4,736]{2,1,0:T(4,128)(2,1)S(1)} async-done(((bf16[64,4,736]{2,1,0:T(4,128)(2,1)}), bf16[64,4,736]{2,1,0:T(4,128)(2,1)S(1)}, u32[]{:S(2)}, u32[]{:S(2)}) %all-to-all-start.2) | async-done | bytes 376864 | tf_op jit(solution)/shard_map/all_to_all | solution.py:312
  193.7 2.1 %shard_map.125 = bf16[16,448]{1,0:T(8,128)(2,1)} custom-call(s32[5]{0:T(128)S(1)} %stack.53.refs_0_.place_ref, bf16[256,736]{1,0:T(8,128)(2,1)S(1)} %reshape.19.back_ref, f32[256,16]{1,0:T(8,128)S(1)} %get-tuple-element.16.slot_ref, bf16[16,448]{1,0:T(8,128)(2,1)S(1)} %constant_dynamic-slice_fusion.own_ref), custom_call_target="tpu_custom_call" | custom-call | bytes 407572 | tf_op jit(solution)/shard_map/pallas_call | solution.py:32
  (66 shorter events, 22.2 us)
Async XLA Ops:
  6.5 83.5 %all-gather.3.cloned.1.call-start = ((), (), s32[]{:S(2)}) async-start(), calls=%async_computation.3 | async-start | bytes 1179648 | tf_op jit(solution)/shard_map/all_gather | solution.py:251
  16.0 15.2 %copy-start = (bf16[1,128,3584]{2,1,0:T(8,128)(2,1)S(1)}, bf16[1,128,3584]{2,1,0:T(8,128)(2,1)}, u32[]{:S(2)}) copy-start(bf16[1,128,3584]{2,1,0:T(8,128)(2,1)} %param.21) | copy-start | bytes 2752516
  16.1 97.3 %all-to-all-start = ((bf16[64,4,3584]{2,1,0:T(4,128)(2,1)}), bf16[64,4,3584]{2,1,0:T(4,128)(2,1)}, u32[]{:S(2)}, u32[]{:S(2)}) async-start(bf16[64,4,3584]{2,1,0:T(4,128)(2,1)} %reshape.16), calls=%async_computation | async-start | bytes 3670016 | tf_op jit(solution)/shard_map/all_to_all | solution.py:262
  31.2 5.3 %copy-start.16 = (bf16[1024,56]{0,1:T(8,128)(2,1)S(1)}, bf16[1024,56]{0,1:T(8,128)(2,1)}, u32[]{:S(2)}) copy-start(bf16[1024,56]{0,1:T(8,128)(2,1)} %param.23) | copy-start | bytes 344068
  33.3 56.7 %collective-permute-start = (bf16[4,128,448]{2,1,0:T(8,128)(2,1)S(1)}, bf16[4,128,448]{2,1,0:T(8,128)(2,1)S(1)}, u32[]{:S(2)}, u32[]{:S(2)}) collective-permute-start(bf16[4,128,448]{2,1,0:T(8,128)(2,1)S(1)} %get-tuple-element.12), channel_id=1, source_target_pairs={{0,1},{1,0},{2,3},{3,2},{4,5},{5,4},{6,7},{7,6},{8,9},{9,8},{10,11... | collective-permute-start | bytes 1376264 | tf_op jit(solution)/shard_map/ppermute | solution.py:275
  36.5 45.0 %collective-permute-start.5 = (bf16[56,1024]{1,0:T(8,128)(2,1)S(1)}, bf16[56,1024]{1,0:T(8,128)(2,1)S(1)}, u32[]{:S(2)}, u32[]{:S(2)}) collective-permute-start(bf16[56,1024]{1,0:T(8,128)(2,1)S(1)} %bitcast.24), channel_id=1, source_target_pairs={{0,64},{64,0},{1,65},{65,1},{2,66},{66,2},{3,67},{67,3},{4,68},{68... | collective-permute-start | bytes 344072 | tf_op jit(solution)/shard_map/ppermute | solution.py:207
  81.5 23.6 %collective-permute-start.6 = (bf16[2,56,1024]{2,1,0:T(8,128)(2,1)S(1)}, bf16[2,56,1024]{2,1,0:T(8,128)(2,1)S(1)}, u32[]{:S(2)}, u32[]{:S(2)}) collective-permute-start(bf16[2,56,1024]{2,1,0:T(8,128)(2,1)S(1)} %pad_maximum_fusion.4.refs_4_), channel_id=1, source_target_pairs={{0,128},{128,256},{256,384},{384,0},{1,129},{129,257},{257,385},{3... | collective-permute-start | bytes 688136 | tf_op jit(solution)/shard_map/ppermute | solution.py:207
  83.4 26.0 %collective-permute-start.7 = (bf16[2,56,1024]{2,1,0:T(8,128)(2,1)S(1)}, bf16[2,56,1024]{2,1,0:T(8,128)(2,1)S(1)}, u32[]{:S(2)}, u32[]{:S(2)}) collective-permute-start(bf16[2,56,1024]{2,1,0:T(8,128)(2,1)S(1)} %pad_maximum_fusion.4.refs_4_), channel_id=1, source_target_pairs={{0,256},{128,384},{256,0},{384,128},{1,257},{129,385},{257,1},{385... | collective-permute-start | bytes 688136 | tf_op jit(solution)/shard_map/ppermute | solution.py:207
  86.4 23.0 %collective-permute-start.8 = (bf16[2,56,1024]{2,1,0:T(8,128)(2,1)S(1)}, bf16[2,56,1024]{2,1,0:T(8,128)(2,1)S(1)}, u32[]{:S(2)}, u32[]{:S(2)}) collective-permute-start(bf16[2,56,1024]{2,1,0:T(8,128)(2,1)S(1)} %pad_maximum_fusion.4.refs_4_), channel_id=1, source_target_pairs={{0,384},{128,0},{256,128},{384,256},{1,385},{129,1},{257,129},{385... | collective-permute-start | bytes 688136 | tf_op jit(solution)/shard_map/ppermute | solution.py:207
  90.0 4.7 %copy-start.5 = (bf16[4,128,448]{2,1,0:T(8,128)(2,1)}, bf16[4,128,448]{2,1,0:T(8,128)(2,1)S(1)}, u32[]{:S(2)}) copy-start(bf16[4,128,448]{2,1,0:T(8,128)(2,1)S(1)} %collective-permute-done.refs_3_) | copy-start | bytes 1376260
  90.0 1.4 copy-start.14
  94.6 5.0 %collective-permute-start.1 = (bf16[16,1024]{1,0:T(8,128)(2,1)S(1)}, bf16[16,1024]{1,0:T(8,128)(2,1)S(1)}, u32[]{:S(2)}, u32[]{:S(2)}) collective-permute-start(bf16[16,1024]{1,0:T(8,128)(2,1)S(1)} %shard_map.121), channel_id=1, source_target_pairs={{0,8},{8,0},{1,9},{9,1},{2,10},{10,2},{3,11},{11,3},{4,12},{12,4},... | collective-permute-start | bytes 98312 | tf_op jit(solution)/shard_map/ppermute | solution.py:207
  99.7 9.8 %collective-permute-start.2 = (bf16[2,16,1024]{2,1,0:T(8,128)(2,1)S(1)}, bf16[2,16,1024]{2,1,0:T(8,128)(2,1)S(1)}, u32[]{:S(2)}, u32[]{:S(2)}) collective-permute-start(bf16[2,16,1024]{2,1,0:T(8,128)(2,1)S(1)} %pad_maximum_fusion.5.refs_0_), channel_id=1, source_target_pairs={{0,16},{16,32},{32,48},{48,0},{1,17},{17,33},{33,49},{49,1},{2,18}... | collective-permute-start | bytes 196616 | tf_op jit(solution)/shard_map/ppermute | solution.py:207
  103.2 7.9 %collective-permute-start.3 = (bf16[2,16,1024]{2,1,0:T(8,128)(2,1)S(1)}, bf16[2,16,1024]{2,1,0:T(8,128)(2,1)S(1)}, u32[]{:S(2)}, u32[]{:S(2)}) collective-permute-start(bf16[2,16,1024]{2,1,0:T(8,128)(2,1)S(1)} %pad_maximum_fusion.5.refs_0_), channel_id=1, source_target_pairs={{0,32},{16,48},{32,0},{48,16},{1,33},{17,49},{33,1},{49,17},{2,34}... | collective-permute-start | bytes 196616 | tf_op jit(solution)/shard_map/ppermute | solution.py:207
  105.2 7.0 %collective-permute-start.4 = (bf16[2,16,1024]{2,1,0:T(8,128)(2,1)S(1)}, bf16[2,16,1024]{2,1,0:T(8,128)(2,1)S(1)}, u32[]{:S(2)}, u32[]{:S(2)}) collective-permute-start(bf16[2,16,1024]{2,1,0:T(8,128)(2,1)S(1)} %pad_maximum_fusion.5.refs_0_), channel_id=1, source_target_pairs={{0,48},{16,0},{32,16},{48,32},{1,49},{17,1},{33,17},{49,33},{2,50}... | collective-permute-start | bytes 196616 | tf_op jit(solution)/shard_map/ppermute | solution.py:207
  113.4 3.1 %copy-start.1 = (bf16[1,3584,128]{2,1,0:T(8,128)(2,1)S(1)}, bf16[1,3584,128]{2,1,0:T(8,128)(2,1)}, u32[]{:S(2)}) copy-start(bf16[1,3584,128]{2,1,0:T(8,128)(2,1)} %param.19) | copy-start | bytes 2752516
  113.4 3.1 %copy-start.11 = (bf16[1,3584]{1,0:T(2,128)(2,1)S(1)}, bf16[1,3584]{1,0:T(2,128)(2,1)}, u32[]{:S(2)}) copy-start(bf16[1,3584]{1,0:T(2,128)(2,1)} %router_ref.1) | copy-start | bytes 21508
  120.2 6.3 %copy-start.8 = (bf16[4,128,448]{2,1,0:T(8,128)(2,1)S(1)}, bf16[4,128,448]{2,1,0:T(8,128)(2,1)}, u32[]{:S(2)}) copy-start(bf16[4,128,448]{2,1,0:T(8,128)(2,1)} %copy-done.7) | copy-start | bytes 1376260
  120.2 6.4 %copy-start.6 = (bf16[4,128,448]{2,1,0:T(8,128)(2,1)S(1)}, bf16[4,128,448]{2,1,0:T(8,128)(2,1)}, u32[]{:S(2)}) copy-start(bf16[4,128,448]{2,1,0:T(8,128)(2,1)} %copy-done.5) | copy-start | bytes 1376260
  120.2 49.6 %all-to-all-start.1 = ((bf16[8,384,128]{2,1,0:T(8,128)(2,1)}), bf16[8,384,128]{2,1,0:T(8,128)(2,1)S(1)}, u32[]{:S(2)}, u32[]{:S(2)}) async-start(bf16[8,384,128]{2,1,0:T(8,128)(2,1)} %copy-done.4), calls=%async_computation.1 | async-start | bytes 1572864 | tf_op jit(solution)/shard_map/all_to_all | solution.py:302
  126.6 38.1 %collective-permute-start.10 = (bf16[2,128,448]{2,1,0:T(8,128)(2,1)S(1)}, bf16[2,128,448]{2,1,0:T(8,128)(2,1)S(1)}, u32[]{:S(2)}, u32[]{:S(2)}) collective-permute-start(bf16[2,128,448]{2,1,0:T(8,128)(2,1)S(1)} %pad_maximum_fusion.2), channel_id=1, source_target_pairs={{0,4},{1,5},{2,6},{3,7},{4,0},{5,1},{6,2},{7,3},{8,12},{9,13},{10,... | collective-permute-start | bytes 688136 | tf_op jit(solution)/shard_map/ppermute | solution.py:207
  133.9 30.8 %collective-permute-start.11 = (bf16[2,128,448]{2,1,0:T(8,128)(2,1)S(1)}, bf16[2,128,448]{2,1,0:T(8,128)(2,1)S(1)}, u32[]{:S(2)}, u32[]{:S(2)}) collective-permute-start(bf16[2,128,448]{2,1,0:T(8,128)(2,1)S(1)} %pad_maximum_fusion.3), channel_id=1, source_target_pairs={{0,6},{1,7},{2,0},{3,1},{4,2},{5,3},{6,4},{7,5},{8,14},{9,15},{10,... | collective-permute-start | bytes 688136 | tf_op jit(solution)/shard_map/ppermute | solution.py:207
  136.2 33.6 %collective-permute-start.9 = (bf16[2,128,448]{2,1,0:T(8,128)(2,1)S(1)}, bf16[2,128,448]{2,1,0:T(8,128)(2,1)S(1)}, u32[]{:S(2)}, u32[]{:S(2)}) collective-permute-start(bf16[2,128,448]{2,1,0:T(8,128)(2,1)S(1)} %pad_maximum_fusion.1), channel_id=1, source_target_pairs={{0,2},{1,3},{2,4},{3,5},{4,6},{5,7},{6,0},{7,1},{8,10},{9,11},{10,... | collective-permute-start | bytes 688136 | tf_op jit(solution)/shard_map/ppermute | solution.py:207
  172.0 21.5 %all-to-all-start.2 = ((bf16[64,4,736]{2,1,0:T(4,128)(2,1)}), bf16[64,4,736]{2,1,0:T(4,128)(2,1)S(1)}, u32[]{:S(2)}, u32[]{:S(2)}) async-start(bf16[64,4,736]{2,1,0:T(4,128)(2,1)} %reshape.18), calls=%async_computation.2 | async-start | bytes 786432 | tf_op jit(solution)/shard_map/all_to_all | solution.py:312
  (9 other events, 8.4 us)
Sparse Core Ops, SparseCore 0:
  11.6 43.7 all-gather.2

commit v4 on v3

--- a/solution.py
+++ b/solution.py
@@ -23,7 +23,7 @@
     in_specs = [
         pl.BlockSpec(memory_space=pltpu.SMEM if i in smem else pltpu.VMEM)
         for i in range(len(args))
-    ] + [pl.BlockSpec(memory_space=pl.ANY) for _ in after]
+    ] + [pl.BlockSpec(memory_space=pltpu.VMEM) for _ in after]
     if after:
         inner, count = body, len(args)
         body = lambda *refs: inner(*refs[:count], *refs[count + len(after) :])
@@ -65,9 +65,8 @@
     )
     place = jnp.where(rank == (slot % SLOTS).astype(F32), named, 0.0)
     place_ref[...] = place
-    send_ref[...] = jnp.dot(
-        place.astype(BF16), normalized, preferred_element_type=F32
-    ).astype(BF16)
+    sent = jnp.dot(place.astype(BF16), normalized, preferred_element_type=F32)
+    send_ref[...] = sent.reshape(send_ref.shape).astype(BF16)
 
 
 def attend(lengths_ref, queries_ref, cache_ref, context_ref):
@@ -86,17 +85,21 @@
     context_ref[...] = jnp.concatenate(found, axis=1).astype(BF16)
 
 
-def lift_heads(place_ref, context_ref, w_uv_ref, values_ref):
+def lift_heads(context_ref, w_uv_ref, values_ref):
     heads, latent, width = w_uv_ref.shape
     rows = values_ref.shape[0]
-    sources = context_ref.shape[0]
-    context = jnp.concatenate([context_ref[k, place_ref[TP]] for k in range(sources)], axis=0)
+    context = context_ref[...].reshape(rows * heads, latent)
     token, entry = iotas(rows, rows * heads)
     for h in range(heads):
         lifted = jnp.dot(context, w_uv_ref[h], preferred_element_type=F32).astype(BF16)
         pick = one_hot(entry == token * heads + h)
         mine = jnp.dot(pick, lifted, preferred_element_type=F32).astype(BF16)
         values_ref[:, h * width : (h + 1) * width] = mine
+
+
+def pair(first_ref, second_ref, out_ref):
+    out_ref[0] = first_ref[...]
+    out_ref[1] = second_ref[...]
 
 
 def split_down(place_ref, w_down_ref, keep_ref, send_ref):
@@ -127,8 +130,8 @@
 
 
 def lift_experts(rows_ref, w_gate_ref, w_up_ref, router_ref, attn_ref, inner_ref, score_ref):
-    rows = rows_ref[...]
-    slots = rows.shape[0]
+    slots, width = score_ref.shape[0], rows_ref.shape[2]
+    rows = rows_ref[...].astype(F32).reshape(slots, width).astype(BF16)
     gate = jnp.dot(rows, w_gate_ref[...], preferred_element_type=F32)
     lifted = jnp.dot(rows, w_up_ref[...], preferred_element_type=F32)
     column = jnp.broadcast_to(router_ref[...], (128, rows.shape[1]))
@@ -248,20 +251,21 @@
         jnp.swapaxes(latent_cache, 1, 2),
         smem=(0,),
     )
-    contexts = lax.all_gather(context, "y", axis=0)
-    out_pair = pair_up(w_out.T, "zh")
+    contexts = lax.all_to_all(context, "y", 0, 0, tiled=True)
+    out_other = shift(w_out.T, "zh", 1)
+    (out_pair,) = kernel_call(
+        pair, [((2, out_cols, depth), BF16)], w_out.T, out_other, after=(contexts,)
+    )
 
     send, place = kernel_call(
         prepare,
-        [((slots, model_width), BF16), ((slots, rows), F32)],
+        [((ep_size, SLOTS, model_width), BF16), ((slots, rows), F32)],
         hidden,
         norm_gain.reshape(1, model_width),
         expert_ids.T,
-        after=(context,),
-    )
-    named_rows = lax.all_to_all(
-        send.reshape(ep_size, SLOTS, model_width), EP, 0, 0, tiled=True
-    ).reshape(slots, model_width)
+        after=(out_other,),
+    )
+    named_rows = lax.all_to_all(send, EP, 0, 0, tiled=True)
 
     out_weights = gather(out_pair, "x")
     keep, pass_on = kernel_call(
@@ -270,7 +274,7 @@
         here,
         w_down[0],
         smem=(0,),
-        after=(send,),
+        after=(context,),
     )
     arrived = lax.ppermute(pass_on, "y", [(i, i ^ 1) for i in range(tp_size)])
     down = [jnp.stack([keep[k], arrived[k]]) for k in range(tp_size // 2)]
@@ -278,16 +282,19 @@
     (values,) = kernel_call(
         lift_heads,
         [((rows, depth), BF16)],
-        here,
         contexts,
         w_uv,
-        smem=(0,),
-        after=(arrived,),
+        after=(*down[1:], *out_weights[1:]),
         flops=30_000_000_000,
     )
     values = gather(pair_up(values, "c"), "zl")
     (attn_parts,) = kernel_call(
-        project, [((tp_size, rows * 8, 128), BF16)], here, *values, *out_weights, smem=(0,)
+        project,
+        [((tp_size, rows * 8, 128), BF16)],
+        here,
+        *values,
+        *out_weights,
+        smem=(0,),
     )
 
     inner, score = kernel_call(

time: 204 us -> 172 us (0.84)
  waiting for transfers between devices: 84.8 us -> 58.2 us
  starting transfers between devices: 74.5 us -> 88 us
  between operations: 13.8 us -> 0.39 us
  local copies, waits for them, and re-layouts: 17 us -> 10.9 us
    ppermute x11, waiting for transfers between devices: 70.9 us -> 23.8 us  [shift(): return lax.ppermute(value, axis, [(i, (i + k) % size) for i in range(size)])]
    all_to_all x1, waiting for transfers between devices: 0.01 us -> 20.6 us  [on_device(): inner = lax.all_to_all(inner, 'y', 0, 0, tiled=True)]
    ppermute x11, starting transfers between devices: 43 us -> 48.9 us  [shift(): return lax.ppermute(value, axis, [(i, (i + k) % size) for i in range(size)])]
    all_to_all x1 -> x2, starting transfers between devices: 15.1 us -> 20.4 us  [the longest x1 14.5 us: on_device(): named_rows = lax.all_to_all(send, EP, 0, 0, tiled=True)]
    reshape x2 -> x0, local copies, waits for them, and re-layouts: 4.49 us -> none  [the longest x1 3.02 us: on_device(): named_rows = lax.all_to_all(send.reshape(ep_size, SLOTS, model_width), EP...]
    unnamed x34 -> x48, local copies, waits for them, and re-layouts: 9.83 us -> 7.49 us
    all_to_all x1, starting transfers between devices: 6.84 us -> 8.92 us  [on_device(): lax.all_to_all(back.reshape(ep_size, SLOTS, PADDED + ATTN), EP, 0, 0, til...]
    pallas_call x8 -> x9, Pallas kernels: 12.4 us -> 12.4 us  [kernel_call(): pl.pallas_call(body, out_shape=tuple((jax.ShapeDtypeStruct(s, d) for s, d...]
  transfers between devices with their start and end apart: 16 -> 16, of which waited for: 7 -> 7; matrix products, arithmetic and copies ran while one was open for 2% -> 2% of each run, Pallas kernels for 3% -> 2%
where the time goes in v4:
time: 172 us; the launch traced here: 171 us
  starting transfers between devices  88 us (51%)
  waiting for transfers between devices  58.2 us (34%)
  Pallas kernels  12.4 us (7%)
  local copies, waits for them, and re-layouts  10.9 us (6%)
    ppermute x11, starting transfers between devices, shift(): return lax.ppermute(value, axis, [(i, (i + k) % size) for i in range(size)])  48.9 us
    ppermute x11, waiting for transfers between devices, shift(): return lax.ppermute(value, axis, [(i, (i + k) % size) for i in range(size)])  23.8 us
    all_to_all x1, waiting for transfers between devices, on_device(): inner = lax.all_to_all(inner, 'y', 0, 0, tiled=True)  20.6 us
    all_to_all x1, starting transfers between devices, on_device(): named_rows = lax.all_to_all(send, EP, 0, 0, tiled=True)  14.5 us
    all_to_all x1, waiting for transfers between devices, on_device(): lax.all_to_all(back.reshape(ep_size, SLOTS, PADDED + ATTN), EP, 0, 0, til...  13.8 us
    pallas_call x9, Pallas kernels, kernel_call(): pl.pallas_call(body, out_shape=tuple((jax.ShapeDtypeStruct(s, d) for s, d...  12.4 us
    all_to_all x1, starting transfers between devices, on_device(): lax.all_to_all(back.reshape(ep_size, SLOTS, PADDED + ATTN), EP, 0, 0, til...  8.92 us
    unnamed x48, local copies, waits for them, and re-layouts  7.49 us
  transfers between devices with their start and end apart: 16, of which 7 were waited for; matrix products, arithmetic and copies ran while one was open for 2% of the time, Pallas kernels for 2%

profile of v4, /device:TPU:1, one launch (start us, length us, event | category | flops | bytes accessed | tf_op | source)
XLA Modules:
  0.0 170.9 jit_solution(1206327940431371507)
XLA Ops:
  2.8 2.2 %shard_map.119.refs_2_ = bf16[8,16,512]{2,1,0:T(8,128)(2,1)} custom-call(s32[2]{0:T(128)S(1)} %copy-done.20, bf16[2,64,576]{2,1,0:T(8,128)(2,1)S(1)} %copy-done.8, bf16[2,576,384]{2,1,0:T(8,128)(2,1)S(1)} %bitcast.16), custom_call_target="tpu_custom_call" | custom-call | bytes 1032200 | tf_op jit(solution)/shard_map/pallas_call | solution.py:32
  6.6 4.0 %collective-permute-start.1 = (bf16[4,128,448]{2,1,0:T(8,128)(2,1)S(1)}, bf16[4,128,448]{2,1,0:T(8,128)(2,1)S(1)}, u32[]{:S(2)}, u32[]{:S(2)}) collective-permute-start(bf16[4,128,448]{2,1,0:T(8,128)(2,1)S(1)} %get-tuple-element.13), channel_id=1, source_target_pairs={{0,1},{1,0},{2,3},{3,2},{4,5},{5,4},{6,7},{7,6},{8,9},{9,8},{10,11... | collective-permute-start | bytes 1376264 | tf_op jit(solution)/shard_map/ppermute | solution.py:279
  10.7 5.9 %all-to-all-start.1 = ((bf16[8,16,512]{2,1,0:T(8,128)(2,1)}), bf16[8,16,512]{2,1,0:T(8,128)(2,1)S(1)}, u32[]{:S(2)}, u32[]{:S(2)}) async-start(bf16[8,16,512]{2,1,0:T(8,128)(2,1)} %shard_map.119.refs_2_), calls=%async_computation.1 | async-start | bytes 262144 | tf_op jit(solution)/shard_map/all_to_all | solution.py:254
  16.6 10.6 %collective-permute-start = (bf16[56,1024]{1,0:T(8,128)(2,1)S(1)}, bf16[56,1024]{1,0:T(8,128)(2,1)S(1)}, u32[]{:S(2)}, u32[]{:S(2)}) collective-permute-start(bf16[56,1024]{1,0:T(8,128)(2,1)S(1)} %bitcast.17), channel_id=1, source_target_pairs={{0,64},{64,0},{1,65},{65,1},{2,66},{66,2},{3,67},{67,3},{4,68},{68... | collective-permute-start | bytes 344072 | tf_op jit(solution)/shard_map/ppermute | solution.py:210
  32.3 14.5 %all-to-all-start = ((bf16[64,4,3584]{2,1,0:T(4,128)(2,1)}), bf16[64,4,3584]{2,1,0:T(4,128)(2,1)S(1)}, u32[]{:S(2)}, u32[]{:S(2)}) async-start(bf16[64,4,3584]{2,1,0:T(4,128)(2,1)} %copy-done), calls=%async_computation | async-start | bytes 3670016 | tf_op jit(solution)/shard_map/all_to_all | solution.py:268
  46.9 3.4 %collective-permute-start.5 = (bf16[2,56,1024]{2,1,0:T(8,128)(2,1)S(1)}, bf16[2,56,1024]{2,1,0:T(8,128)(2,1)S(1)}, u32[]{:S(2)}, u32[]{:S(2)}) collective-permute-start(bf16[2,56,1024]{2,1,0:T(8,128)(2,1)S(1)} %shard_map.121.refs_4_), channel_id=1, source_target_pairs={{0,128},{128,256},{256,384},{384,0},{1,129},{129,257},{257,385},{3... | collective-permute-start | bytes 688136 | tf_op jit(solution)/shard_map/ppermute | solution.py:210
  50.3 4.5 %collective-permute-start.6 = (bf16[2,56,1024]{2,1,0:T(8,128)(2,1)S(1)}, bf16[2,56,1024]{2,1,0:T(8,128)(2,1)S(1)}, u32[]{:S(2)}, u32[]{:S(2)}) collective-permute-start(bf16[2,56,1024]{2,1,0:T(8,128)(2,1)S(1)} %shard_map.121.refs_4_), channel_id=1, source_target_pairs={{0,256},{128,384},{256,0},{384,128},{1,257},{129,385},{257,1},{385... | collective-permute-start | bytes 688136 | tf_op jit(solution)/shard_map/ppermute | solution.py:210
  54.8 3.0 %collective-permute-start.7 = (bf16[2,56,1024]{2,1,0:T(8,128)(2,1)S(1)}, bf16[2,56,1024]{2,1,0:T(8,128)(2,1)S(1)}, u32[]{:S(2)}, u32[]{:S(2)}) collective-permute-start(bf16[2,56,1024]{2,1,0:T(8,128)(2,1)S(1)} %shard_map.121.refs_4_), channel_id=1, source_target_pairs={{0,384},{128,0},{256,128},{384,256},{1,385},{129,1},{257,129},{385... | collective-permute-start | bytes 688136 | tf_op jit(solution)/shard_map/ppermute | solution.py:210
  58.5 4.3 %collective-permute-start.2 = (bf16[2,128,448]{2,1,0:T(8,128)(2,1)S(1)}, bf16[2,128,448]{2,1,0:T(8,128)(2,1)S(1)}, u32[]{:S(2)}, u32[]{:S(2)}) collective-permute-start(bf16[2,128,448]{2,1,0:T(8,128)(2,1)S(1)} %pad_maximum_fusion), channel_id=1, source_target_pairs={{0,2},{1,3},{2,4},{3,5},{4,6},{5,7},{6,0},{7,1},{8,10},{9,11},{10,... | collective-permute-start | bytes 688136 | tf_op jit(solution)/shard_map/ppermute | solution.py:210
  62.8 5.2 %collective-permute-start.3 = (bf16[2,128,448]{2,1,0:T(8,128)(2,1)S(1)}, bf16[2,128,448]{2,1,0:T(8,128)(2,1)S(1)}, u32[]{:S(2)}, u32[]{:S(2)}) collective-permute-start(bf16[2,128,448]{2,1,0:T(8,128)(2,1)S(1)} %pad_maximum_fusion.1), channel_id=1, source_target_pairs={{0,4},{1,5},{2,6},{3,7},{4,0},{5,1},{6,2},{7,3},{8,12},{9,13},{10,... | collective-permute-start | bytes 688136 | tf_op jit(solution)/shard_map/ppermute | solution.py:210
  68.1 5.2 %collective-permute-start.4 = (bf16[2,128,448]{2,1,0:T(8,128)(2,1)S(1)}, bf16[2,128,448]{2,1,0:T(8,128)(2,1)S(1)}, u32[]{:S(2)}, u32[]{:S(2)}) collective-permute-start(bf16[2,128,448]{2,1,0:T(8,128)(2,1)S(1)} %pad_maximum_fusion.2), channel_id=1, source_target_pairs={{0,6},{1,7},{2,0},{3,1},{4,2},{5,3},{6,4},{7,5},{8,14},{9,15},{10,... | collective-permute-start | bytes 688136 | tf_op jit(solution)/shard_map/ppermute | solution.py:210
  73.4 9.8 %collective-permute-done.3.refs_3_ = bf16[2,128,448]{2,1,0:T(8,128)(2,1)S(1)} collective-permute-done((bf16[2,128,448]{2,1,0:T(8,128)(2,1)S(1)}, bf16[2,128,448]{2,1,0:T(8,128)(2,1)S(1)}, u32[]{:S(2)}, u32[]{:S(2)}) %collective-permute-start.3) | collective-permute-done | bytes 229408 | tf_op jit(solution)/shard_map/ppermute | solution.py:210
  83.2 9.8 %collective-permute-done.4.refs_4_ = bf16[2,128,448]{2,1,0:T(8,128)(2,1)S(1)} collective-permute-done((bf16[2,128,448]{2,1,0:T(8,128)(2,1)S(1)}, bf16[2,128,448]{2,1,0:T(8,128)(2,1)S(1)}, u32[]{:S(2)}, u32[]{:S(2)}) %collective-permute-start.4) | collective-permute-done | bytes 229408 | tf_op jit(solution)/shard_map/ppermute | solution.py:210
  94.4 2.5 %collective-permute-start.8 = (bf16[16,1024]{1,0:T(8,128)(2,1)S(1)}, bf16[16,1024]{1,0:T(8,128)(2,1)S(1)}, u32[]{:S(2)}, u32[]{:S(2)}) collective-permute-start(bf16[16,1024]{1,0:T(8,128)(2,1)S(1)} %shard_map.122), channel_id=1, source_target_pairs={{0,8},{8,0},{1,9},{9,1},{2,10},{10,2},{3,11},{11,3},{4,12},{12,4},... | collective-permute-start | bytes 98312 | tf_op jit(solution)/shard_map/ppermute | solution.py:210
  97.8 3.1 %collective-permute-start.9 = (bf16[2,16,1024]{2,1,0:T(8,128)(2,1)S(1)}, bf16[2,16,1024]{2,1,0:T(8,128)(2,1)S(1)}, u32[]{:S(2)}, u32[]{:S(2)}) collective-permute-start(bf16[2,16,1024]{2,1,0:T(8,128)(2,1)S(1)} %pad_maximum_fusion.4.refs_0_), channel_id=1, source_target_pairs={{0,16},{16,32},{32,48},{48,0},{1,17},{17,33},{33,49},{49,1},{2,18}... | collective-permute-start | bytes 196616 | tf_op jit(solution)/shard_map/ppermute | solution.py:210
  100.9 4.0 %collective-permute-start.10 = (bf16[2,16,1024]{2,1,0:T(8,128)(2,1)S(1)}, bf16[2,16,1024]{2,1,0:T(8,128)(2,1)S(1)}, u32[]{:S(2)}, u32[]{:S(2)}) collective-permute-start(bf16[2,16,1024]{2,1,0:T(8,128)(2,1)S(1)} %pad_maximum_fusion.4.refs_0_), channel_id=1, source_target_pairs={{0,32},{16,48},{32,0},{48,16},{1,33},{17,49},{33,1},{49,17},{2,34}... | collective-permute-start | bytes 196616 | tf_op jit(solution)/shard_map/ppermute | solution.py:210
  104.9 3.1 %collective-permute-start.11 = (bf16[2,16,1024]{2,1,0:T(8,128)(2,1)S(1)}, bf16[2,16,1024]{2,1,0:T(8,128)(2,1)S(1)}, u32[]{:S(2)}, u32[]{:S(2)}) collective-permute-start(bf16[2,16,1024]{2,1,0:T(8,128)(2,1)S(1)} %pad_maximum_fusion.4.refs_0_), channel_id=1, source_target_pairs={{0,48},{16,0},{32,16},{48,32},{1,49},{17,1},{33,17},{49,33},{2,50}... | collective-permute-start | bytes 196616 | tf_op jit(solution)/shard_map/ppermute | solution.py:210
  108.0 1.9 %collective-permute-done.11.refs_3_ = bf16[2,16,1024]{2,1,0:T(8,128)(2,1)S(1)} collective-permute-done((bf16[2,16,1024]{2,1,0:T(8,128)(2,1)S(1)}, bf16[2,16,1024]{2,1,0:T(8,128)(2,1)S(1)}, u32[]{:S(2)}, u32[]{:S(2)}) %collective-permute-start.11) | collective-permute-done | bytes 65568 | tf_op jit(solution)/shard_map/ppermute | solution.py:210
  112.4 1.6 shard_map.124
  115.5 5.7 %all-to-all-start.2 = ((bf16[8,384,128]{2,1,0:T(8,128)(2,1)}), bf16[8,384,128]{2,1,0:T(8,128)(2,1)S(1)}, u32[]{:S(2)}, u32[]{:S(2)}) async-start(bf16[8,384,128]{2,1,0:T(8,128)(2,1)} %copy-done.5), calls=%async_computation.2 | async-start | bytes 1572864 | tf_op jit(solution)/shard_map/all_to_all | solution.py:309
  122.2 20.6 %all-to-all-done.2.refs_0_ = bf16[8,384,128]{2,1,0:T(8,128)(2,1)S(1)} async-done(((bf16[8,384,128]{2,1,0:T(8,128)(2,1)}), bf16[8,384,128]{2,1,0:T(8,128)(2,1)S(1)}, u32[]{:S(2)}, u32[]{:S(2)}) %all-to-all-start.2) | async-done | bytes 786464 | tf_op jit(solution)/shard_map/all_to_all | solution.py:309
  145.0 8.9 %all-to-all-start.3 = ((bf16[64,4,736]{2,1,0:T(4,128)(2,1)}), bf16[64,4,736]{2,1,0:T(4,128)(2,1)S(1)}, u32[]{:S(2)}, u32[]{:S(2)}) async-start(bf16[64,4,736]{2,1,0:T(4,128)(2,1)} %reshape.10), calls=%async_computation.3 | async-start | bytes 786432 | tf_op jit(solution)/shard_map/all_to_all | solution.py:319
  154.8 13.8 %all-to-all-done.3 = bf16[64,4,736]{2,1,0:T(4,128)(2,1)S(1)} async-done(((bf16[64,4,736]{2,1,0:T(4,128)(2,1)}), bf16[64,4,736]{2,1,0:T(4,128)(2,1)S(1)}, u32[]{:S(2)}, u32[]{:S(2)}) %all-to-all-start.3) | async-done | bytes 376864 | tf_op jit(solution)/shard_map/all_to_all | solution.py:319
  168.8 2.1 %shard_map.126 = bf16[16,448]{1,0:T(8,128)(2,1)} custom-call(s32[5]{0:T(128)S(1)} %copy-done.18, bf16[256,736]{1,0:T(8,128)(2,1)S(1)} %reshape.11.back_ref, f32[256,16]{1,0:T(8,128)S(1)} %copy-done.11, bf16[16,448]{1,0:T(8,128)(2,1)S(1)} %constant_dynamic-slice_fusion.own_ref), custom_call_target="tpu_custom_call" | custom-call | bytes 407572 | tf_op jit(solution)/shard_map/pallas_call | solution.py:32
  (77 shorter events, 20.8 us)
Async XLA Ops:
  2.8 26.7 %copy-start.9 = (bf16[16,3584]{1,0:T(8,128)(2,1)S(1)}, bf16[16,3584]{1,0:T(8,128)(2,1)}, u32[]{:S(2)}) copy-start(bf16[16,3584]{1,0:T(8,128)(2,1)} %refs_0_.1) | copy-start | bytes 344068
  2.8 26.7 %copy-start.19 = (s32[16,8]{0,1:T(8,128)S(1)}, s32[16,8]{0,1:T(8,128)}, u32[]{:S(2)}) copy-start(s32[16,8]{0,1:T(8,128)} %param.17) | copy-start | bytes 1540
  6.6 51.2 %collective-permute-start.1 = (bf16[4,128,448]{2,1,0:T(8,128)(2,1)S(1)}, bf16[4,128,448]{2,1,0:T(8,128)(2,1)S(1)}, u32[]{:S(2)}, u32[]{:S(2)}) collective-permute-start(bf16[4,128,448]{2,1,0:T(8,128)(2,1)S(1)} %get-tuple-element.13), channel_id=1, source_target_pairs={{0,1},{1,0},{2,3},{3,2},{4,5},{5,4},{6,7},{7,6},{8,9},{9,8},{10,11... | collective-permute-start | bytes 1376264 | tf_op jit(solution)/shard_map/ppermute | solution.py:279
  10.7 21.7 %all-to-all-start.1 = ((bf16[8,16,512]{2,1,0:T(8,128)(2,1)}), bf16[8,16,512]{2,1,0:T(8,128)(2,1)S(1)}, u32[]{:S(2)}, u32[]{:S(2)}) async-start(bf16[8,16,512]{2,1,0:T(8,128)(2,1)} %shard_map.119.refs_2_), calls=%async_computation.1 | async-start | bytes 262144 | tf_op jit(solution)/shard_map/all_to_all | solution.py:254
  16.6 12.9 %collective-permute-start = (bf16[56,1024]{1,0:T(8,128)(2,1)S(1)}, bf16[56,1024]{1,0:T(8,128)(2,1)S(1)}, u32[]{:S(2)}, u32[]{:S(2)}) collective-permute-start(bf16[56,1024]{1,0:T(8,128)(2,1)S(1)} %bitcast.17), channel_id=1, source_target_pairs={{0,64},{64,0},{1,65},{65,1},{2,66},{66,2},{3,67},{67,3},{4,68},{68... | collective-permute-start | bytes 344072 | tf_op jit(solution)/shard_map/ppermute | solution.py:210
  32.3 78.8 %all-to-all-start = ((bf16[64,4,3584]{2,1,0:T(4,128)(2,1)}), bf16[64,4,3584]{2,1,0:T(4,128)(2,1)S(1)}, u32[]{:S(2)}, u32[]{:S(2)}) async-start(bf16[64,4,3584]{2,1,0:T(4,128)(2,1)} %copy-done), calls=%async_computation | async-start | bytes 3670016 | tf_op jit(solution)/shard_map/all_to_all | solution.py:268
  46.8 46.1 %copy-start.21 = (bf16[8,512,128]{2,1,0:T(8,128)(2,1)S(1)}, bf16[8,512,128]{2,1,0:T(8,128)(2,1)}, u32[]{:S(2)}) copy-start(bf16[8,512,128]{2,1,0:T(8,128)(2,1)} %refs_1_.1) | copy-start | bytes 3145732
  46.9 21.3 %collective-permute-start.5 = (bf16[2,56,1024]{2,1,0:T(8,128)(2,1)S(1)}, bf16[2,56,1024]{2,1,0:T(8,128)(2,1)S(1)}, u32[]{:S(2)}, u32[]{:S(2)}) collective-permute-start(bf16[2,56,1024]{2,1,0:T(8,128)(2,1)S(1)} %shard_map.121.refs_4_), channel_id=1, source_target_pairs={{0,128},{128,256},{256,384},{384,0},{1,129},{129,257},{257,385},{3... | collective-permute-start | bytes 688136 | tf_op jit(solution)/shard_map/ppermute | solution.py:210
  50.3 23.0 %collective-permute-start.6 = (bf16[2,56,1024]{2,1,0:T(8,128)(2,1)S(1)}, bf16[2,56,1024]{2,1,0:T(8,128)(2,1)S(1)}, u32[]{:S(2)}, u32[]{:S(2)}) collective-permute-start(bf16[2,56,1024]{2,1,0:T(8,128)(2,1)S(1)} %shard_map.121.refs_4_), channel_id=1, source_target_pairs={{0,256},{128,384},{256,0},{384,128},{1,257},{129,385},{257,1},{385... | collective-permute-start | bytes 688136 | tf_op jit(solution)/shard_map/ppermute | solution.py:210
  54.8 18.5 %collective-permute-start.7 = (bf16[2,56,1024]{2,1,0:T(8,128)(2,1)S(1)}, bf16[2,56,1024]{2,1,0:T(8,128)(2,1)S(1)}, u32[]{:S(2)}, u32[]{:S(2)}) collective-permute-start(bf16[2,56,1024]{2,1,0:T(8,128)(2,1)S(1)} %shard_map.121.refs_4_), channel_id=1, source_target_pairs={{0,384},{128,0},{256,128},{384,256},{1,385},{129,1},{257,129},{385... | collective-permute-start | bytes 688136 | tf_op jit(solution)/shard_map/ppermute | solution.py:210
  58.5 14.8 %collective-permute-start.2 = (bf16[2,128,448]{2,1,0:T(8,128)(2,1)S(1)}, bf16[2,128,448]{2,1,0:T(8,128)(2,1)S(1)}, u32[]{:S(2)}, u32[]{:S(2)}) collective-permute-start(bf16[2,128,448]{2,1,0:T(8,128)(2,1)S(1)} %pad_maximum_fusion), channel_id=1, source_target_pairs={{0,2},{1,3},{2,4},{3,5},{4,6},{5,7},{6,0},{7,1},{8,10},{9,11},{10,... | collective-permute-start | bytes 688136 | tf_op jit(solution)/shard_map/ppermute | solution.py:210
  62.8 20.3 %collective-permute-start.3 = (bf16[2,128,448]{2,1,0:T(8,128)(2,1)S(1)}, bf16[2,128,448]{2,1,0:T(8,128)(2,1)S(1)}, u32[]{:S(2)}, u32[]{:S(2)}) collective-permute-start(bf16[2,128,448]{2,1,0:T(8,128)(2,1)S(1)} %pad_maximum_fusion.1), channel_id=1, source_target_pairs={{0,4},{1,5},{2,6},{3,7},{4,0},{5,1},{6,2},{7,3},{8,12},{9,13},{10,... | collective-permute-start | bytes 688136 | tf_op jit(solution)/shard_map/ppermute | solution.py:210
  68.1 41.8 %copy-start.17 = (s32[5]{0:T(128)S(1)}, s32[5]{0:T(128)}, u32[]{:S(2)}) copy-start(s32[5]{0:T(128)} %copy-done.16) | copy-start | bytes 64
  68.1 43.1 %copy-start.15 = (bf16[1,3584]{1,0:T(2,128)(2,1)S(1)}, bf16[1,3584]{1,0:T(2,128)(2,1)}, u32[]{:S(2)}) copy-start(bf16[1,3584]{1,0:T(2,128)(2,1)} %router_ref.1) | copy-start | bytes 21508
  68.1 24.8 %collective-permute-start.4 = (bf16[2,128,448]{2,1,0:T(8,128)(2,1)S(1)}, bf16[2,128,448]{2,1,0:T(8,128)(2,1)S(1)}, u32[]{:S(2)}, u32[]{:S(2)}) collective-permute-start(bf16[2,128,448]{2,1,0:T(8,128)(2,1)S(1)} %pad_maximum_fusion.2), channel_id=1, source_target_pairs={{0,6},{1,7},{2,0},{3,1},{4,2},{5,3},{6,4},{7,5},{8,14},{9,15},{10,... | collective-permute-start | bytes 688136 | tf_op jit(solution)/shard_map/ppermute | solution.py:210
  94.4 3.4 %collective-permute-start.8 = (bf16[16,1024]{1,0:T(8,128)(2,1)S(1)}, bf16[16,1024]{1,0:T(8,128)(2,1)S(1)}, u32[]{:S(2)}, u32[]{:S(2)}) collective-permute-start(bf16[16,1024]{1,0:T(8,128)(2,1)S(1)} %shard_map.122), channel_id=1, source_target_pairs={{0,8},{8,0},{1,9},{9,1},{2,10},{10,2},{3,11},{11,3},{4,12},{12,4},... | collective-permute-start | bytes 98312 | tf_op jit(solution)/shard_map/ppermute | solution.py:210
  97.8 10.2 %collective-permute-start.9 = (bf16[2,16,1024]{2,1,0:T(8,128)(2,1)S(1)}, bf16[2,16,1024]{2,1,0:T(8,128)(2,1)S(1)}, u32[]{:S(2)}, u32[]{:S(2)}) collective-permute-start(bf16[2,16,1024]{2,1,0:T(8,128)(2,1)S(1)} %pad_maximum_fusion.4.refs_0_), channel_id=1, source_target_pairs={{0,16},{16,32},{32,48},{48,0},{1,17},{17,33},{33,49},{49,1},{2,18}... | collective-permute-start | bytes 196616 | tf_op jit(solution)/shard_map/ppermute | solution.py:210
  100.9 7.1 %collective-permute-start.10 = (bf16[2,16,1024]{2,1,0:T(8,128)(2,1)S(1)}, bf16[2,16,1024]{2,1,0:T(8,128)(2,1)S(1)}, u32[]{:S(2)}, u32[]{:S(2)}) collective-permute-start(bf16[2,16,1024]{2,1,0:T(8,128)(2,1)S(1)} %pad_maximum_fusion.4.refs_0_), channel_id=1, source_target_pairs={{0,32},{16,48},{32,0},{48,16},{1,33},{17,49},{33,1},{49,17},{2,34}... | collective-permute-start | bytes 196616 | tf_op jit(solution)/shard_map/ppermute | solution.py:210
  104.9 5.0 %collective-permute-start.11 = (bf16[2,16,1024]{2,1,0:T(8,128)(2,1)S(1)}, bf16[2,16,1024]{2,1,0:T(8,128)(2,1)S(1)}, u32[]{:S(2)}, u32[]{:S(2)}) collective-permute-start(bf16[2,16,1024]{2,1,0:T(8,128)(2,1)S(1)} %pad_maximum_fusion.4.refs_0_), channel_id=1, source_target_pairs={{0,48},{16,0},{32,16},{48,32},{1,49},{17,1},{33,17},{49,33},{2,50}... | collective-permute-start | bytes 196616 | tf_op jit(solution)/shard_map/ppermute | solution.py:210
  115.5 27.3 %copy-start.7 = (bf16[2,128,448]{2,1,0:T(8,128)(2,1)S(1)}, bf16[2,128,448]{2,1,0:T(8,128)(2,1)}, u32[]{:S(2)}) copy-start(bf16[2,128,448]{2,1,0:T(8,128)(2,1)} %copy-done.6) | copy-start | bytes 688132
  115.5 27.3 %copy-start.18 = (s32[5]{0:T(128)S(1)}, s32[5]{0:T(128)}, u32[]{:S(2)}) copy-start(s32[5]{0:T(128)} %copy-done.16) | copy-start | bytes 64
  115.5 27.3 %copy-start.14 = (bf16[256,128]{1,0:T(8,128)(2,1)S(1)}, bf16[256,128]{1,0:T(8,128)(2,1)}, u32[]{:S(2)}) copy-start(bf16[256,128]{1,0:T(8,128)(2,1)} %copy-done.13) | copy-start | bytes 196612
  115.5 27.2 %all-to-all-start.2 = ((bf16[8,384,128]{2,1,0:T(8,128)(2,1)}), bf16[8,384,128]{2,1,0:T(8,128)(2,1)S(1)}, u32[]{:S(2)}, u32[]{:S(2)}) async-start(bf16[8,384,128]{2,1,0:T(8,128)(2,1)} %copy-done.5), calls=%async_computation.2 | async-start | bytes 1572864 | tf_op jit(solution)/shard_map/all_to_all | solution.py:309
  145.0 23.5 %all-to-all-start.3 = ((bf16[64,4,736]{2,1,0:T(4,128)(2,1)}), bf16[64,4,736]{2,1,0:T(4,128)(2,1)S(1)}, u32[]{:S(2)}, u32[]{:S(2)}) async-start(bf16[64,4,736]{2,1,0:T(4,128)(2,1)} %reshape.10), calls=%async_computation.3 | async-start | bytes 786432 | tf_op jit(solution)/shard_map/all_to_all | solution.py:319
  (16 other events, 141.4 us)

commit v5 on v4

v5 whole, which is shorter than its diff:
```python
import jax
import jax.numpy as jnp
from jax import lax
from jax.experimental import pallas as pl
from jax.experimental.pallas import tpu as pltpu
from jax.sharding import Mesh, PartitionSpec as P

ROUTE_SCALE = 2.5
EPSILON = 1e-06
SCORE_SCALE = 192.0 ** (-0.5)
SLOTS = 4
EP = ("x", "zh", "zl", "c")
TP, X, ZH, ZL, CORE = range(5)
PADDED = 512
NT = (((1,), (1,)), ((), ()))
TN = (((0,), (0,)), ((), ()))
F32 = jnp.float32
BF16 = jnp.bfloat16


def kernel_call(body, outs, *args, smem=(), after=(), flops=0):
    in_specs = [
        pl.BlockSpec(memory_space=pltpu.SMEM if i in smem else pltpu.VMEM)
        for i in range(len(args))
    ] + [pl.BlockSpec(memory_space=pltpu.VMEM) for _ in after]
    if after:
        inner, count = body, len(args)
        body = lambda *refs: inner(*refs[:count], *refs[count + len(after) :])
    vmem = pl.BlockSpec(memory_space=pltpu.VMEM)
    nbytes = sum(a.size * a.dtype.itemsize for a in args)
    return pl.pallas_call(
        body,
        out_shape=tuple(jax.ShapeDtypeStruct(s, d) for s, d in outs),
        in_specs=in_specs,
        out_specs=tuple(vmem for _ in outs),
        compiler_params=pltpu.CompilerParams(vmem_limit_bytes=40 << 20),
        cost_estimate=pl.CostEstimate(flops=flops, bytes_accessed=nbytes, transcendentals=0),
    )(*args, *after)


def one_hot(condition):
    return condition.astype(F32).astype(BF16)


def iotas(*shape):
    return lax.broadcasted_iota(jnp.int32, shape, 0), lax.broadcasted_iota(jnp.int32, shape, 1)


def prepare(hidden_ref, gain_ref, ids_ref, send_ref, place_ref):
    values = hidden_ref[...].astype(F32)
    factor = lax.rsqrt(jnp.mean(values * values, axis=-1, keepdims=True) + EPSILON)
    normalized = (values * factor * gain_ref[...].astype(F32)).astype(BF16)
    slots, rows = place_ref.shape
    slot = lax.broadcasted_iota(jnp.int32, (slots, rows), 0)
    named = jnp.zeros((slots, rows), jnp.bool_)
    for k in range(ids_ref.shape[0]):
        named = named | (ids_ref[k : k + 1, :] == slot // SLOTS)
    named = named.astype(F32)
    earlier = lax.broadcasted_iota(jnp.int32, (rows, rows), 0) < lax.broadcasted_iota(
        jnp.int32, (rows, rows), 1
    )
    rank = jnp.dot(
        named.astype(BF16), earlier.astype(F32).astype(BF16), preferred_element_type=F32
    )
    place = jnp.where(rank == (slot % SLOTS).astype(F32), named, 0.0)
    place_ref[...] = place
    sent = jnp.dot(place.astype(BF16), normalized, preferred_element_type=F32)
    send_ref[...] = sent.reshape(send_ref.shape).astype(BF16)


def attend(lengths_ref, queries_ref, cache_ref, context_ref):
    rows, heads, _ = queries_ref.shape
    groups, _, latent = context_ref.shape
    found = []
    for r in range(rows):
        keys = cache_ref[r]
        scores = jnp.dot(queries_ref[r], keys, preferred_element_type=F32) * SCORE_SCALE
        positions = lax.broadcasted_iota(jnp.int32, scores.shape, 1)
        scores = jnp.where(positions < lengths_ref[r], scores, -1e30)
        raised = jnp.exp(scores - jnp.max(scores, axis=-1, keepdims=True))
        soft = (raised / jnp.sum(raised, axis=-1, keepdims=True)).astype(BF16)
        context = lax.dot_general(soft, keys[:latent], NT, preferred_element_type=F32)
        found.append(context.reshape(groups, heads // groups, latent))
    context_ref[...] = jnp.concatenate(found, axis=1).astype(BF16)


def lift_heads(inner_ref, w_uv_ref, values_ref):
    heads, latent, width = w_uv_ref.shape
    rows = values_ref.shape[0]
    sources, depth, lanes = inner_ref.shape
    share = rows * heads // sources
    first = depth - share * latent // lanes
    context = jnp.concatenate(
        [
            inner_ref[:, first + q * share : first + (q + 1) * share, :]
            for q in range(latent // lanes)
        ],
        axis=2,
    ).reshape(rows * heads, latent)
    token, entry = iotas(rows, rows * heads)
    for h in range(heads):
        lifted = jnp.dot(context, w_uv_ref[h], preferred_element_type=F32).astype(BF16)
        pick = one_hot(entry == token * heads + h)
        mine = jnp.dot(pick, lifted, preferred_element_type=F32).astype(BF16)
        values_ref[:, h * width : (h + 1) * width] = mine


def split_down(place_ref, w_down_ref, *out_refs):
    slices = len(out_refs)
    width = out_refs[0].shape[1]
    for s in range(slices):
        for k in range(slices):

            @pl.when((s - place_ref[TP] + slices) % slices == k)
            def _(s=s, k=k):
                out_refs[k][...] = w_down_ref[:, s * width : (s + 1) * width]


def project(place_ref, *refs):
    *parts, out_ref = refs
    slices = 8
    values = jnp.concatenate(
        [part[...].reshape(-1, part.shape[2]) for part in parts[:4]], axis=0
    )
    rows = values.shape[0] // slices
    for k in range(4):
        for j in range(2):
            weights = parts[4 + k][j]
            part = lax.dot_general(values, weights, NT, preferred_element_type=F32)
            part = jnp.concatenate(
                [part, jnp.zeros((part.shape[0], 64 - part.shape[1]), F32)], axis=1
            ).reshape(slices, rows, 64)
            part = jnp.concatenate([part[:, : rows // 2], part[:, rows // 2 :]], axis=2)
            part = part.astype(BF16)
            tp = (place_ref[X] - k + 4) % 4 * 2 + (place_ref[ZH] + j) % 2
            for b in range(slices):
                zl = (place_ref[ZL] - b // 2 + 4) % 4
                core = (place_ref[CORE] + b) % 2
                out_ref[(zl * 2 + core) * slices + tp] = part[b]


def lift_experts(rows_ref, w_gate_ref, w_up_ref, router_ref, context_ref, inner_ref, score_ref):
    slots, width = score_ref.shape[0], rows_ref.shape[2]
    rows = rows_ref[...].astype(F32).reshape(slots, width).astype(BF16)
    gate = jnp.dot(rows, w_gate_ref[...], preferred_element_type=F32)
    lifted = jnp.dot(rows, w_up_ref[...], preferred_element_type=F32)
    column = jnp.broadcast_to(router_ref[...], (128, width))
    logits = lax.dot_general(rows, column, NT, preferred_element_type=F32)
    inner = (gate / (1.0 + jnp.exp(-gate)) * lifted).astype(BF16)
    copies, share, latent = context_ref.shape
    lanes = inner_ref.shape[2]
    for copy in range(copies):
        inner_ref[copy, :slots] = inner
        for q in range(latent // lanes):
            first = slots + q * share
            inner_ref[copy, first : first + share] = context_ref[
                copy, :, q * lanes : (q + 1) * lanes
            ]
    score_ref[...] = (1.0 / (1.0 + jnp.exp(-logits))).astype(BF16)


def lower_experts(place_ref, *refs):
    inner_ref, *parts, score_ref, back_ref = refs
    sources = inner_ref.shape[0]
    blocks, _, padded = back_ref.shape
    slots = score_ref.shape[0]
    width = parts[0].shape[1]
    total = jnp.zeros((slots, width), F32)
    for k in range(sources):
        source = (place_ref[TP] - k + sources) % sources
        total += jnp.dot(inner_ref[source, :slots], parts[k][...], preferred_element_type=F32)
    total = jnp.concatenate([total, score_ref[:, : padded - width].astype(F32)], axis=1)
    back_ref[...] = total.reshape(blocks, SLOTS, padded).astype(BF16)


def merge_experts(back_ref, slot_ref, own_ref, out_ref):
    slots, width = slot_ref.shape[0], out_ref.shape[1]
    back = back_ref[...].astype(F32).reshape(slots, back_ref.shape[2])
    share = slot_ref[...] * back[:, width : width + 1]
    share = ROUTE_SCALE * share / jnp.sum(share, axis=0, keepdims=True)
    upper = share.astype(BF16)
    lower = (share - upper.astype(F32)).astype(BF16)
    parts = back[:, :width].astype(BF16)
    merged = lax.dot_general(upper, parts, TN, preferred_element_type=F32) + lax.dot_general(
        lower, parts, TN, preferred_element_type=F32
    )
    out_ref[...] = own_ref[...].astype(F32) + merged


def add_attention(parts_ref, sum_ref, out_ref):
    rows, width = out_ref.shape
    blocks, held, lanes = parts_ref.shape
    slices = blocks // 8
    cols = width // 8
    attn = jnp.sum(
        parts_ref[...].astype(F32).reshape(8, slices, held, lanes), axis=1
    ).reshape(8 * held, lanes)
    attn = attn.astype(BF16)
    merged = sum_ref[...]
    lane_in, lane_out = iotas(lanes, width)
    row, lane = iotas(8 * held, width)
    token, entry = iotas(rows, 8 * held)
    for q in range(2):
        spread = one_hot(lane_out % cols + q * (lanes // 2) == lane_in)
        mine = jnp.dot(attn, spread, preferred_element_type=F32)
        mine = jnp.where(lane // cols == row // held, mine, 0.0).astype(BF16)
        pick = one_hot(token == entry % held + q * held)
        merged += jnp.dot(pick, mine, preferred_element_type=F32)
    out_ref[...] = merged.astype(BF16)


def shift(value, axis, k):
    size = lax.axis_size(axis)
    return lax.ppermute(value, axis, [(i, (i + k) % size) for i in range(size)])


def pair_up(value, axis):
    return jnp.stack([value, shift(value, axis, 1)])


def gather(value, axis):
    return [value] + [shift(value, axis, k) for k in range(1, lax.axis_size(axis))]


def on_device(
    hidden,
    norm_gain,
    queries,
    latent_cache,
    lengths,
    expert_ids,
    router,
    w_gate,
    w_up,
    w_down,
    w_uv,
    w_out,
):
    rows, model_width = hidden.shape
    ep_size = lax.axis_size(EP)
    tp_size = lax.axis_size("y")
    slots = ep_size * SLOTS
    width = model_width // tp_size
    hidden_units = w_gate.shape[2]
    heads, latent, value_width = w_uv.shape
    out_cols, depth = w_out.shape[1], w_out.shape[0]
    here = jnp.stack([lax.axis_index(a) for a in ("y", "x", "zh", "zl", "c")]).astype(jnp.int32)
    tp = here[0]

    send, place = kernel_call(
        prepare,
        [((ep_size, SLOTS, model_width), BF16), ((slots, rows), F32)],
        hidden,
        norm_gain.reshape(1, model_width),
        expert_ids.T,
    )
    named_rows = lax.all_to_all(send, EP, 0, 0, tiled=True)

    down = kernel_call(
        split_down, [((hidden_units, width), BF16)] * tp_size, here, w_down[0], smem=(0,)
    )
    down = [down[0]] + [shift(down[k], "y", k) for k in range(1, tp_size)]

    (context,) = kernel_call(
        attend,
        [((tp_size, 2 * heads, latent), BF16)],
        lengths,
        queries,
        jnp.swapaxes(latent_cache, 1, 2),
        smem=(0,),
        after=down[1:],
    )

    out_other = shift(w_out.T, "zh", 1)
    inner, score = kernel_call(
        lift_experts,
        [((tp_size, slots + 8 * heads, hidden_units), BF16), ((slots, 128), BF16)],
        named_rows,
        w_gate[0],
        w_up[0],
        router,
        context,
        after=(out_other,),
    )
    inner = lax.all_to_all(inner, "y", 0, 0, tiled=True)

    out_weights = gather(jnp.stack([w_out.T, out_other]), "x")
    (values,) = kernel_call(
        lift_heads,
        [((rows, depth), BF16)],
        inner,
        w_uv,
        after=out_weights[1:],
        flops=10_000_000_000,
    )
    values = gather(pair_up(values, "c"), "zl")
    (attn_parts,) = kernel_call(
        project,
        [((8 * tp_size, rows // 2, 128), BF16)],
        here,
        *values,
        *out_weights,
        smem=(0,),
    )
    attn_parts = lax.all_to_all(attn_parts, ("zl", "c", "y"), 0, 0, tiled=True)

    (back,) = kernel_call(
        lower_experts,
        [((ep_size, SLOTS, PADDED), BF16)],
        here,
        inner,
        *down,
        score,
        smem=(0,),
    )
    back = lax.all_to_all(back, EP, 0, 0, tiled=True)
    own = lax.dynamic_slice_in_dim(hidden, tp * width, width, 1)
    (merged,) = kernel_call(merge_experts, [((rows, width), F32)], back, place, own)
    (out,) = kernel_call(add_attention, [((rows, width), BF16)], attn_parts, merged)
    return out


def solution(mesh):
    split = Mesh(mesh.devices.reshape(4, 2, 4, 2, 8), ("x", "zh", "zl", "c", "y"))
    return jax.shard_map(
        on_device,
        mesh=split,
        in_specs=(
            P(EP, None),
            P(),
            P(EP + ("y",), None, None),
            P(EP + ("y",), None, None),
            P(EP + ("y",)),
            P(EP, None),
            P(EP, None),
            P(EP, None, "y"),
            P(EP, None, "y"),
            P(EP, "y", None),
            P("y", None, None),
            P("y", EP),
        ),
        out_specs=P(EP, "y"),
        check_vma=False,
    )
```

time: 172 us -> 155 us (0.901)
  waiting for transfers between devices: 58.2 us -> 29.1 us
  local copies, waits for them, and re-layouts: 10.9 us -> 16.7 us
  starting transfers between devices: 88 us -> 92.5 us
    ppermute x11 -> x15, waiting for transfers between devices: 23.8 us -> 9.28 us  [shift(): return lax.ppermute(value, axis, [(i, (i + k) % size) for i in range(size)])]
    all_to_all x1, waiting for transfers between devices: 20.6 us -> 11.3 us  [on_device(): inner = lax.all_to_all(inner, 'y', 0, 0, tiled=True)]
    ppermute x11 -> x15, starting transfers between devices: 48.9 us -> 56.9 us  [shift(): return lax.ppermute(value, axis, [(i, (i + k) % size) for i in range(size)])]
    unnamed x48 -> x50, local copies, waits for them, and re-layouts: 7.49 us -> 15.1 us
    all_to_all x2, waiting for transfers between devices: 13.8 us -> 8.48 us  [the longest x1 8.48 us: on_device(): attn_parts = lax.all_to_all(attn_parts, ('zl', 'c', 'y'), 0, 0, tiled=True)]
    ppermute x1 -> x0, starting transfers between devices: 4.03 us -> none  [on_device(): arrived = lax.ppermute(pass_on, 'y', [(i, i ^ 1) for i in range(tp_size)])]
  transfers between devices with their start and end apart: 16 -> 19, of which waited for: 7 -> 7; matrix products, arithmetic and copies ran while one was open for 2% -> 1% of each run, Pallas kernels for 2% -> 6%
where the time goes in v5:
time: 155 us; the launch traced here: 153 us
  starting transfers between devices  92.5 us (60%)
  waiting for transfers between devices  29.1 us (19%)
  local copies, waits for them, and re-layouts  16.7 us (11%)
  Pallas kernels  13.3 us (9%)
    ppermute x15, starting transfers between devices, shift(): return lax.ppermute(value, axis, [(i, (i + k) % size) for i in range(size)])  56.9 us
    unnamed x50, local copies, waits for them, and re-layouts  15.1 us
    all_to_all x1, starting transfers between devices, on_device(): named_rows = lax.all_to_all(send, EP, 0, 0, tiled=True)  15 us
    pallas_call x9, Pallas kernels, kernel_call(): pl.pallas_call(body, out_shape=tuple((jax.ShapeDtypeStruct(s, d) for s, d...  13.3 us
    all_to_all x1, waiting for transfers between devices, on_device(): inner = lax.all_to_all(inner, 'y', 0, 0, tiled=True)  11.3 us
    ppermute x15, waiting for transfers between devices, shift(): return lax.ppermute(value, axis, [(i, (i + k) % size) for i in range(size)])  9.28 us
    all_to_all x1, waiting for transfers between devices, on_device(): attn_parts = lax.all_to_all(attn_parts, ('zl', 'c', 'y'), 0, 0, tiled=True)  8.48 us
    all_to_all x1, starting transfers between devices, on_device(): attn_parts = lax.all_to_all(attn_parts, ('zl', 'c', 'y'), 0, 0, tiled=True)  7.79 us
  transfers between devices with their start and end apart: 19, of which 7 were waited for; matrix products, arithmetic and copies ran while one was open for 1% of the time, Pallas kernels for 6%

profile of v5, /device:TPU:1, one launch (start us, length us, event | category | flops | bytes accessed | tf_op | source)
XLA Modules:
  0.0 153.0 jit_solution(6790902712595006437)
XLA Ops:
  5.1 15.0 %all-to-all-start = ((bf16[64,4,3584]{2,1,0:T(4,128)(2,1)}), bf16[64,4,3584]{2,1,0:T(4,128)(2,1)S(1)}, u32[]{:S(2)}, u32[]{:S(2)}) async-start(bf16[64,4,3584]{2,1,0:T(4,128)(2,1)} %copy-done), calls=%async_computation | async-start | bytes 3670016 | tf_op jit(solution)/shard_map/all_to_all | solution.py:257
  23.2 3.3 %collective-permute-start = (bf16[128,448]{1,0:T(8,128)(2,1)S(1)}, bf16[128,448]{1,0:T(8,128)(2,1)S(1)}, u32[]{:S(2)}, u32[]{:S(2)}) collective-permute-start(bf16[128,448]{1,0:T(8,128)(2,1)S(1)} %get-tuple-element.18), channel_id=1, source_target_pairs={{0,1},{1,2},{2,3},{3,4},{4,5},{5,6},{6,7},{7,0},{8,9},{9,10},{10,1... | collective-permute-start | bytes 344072 | tf_op jit(solution)/shard_map/ppermute | solution.py:214
  26.5 4.2 %collective-permute-start.1 = (bf16[128,448]{1,0:T(8,128)(2,1)S(1)}, bf16[128,448]{1,0:T(8,128)(2,1)S(1)}, u32[]{:S(2)}, u32[]{:S(2)}) collective-permute-start(bf16[128,448]{1,0:T(8,128)(2,1)S(1)} %get-tuple-element.19), channel_id=1, source_target_pairs={{0,2},{1,3},{2,4},{3,5},{4,6},{5,7},{6,0},{7,1},{8,10},{9,11},{10,... | collective-permute-start | bytes 344072 | tf_op jit(solution)/shard_map/ppermute | solution.py:214
  30.7 4.6 %collective-permute-start.2 = (bf16[128,448]{1,0:T(8,128)(2,1)S(1)}, bf16[128,448]{1,0:T(8,128)(2,1)S(1)}, u32[]{:S(2)}, u32[]{:S(2)}) collective-permute-start(bf16[128,448]{1,0:T(8,128)(2,1)S(1)} %get-tuple-element.20), channel_id=1, source_target_pairs={{0,3},{1,4},{2,5},{3,6},{4,7},{5,0},{6,1},{7,2},{8,11},{9,12},{10,... | collective-permute-start | bytes 344072 | tf_op jit(solution)/shard_map/ppermute | solution.py:214
  35.4 3.5 %collective-permute-start.3 = (bf16[128,448]{1,0:T(8,128)(2,1)S(1)}, bf16[128,448]{1,0:T(8,128)(2,1)S(1)}, u32[]{:S(2)}, u32[]{:S(2)}) collective-permute-start(bf16[128,448]{1,0:T(8,128)(2,1)S(1)} %get-tuple-element.21), channel_id=1, source_target_pairs={{0,4},{1,5},{2,6},{3,7},{4,0},{5,1},{6,2},{7,3},{8,12},{9,13},{10,... | collective-permute-start | bytes 344072 | tf_op jit(solution)/shard_map/ppermute | solution.py:214
  38.9 4.9 %collective-permute-start.4 = (bf16[128,448]{1,0:T(8,128)(2,1)S(1)}, bf16[128,448]{1,0:T(8,128)(2,1)S(1)}, u32[]{:S(2)}, u32[]{:S(2)}) collective-permute-start(bf16[128,448]{1,0:T(8,128)(2,1)S(1)} %get-tuple-element.22), channel_id=1, source_target_pairs={{0,5},{1,6},{2,7},{3,0},{4,1},{5,2},{6,3},{7,4},{8,13},{9,14},{10,... | collective-permute-start | bytes 344072 | tf_op jit(solution)/shard_map/ppermute | solution.py:214
  43.8 5.0 %collective-permute-start.5 = (bf16[128,448]{1,0:T(8,128)(2,1)S(1)}, bf16[128,448]{1,0:T(8,128)(2,1)S(1)}, u32[]{:S(2)}, u32[]{:S(2)}) collective-permute-start(bf16[128,448]{1,0:T(8,128)(2,1)S(1)} %get-tuple-element.23), channel_id=1, source_target_pairs={{0,6},{1,7},{2,0},{3,1},{4,2},{5,3},{6,4},{7,5},{8,14},{9,15},{10,... | collective-permute-start | bytes 344072 | tf_op jit(solution)/shard_map/ppermute | solution.py:214
  48.8 3.0 %collective-permute-start.6 = (bf16[128,448]{1,0:T(8,128)(2,1)S(1)}, bf16[128,448]{1,0:T(8,128)(2,1)S(1)}, u32[]{:S(2)}, u32[]{:S(2)}) collective-permute-start(bf16[128,448]{1,0:T(8,128)(2,1)S(1)} %get-tuple-element.24), channel_id=1, source_target_pairs={{0,7},{1,0},{2,1},{3,2},{4,3},{5,4},{6,5},{7,6},{8,15},{9,8},{10,9... | collective-permute-start | bytes 344072 | tf_op jit(solution)/shard_map/ppermute | solution.py:214
  51.8 7.2 %collective-permute-start.7 = (bf16[56,1024]{1,0:T(8,128)(2,1)}, bf16[56,1024]{1,0:T(8,128)(2,1)S(1)}, u32[]{:S(2)}, u32[]{:S(2)}) collective-permute-start(bf16[56,1024]{1,0:T(8,128)(2,1)} %bitcast.23), channel_id=1, source_target_pairs={{0,64},{64,0},{1,65},{65,1},{2,66},{66,2},{3,67},{67,3},{4,68},{68... | collective-permute-start | bytes 344072 | tf_op jit(solution)/shard_map/ppermute | solution.py:214
  59.0 3.7 %collective-permute-done.5.refs_8_.refs_7_ = bf16[128,448]{1,0:T(8,128)(2,1)S(1)} collective-permute-done((bf16[128,448]{1,0:T(8,128)(2,1)S(1)}, bf16[128,448]{1,0:T(8,128)(2,1)S(1)}, u32[]{:S(2)}, u32[]{:S(2)}) %collective-permute-start.5) | collective-permute-done | bytes 114720 | tf_op jit(solution)/shard_map/ppermute | solution.py:214
  74.2 2.5 %shard_map.121 = (bf16[8,320,128]{2,1,0:T(8,128)(2,1)}, bf16[256,128]{1,0:T(8,128)(2,1)S(1)}) custom-call(bf16[64,4,3584]{2,1,0:T(4,128)(2,1)S(1)} %all-to-all-done.refs_0_, bf16[3584,128]{1,0:T(8,128)(2,1)S(1)} %bitcast.17, bf16[3584,128]{1,0:T(8,128)(2,1)S(1)} %bitcast.18, bf16[1,3584]{1,0:T(2,128)(2,1)S(1)} %copy-done.19, ...), custom_call_target="tpu_custom_call" | custom-call | bytes 3808256 | tf_op jit(solution)/shard_map/pallas_call | solution.py:31
  77.3 7.0 %all-to-all-start.1 = ((bf16[8,320,128]{2,1,0:T(8,128)(2,1)}), bf16[8,320,128]{2,1,0:T(8,128)(2,1)S(1)}, u32[]{:S(2)}, u32[]{:S(2)}) async-start(bf16[8,320,128]{2,1,0:T(8,128)(2,1)} %get-tuple-element.25), calls=%async_computation.1 | async-start | bytes 1310720 | tf_op jit(solution)/shard_map/all_to_all | solution.py:285
  87.1 3.0 %collective-permute-start.9 = (bf16[2,56,1024]{2,1,0:T(8,128)(2,1)S(1)}, bf16[2,56,1024]{2,1,0:T(8,128)(2,1)S(1)}, u32[]{:S(2)}, u32[]{:S(2)}) collective-permute-start(bf16[2,56,1024]{2,1,0:T(8,128)(2,1)S(1)} %pad_maximum_fusion.refs_4_), channel_id=1, source_target_pairs={{0,256},{128,384},{256,0},{384,128},{1,257},{129,385},{257,1},{385... | collective-permute-start | bytes 688136 | tf_op jit(solution)/shard_map/ppermute | solution.py:214
  90.1 3.5 %collective-permute-start.10 = (bf16[2,56,1024]{2,1,0:T(8,128)(2,1)S(1)}, bf16[2,56,1024]{2,1,0:T(8,128)(2,1)S(1)}, u32[]{:S(2)}, u32[]{:S(2)}) collective-permute-start(bf16[2,56,1024]{2,1,0:T(8,128)(2,1)S(1)} %pad_maximum_fusion.refs_4_), channel_id=1, source_target_pairs={{0,384},{128,0},{256,128},{384,256},{1,385},{129,1},{257,129},{385... | collective-permute-start | bytes 688136 | tf_op jit(solution)/shard_map/ppermute | solution.py:214
  93.7 11.3 %all-to-all-done.1.refs_0_ = bf16[8,320,128]{2,1,0:T(8,128)(2,1)S(1)} async-done(((bf16[8,320,128]{2,1,0:T(8,128)(2,1)}), bf16[8,320,128]{2,1,0:T(8,128)(2,1)S(1)}, u32[]{:S(2)}, u32[]{:S(2)}) %all-to-all-start.1) | async-done | bytes 655392 | tf_op jit(solution)/shard_map/all_to_all | solution.py:285
  106.5 1.9 %shard_map.124 = bf16[64,4,512]{2,1,0:T(4,128)(2,1)} custom-call(s32[5]{0:T(128)S(1)} %copy-done.21, bf16[8,320,128]{2,1,0:T(8,128)(2,1)S(1)} %all-to-all-done.1.refs_0_, bf16[128,448]{1,0:T(8,128)(2,1)S(1)} %copy-done.16, bf16[128,448]{1,0:T(8,128)(2,1)S(1)} %collective-permute-done.refs_3_.refs_2_, ...), custom_call_target="tpu_custom_call" | custom-call | bytes 1638420 | tf_op jit(solution)/shard_map/pallas_call | solution.py:31
  108.5 5.9 %all-to-all-start.3 = ((bf16[64,4,512]{2,1,0:T(4,128)(2,1)}), bf16[64,4,512]{2,1,0:T(4,128)(2,1)S(1)}, u32[]{:S(2)}, u32[]{:S(2)}) async-start(bf16[64,4,512]{2,1,0:T(4,128)(2,1)} %shard_map.124), calls=%async_computation.3 | async-start | bytes 524288 | tf_op jit(solution)/shard_map/all_to_all | solution.py:316
  117.0 2.5 %collective-permute-start.11 = (bf16[16,1024]{1,0:T(8,128)(2,1)S(1)}, bf16[16,1024]{1,0:T(8,128)(2,1)S(1)}, u32[]{:S(2)}, u32[]{:S(2)}) collective-permute-start(bf16[16,1024]{1,0:T(8,128)(2,1)S(1)} %shard_map.122), channel_id=1, source_target_pairs={{0,8},{8,0},{1,9},{9,1},{2,10},{10,2},{3,11},{11,3},{4,12},{12,4},... | collective-permute-start | bytes 98312 | tf_op jit(solution)/shard_map/ppermute | solution.py:214
  120.4 3.2 %collective-permute-start.12 = (bf16[2,16,1024]{2,1,0:T(8,128)(2,1)S(1)}, bf16[2,16,1024]{2,1,0:T(8,128)(2,1)S(1)}, u32[]{:S(2)}, u32[]{:S(2)}) collective-permute-start(bf16[2,16,1024]{2,1,0:T(8,128)(2,1)S(1)} %pad_maximum_fusion.1.refs_0_), channel_id=1, source_target_pairs={{0,16},{16,32},{32,48},{48,0},{1,17},{17,33},{33,49},{49,1},{2,18}... | collective-permute-start | bytes 196616 | tf_op jit(solution)/shard_map/ppermute | solution.py:214
  123.6 4.0 %collective-permute-start.13 = (bf16[2,16,1024]{2,1,0:T(8,128)(2,1)S(1)}, bf16[2,16,1024]{2,1,0:T(8,128)(2,1)S(1)}, u32[]{:S(2)}, u32[]{:S(2)}) collective-permute-start(bf16[2,16,1024]{2,1,0:T(8,128)(2,1)S(1)} %pad_maximum_fusion.1.refs_0_), channel_id=1, source_target_pairs={{0,32},{16,48},{32,0},{48,16},{1,33},{17,49},{33,1},{49,17},{2,34}... | collective-permute-start | bytes 196616 | tf_op jit(solution)/shard_map/ppermute | solution.py:214
  127.6 3.1 %collective-permute-start.14 = (bf16[2,16,1024]{2,1,0:T(8,128)(2,1)S(1)}, bf16[2,16,1024]{2,1,0:T(8,128)(2,1)S(1)}, u32[]{:S(2)}, u32[]{:S(2)}) collective-permute-start(bf16[2,16,1024]{2,1,0:T(8,128)(2,1)S(1)} %pad_maximum_fusion.1.refs_0_), channel_id=1, source_target_pairs={{0,48},{16,0},{32,16},{48,32},{1,49},{17,1},{33,17},{49,33},{2,50}... | collective-permute-start | bytes 196616 | tf_op jit(solution)/shard_map/ppermute | solution.py:214
  132.6 2.0 %shard_map.123 = bf16[64,8,128]{2,1,0:T(8,128)(2,1)} custom-call(s32[5]{0:T(128)S(1)} %copy-done.21, bf16[2,16,1024]{2,1,0:T(8,128)(2,1)S(1)} %pad_maximum_fusion.1.refs_0_, bf16[2,16,1024]{2,1,0:T(8,128)(2,1)S(1)} %collective-permute-done.12.refs_1_, bf16[2,16,1024]{2,1,0:T(8,128)(2,1)S(1)} %collective-permute-done.13.refs_2_, ...), custom_call_target="tpu_custom_call" | custom-call | bytes 1179668 | tf_op jit(solution)/shard_map/pallas_call | solution.py:31
  134.6 7.8 %all-to-all-start.2 = ((bf16[64,8,128]{2,1,0:T(8,128)(2,1)}), bf16[64,8,128]{2,1,0:T(8,128)(2,1)S(1)}, u32[]{:S(2)}, u32[]{:S(2)}) async-start(bf16[64,8,128]{2,1,0:T(8,128)(2,1)} %shard_map.123), calls=%async_computation.2 | async-start | bytes 262144 | tf_op jit(solution)/shard_map/all_to_all | solution.py:305
  143.5 8.5 %all-to-all-done.2.parts_ref = bf16[64,8,128]{2,1,0:T(8,128)(2,1)S(1)} async-done(((bf16[64,8,128]{2,1,0:T(8,128)(2,1)}), bf16[64,8,128]{2,1,0:T(8,128)(2,1)S(1)}, u32[]{:S(2)}, u32[]{:S(2)}) %all-to-all-start.2) | async-done | bytes 131104 | tf_op jit(solution)/shard_map/all_to_all | solution.py:305
  (78 shorter events, 32.2 us)
Async XLA Ops:
  5.1 66.1 %all-to-all-start = ((bf16[64,4,3584]{2,1,0:T(4,128)(2,1)}), bf16[64,4,3584]{2,1,0:T(4,128)(2,1)S(1)}, u32[]{:S(2)}, u32[]{:S(2)}) async-start(bf16[64,4,3584]{2,1,0:T(4,128)(2,1)} %copy-done), calls=%async_computation | async-start | bytes 3670016 | tf_op jit(solution)/shard_map/all_to_all | solution.py:257
  20.1 51.1 %copy-start.19 = (bf16[1,3584]{1,0:T(2,128)(2,1)S(1)}, bf16[1,3584]{1,0:T(2,128)(2,1)}, u32[]{:S(2)}) copy-start(bf16[1,3584]{1,0:T(2,128)(2,1)} %refs_3_.1) | copy-start | bytes 21508
  23.2 48.0 %copy-start.2 = (bf16[1,3584,128]{2,1,0:T(8,128)(2,1)S(1)}, bf16[1,3584,128]{2,1,0:T(8,128)(2,1)}, u32[]{:S(2)}) copy-start(bf16[1,3584,128]{2,1,0:T(8,128)(2,1)} %param.19) | copy-start | bytes 2752516
  23.2 20.6 %collective-permute-start = (bf16[128,448]{1,0:T(8,128)(2,1)S(1)}, bf16[128,448]{1,0:T(8,128)(2,1)S(1)}, u32[]{:S(2)}, u32[]{:S(2)}) collective-permute-start(bf16[128,448]{1,0:T(8,128)(2,1)S(1)} %get-tuple-element.18), channel_id=1, source_target_pairs={{0,1},{1,2},{2,3},{3,4},{4,5},{5,6},{6,7},{7,0},{8,9},{9,10},{10,1... | collective-permute-start | bytes 344072 | tf_op jit(solution)/shard_map/ppermute | solution.py:214
  26.5 22.3 %collective-permute-start.1 = (bf16[128,448]{1,0:T(8,128)(2,1)S(1)}, bf16[128,448]{1,0:T(8,128)(2,1)S(1)}, u32[]{:S(2)}, u32[]{:S(2)}) collective-permute-start(bf16[128,448]{1,0:T(8,128)(2,1)S(1)} %get-tuple-element.19), channel_id=1, source_target_pairs={{0,2},{1,3},{2,4},{3,5},{4,6},{5,7},{6,0},{7,1},{8,10},{9,11},{10,... | collective-permute-start | bytes 344072 | tf_op jit(solution)/shard_map/ppermute | solution.py:214
  30.7 21.1 %collective-permute-start.2 = (bf16[128,448]{1,0:T(8,128)(2,1)S(1)}, bf16[128,448]{1,0:T(8,128)(2,1)S(1)}, u32[]{:S(2)}, u32[]{:S(2)}) collective-permute-start(bf16[128,448]{1,0:T(8,128)(2,1)S(1)} %get-tuple-element.20), channel_id=1, source_target_pairs={{0,3},{1,4},{2,5},{3,6},{4,7},{5,0},{6,1},{7,2},{8,11},{9,12},{10,... | collective-permute-start | bytes 344072 | tf_op jit(solution)/shard_map/ppermute | solution.py:214
  35.4 23.6 %collective-permute-start.3 = (bf16[128,448]{1,0:T(8,128)(2,1)S(1)}, bf16[128,448]{1,0:T(8,128)(2,1)S(1)}, u32[]{:S(2)}, u32[]{:S(2)}) collective-permute-start(bf16[128,448]{1,0:T(8,128)(2,1)S(1)} %get-tuple-element.21), channel_id=1, source_target_pairs={{0,4},{1,5},{2,6},{3,7},{4,0},{5,1},{6,2},{7,3},{8,12},{9,13},{10,... | collective-permute-start | bytes 344072 | tf_op jit(solution)/shard_map/ppermute | solution.py:214
  38.9 20.1 %collective-permute-start.4 = (bf16[128,448]{1,0:T(8,128)(2,1)S(1)}, bf16[128,448]{1,0:T(8,128)(2,1)S(1)}, u32[]{:S(2)}, u32[]{:S(2)}) collective-permute-start(bf16[128,448]{1,0:T(8,128)(2,1)S(1)} %get-tuple-element.22), channel_id=1, source_target_pairs={{0,5},{1,6},{2,7},{3,0},{4,1},{5,2},{6,3},{7,4},{8,13},{9,14},{10,... | collective-permute-start | bytes 344072 | tf_op jit(solution)/shard_map/ppermute | solution.py:214
  43.8 18.9 %collective-permute-start.5 = (bf16[128,448]{1,0:T(8,128)(2,1)S(1)}, bf16[128,448]{1,0:T(8,128)(2,1)S(1)}, u32[]{:S(2)}, u32[]{:S(2)}) collective-permute-start(bf16[128,448]{1,0:T(8,128)(2,1)S(1)} %get-tuple-element.23), channel_id=1, source_target_pairs={{0,6},{1,7},{2,0},{3,1},{4,2},{5,3},{6,4},{7,5},{8,14},{9,15},{10,... | collective-permute-start | bytes 344072 | tf_op jit(solution)/shard_map/ppermute | solution.py:214
  48.8 15.0 %collective-permute-start.6 = (bf16[128,448]{1,0:T(8,128)(2,1)S(1)}, bf16[128,448]{1,0:T(8,128)(2,1)S(1)}, u32[]{:S(2)}, u32[]{:S(2)}) collective-permute-start(bf16[128,448]{1,0:T(8,128)(2,1)S(1)} %get-tuple-element.24), channel_id=1, source_target_pairs={{0,7},{1,0},{2,1},{3,2},{4,3},{5,4},{6,5},{7,6},{8,15},{9,8},{10,9... | collective-permute-start | bytes 344072 | tf_op jit(solution)/shard_map/ppermute | solution.py:214
  51.8 18.7 %collective-permute-start.7 = (bf16[56,1024]{1,0:T(8,128)(2,1)}, bf16[56,1024]{1,0:T(8,128)(2,1)S(1)}, u32[]{:S(2)}, u32[]{:S(2)}) collective-permute-start(bf16[56,1024]{1,0:T(8,128)(2,1)} %bitcast.23), channel_id=1, source_target_pairs={{0,64},{64,0},{1,65},{65,1},{2,66},{66,2},{3,67},{67,3},{4,68},{68... | collective-permute-start | bytes 344072 | tf_op jit(solution)/shard_map/ppermute | solution.py:214
  77.3 27.7 %copy-start.6 = (bf16[128,448]{1,0:T(8,128)(2,1)S(1)}, bf16[128,448]{1,0:T(8,128)(2,1)}, u32[]{:S(2)}) copy-start(bf16[128,448]{1,0:T(8,128)(2,1)} %copy-done.5) | copy-start | bytes 344068
  77.3 27.7 %copy-start.16 = (bf16[128,448]{1,0:T(8,128)(2,1)S(1)}, bf16[128,448]{1,0:T(8,128)(2,1)}, u32[]{:S(2)}) copy-start(bf16[128,448]{1,0:T(8,128)(2,1)} %copy-done.15) | copy-start | bytes 344068
  77.3 27.7 %all-to-all-start.1 = ((bf16[8,320,128]{2,1,0:T(8,128)(2,1)}), bf16[8,320,128]{2,1,0:T(8,128)(2,1)S(1)}, u32[]{:S(2)}, u32[]{:S(2)}) async-start(bf16[8,320,128]{2,1,0:T(8,128)(2,1)} %get-tuple-element.25), calls=%async_computation.1 | async-start | bytes 1310720 | tf_op jit(solution)/shard_map/all_to_all | solution.py:285
  85.2 29.1 %collective-permute-start.8 = (bf16[2,56,1024]{2,1,0:T(8,128)(2,1)S(1)}, bf16[2,56,1024]{2,1,0:T(8,128)(2,1)S(1)}, u32[]{:S(2)}, u32[]{:S(2)}) collective-permute-start(bf16[2,56,1024]{2,1,0:T(8,128)(2,1)S(1)} %pad_maximum_fusion.refs_4_), channel_id=1, source_target_pairs={{0,128},{128,256},{256,384},{384,0},{1,129},{129,257},{257,385},{3... | collective-permute-start | bytes 688136 | tf_op jit(solution)/shard_map/ppermute | solution.py:214
  87.1 27.2 %collective-permute-start.9 = (bf16[2,56,1024]{2,1,0:T(8,128)(2,1)S(1)}, bf16[2,56,1024]{2,1,0:T(8,128)(2,1)S(1)}, u32[]{:S(2)}, u32[]{:S(2)}) collective-permute-start(bf16[2,56,1024]{2,1,0:T(8,128)(2,1)S(1)} %pad_maximum_fusion.refs_4_), channel_id=1, source_target_pairs={{0,256},{128,384},{256,0},{384,128},{1,257},{129,385},{257,1},{385... | collective-permute-start | bytes 688136 | tf_op jit(solution)/shard_map/ppermute | solution.py:214
  90.1 24.2 %collective-permute-start.10 = (bf16[2,56,1024]{2,1,0:T(8,128)(2,1)S(1)}, bf16[2,56,1024]{2,1,0:T(8,128)(2,1)S(1)}, u32[]{:S(2)}, u32[]{:S(2)}) collective-permute-start(bf16[2,56,1024]{2,1,0:T(8,128)(2,1)S(1)} %pad_maximum_fusion.refs_4_), channel_id=1, source_target_pairs={{0,384},{128,0},{256,128},{384,256},{1,385},{129,1},{257,129},{385... | collective-permute-start | bytes 688136 | tf_op jit(solution)/shard_map/ppermute | solution.py:214
  108.5 26.1 %all-to-all-start.3 = ((bf16[64,4,512]{2,1,0:T(4,128)(2,1)}), bf16[64,4,512]{2,1,0:T(4,128)(2,1)S(1)}, u32[]{:S(2)}, u32[]{:S(2)}) async-start(bf16[64,4,512]{2,1,0:T(4,128)(2,1)} %shard_map.124), calls=%async_computation.3 | async-start | bytes 524288 | tf_op jit(solution)/shard_map/all_to_all | solution.py:316
  117.0 26.1 %copy-start.14 = (f32[256,16]{1,0:T(8,128)S(1)}, f32[256,16]{1,0:T(8,128)}, u32[]{:S(2)}) copy-start(f32[256,16]{1,0:T(8,128)} %copy-done.13) | copy-start | bytes 49156
  117.0 3.3 %collective-permute-start.11 = (bf16[16,1024]{1,0:T(8,128)(2,1)S(1)}, bf16[16,1024]{1,0:T(8,128)(2,1)S(1)}, u32[]{:S(2)}, u32[]{:S(2)}) collective-permute-start(bf16[16,1024]{1,0:T(8,128)(2,1)S(1)} %shard_map.122), channel_id=1, source_target_pairs={{0,8},{8,0},{1,9},{9,1},{2,10},{10,2},{3,11},{11,3},{4,12},{12,4},... | collective-permute-start | bytes 98312 | tf_op jit(solution)/shard_map/ppermute | solution.py:214
  120.4 10.3 %collective-permute-start.12 = (bf16[2,16,1024]{2,1,0:T(8,128)(2,1)S(1)}, bf16[2,16,1024]{2,1,0:T(8,128)(2,1)S(1)}, u32[]{:S(2)}, u32[]{:S(2)}) collective-permute-start(bf16[2,16,1024]{2,1,0:T(8,128)(2,1)S(1)} %pad_maximum_fusion.1.refs_0_), channel_id=1, source_target_pairs={{0,16},{16,32},{32,48},{48,0},{1,17},{17,33},{33,49},{49,1},{2,18}... | collective-permute-start | bytes 196616 | tf_op jit(solution)/shard_map/ppermute | solution.py:214
  123.6 7.1 %collective-permute-start.13 = (bf16[2,16,1024]{2,1,0:T(8,128)(2,1)S(1)}, bf16[2,16,1024]{2,1,0:T(8,128)(2,1)S(1)}, u32[]{:S(2)}, u32[]{:S(2)}) collective-permute-start(bf16[2,16,1024]{2,1,0:T(8,128)(2,1)S(1)} %pad_maximum_fusion.1.refs_0_), channel_id=1, source_target_pairs={{0,32},{16,48},{32,0},{48,16},{1,33},{17,49},{33,1},{49,17},{2,34}... | collective-permute-start | bytes 196616 | tf_op jit(solution)/shard_map/ppermute | solution.py:214
  127.6 5.0 %collective-permute-start.14 = (bf16[2,16,1024]{2,1,0:T(8,128)(2,1)S(1)}, bf16[2,16,1024]{2,1,0:T(8,128)(2,1)S(1)}, u32[]{:S(2)}, u32[]{:S(2)}) collective-permute-start(bf16[2,16,1024]{2,1,0:T(8,128)(2,1)S(1)} %pad_maximum_fusion.1.refs_0_), channel_id=1, source_target_pairs={{0,48},{16,0},{32,16},{48,32},{1,49},{17,1},{33,17},{49,33},{2,50}... | collective-permute-start | bytes 196616 | tf_op jit(solution)/shard_map/ppermute | solution.py:214
  134.6 17.4 %all-to-all-start.2 = ((bf16[64,8,128]{2,1,0:T(8,128)(2,1)}), bf16[64,8,128]{2,1,0:T(8,128)(2,1)S(1)}, u32[]{:S(2)}, u32[]{:S(2)}) async-start(bf16[64,8,128]{2,1,0:T(8,128)(2,1)} %shard_map.123), calls=%async_computation.2 | async-start | bytes 262144 | tf_op jit(solution)/shard_map/all_to_all | solution.py:305
  (20 other events, 35.1 us)

commit v6 on v5

--- a/solution.py
+++ b/solution.py
@@ -10,30 +10,60 @@
 SCORE_SCALE = 192.0 ** (-0.5)
 SLOTS = 4
 EP = ("x", "zh", "zl", "c")
-TP, X, ZH, ZL, CORE = range(5)
-PADDED = 512
+PADDED = 1024
+GROUP = 4
 NT = (((1,), (1,)), ((), ()))
 TN = (((0,), (0,)), ((), ()))
 F32 = jnp.float32
 BF16 = jnp.bfloat16
 
 
-def kernel_call(body, outs, *args, smem=(), after=(), flops=0):
-    in_specs = [
-        pl.BlockSpec(memory_space=pltpu.SMEM if i in smem else pltpu.VMEM)
-        for i in range(len(args))
-    ] + [pl.BlockSpec(memory_space=pltpu.VMEM) for _ in after]
-    if after:
-        inner, count = body, len(args)
-        body = lambda *refs: inner(*refs[:count], *refs[count + len(after) :])
-    vmem = pl.BlockSpec(memory_space=pltpu.VMEM)
+def kernel_call(body, outs, *args, smem=(), load=(), store=(), after=(), flops=0, vmem=16):
+    def place(n, moved):
+        space = pltpu.HBM if n in moved else pltpu.VMEM
+        return pl.BlockSpec(memory_space=space)
+
+    def scratch(a, n):
+        return (pltpu.SMEM if n in smem else pltpu.VMEM)(a.shape, a.dtype)
+
+    shapes = [jax.ShapeDtypeStruct(s, d) for s, d in outs]
+    count = len(args) + len(after)
+
+    def kernel(*refs):
+        given = list(refs[: len(args)])
+        made = list(refs[count : count + len(outs)])
+        held = list(refs[count + len(outs) :])
+        sems = held.pop() if load or store else None
+        copies = []
+        for i, n in enumerate(load):
+            copies.append(pltpu.make_async_copy(given[n], held[i], sems.at[i]))
+            copies[-1].start()
+            given[n] = held[i]
+        for copy in copies:
+            copy.wait()
+        copies = []
+        for i, n in enumerate(store, len(load)):
+            copies.append(pltpu.make_async_copy(held[i], made[n], sems.at[i]))
+            made[n] = held[i]
+        body(*given, *made)
+        for copy in copies:
+            copy.start()
+        for copy in copies:
+            copy.wait()
+
+    scratch_shapes = [scratch(args[n], n) for n in load]
+    scratch_shapes += [pltpu.VMEM(shapes[n].shape, shapes[n].dtype) for n in store]
+    if scratch_shapes:
+        scratch_shapes.append(pltpu.SemaphoreType.DMA((len(load) + len(store),)))
     nbytes = sum(a.size * a.dtype.itemsize for a in args)
     return pl.pallas_call(
-        body,
-        out_shape=tuple(jax.ShapeDtypeStruct(s, d) for s, d in outs),
-        in_specs=in_specs,
-        out_specs=tuple(vmem for _ in outs),
-        compiler_params=pltpu.CompilerParams(vmem_limit_bytes=40 << 20),
+        kernel,
+        out_shape=tuple(shapes),
+        in_specs=[place(n, load) for n in range(len(args))]
+        + [pl.BlockSpec(memory_space=pl.ANY) for _ in after],
+        out_specs=tuple(place(n, store) for n in range(len(outs))),
+        scratch_shapes=scratch_shapes,
+        compiler_params=pltpu.CompilerParams(vmem_limit_bytes=vmem << 20),
         cost_estimate=pl.CostEstimate(flops=flops, bytes_accessed=nbytes, transcendentals=0),
     )(*args, *after)
 
@@ -49,7 +79,8 @@
 def prepare(hidden_ref, gain_ref, ids_ref, send_ref, place_ref):
     values = hidden_ref[...].astype(F32)
     factor = lax.rsqrt(jnp.mean(values * values, axis=-1, keepdims=True) + EPSILON)
-    normalized = (values * factor * gain_ref[...].astype(F32)).astype(BF16)
+    gain = gain_ref[...].astype(F32).reshape(1, values.shape[1])
+    normalized = (values * factor * gain).astype(BF16)
     slots, rows = place_ref.shape
     slot = lax.broadcasted_iota(jnp.int32, (slots, rows), 0)
     named = jnp.zeros((slots, rows), jnp.bool_)
@@ -105,18 +136,22 @@
         values_ref[:, h * width : (h + 1) * width] = mine
 
 
-def split_down(place_ref, w_down_ref, *out_refs):
-    slices = len(out_refs)
-    width = out_refs[0].shape[1]
-    for s in range(slices):
-        for k in range(slices):
-
-            @pl.when((s - place_ref[TP] + slices) % slices == k)
+def split_down(w_down_ref, *out_refs):
+    group = len(out_refs)
+    width = out_refs[0].shape[1] // 2
+    for s in range(group):
+        for k in range(group):
+
+            @pl.when(lax.axis_index("y") % group ^ k == s)
             def _(s=s, k=k):
-                out_refs[k][...] = w_down_ref[:, s * width : (s + 1) * width]
-
-
-def project(place_ref, *refs):
+                for half in range(2):
+                    first = (half * group + s) * width
+                    out_refs[k][:, half * width : (half + 1) * width] = w_down_ref[
+                        :, first : first + width
+                    ]
+
+
+def project(*refs):
     *parts, out_ref = refs
     slices = 8
     values = jnp.concatenate(
@@ -132,10 +167,10 @@
             ).reshape(slices, rows, 64)
             part = jnp.concatenate([part[:, : rows // 2], part[:, rows // 2 :]], axis=2)
             part = part.astype(BF16)
-            tp = (place_ref[X] - k + 4) % 4 * 2 + (place_ref[ZH] + j) % 2
+            tp = (lax.axis_index("x") - k + 4) % 4 * 2 + (lax.axis_index("zh") + j) % 2
             for b in range(slices):
-                zl = (place_ref[ZL] - b // 2 + 4) % 4
-                core = (place_ref[CORE] + b) % 2
+                zl = lax.axis_index("zl") ^ (b // 2)
+                core = (lax.axis_index("c") + b) % 2
                 out_ref[(zl * 2 + core) * slices + tp] = part[b]
 
 
@@ -159,35 +194,37 @@
     score_ref[...] = (1.0 / (1.0 + jnp.exp(-logits))).astype(BF16)
 
 
-def lower_experts(place_ref, *refs):
+def lower_experts(*refs):
     inner_ref, *parts, score_ref, back_ref = refs
-    sources = inner_ref.shape[0]
     blocks, _, padded = back_ref.shape
     slots = score_ref.shape[0]
     width = parts[0].shape[1]
     total = jnp.zeros((slots, width), F32)
-    for k in range(sources):
-        source = (place_ref[TP] - k + sources) % sources
+    for k in range(len(parts)):
+        source = lax.axis_index("y") ^ k
         total += jnp.dot(inner_ref[source, :slots], parts[k][...], preferred_element_type=F32)
     total = jnp.concatenate([total, score_ref[:, : padded - width].astype(F32)], axis=1)
     back_ref[...] = total.reshape(blocks, SLOTS, padded).astype(BF16)
 
 
-def merge_experts(back_ref, slot_ref, own_ref, out_ref):
-    slots, width = slot_ref.shape[0], out_ref.shape[1]
+def merge_experts(back_ref, slot_ref, own_ref, keep_ref, pass_ref):
+    slots, width = slot_ref.shape[0], own_ref.shape[1]
     back = back_ref[...].astype(F32).reshape(slots, back_ref.shape[2])
-    share = slot_ref[...] * back[:, width : width + 1]
+    share = slot_ref[...] * back[:, 2 * width : 2 * width + 1]
     share = ROUTE_SCALE * share / jnp.sum(share, axis=0, keepdims=True)
     upper = share.astype(BF16)
     lower = (share - upper.astype(F32)).astype(BF16)
-    parts = back[:, :width].astype(BF16)
+    parts = back[:, : 2 * width].astype(BF16)
     merged = lax.dot_general(upper, parts, TN, preferred_element_type=F32) + lax.dot_general(
         lower, parts, TN, preferred_element_type=F32
     )
-    out_ref[...] = own_ref[...].astype(F32) + merged
-
-
-def add_attention(parts_ref, sum_ref, out_ref):
+    first = lax.axis_index("y") < 4
+    near, far = merged[:, :width], merged[:, width:]
+    keep_ref[...] = own_ref[...].astype(F32) + jnp.where(first, near, far)
+    pass_ref[...] = jnp.where(first, far, near)
+
+
+def add_attention(parts_ref, keep_ref, passed_ref, out_ref):
     rows, width = out_ref.shape
     blocks, held, lanes = parts_ref.shape
     slices = blocks // 8
@@ -196,7 +233,7 @@
         parts_ref[...].astype(F32).reshape(8, slices, held, lanes), axis=1
     ).reshape(8 * held, lanes)
     attn = attn.astype(BF16)
-    merged = sum_ref[...]
+    merged = keep_ref[...] + passed_ref[...]
     lane_in, lane_out = iotas(lanes, width)
     row, lane = iotas(8 * held, width)
     token, entry = iotas(rows, 8 * held)
@@ -220,6 +257,14 @@
 
 def gather(value, axis):
     return [value] + [shift(value, axis, k) for k in range(1, lax.axis_size(axis))]
+
+
+def swap(value, axis, k):
+    return lax.ppermute(value, axis, [(i, i ^ k) for i in range(lax.axis_size(axis))])
+
+
+def trade(value, axis):
+    return [value] + [swap(value, axis, k) for k in range(1, lax.axis_size(axis))]
 
 
 def on_device(
@@ -244,22 +289,28 @@
     hidden_units = w_gate.shape[2]
     heads, latent, value_width = w_uv.shape
     out_cols, depth = w_out.shape[1], w_out.shape[0]
-    here = jnp.stack([lax.axis_index(a) for a in ("y", "x", "zh", "zl", "c")]).astype(jnp.int32)
-    tp = here[0]
+    tp = lax.axis_index("y")
 
     send, place = kernel_call(
         prepare,
         [((ep_size, SLOTS, model_width), BF16), ((slots, rows), F32)],
         hidden,
-        norm_gain.reshape(1, model_width),
+        norm_gain,
         expert_ids.T,
+        load=(0, 1, 2),
+        store=(0, 1),
+        vmem=60,
     )
     named_rows = lax.all_to_all(send, EP, 0, 0, tiled=True)
 
     down = kernel_call(
-        split_down, [((hidden_units, width), BF16)] * tp_size, here, w_down[0], smem=(0,)
-    )
-    down = [down[0]] + [shift(down[k], "y", k) for k in range(1, tp_size)]
+        split_down,
+        [((hidden_units, 2 * width), BF16)] * GROUP,
+        w_down[0],
+        load=(0,),
+        store=(0,),
+    )
+    down = [down[0]] + [swap(down[k], "y", k) for k in range(1, GROUP)]
 
     (context,) = kernel_call(
         attend,
@@ -268,7 +319,7 @@
         queries,
         jnp.swapaxes(latent_cache, 1, 2),
         smem=(0,),
-        after=down[1:],
+        load=(0, 1, 2),
     )
 
     out_other = shift(w_out.T, "zh", 1)
@@ -280,7 +331,9 @@
         w_up[0],
         router,
         context,
-        after=(out_other,),
+        load=(1, 2, 3),
+        store=(1,),
+        after=down[1:],
     )
     inner = lax.all_to_all(inner, "y", 0, 0, tiled=True)
 
@@ -290,33 +343,38 @@
         [((rows, depth), BF16)],
         inner,
         w_uv,
+        load=(1,),
         after=out_weights[1:],
         flops=10_000_000_000,
     )
-    values = gather(pair_up(values, "c"), "zl")
+    pairs = pair_up(values, "c")
+    all_values = trade(pairs, "zl")
     (attn_parts,) = kernel_call(
         project,
         [((8 * tp_size, rows // 2, 128), BF16)],
-        here,
-        *values,
+        *all_values,
         *out_weights,
-        smem=(0,),
     )
     attn_parts = lax.all_to_all(attn_parts, ("zl", "c", "y"), 0, 0, tiled=True)
 
     (back,) = kernel_call(
         lower_experts,
         [((ep_size, SLOTS, PADDED), BF16)],
-        here,
         inner,
         *down,
         score,
-        smem=(0,),
+        load=(1, 1 + GROUP),
+        after=(values,),
     )
     back = lax.all_to_all(back, EP, 0, 0, tiled=True)
     own = lax.dynamic_slice_in_dim(hidden, tp * width, width, 1)
-    (merged,) = kernel_call(merge_experts, [((rows, width), F32)], back, place, own)
-    (out,) = kernel_call(add_attention, [((rows, width), BF16)], attn_parts, merged)
+    keep, passed = kernel_call(
+        merge_experts, [((rows, width), F32)] * 2, back, place, own, load=(1,)
+    )
+    passed = swap(passed, "y", GROUP)
+    (out,) = kernel_call(
+        add_attention, [((rows, width), BF16)], attn_parts, keep, passed
+    )
     return out
 
 

time: 155 us -> 161 us (1.039)
  waiting for transfers between devices: 29.1 us -> 50.8 us
  starting transfers between devices: 92.5 us -> 83.7 us
  local copies, waits for them, and re-layouts: 16.7 us -> 9.64 us
    ppermute x15 -> x5, starting transfers between devices: 56.9 us -> 18.4 us  [shift(): return lax.ppermute(value, axis, [(i, (i + k) % size) for i in range(size)])]
    ppermute x0 -> x7, starting transfers between devices: none -> 25.8 us  [swap(): lax.ppermute(value, axis, [(i, i ^ k) for i in range(lax.axis_size(axis))])]
    all_to_all x1, waiting for transfers between devices: 0.01 us -> 20.1 us  [on_device(): named_rows = lax.all_to_all(send, EP, 0, 0, tiled=True)]
    ppermute x0 -> x7, waiting for transfers between devices: none -> 16.1 us  [swap(): lax.ppermute(value, axis, [(i, i ^ k) for i in range(lax.axis_size(axis))])]
    all_to_all x1, waiting for transfers between devices: 11.3 us -> 0.01 us  [on_device(): inner = lax.all_to_all(inner, 'y', 0, 0, tiled=True)]
    all_to_all x1, waiting for transfers between devices: 8.48 us -> 0.92 us  [on_device(): attn_parts = lax.all_to_all(attn_parts, ('zl', 'c', 'y'), 0, 0, tiled=True)]
    unnamed x50 -> x28, local copies, waits for them, and re-layouts: 15.1 us -> 8.83 us
    ppermute x15 -> x5, waiting for transfers between devices: 9.28 us -> 13.6 us  [shift(): return lax.ppermute(value, axis, [(i, (i + k) % size) for i in range(size)])]
  transfers between devices with their start and end apart: 19 -> 16, of which waited for: 7 -> 10; matrix products, arithmetic and copies ran while one was open for 1% -> 1% of each run, Pallas kernels for 6% -> 3%
where the time goes in v6:
time: 161 us; the launch traced here: 160 us
  starting transfers between devices  83.7 us (52%)
  waiting for transfers between devices  50.8 us (32%)
  Pallas kernels  14.4 us (9%)
  local copies, waits for them, and re-layouts  9.64 us (6%)
    ppermute x7, starting transfers between devices, swap(): lax.ppermute(value, axis, [(i, i ^ k) for i in range(lax.axis_size(axis))])  25.8 us
    all_to_all x1, waiting for transfers between devices, on_device(): named_rows = lax.all_to_all(send, EP, 0, 0, tiled=True)  20.1 us
    ppermute x5, starting transfers between devices, shift(): return lax.ppermute(value, axis, [(i, (i + k) % size) for i in range(size)])  18.4 us
    ppermute x7, waiting for transfers between devices, swap(): lax.ppermute(value, axis, [(i, i ^ k) for i in range(lax.axis_size(axis))])  16.1 us
    all_to_all x1, starting transfers between devices, on_device(): named_rows = lax.all_to_all(send, EP, 0, 0, tiled=True)  14.8 us
    pallas_call x9, Pallas kernels, kernel_call(): pl.pallas_call(kernel, out_shape=tuple(shapes), in_specs=[place(n, load)...  14.4 us
    ppermute x5, waiting for transfers between devices, shift(): return lax.ppermute(value, axis, [(i, (i + k) % size) for i in range(size)])  13.6 us
    all_to_all x1, starting transfers between devices, on_device(): back = lax.all_to_all(back, EP, 0, 0, tiled=True)  9.07 us
  transfers between devices with their start and end apart: 16, of which 10 were waited for; matrix products, arithmetic and copies ran while one was open for 1% of the time, Pallas kernels for 3%

profile of v6, /device:TPU:1, one launch (start us, length us, event | category | flops | bytes accessed | tf_op | source)
XLA Modules:
  0.0 159.8 jit_solution(3337775329617315376)
XLA Ops:
  0.0 3.1 %shard_map.118 = (bf16[64,4,3584]{2,1,0:T(4,128)(2,1)}, f32[256,16]{1,0:T(8,128)}) custom-call(bf16[16,3584]{1,0:T(8,128)(2,1)} %refs_0_.2, bf16[3584]{0:T(1024)(128)(2,1)} %refs_1_.3, s32[8,16]{1,0:T(8,128)} %bitcast.20), custom_call_target="tpu_custom_call" | custom-call | bytes 122368 | tf_op jit(solution)/shard_map/pallas_call | solution.py:59
  3.2 14.8 %all-to-all-start = ((bf16[64,4,3584]{2,1,0:T(4,128)(2,1)}), bf16[64,4,3584]{2,1,0:T(4,128)(2,1)S(1)}, u32[]{:S(2)}, u32[]{:S(2)}) async-start(bf16[64,4,3584]{2,1,0:T(4,128)(2,1)} %get-tuple-element.15), calls=%async_computation | async-start | bytes 3670016 | tf_op jit(solution)/shard_map/all_to_all | solution.py:304
  21.0 3.2 %collective-permute-start = (bf16[128,896]{1,0:T(8,128)(2,1)S(1)}, bf16[128,896]{1,0:T(8,128)(2,1)S(1)}, u32[]{:S(2)}, u32[]{:S(2)}) collective-permute-start(bf16[128,896]{1,0:T(8,128)(2,1)S(1)} %get-tuple-element.16), channel_id=1, source_target_pairs={{0,1},{1,0},{2,3},{3,2},{4,5},{5,4},{6,7},{7,6},{8,9},{9,8},{10,11... | collective-permute-start | bytes 688136 | tf_op jit(solution)/shard_map/ppermute | solution.py:263
  24.2 4.2 %collective-permute-start.1 = (bf16[128,896]{1,0:T(8,128)(2,1)S(1)}, bf16[128,896]{1,0:T(8,128)(2,1)S(1)}, u32[]{:S(2)}, u32[]{:S(2)}) collective-permute-start(bf16[128,896]{1,0:T(8,128)(2,1)S(1)} %get-tuple-element.17), channel_id=1, source_target_pairs={{0,2},{1,3},{2,0},{3,1},{4,6},{5,7},{6,4},{7,5},{8,10},{9,11},{10,... | collective-permute-start | bytes 688136 | tf_op jit(solution)/shard_map/ppermute | solution.py:263
  28.4 1.9 %collective-permute-start.2 = (bf16[128,896]{1,0:T(8,128)(2,1)S(1)}, bf16[128,896]{1,0:T(8,128)(2,1)S(1)}, u32[]{:S(2)}, u32[]{:S(2)}) collective-permute-start(bf16[128,896]{1,0:T(8,128)(2,1)S(1)} %get-tuple-element.18), channel_id=1, source_target_pairs={{0,3},{1,2},{2,1},{3,0},{4,7},{5,6},{6,5},{7,4},{8,11},{9,10},{10,... | collective-permute-start | bytes 688136 | tf_op jit(solution)/shard_map/ppermute | solution.py:263
  34.6 8.6 %collective-permute-done.1.refs_6_.refs_3_ = bf16[128,896]{1,0:T(8,128)(2,1)S(1)} collective-permute-done((bf16[128,896]{1,0:T(8,128)(2,1)S(1)}, bf16[128,896]{1,0:T(8,128)(2,1)S(1)}, u32[]{:S(2)}, u32[]{:S(2)}) %collective-permute-start.1) | collective-permute-done | bytes 229408 | tf_op jit(solution)/shard_map/ppermute | solution.py:263
  43.3 20.1 %all-to-all-done.refs_0_ = bf16[64,4,3584]{2,1,0:T(4,128)(2,1)S(1)} async-done(((bf16[64,4,3584]{2,1,0:T(4,128)(2,1)}), bf16[64,4,3584]{2,1,0:T(4,128)(2,1)S(1)}, u32[]{:S(2)}, u32[]{:S(2)}) %all-to-all-start) | async-done | bytes 1835040 | tf_op jit(solution)/shard_map/all_to_all | solution.py:304
  65.5 2.2 %shard_map.121 = (bf16[8,320,128]{2,1,0:T(8,128)(2,1)S(1)}, bf16[256,128]{1,0:T(8,128)(2,1)S(1)}) custom-call(bf16[64,4,3584]{2,1,0:T(4,128)(2,1)S(1)} %all-to-all-done.refs_0_, bf16[3584,128]{1,0:T(8,128)(2,1)S(1)} %bitcast.11, bf16[3584,128]{1,0:T(8,128)(2,1)S(1)} %bitcast.12, bf16[1,3584]{1,0:T(2,128)(2,1)S(1)} %copy-done.11, ...), custom_call_target="tpu_custom_call" | custom-call | bytes 3808256 | tf_op jit(solution)/shard_map/pallas_call | solution.py:59
  68.6 6.8 %all-to-all-start.1 = ((bf16[8,320,128]{2,1,0:T(8,128)(2,1)}), bf16[8,320,128]{2,1,0:T(8,128)(2,1)S(1)}, u32[]{:S(2)}, u32[]{:S(2)}) async-start(bf16[8,320,128]{2,1,0:T(8,128)(2,1)} %copy-done.4), calls=%async_computation.1 | async-start | bytes 1310720 | tf_op jit(solution)/shard_map/all_to_all | solution.py:338
  75.4 4.4 %collective-permute-start.3 = (bf16[56,1024]{1,0:T(8,128)(2,1)}, bf16[56,1024]{1,0:T(8,128)(2,1)S(1)}, u32[]{:S(2)}, u32[]{:S(2)}) collective-permute-start(bf16[56,1024]{1,0:T(8,128)(2,1)} %bitcast.16), channel_id=1, source_target_pairs={{0,64},{64,0},{1,65},{65,1},{2,66},{66,2},{3,67},{67,3},{4,68},{68... | collective-permute-start | bytes 344072 | tf_op jit(solution)/shard_map/ppermute | solution.py:251
  79.8 6.9 %collective-permute-done.3 = bf16[56,1024]{1,0:T(8,128)(2,1)S(1)} collective-permute-done((bf16[56,1024]{1,0:T(8,128)(2,1)}, bf16[56,1024]{1,0:T(8,128)(2,1)S(1)}, u32[]{:S(2)}, u32[]{:S(2)}) %collective-permute-start.3) | collective-permute-done | bytes 114720 | tf_op jit(solution)/shard_map/ppermute | solution.py:251
  87.6 5.3 %collective-permute-start.4 = (bf16[2,56,1024]{2,1,0:T(8,128)(2,1)S(1)}, bf16[2,56,1024]{2,1,0:T(8,128)(2,1)S(1)}, u32[]{:S(2)}, u32[]{:S(2)}) collective-permute-start(bf16[2,56,1024]{2,1,0:T(8,128)(2,1)S(1)} %pad_maximum_fusion.refs_4_), channel_id=1, source_target_pairs={{0,128},{128,256},{256,384},{384,0},{1,129},{129,257},{257,385},{3... | collective-permute-start | bytes 688136 | tf_op jit(solution)/shard_map/ppermute | solution.py:251
  94.9 4.3 %collective-permute-start.6 = (bf16[2,56,1024]{2,1,0:T(8,128)(2,1)S(1)}, bf16[2,56,1024]{2,1,0:T(8,128)(2,1)S(1)}, u32[]{:S(2)}, u32[]{:S(2)}) collective-permute-start(bf16[2,56,1024]{2,1,0:T(8,128)(2,1)S(1)} %pad_maximum_fusion.refs_4_), channel_id=1, source_target_pairs={{0,384},{128,0},{256,128},{384,256},{1,385},{129,1},{257,129},{385... | collective-permute-start | bytes 688136 | tf_op jit(solution)/shard_map/ppermute | solution.py:251
  99.2 3.6 %collective-permute-done.5.refs_3_.refs_6_ = bf16[2,56,1024]{2,1,0:T(8,128)(2,1)S(1)} collective-permute-done((bf16[2,56,1024]{2,1,0:T(8,128)(2,1)S(1)}, bf16[2,56,1024]{2,1,0:T(8,128)(2,1)S(1)}, u32[]{:S(2)}, u32[]{:S(2)}) %collective-permute-start.5) | collective-permute-done | bytes 229408 | tf_op jit(solution)/shard_map/ppermute | solution.py:251
  102.9 2.3 %collective-permute-done.6.refs_4_.refs_7_ = bf16[2,56,1024]{2,1,0:T(8,128)(2,1)S(1)} collective-permute-done((bf16[2,56,1024]{2,1,0:T(8,128)(2,1)S(1)}, bf16[2,56,1024]{2,1,0:T(8,128)(2,1)S(1)}, u32[]{:S(2)}, u32[]{:S(2)}) %collective-permute-start.6) | collective-permute-done | bytes 229408 | tf_op jit(solution)/shard_map/ppermute | solution.py:251
  109.8 9.1 %all-to-all-start.3 = ((bf16[64,4,1024]{2,1,0:T(4,128)(2,1)}), bf16[64,4,1024]{2,1,0:T(4,128)(2,1)S(1)}, u32[]{:S(2)}, u32[]{:S(2)}) async-start(bf16[64,4,1024]{2,1,0:T(4,128)(2,1)} %shard_map.124), calls=%async_computation.3 | async-start | bytes 1048576 | tf_op jit(solution)/shard_map/all_to_all | solution.py:369
  118.9 2.4 %collective-permute-start.7 = (bf16[16,1024]{1,0:T(8,128)(2,1)S(1)}, bf16[16,1024]{1,0:T(8,128)(2,1)S(1)}, u32[]{:S(2)}, u32[]{:S(2)}) collective-permute-start(bf16[16,1024]{1,0:T(8,128)(2,1)S(1)} %shard_map.122.refs_6_), channel_id=1, source_target_pairs={{0,8},{8,0},{1,9},{9,1},{2,10},{10,2},{3,11},{11,3},{4,12},{12,4},... | collective-permute-start | bytes 98312 | tf_op jit(solution)/shard_map/ppermute | solution.py:251
  122.1 3.2 %collective-permute-start.8 = (bf16[2,16,1024]{2,1,0:T(8,128)(2,1)S(1)}, bf16[2,16,1024]{2,1,0:T(8,128)(2,1)S(1)}, u32[]{:S(2)}, u32[]{:S(2)}) collective-permute-start(bf16[2,16,1024]{2,1,0:T(8,128)(2,1)S(1)} %pad_maximum_fusion.1.refs_0_), channel_id=1, source_target_pairs={{0,16},{16,0},{32,48},{48,32},{1,17},{17,1},{33,49},{49,33},{2,18}... | collective-permute-start | bytes 196616 | tf_op jit(solution)/shard_map/ppermute | solution.py:263
  125.3 4.0 %collective-permute-start.9 = (bf16[2,16,1024]{2,1,0:T(8,128)(2,1)S(1)}, bf16[2,16,1024]{2,1,0:T(8,128)(2,1)S(1)}, u32[]{:S(2)}, u32[]{:S(2)}) collective-permute-start(bf16[2,16,1024]{2,1,0:T(8,128)(2,1)S(1)} %pad_maximum_fusion.1.refs_0_), channel_id=1, source_target_pairs={{0,32},{16,48},{32,0},{48,16},{1,33},{17,49},{33,1},{49,17},{2,34}... | collective-permute-start | bytes 196616 | tf_op jit(solution)/shard_map/ppermute | solution.py:263
  129.3 2.1 %collective-permute-start.10 = (bf16[2,16,1024]{2,1,0:T(8,128)(2,1)S(1)}, bf16[2,16,1024]{2,1,0:T(8,128)(2,1)S(1)}, u32[]{:S(2)}, u32[]{:S(2)}) collective-permute-start(bf16[2,16,1024]{2,1,0:T(8,128)(2,1)S(1)} %pad_maximum_fusion.1.refs_0_), channel_id=1, source_target_pairs={{0,48},{16,32},{32,16},{48,0},{1,49},{17,33},{33,17},{49,1},{2,50}... | collective-permute-start | bytes 196616 | tf_op jit(solution)/shard_map/ppermute | solution.py:263
  131.4 3.5 %collective-permute-done.8.refs_1_ = bf16[2,16,1024]{2,1,0:T(8,128)(2,1)S(1)} collective-permute-done((bf16[2,16,1024]{2,1,0:T(8,128)(2,1)S(1)}, bf16[2,16,1024]{2,1,0:T(8,128)(2,1)S(1)}, u32[]{:S(2)}, u32[]{:S(2)}) %collective-permute-start.8) | collective-permute-done | bytes 65568 | tf_op jit(solution)/shard_map/ppermute | solution.py:263
  134.9 3.2 %collective-permute-done.10.refs_3_ = bf16[2,16,1024]{2,1,0:T(8,128)(2,1)S(1)} collective-permute-done((bf16[2,16,1024]{2,1,0:T(8,128)(2,1)S(1)}, bf16[2,16,1024]{2,1,0:T(8,128)(2,1)S(1)}, u32[]{:S(2)}, u32[]{:S(2)}) %collective-permute-start.10) | collective-permute-done | bytes 65568 | tf_op jit(solution)/shard_map/ppermute | solution.py:263
  139.6 8.8 %all-to-all-start.2 = ((bf16[64,8,128]{2,1,0:T(8,128)(2,1)}), bf16[64,8,128]{2,1,0:T(8,128)(2,1)S(1)}, u32[]{:S(2)}, u32[]{:S(2)}) async-start(bf16[64,8,128]{2,1,0:T(8,128)(2,1)} %shard_map.123), calls=%async_computation.2 | async-start | bytes 262144 | tf_op jit(solution)/shard_map/all_to_all | solution.py:358
  149.9 7.2 %collective-permute-start.11 = (f32[16,448]{1,0:T(8,128)S(1)}, f32[16,448]{1,0:T(8,128)S(1)}, u32[]{:S(2)}, u32[]{:S(2)}) collective-permute-start(f32[16,448]{1,0:T(8,128)S(1)} %get-tuple-element.24), channel_id=1, source_target_pairs={{0,4},{1,5},{2,6},{3,7},{4,0},{5,1},{6,2},{7,3},{8,12},{9,13},{10,... | collective-permute-start | bytes 86024 | tf_op jit(solution)/shard_map/ppermute | solution.py:263
  (48 shorter events, 24.1 us)
Async XLA Ops:
  3.1 27.2 %copy-start.12 = (s32[2]{0:T(128)S(1)}, s32[2]{0:T(128)}, u32[]{:S(2)}) copy-start(s32[2]{0:T(128)} %refs_0_.3) | copy-start | bytes 28
  3.1 60.3 %copy-start.11 = (bf16[1,3584]{1,0:T(2,128)(2,1)S(1)}, bf16[1,3584]{1,0:T(2,128)(2,1)}, u32[]{:S(2)}) copy-start(bf16[1,3584]{1,0:T(2,128)(2,1)} %refs_3_.1) | copy-start | bytes 21508
  3.2 60.3 %all-to-all-start = ((bf16[64,4,3584]{2,1,0:T(4,128)(2,1)}), bf16[64,4,3584]{2,1,0:T(4,128)(2,1)S(1)}, u32[]{:S(2)}, u32[]{:S(2)}) async-start(bf16[64,4,3584]{2,1,0:T(4,128)(2,1)} %get-tuple-element.15), calls=%async_computation | async-start | bytes 3670016 | tf_op jit(solution)/shard_map/all_to_all | solution.py:304
  18.0 45.4 %copy-start = (bf16[1,3584,128]{2,1,0:T(8,128)(2,1)S(1)}, bf16[1,3584,128]{2,1,0:T(8,128)(2,1)}, u32[]{:S(2)}) copy-start(bf16[1,3584,128]{2,1,0:T(8,128)(2,1)} %param.19) | copy-start | bytes 2752516
  18.0 1.3 copy-start.2
  21.0 13.7 %collective-permute-start = (bf16[128,896]{1,0:T(8,128)(2,1)S(1)}, bf16[128,896]{1,0:T(8,128)(2,1)S(1)}, u32[]{:S(2)}, u32[]{:S(2)}) collective-permute-start(bf16[128,896]{1,0:T(8,128)(2,1)S(1)} %get-tuple-element.16), channel_id=1, source_target_pairs={{0,1},{1,0},{2,3},{3,2},{4,5},{5,4},{6,7},{7,6},{8,9},{9,8},{10,11... | collective-permute-start | bytes 688136 | tf_op jit(solution)/shard_map/ppermute | solution.py:263
  24.2 19.1 %collective-permute-start.1 = (bf16[128,896]{1,0:T(8,128)(2,1)S(1)}, bf16[128,896]{1,0:T(8,128)(2,1)S(1)}, u32[]{:S(2)}, u32[]{:S(2)}) collective-permute-start(bf16[128,896]{1,0:T(8,128)(2,1)S(1)} %get-tuple-element.17), channel_id=1, source_target_pairs={{0,2},{1,3},{2,0},{3,1},{4,6},{5,7},{6,4},{7,5},{8,10},{9,11},{10,... | collective-permute-start | bytes 688136 | tf_op jit(solution)/shard_map/ppermute | solution.py:263
  28.4 14.9 %collective-permute-start.2 = (bf16[128,896]{1,0:T(8,128)(2,1)S(1)}, bf16[128,896]{1,0:T(8,128)(2,1)S(1)}, u32[]{:S(2)}, u32[]{:S(2)}) collective-permute-start(bf16[128,896]{1,0:T(8,128)(2,1)S(1)} %get-tuple-element.18), channel_id=1, source_target_pairs={{0,3},{1,2},{2,1},{3,0},{4,7},{5,6},{6,5},{7,4},{8,11},{9,10},{10,... | collective-permute-start | bytes 688136 | tf_op jit(solution)/shard_map/ppermute | solution.py:263
  63.4 1.2 copy-start.1
  68.6 36.6 %all-to-all-start.1 = ((bf16[8,320,128]{2,1,0:T(8,128)(2,1)}), bf16[8,320,128]{2,1,0:T(8,128)(2,1)S(1)}, u32[]{:S(2)}, u32[]{:S(2)}) async-start(bf16[8,320,128]{2,1,0:T(8,128)(2,1)} %copy-done.4), calls=%async_computation.1 | async-start | bytes 1310720 | tf_op jit(solution)/shard_map/all_to_all | solution.py:338
  75.4 11.3 %collective-permute-start.3 = (bf16[56,1024]{1,0:T(8,128)(2,1)}, bf16[56,1024]{1,0:T(8,128)(2,1)S(1)}, u32[]{:S(2)}, u32[]{:S(2)}) collective-permute-start(bf16[56,1024]{1,0:T(8,128)(2,1)} %bitcast.16), channel_id=1, source_target_pairs={{0,64},{64,0},{1,65},{65,1},{2,66},{66,2},{3,67},{67,3},{4,68},{68... | collective-permute-start | bytes 344072 | tf_op jit(solution)/shard_map/ppermute | solution.py:251
  87.6 20.3 %copy-start.8 = (bf16[128,896]{1,0:T(8,128)(2,1)S(1)}, bf16[128,896]{1,0:T(8,128)(2,1)}, u32[]{:S(2)}) copy-start(bf16[128,896]{1,0:T(8,128)(2,1)} %copy-done.7) | copy-start | bytes 688132
  87.6 11.6 %collective-permute-start.4 = (bf16[2,56,1024]{2,1,0:T(8,128)(2,1)S(1)}, bf16[2,56,1024]{2,1,0:T(8,128)(2,1)S(1)}, u32[]{:S(2)}, u32[]{:S(2)}) collective-permute-start(bf16[2,56,1024]{2,1,0:T(8,128)(2,1)S(1)} %pad_maximum_fusion.refs_4_), channel_id=1, source_target_pairs={{0,128},{128,256},{256,384},{384,0},{1,129},{129,257},{257,385},{3... | collective-permute-start | bytes 688136 | tf_op jit(solution)/shard_map/ppermute | solution.py:251
  93.0 9.9 %collective-permute-start.5 = (bf16[2,56,1024]{2,1,0:T(8,128)(2,1)S(1)}, bf16[2,56,1024]{2,1,0:T(8,128)(2,1)S(1)}, u32[]{:S(2)}, u32[]{:S(2)}) collective-permute-start(bf16[2,56,1024]{2,1,0:T(8,128)(2,1)S(1)} %pad_maximum_fusion.refs_4_), channel_id=1, source_target_pairs={{0,256},{128,384},{256,0},{384,128},{1,257},{129,385},{257,1},{385... | collective-permute-start | bytes 688136 | tf_op jit(solution)/shard_map/ppermute | solution.py:251
  94.9 10.2 %collective-permute-start.6 = (bf16[2,56,1024]{2,1,0:T(8,128)(2,1)S(1)}, bf16[2,56,1024]{2,1,0:T(8,128)(2,1)S(1)}, u32[]{:S(2)}, u32[]{:S(2)}) collective-permute-start(bf16[2,56,1024]{2,1,0:T(8,128)(2,1)S(1)} %pad_maximum_fusion.refs_4_), channel_id=1, source_target_pairs={{0,384},{128,0},{256,128},{384,256},{1,385},{129,1},{257,129},{385... | collective-permute-start | bytes 688136 | tf_op jit(solution)/shard_map/ppermute | solution.py:251
  105.2 1.2 copy-start.13
  109.8 39.4 %copy-start.10 = (f32[256,16]{1,0:T(8,128)S(1)}, f32[256,16]{1,0:T(8,128)}, u32[]{:S(2)}) copy-start(f32[256,16]{1,0:T(8,128)} %get-tuple-element.22.refs_1_) | copy-start | bytes 49156
  109.8 29.7 %all-to-all-start.3 = ((bf16[64,4,1024]{2,1,0:T(4,128)(2,1)}), bf16[64,4,1024]{2,1,0:T(4,128)(2,1)S(1)}, u32[]{:S(2)}, u32[]{:S(2)}) async-start(bf16[64,4,1024]{2,1,0:T(4,128)(2,1)} %shard_map.124), calls=%async_computation.3 | async-start | bytes 1048576 | tf_op jit(solution)/shard_map/all_to_all | solution.py:369
  118.9 3.2 %collective-permute-start.7 = (bf16[16,1024]{1,0:T(8,128)(2,1)S(1)}, bf16[16,1024]{1,0:T(8,128)(2,1)S(1)}, u32[]{:S(2)}, u32[]{:S(2)}) collective-permute-start(bf16[16,1024]{1,0:T(8,128)(2,1)S(1)} %shard_map.122.refs_6_), channel_id=1, source_target_pairs={{0,8},{8,0},{1,9},{9,1},{2,10},{10,2},{3,11},{11,3},{4,12},{12,4},... | collective-permute-start | bytes 98312 | tf_op jit(solution)/shard_map/ppermute | solution.py:251
  122.1 12.8 %collective-permute-start.8 = (bf16[2,16,1024]{2,1,0:T(8,128)(2,1)S(1)}, bf16[2,16,1024]{2,1,0:T(8,128)(2,1)S(1)}, u32[]{:S(2)}, u32[]{:S(2)}) collective-permute-start(bf16[2,16,1024]{2,1,0:T(8,128)(2,1)S(1)} %pad_maximum_fusion.1.refs_0_), channel_id=1, source_target_pairs={{0,16},{16,0},{32,48},{48,32},{1,17},{17,1},{33,49},{49,33},{2,18}... | collective-permute-start | bytes 196616 | tf_op jit(solution)/shard_map/ppermute | solution.py:263
  125.3 9.6 %collective-permute-start.9 = (bf16[2,16,1024]{2,1,0:T(8,128)(2,1)S(1)}, bf16[2,16,1024]{2,1,0:T(8,128)(2,1)S(1)}, u32[]{:S(2)}, u32[]{:S(2)}) collective-permute-start(bf16[2,16,1024]{2,1,0:T(8,128)(2,1)S(1)} %pad_maximum_fusion.1.refs_0_), channel_id=1, source_target_pairs={{0,32},{16,48},{32,0},{48,16},{1,33},{17,49},{33,1},{49,17},{2,34}... | collective-permute-start | bytes 196616 | tf_op jit(solution)/shard_map/ppermute | solution.py:263
  129.3 8.8 %collective-permute-start.10 = (bf16[2,16,1024]{2,1,0:T(8,128)(2,1)S(1)}, bf16[2,16,1024]{2,1,0:T(8,128)(2,1)S(1)}, u32[]{:S(2)}, u32[]{:S(2)}) collective-permute-start(bf16[2,16,1024]{2,1,0:T(8,128)(2,1)S(1)} %pad_maximum_fusion.1.refs_0_), channel_id=1, source_target_pairs={{0,48},{16,32},{32,16},{48,0},{1,49},{17,33},{33,17},{49,1},{2,50}... | collective-permute-start | bytes 196616 | tf_op jit(solution)/shard_map/ppermute | solution.py:263
  139.6 18.5 %all-to-all-start.2 = ((bf16[64,8,128]{2,1,0:T(8,128)(2,1)}), bf16[64,8,128]{2,1,0:T(8,128)(2,1)S(1)}, u32[]{:S(2)}, u32[]{:S(2)}) async-start(bf16[64,8,128]{2,1,0:T(8,128)(2,1)} %shard_map.123), calls=%async_computation.2 | async-start | bytes 262144 | tf_op jit(solution)/shard_map/all_to_all | solution.py:358
  149.9 8.9 %collective-permute-start.11 = (f32[16,448]{1,0:T(8,128)S(1)}, f32[16,448]{1,0:T(8,128)S(1)}, u32[]{:S(2)}, u32[]{:S(2)}) collective-permute-start(f32[16,448]{1,0:T(8,128)S(1)} %get-tuple-element.24), channel_id=1, source_target_pairs={{0,4},{1,5},{2,6},{3,7},{4,0},{5,1},{6,2},{7,3},{8,12},{9,13},{10,... | collective-permute-start | bytes 86024 | tf_op jit(solution)/shard_map/ppermute | solution.py:263
  (6 other events, 5.2 us)

commit v7 on v6

--- a/solution.py
+++ b/solution.py
@@ -151,27 +151,33 @@
                     ]
 
 
+def mark(out_ref):
+    out_ref[...] = jnp.zeros(out_ref.shape, F32)
+
+
 def project(*refs):
     *parts, out_ref = refs
-    slices = 8
-    values = jnp.concatenate(
-        [part[...].reshape(-1, part.shape[2]) for part in parts[:4]], axis=0
-    )
-    rows = values.shape[0] // slices
+    blocks, slices = 4, 8
+    rows = parts[0].shape[0]
+    values = jnp.concatenate([part[...] for part in parts[:blocks]], axis=0)
+    first = lax.axis_index("c") == 0
     for k in range(4):
         for j in range(2):
-            weights = parts[4 + k][j]
-            part = lax.dot_general(values, weights, NT, preferred_element_type=F32)
+            cols = parts[blocks + k].shape[2]
+            mine, other = [
+                lax.dot_general(
+                    values, parts[blocks + k][j, core], NT, preferred_element_type=F32
+                )
+                for core in range(2)
+            ]
+            pad = jnp.zeros((mine.shape[0], 128 - 2 * cols), F32)
             part = jnp.concatenate(
-                [part, jnp.zeros((part.shape[0], 64 - part.shape[1]), F32)], axis=1
-            ).reshape(slices, rows, 64)
-            part = jnp.concatenate([part[:, : rows // 2], part[:, rows // 2 :]], axis=2)
-            part = part.astype(BF16)
+                [jnp.where(first, mine, other), jnp.where(first, other, mine), pad], axis=1
+            )
+            part = part.reshape(blocks, rows, 128).astype(BF16)
             tp = (lax.axis_index("x") - k + 4) % 4 * 2 + (lax.axis_index("zh") + j) % 2
-            for b in range(slices):
-                zl = lax.axis_index("zl") ^ (b // 2)
-                core = (lax.axis_index("c") + b) % 2
-                out_ref[(zl * 2 + core) * slices + tp] = part[b]
+            for b in range(blocks):
+                out_ref[(lax.axis_index("zl") ^ b) * slices + tp] = part[b]
 
 
 def lift_experts(rows_ref, w_gate_ref, w_up_ref, router_ref, context_ref, inner_ref, score_ref):
@@ -226,24 +232,18 @@
 
 def add_attention(parts_ref, keep_ref, passed_ref, out_ref):
     rows, width = out_ref.shape
-    blocks, held, lanes = parts_ref.shape
-    slices = blocks // 8
-    cols = width // 8
-    attn = jnp.sum(
-        parts_ref[...].astype(F32).reshape(8, slices, held, lanes), axis=1
-    ).reshape(8 * held, lanes)
-    attn = attn.astype(BF16)
-    merged = keep_ref[...] + passed_ref[...]
-    lane_in, lane_out = iotas(lanes, width)
-    row, lane = iotas(8 * held, width)
-    token, entry = iotas(rows, 8 * held)
-    for q in range(2):
-        spread = one_hot(lane_out % cols + q * (lanes // 2) == lane_in)
-        mine = jnp.dot(attn, spread, preferred_element_type=F32)
-        mine = jnp.where(lane // cols == row // held, mine, 0.0).astype(BF16)
-        pick = one_hot(token == entry % held + q * held)
-        merged += jnp.dot(pick, mine, preferred_element_type=F32)
-    out_ref[...] = merged.astype(BF16)
+    blocks = 4
+    slices = parts_ref.shape[0] // blocks
+    attn = jnp.concatenate(
+        [
+            jnp.sum(parts_ref[b * slices : (b + 1) * slices].astype(F32), axis=0)[
+                :, : width // blocks
+            ]
+            for b in range(blocks)
+        ],
+        axis=1,
+    )
+    out_ref[...] = (keep_ref[...] + passed_ref[...] + attn).astype(BF16)
 
 
 def shift(value, axis, k):
@@ -320,9 +320,11 @@
         jnp.swapaxes(latent_cache, 1, 2),
         smem=(0,),
         load=(0, 1, 2),
-    )
-
-    out_other = shift(w_out.T, "zh", 1)
+        after=down[1:],
+    )
+
+    out_pair = pair_up(w_out.T, "c")
+    out_other = shift(out_pair, "zh", 1)
     inner, score = kernel_call(
         lift_experts,
         [((tp_size, slots + 8 * heads, hidden_units), BF16), ((slots, 128), BF16)],
@@ -332,30 +334,33 @@
         router,
         context,
         load=(1, 2, 3),
-        store=(1,),
-        after=down[1:],
+        store=(0, 1),
+        after=(out_other,),
     )
     inner = lax.all_to_all(inner, "y", 0, 0, tiled=True)
 
-    out_weights = gather(jnp.stack([w_out.T, out_other]), "x")
+    out_weights = gather(jnp.stack([out_pair, out_other]), "x")
     (values,) = kernel_call(
         lift_heads,
         [((rows, depth), BF16)],
         inner,
         w_uv,
         load=(1,),
-        after=out_weights[1:],
         flops=10_000_000_000,
     )
-    pairs = pair_up(values, "c")
-    all_values = trade(pairs, "zl")
+
+    all_values = trade(values, "zl")
+    (gathered,) = kernel_call(
+        mark, [((8, 128), F32)], after=out_weights[1:], flops=10_000_000_000
+    )
     (attn_parts,) = kernel_call(
         project,
-        [((8 * tp_size, rows // 2, 128), BF16)],
+        [((4 * tp_size, rows, 128), BF16)],
         *all_values,
         *out_weights,
-    )
-    attn_parts = lax.all_to_all(attn_parts, ("zl", "c", "y"), 0, 0, tiled=True)
+        after=(gathered,),
+    )
+    attn_parts = lax.all_to_all(attn_parts, ("zl", "y"), 0, 0, tiled=True)
 
     (back,) = kernel_call(
         lower_experts,
@@ -364,7 +369,6 @@
         *down,
         score,
         load=(1, 1 + GROUP),
-        after=(values,),
     )
     back = lax.all_to_all(back, EP, 0, 0, tiled=True)
     own = lax.dynamic_slice_in_dim(hidden, tp * width, width, 1)

time: 161 us -> 153 us (0.950)
  waiting for transfers between devices: 50.8 us -> 39.3 us
  other arithmetic: 0.93 us -> 2.7 us
    all_to_all x1, waiting for transfers between devices: 20.1 us -> 0.01 us  [on_device(): named_rows = lax.all_to_all(send, EP, 0, 0, tiled=True)]
    ppermute x5, waiting for transfers between devices: 13.6 us -> 21.7 us  [shift(): return lax.ppermute(value, axis, [(i, (i + k) % size) for i in range(size)])]
    all_to_all x1, waiting for transfers between devices: 0.01 us -> 5.82 us  [on_device(): inner = lax.all_to_all(inner, 'y', 0, 0, tiled=True)]
    ppermute x7, waiting for transfers between devices: 16.1 us -> 10.8 us  [swap(): lax.ppermute(value, axis, [(i, i ^ k) for i in range(lax.axis_size(axis))])]
    all_to_all x1, starting transfers between devices: 8.85 us -> 3.84 us  [on_device(): attn_parts = lax.all_to_all(attn_parts, ('zl', 'y'), 0, 0, tiled=True)]
    all_to_all x1, starting transfers between devices: 9.07 us -> 12.1 us  [on_device(): back = lax.all_to_all(back, EP, 0, 0, tiled=True)]
    another operation x2, other arithmetic: 0.93 us -> 2.7 us  [on_device(): out_weights = gather(jnp.stack([out_pair, out_other]), 'x')]
    ppermute x5, starting transfers between devices: 18.4 us -> 20.1 us  [shift(): return lax.ppermute(value, axis, [(i, (i + k) % size) for i in range(size)])]
  transfers between devices with their start and end apart: 16 -> 16, of which waited for: 10 -> 7; matrix products, arithmetic and copies ran while one was open for 1% -> 2% of each run, Pallas kernels for 3% -> 6%
where the time goes in v7:
time: 153 us; the launch traced here: 151 us
  starting transfers between devices  83.5 us (55%)
  waiting for transfers between devices  39.3 us (26%)
  Pallas kernels  15.3 us (10%)
  local copies, waits for them, and re-layouts  9.82 us (6%)
  other arithmetic  2.7 us (2%)
    ppermute x7, starting transfers between devices, swap(): lax.ppermute(value, axis, [(i, i ^ k) for i in range(lax.axis_size(axis))])  25.7 us
    ppermute x5, waiting for transfers between devices, shift(): return lax.ppermute(value, axis, [(i, (i + k) % size) for i in range(size)])  21.7 us
    ppermute x5, starting transfers between devices, shift(): return lax.ppermute(value, axis, [(i, (i + k) % size) for i in range(size)])  20.1 us
    pallas_call x10, Pallas kernels, kernel_call(): pl.pallas_call(kernel, out_shape=tuple(shapes), in_specs=[place(n, load)...  15.3 us
    all_to_all x1, starting transfers between devices, on_device(): named_rows = lax.all_to_all(send, EP, 0, 0, tiled=True)  15 us
    all_to_all x1, starting transfers between devices, on_device(): back = lax.all_to_all(back, EP, 0, 0, tiled=True)  12.1 us
    ppermute x7, waiting for transfers between devices, swap(): lax.ppermute(value, axis, [(i, i ^ k) for i in range(lax.axis_size(axis))])  10.8 us
    unnamed x32, local copies, waits for them, and re-layouts  9.01 us
  transfers between devices with their start and end apart: 16, of which 7 were waited for; matrix products, arithmetic and copies ran while one was open for 2% of the time, Pallas kernels for 6%

profile of v7, /device:TPU:1, one launch (start us, length us, event | category | flops | bytes accessed | tf_op | source)
XLA Modules:
  0.0 150.9 jit_solution(8388936598444675349)
XLA Ops:
  0.0 3.1 %shard_map.118 = (bf16[64,4,3584]{2,1,0:T(4,128)(2,1)}, f32[256,16]{1,0:T(8,128)}) custom-call(bf16[16,3584]{1,0:T(8,128)(2,1)} %refs_0_.2, bf16[3584]{0:T(1024)(128)(2,1)} %refs_1_.3, s32[8,16]{1,0:T(8,128)} %bitcast.18), custom_call_target="tpu_custom_call" | custom-call | bytes 122368 | tf_op jit(solution)/shard_map/pallas_call | solution.py:59
  3.1 15.0 %all-to-all-start = ((bf16[64,4,3584]{2,1,0:T(4,128)(2,1)}), bf16[64,4,3584]{2,1,0:T(4,128)(2,1)S(1)}, u32[]{:S(2)}, u32[]{:S(2)}) async-start(bf16[64,4,3584]{2,1,0:T(4,128)(2,1)} %get-tuple-element.15), calls=%async_computation | async-start | bytes 3670016 | tf_op jit(solution)/shard_map/all_to_all | solution.py:304
  18.2 2.5 %collective-permute-start.3 = (bf16[56,1024]{1,0:T(8,128)(2,1)}, bf16[56,1024]{1,0:T(8,128)(2,1)S(1)}, u32[]{:S(2)}, u32[]{:S(2)}) collective-permute-start(bf16[56,1024]{1,0:T(8,128)(2,1)} %bitcast.5), channel_id=1, source_target_pairs={{0,8},{8,0},{1,9},{9,1},{2,10},{10,2},{3,11},{11,3},{4,12},{12,4},... | collective-permute-start | bytes 344072 | tf_op jit(solution)/shard_map/ppermute | solution.py:251
  22.4 3.3 %collective-permute-start = (bf16[128,896]{1,0:T(8,128)(2,1)S(1)}, bf16[128,896]{1,0:T(8,128)(2,1)S(1)}, u32[]{:S(2)}, u32[]{:S(2)}) collective-permute-start(bf16[128,896]{1,0:T(8,128)(2,1)S(1)} %get-tuple-element.16), channel_id=1, source_target_pairs={{0,1},{1,0},{2,3},{3,2},{4,5},{5,4},{6,7},{7,6},{8,9},{9,8},{10,11... | collective-permute-start | bytes 688136 | tf_op jit(solution)/shard_map/ppermute | solution.py:263
  25.7 4.2 %collective-permute-start.1 = (bf16[128,896]{1,0:T(8,128)(2,1)S(1)}, bf16[128,896]{1,0:T(8,128)(2,1)S(1)}, u32[]{:S(2)}, u32[]{:S(2)}) collective-permute-start(bf16[128,896]{1,0:T(8,128)(2,1)S(1)} %get-tuple-element.17), channel_id=1, source_target_pairs={{0,2},{1,3},{2,0},{3,1},{4,6},{5,7},{6,4},{7,5},{8,10},{9,11},{10,... | collective-permute-start | bytes 688136 | tf_op jit(solution)/shard_map/ppermute | solution.py:263
  29.9 1.9 %collective-permute-start.2 = (bf16[128,896]{1,0:T(8,128)(2,1)S(1)}, bf16[128,896]{1,0:T(8,128)(2,1)S(1)}, u32[]{:S(2)}, u32[]{:S(2)}) collective-permute-start(bf16[128,896]{1,0:T(8,128)(2,1)S(1)} %get-tuple-element.18), channel_id=1, source_target_pairs={{0,3},{1,2},{2,1},{3,0},{4,7},{5,6},{6,5},{7,4},{8,11},{9,10},{10,... | collective-permute-start | bytes 688136 | tf_op jit(solution)/shard_map/ppermute | solution.py:263
  33.5 7.1 %collective-permute-start.4 = (bf16[2,56,1024]{2,1,0:T(8,128)(2,1)S(1)}, bf16[2,56,1024]{2,1,0:T(8,128)(2,1)S(1)}, u32[]{:S(2)}, u32[]{:S(2)}) collective-permute-start(bf16[2,56,1024]{2,1,0:T(8,128)(2,1)S(1)} %get-tuple-element.26), channel_id=1, source_target_pairs={{0,64},{64,0},{1,65},{65,1},{2,66},{66,2},{3,67},{67,3},{4,68},{68... | collective-permute-start | bytes 688136 | tf_op jit(solution)/shard_map/ppermute | solution.py:251
  40.6 4.6 %collective-permute-done.1.refs_4_.refs_3_ = bf16[128,896]{1,0:T(8,128)(2,1)S(1)} collective-permute-done((bf16[128,896]{1,0:T(8,128)(2,1)S(1)}, bf16[128,896]{1,0:T(8,128)(2,1)S(1)}, u32[]{:S(2)}, u32[]{:S(2)}) %collective-permute-start.1) | collective-permute-done | bytes 229408 | tf_op jit(solution)/shard_map/ppermute | solution.py:263
  48.4 21.7 %collective-permute-done.4.refs_5_ = bf16[2,56,1024]{2,1,0:T(8,128)(2,1)S(1)} collective-permute-done((bf16[2,56,1024]{2,1,0:T(8,128)(2,1)S(1)}, bf16[2,56,1024]{2,1,0:T(8,128)(2,1)S(1)}, u32[]{:S(2)}, u32[]{:S(2)}) %collective-permute-start.4) | collective-permute-done | bytes 229408 | tf_op jit(solution)/shard_map/ppermute | solution.py:251
  73.9 2.4 %shard_map.121 = (bf16[8,320,128]{2,1,0:T(8,128)(2,1)S(1)}, bf16[256,128]{1,0:T(8,128)(2,1)S(1)}) custom-call(bf16[64,4,3584]{2,1,0:T(4,128)(2,1)S(1)} %all-to-all-done.refs_0_, bf16[3584,128]{1,0:T(8,128)(2,1)S(1)} %bitcast.13, bf16[3584,128]{1,0:T(8,128)(2,1)S(1)} %bitcast.14, bf16[1,3584]{1,0:T(2,128)(2,1)S(1)} %copy-done.13, ...), custom_call_target="tpu_custom_call" | custom-call | bytes 3808256 | tf_op jit(solution)/shard_map/pallas_call | solution.py:59
  77.1 6.8 %all-to-all-start.1 = ((bf16[8,320,128]{2,1,0:T(8,128)(2,1)}), bf16[8,320,128]{2,1,0:T(8,128)(2,1)S(1)}, u32[]{:S(2)}, u32[]{:S(2)}) async-start(bf16[8,320,128]{2,1,0:T(8,128)(2,1)} %copy-done.6), calls=%async_computation.1 | async-start | bytes 1310720 | tf_op jit(solution)/shard_map/all_to_all | solution.py:340
  85.1 3.0 %collective-permute-start.8 = (bf16[2,2,56,1024]{3,2,1,0:T(8,128)(2,1)S(1)}, bf16[2,2,56,1024]{3,2,1,0:T(8,128)(2,1)S(1)}, u32[]{:S(2)}, u32[]{:S(2)}) collective-permute-start(bf16[2,2,56,1024]{3,2,1,0:T(8,128)(2,1)S(1)} %pad_maximum_fusion.refs_4_), channel_id=1, source_target_pairs={{0,128},{128,256},{256,384},{384,0},{1,129},{129,257},{257,385},{3... | collective-permute-start | bytes 1376264 | tf_op jit(solution)/shard_map/ppermute | solution.py:251
  88.1 4.5 %collective-permute-start.9 = (bf16[2,2,56,1024]{3,2,1,0:T(8,128)(2,1)S(1)}, bf16[2,2,56,1024]{3,2,1,0:T(8,128)(2,1)S(1)}, u32[]{:S(2)}, u32[]{:S(2)}) collective-permute-start(bf16[2,2,56,1024]{3,2,1,0:T(8,128)(2,1)S(1)} %pad_maximum_fusion.refs_4_), channel_id=1, source_target_pairs={{0,256},{128,384},{256,0},{384,128},{1,257},{129,385},{257,1},{385... | collective-permute-start | bytes 1376264 | tf_op jit(solution)/shard_map/ppermute | solution.py:251
  92.6 3.0 %collective-permute-start.10 = (bf16[2,2,56,1024]{3,2,1,0:T(8,128)(2,1)S(1)}, bf16[2,2,56,1024]{3,2,1,0:T(8,128)(2,1)}, u32[]{:S(2)}, u32[]{:S(2)}) collective-permute-start(bf16[2,2,56,1024]{3,2,1,0:T(8,128)(2,1)S(1)} %pad_maximum_fusion.refs_4_), channel_id=1, source_target_pairs={{0,384},{128,0},{256,128},{384,256},{1,385},{129,1},{257,129},{385... | collective-permute-start | bytes 1376264 | tf_op jit(solution)/shard_map/ppermute | solution.py:251
  95.6 5.8 %all-to-all-done.1.refs_0_ = bf16[8,320,128]{2,1,0:T(8,128)(2,1)S(1)} async-done(((bf16[8,320,128]{2,1,0:T(8,128)(2,1)}), bf16[8,320,128]{2,1,0:T(8,128)(2,1)S(1)}, u32[]{:S(2)}, u32[]{:S(2)}) %all-to-all-start.1) | async-done | bytes 655392 | tf_op jit(solution)/shard_map/all_to_all | solution.py:340
  104.2 12.1 %all-to-all-start.3 = ((bf16[64,4,1024]{2,1,0:T(4,128)(2,1)}), bf16[64,4,1024]{2,1,0:T(4,128)(2,1)S(1)}, u32[]{:S(2)}, u32[]{:S(2)}) async-start(bf16[64,4,1024]{2,1,0:T(4,128)(2,1)} %shard_map.125), calls=%async_computation.3 | async-start | bytes 1048576 | tf_op jit(solution)/shard_map/all_to_all | solution.py:373
  119.1 3.3 %collective-permute-start.5 = (bf16[16,1024]{1,0:T(8,128)(2,1)S(1)}, bf16[16,1024]{1,0:T(8,128)(2,1)S(1)}, u32[]{:S(2)}, u32[]{:S(2)}) collective-permute-start(bf16[16,1024]{1,0:T(8,128)(2,1)S(1)} %shard_map.122.refs_0_), channel_id=1, source_target_pairs={{0,16},{16,0},{32,48},{48,32},{1,17},{17,1},{33,49},{49,33},{2,18}... | collective-permute-start | bytes 98312 | tf_op jit(solution)/shard_map/ppermute | solution.py:263
  122.4 4.0 %collective-permute-start.6 = (bf16[16,1024]{1,0:T(8,128)(2,1)S(1)}, bf16[16,1024]{1,0:T(8,128)(2,1)S(1)}, u32[]{:S(2)}, u32[]{:S(2)}) collective-permute-start(bf16[16,1024]{1,0:T(8,128)(2,1)S(1)} %shard_map.122.refs_0_), channel_id=1, source_target_pairs={{0,32},{16,48},{32,0},{48,16},{1,33},{17,49},{33,1},{49,17},{2,34}... | collective-permute-start | bytes 98312 | tf_op jit(solution)/shard_map/ppermute | solution.py:263
  126.4 2.0 %collective-permute-start.7 = (bf16[16,1024]{1,0:T(8,128)(2,1)S(1)}, bf16[16,1024]{1,0:T(8,128)(2,1)S(1)}, u32[]{:S(2)}, u32[]{:S(2)}) collective-permute-start(bf16[16,1024]{1,0:T(8,128)(2,1)S(1)} %shard_map.122.refs_0_), channel_id=1, source_target_pairs={{0,48},{16,32},{32,16},{48,0},{1,49},{17,33},{33,17},{49,1},{2,50}... | collective-permute-start | bytes 98312 | tf_op jit(solution)/shard_map/ppermute | solution.py:263
  128.4 2.3 %collective-permute-done.5.refs_1_ = bf16[16,1024]{1,0:T(8,128)(2,1)S(1)} collective-permute-done((bf16[16,1024]{1,0:T(8,128)(2,1)S(1)}, bf16[16,1024]{1,0:T(8,128)(2,1)S(1)}, u32[]{:S(2)}, u32[]{:S(2)}) %collective-permute-start.5) | collective-permute-done | bytes 32800 | tf_op jit(solution)/shard_map/ppermute | solution.py:263
  130.7 2.9 %collective-permute-done.7.refs_3_ = bf16[16,1024]{1,0:T(8,128)(2,1)S(1)} collective-permute-done((bf16[16,1024]{1,0:T(8,128)(2,1)S(1)}, bf16[16,1024]{1,0:T(8,128)(2,1)S(1)}, u32[]{:S(2)}, u32[]{:S(2)}) %collective-permute-start.7) | collective-permute-done | bytes 32800 | tf_op jit(solution)/shard_map/ppermute | solution.py:263
  133.6 2.4 %shard_map.124 = bf16[32,16,128]{2,1,0:T(8,128)(2,1)} custom-call(bf16[16,1024]{1,0:T(8,128)(2,1)S(1)} %shard_map.122.refs_0_, bf16[16,1024]{1,0:T(8,128)(2,1)S(1)} %collective-permute-done.5.refs_1_, bf16[16,1024]{1,0:T(8,128)(2,1)S(1)} %collective-permute-done.6.refs_2_, bf16[16,1024]{1,0:T(8,128)(2,1)S(1)} %collective-permute-done.7.refs_3_, ...), custom_call_target="tpu_custom_call" | custom-call | bytes 1966080 | tf_op jit(solution)/shard_map/pallas_call | solution.py:59
  136.0 3.8 %all-to-all-start.2 = ((bf16[32,16,128]{2,1,0:T(8,128)(2,1)}), bf16[32,16,128]{2,1,0:T(8,128)(2,1)S(1)}, u32[]{:S(2)}, u32[]{:S(2)}) async-start(bf16[32,16,128]{2,1,0:T(8,128)(2,1)} %shard_map.124), calls=%async_computation.2 | async-start | bytes 262144 | tf_op jit(solution)/shard_map/all_to_all | solution.py:363
  141.4 7.0 %collective-permute-start.11 = (f32[16,448]{1,0:T(8,128)S(1)}, f32[16,448]{1,0:T(8,128)S(1)}, u32[]{:S(2)}, u32[]{:S(2)}) collective-permute-start(f32[16,448]{1,0:T(8,128)S(1)} %get-tuple-element.24), channel_id=1, source_target_pairs={{0,4},{1,5},{2,6},{3,7},{4,0},{5,1},{6,2},{7,3},{8,12},{9,13},{10,... | collective-permute-start | bytes 86024 | tf_op jit(solution)/shard_map/ppermute | solution.py:263
  (53 shorter events, 21.8 us)
Async XLA Ops:
  3.1 17.5 %copy-start = (bf16[1,128,3584]{2,1,0:T(8,128)(2,1)S(1)}, bf16[1,128,3584]{2,1,0:T(8,128)(2,1)}, u32[]{:S(2)}) copy-start(bf16[1,128,3584]{2,1,0:T(8,128)(2,1)} %param.21) | copy-start | bytes 2752516
  3.1 42.1 %copy-start.14 = (s32[2]{0:T(128)S(1)}, s32[2]{0:T(128)}, u32[]{:S(2)}) copy-start(s32[2]{0:T(128)} %refs_0_.3) | copy-start | bytes 28
  3.1 67.7 %all-to-all-start = ((bf16[64,4,3584]{2,1,0:T(4,128)(2,1)}), bf16[64,4,3584]{2,1,0:T(4,128)(2,1)S(1)}, u32[]{:S(2)}, u32[]{:S(2)}) async-start(bf16[64,4,3584]{2,1,0:T(4,128)(2,1)} %get-tuple-element.15), calls=%async_computation | async-start | bytes 3670016 | tf_op jit(solution)/shard_map/all_to_all | solution.py:304
  18.1 27.1 %copy-start.5 = (bf16[2,384,576]{1,2,0:T(8,128)(2,1)S(1)}, bf16[2,384,576]{1,2,0:T(8,128)(2,1)}, u32[]{:S(2)}) copy-start(bf16[2,384,576]{1,2,0:T(8,128)(2,1)} %param.15) | copy-start | bytes 2654212
  18.1 52.7 %copy-start.13 = (bf16[1,3584]{1,0:T(2,128)(2,1)S(1)}, bf16[1,3584]{1,0:T(2,128)(2,1)}, u32[]{:S(2)}) copy-start(bf16[1,3584]{1,0:T(2,128)(2,1)} %refs_3_.1) | copy-start | bytes 21508
  18.2 13.7 %collective-permute-start.3 = (bf16[56,1024]{1,0:T(8,128)(2,1)}, bf16[56,1024]{1,0:T(8,128)(2,1)S(1)}, u32[]{:S(2)}, u32[]{:S(2)}) collective-permute-start(bf16[56,1024]{1,0:T(8,128)(2,1)} %bitcast.5), channel_id=1, source_target_pairs={{0,8},{8,0},{1,9},{9,1},{2,10},{10,2},{3,11},{11,3},{4,12},{12,4},... | collective-permute-start | bytes 344072 | tf_op jit(solution)/shard_map/ppermute | solution.py:251
  22.4 48.5 %copy-start.1 = (bf16[1,3584,128]{2,1,0:T(8,128)(2,1)S(1)}, bf16[1,3584,128]{2,1,0:T(8,128)(2,1)}, u32[]{:S(2)}) copy-start(bf16[1,3584,128]{2,1,0:T(8,128)(2,1)} %param.19) | copy-start | bytes 2752516
  22.4 18.2 %collective-permute-start = (bf16[128,896]{1,0:T(8,128)(2,1)S(1)}, bf16[128,896]{1,0:T(8,128)(2,1)S(1)}, u32[]{:S(2)}, u32[]{:S(2)}) collective-permute-start(bf16[128,896]{1,0:T(8,128)(2,1)S(1)} %get-tuple-element.16), channel_id=1, source_target_pairs={{0,1},{1,0},{2,3},{3,2},{4,5},{5,4},{6,7},{7,6},{8,9},{9,8},{10,11... | collective-permute-start | bytes 688136 | tf_op jit(solution)/shard_map/ppermute | solution.py:263
  25.7 19.5 %collective-permute-start.1 = (bf16[128,896]{1,0:T(8,128)(2,1)S(1)}, bf16[128,896]{1,0:T(8,128)(2,1)S(1)}, u32[]{:S(2)}, u32[]{:S(2)}) collective-permute-start(bf16[128,896]{1,0:T(8,128)(2,1)S(1)} %get-tuple-element.17), channel_id=1, source_target_pairs={{0,2},{1,3},{2,0},{3,1},{4,6},{5,7},{6,4},{7,5},{8,10},{9,11},{10,... | collective-permute-start | bytes 688136 | tf_op jit(solution)/shard_map/ppermute | solution.py:263
  29.9 15.3 %collective-permute-start.2 = (bf16[128,896]{1,0:T(8,128)(2,1)S(1)}, bf16[128,896]{1,0:T(8,128)(2,1)S(1)}, u32[]{:S(2)}, u32[]{:S(2)}) collective-permute-start(bf16[128,896]{1,0:T(8,128)(2,1)S(1)} %get-tuple-element.18), channel_id=1, source_target_pairs={{0,3},{1,2},{2,1},{3,0},{4,7},{5,6},{6,5},{7,4},{8,11},{9,10},{10,... | collective-permute-start | bytes 688136 | tf_op jit(solution)/shard_map/ppermute | solution.py:263
  33.5 36.6 %collective-permute-start.4 = (bf16[2,56,1024]{2,1,0:T(8,128)(2,1)S(1)}, bf16[2,56,1024]{2,1,0:T(8,128)(2,1)S(1)}, u32[]{:S(2)}, u32[]{:S(2)}) collective-permute-start(bf16[2,56,1024]{2,1,0:T(8,128)(2,1)S(1)} %get-tuple-element.26), channel_id=1, source_target_pairs={{0,64},{64,0},{1,65},{65,1},{2,66},{66,2},{3,67},{67,3},{4,68},{68... | collective-permute-start | bytes 688136 | tf_op jit(solution)/shard_map/ppermute | solution.py:251
  70.8 1.2 copy-start.2
  77.1 24.3 %all-to-all-start.1 = ((bf16[8,320,128]{2,1,0:T(8,128)(2,1)}), bf16[8,320,128]{2,1,0:T(8,128)(2,1)S(1)}, u32[]{:S(2)}, u32[]{:S(2)}) async-start(bf16[8,320,128]{2,1,0:T(8,128)(2,1)} %copy-done.6), calls=%async_computation.1 | async-start | bytes 1310720 | tf_op jit(solution)/shard_map/all_to_all | solution.py:340
  85.1 41.3 %collective-permute-start.8 = (bf16[2,2,56,1024]{3,2,1,0:T(8,128)(2,1)S(1)}, bf16[2,2,56,1024]{3,2,1,0:T(8,128)(2,1)S(1)}, u32[]{:S(2)}, u32[]{:S(2)}) collective-permute-start(bf16[2,2,56,1024]{3,2,1,0:T(8,128)(2,1)S(1)} %pad_maximum_fusion.refs_4_), channel_id=1, source_target_pairs={{0,128},{128,256},{256,384},{384,0},{1,129},{129,257},{257,385},{3... | collective-permute-start | bytes 1376264 | tf_op jit(solution)/shard_map/ppermute | solution.py:251
  88.1 40.3 %collective-permute-start.9 = (bf16[2,2,56,1024]{3,2,1,0:T(8,128)(2,1)S(1)}, bf16[2,2,56,1024]{3,2,1,0:T(8,128)(2,1)S(1)}, u32[]{:S(2)}, u32[]{:S(2)}) collective-permute-start(bf16[2,2,56,1024]{3,2,1,0:T(8,128)(2,1)S(1)} %pad_maximum_fusion.refs_4_), channel_id=1, source_target_pairs={{0,256},{128,384},{256,0},{384,128},{1,257},{129,385},{257,1},{385... | collective-permute-start | bytes 1376264 | tf_op jit(solution)/shard_map/ppermute | solution.py:251
  92.6 35.8 %collective-permute-start.10 = (bf16[2,2,56,1024]{3,2,1,0:T(8,128)(2,1)S(1)}, bf16[2,2,56,1024]{3,2,1,0:T(8,128)(2,1)}, u32[]{:S(2)}, u32[]{:S(2)}) collective-permute-start(bf16[2,2,56,1024]{3,2,1,0:T(8,128)(2,1)S(1)} %pad_maximum_fusion.refs_4_), channel_id=1, source_target_pairs={{0,384},{128,0},{256,128},{384,256},{1,385},{129,1},{257,129},{385... | collective-permute-start | bytes 1376264 | tf_op jit(solution)/shard_map/ppermute | solution.py:251
  104.2 31.8 %all-to-all-start.3 = ((bf16[64,4,1024]{2,1,0:T(4,128)(2,1)}), bf16[64,4,1024]{2,1,0:T(4,128)(2,1)S(1)}, u32[]{:S(2)}, u32[]{:S(2)}) async-start(bf16[64,4,1024]{2,1,0:T(4,128)(2,1)} %shard_map.125), calls=%async_computation.3 | async-start | bytes 1048576 | tf_op jit(solution)/shard_map/all_to_all | solution.py:373
  116.3 1.2 copy-start.15
  119.1 11.6 %collective-permute-start.5 = (bf16[16,1024]{1,0:T(8,128)(2,1)S(1)}, bf16[16,1024]{1,0:T(8,128)(2,1)S(1)}, u32[]{:S(2)}, u32[]{:S(2)}) collective-permute-start(bf16[16,1024]{1,0:T(8,128)(2,1)S(1)} %shard_map.122.refs_0_), channel_id=1, source_target_pairs={{0,16},{16,0},{32,48},{48,32},{1,17},{17,1},{33,49},{49,33},{2,18}... | collective-permute-start | bytes 98312 | tf_op jit(solution)/shard_map/ppermute | solution.py:263
  122.4 8.3 %collective-permute-start.6 = (bf16[16,1024]{1,0:T(8,128)(2,1)S(1)}, bf16[16,1024]{1,0:T(8,128)(2,1)S(1)}, u32[]{:S(2)}, u32[]{:S(2)}) collective-permute-start(bf16[16,1024]{1,0:T(8,128)(2,1)S(1)} %shard_map.122.refs_0_), channel_id=1, source_target_pairs={{0,32},{16,48},{32,0},{48,16},{1,33},{17,49},{33,1},{49,17},{2,34}... | collective-permute-start | bytes 98312 | tf_op jit(solution)/shard_map/ppermute | solution.py:263
  126.4 7.2 %collective-permute-start.7 = (bf16[16,1024]{1,0:T(8,128)(2,1)S(1)}, bf16[16,1024]{1,0:T(8,128)(2,1)S(1)}, u32[]{:S(2)}, u32[]{:S(2)}) collective-permute-start(bf16[16,1024]{1,0:T(8,128)(2,1)S(1)} %shard_map.122.refs_0_), channel_id=1, source_target_pairs={{0,48},{16,32},{32,16},{48,0},{1,49},{17,33},{33,17},{49,1},{2,50}... | collective-permute-start | bytes 98312 | tf_op jit(solution)/shard_map/ppermute | solution.py:263
  128.4 12.3 %copy-start.12 = (f32[256,16]{1,0:T(8,128)S(1)}, f32[256,16]{1,0:T(8,128)}, u32[]{:S(2)}) copy-start(f32[256,16]{1,0:T(8,128)} %get-tuple-element.22.refs_1_) | copy-start | bytes 49156
  136.0 13.2 %all-to-all-start.2 = ((bf16[32,16,128]{2,1,0:T(8,128)(2,1)}), bf16[32,16,128]{2,1,0:T(8,128)(2,1)S(1)}, u32[]{:S(2)}, u32[]{:S(2)}) async-start(bf16[32,16,128]{2,1,0:T(8,128)(2,1)} %shard_map.124), calls=%async_computation.2 | async-start | bytes 262144 | tf_op jit(solution)/shard_map/all_to_all | solution.py:363
  141.4 8.9 %collective-permute-start.11 = (f32[16,448]{1,0:T(8,128)S(1)}, f32[16,448]{1,0:T(8,128)S(1)}, u32[]{:S(2)}, u32[]{:S(2)}) collective-permute-start(f32[16,448]{1,0:T(8,128)S(1)} %get-tuple-element.24), channel_id=1, source_target_pairs={{0,4},{1,5},{2,6},{3,7},{4,0},{5,1},{6,2},{7,3},{8,12},{9,13},{10,... | collective-permute-start | bytes 86024 | tf_op jit(solution)/shard_map/ppermute | solution.py:263
  (8 other events, 6.6 us)

commit v8 on v7

--- a/solution.py
+++ b/solution.py
@@ -12,6 +12,7 @@
 EP = ("x", "zh", "zl", "c")
 PADDED = 1024
 GROUP = 4
+HELD = (0, 3, 5)
 NT = (((1,), (1,)), ((), ()))
 TN = (((0,), (0,)), ((), ()))
 F32 = jnp.float32
@@ -80,7 +81,17 @@
     values = hidden_ref[...].astype(F32)
     factor = lax.rsqrt(jnp.mean(values * values, axis=-1, keepdims=True) + EPSILON)
     gain = gain_ref[...].astype(F32).reshape(1, values.shape[1])
-    normalized = (values * factor * gain).astype(BF16)
+    normalized = values * factor * gain
+    width = values.shape[1] // 8
+    pad = jnp.zeros((values.shape[0], send_ref.shape[2] - 3 * width), F32)
+    sent = jnp.zeros((values.shape[0], send_ref.shape[2]), F32)
+    for s in range(8):
+        taken = [
+            normalized[:, (s + k) % 8 * width : ((s + k) % 8 + 1) * width] for k in HELD
+        ]
+        taken = jnp.concatenate([*taken, pad], axis=1)
+        sent = jnp.where(lax.axis_index("y") == s, taken, sent)
+    normalized = sent.astype(BF16)
     slots, rows = place_ref.shape
     slot = lax.broadcasted_iota(jnp.int32, (slots, rows), 0)
     named = jnp.zeros((slots, rows), jnp.bool_)
@@ -180,13 +191,65 @@
                 out_ref[(lax.axis_index("zl") ^ b) * slices + tp] = part[b]
 
 
-def lift_experts(rows_ref, w_gate_ref, w_up_ref, router_ref, context_ref, inner_ref, score_ref):
-    slots, width = score_ref.shape[0], rows_ref.shape[2]
-    rows = rows_ref[...].astype(F32).reshape(slots, width).astype(BF16)
-    gate = jnp.dot(rows, w_gate_ref[...], preferred_element_type=F32)
-    lifted = jnp.dot(rows, w_up_ref[...], preferred_element_type=F32)
-    column = jnp.broadcast_to(router_ref[...], (128, width))
-    logits = lax.dot_general(rows, column, NT, preferred_element_type=F32)
+def relay(rows_ref, held_ref, up_ref, down_ref):
+    slots, width = held_ref.shape
+    rows = rows_ref[...].astype(F32).reshape(slots, width)
+    held_ref[...] = rows.astype(BF16)
+    w = 448
+    pad = jnp.zeros((slots, 64), F32)
+    up_ref[...] = jnp.concatenate(
+        [rows[:, : 2 * w], rows[:, 2 * w + 256 : 3 * w], pad], axis=1
+    ).astype(BF16)
+    down_ref[...] = jnp.concatenate(
+        [rows[:, :w], rows[:, 2 * w : 3 * w], rows[:, w : w + 256]], axis=1
+    ).astype(BF16)
+
+
+def lift_experts(
+    held_ref,
+    before_ref,
+    after_ref,
+    w_gate_ref,
+    w_up_ref,
+    router_ref,
+    context_ref,
+    inner_ref,
+    score_ref,
+):
+    slots = score_ref.shape[0]
+    w = router_ref.shape[1]
+    units = w_gate_ref.shape[1]
+    tp = lax.axis_index("y")
+
+    def weights(pieces):
+        both, scores = [], []
+        total = 0
+        for k, first, size in pieces:
+            s = (tp + k) % 8
+            rows = pl.ds(pl.multiple_of(s * w + first, 64), size)
+            both.append(jnp.concatenate([w_gate_ref[rows, :], w_up_ref[rows, :]], axis=1))
+            scores.append(router_ref[pl.ds(s, 1), :][:, first : first + size])
+            total += size
+        pad = -total % 128
+        if pad:
+            both.append(jnp.zeros((pad, 2 * units), BF16))
+            scores.append(jnp.zeros((1, pad), F32))
+        scores = jnp.concatenate(scores, axis=1)
+        return jnp.concatenate(both, axis=0), scores.astype(BF16)
+
+    lifted = jnp.zeros((slots, 2 * units), F32)
+    logits = jnp.zeros((slots, 128), F32)
+    for ref, pieces in (
+        (held_ref, [(k, 0, w) for k in HELD]),
+        (before_ref, [(7, 0, w), (2, 0, w), (4, 256, w - 256)]),
+        (after_ref, [(1, 0, w), (6, 0, w), (4, 0, 256)]),
+    ):
+        both, scores = weights(pieces)
+        rows = ref[...]
+        lifted += jnp.dot(rows, both, preferred_element_type=F32)
+        column = jnp.broadcast_to(scores, (128, scores.shape[1]))
+        logits += lax.dot_general(rows, column, NT, preferred_element_type=F32)
+    gate, lifted = lifted[:, :units], lifted[:, units:]
     inner = (gate / (1.0 + jnp.exp(-gate)) * lifted).astype(BF16)
     copies, share, latent = context_ref.shape
     lanes = inner_ref.shape[2]
@@ -291,9 +354,11 @@
     out_cols, depth = w_out.shape[1], w_out.shape[0]
     tp = lax.axis_index("y")
 
+    router_rows = router.reshape(tp_size, width).astype(F32)
+
     send, place = kernel_call(
         prepare,
-        [((ep_size, SLOTS, model_width), BF16), ((slots, rows), F32)],
+        [((ep_size, SLOTS, 3 * width + 64), BF16), ((slots, rows), F32)],
         hidden,
         norm_gain,
         expert_ids.T,
@@ -320,22 +385,37 @@
         jnp.swapaxes(latent_cache, 1, 2),
         smem=(0,),
         load=(0, 1, 2),
-        after=down[1:],
     )
 
     out_pair = pair_up(w_out.T, "c")
     out_other = shift(out_pair, "zh", 1)
+    (crossed,) = kernel_call(mark, [((8, 128), F32)], after=(out_other,))
+    (moved,) = kernel_call(mark, [((8, 128), F32)], after=down[1:], flops=20_000_000_000)
+
+    held, up, below = kernel_call(
+        relay,
+        [
+            ((slots, 3 * width + 64), BF16),
+            ((slots, 2 * width + 256), BF16),
+            ((slots, 2 * width + 256), BF16),
+        ],
+        named_rows,
+        after=(context,),
+    )
+
     inner, score = kernel_call(
         lift_experts,
         [((tp_size, slots + 8 * heads, hidden_units), BF16), ((slots, 128), BF16)],
-        named_rows,
+        held,
+        shift(up, "y", 1),
+        shift(below, "y", -1),
         w_gate[0],
         w_up[0],
-        router,
+        router_rows,
         context,
-        load=(1, 2, 3),
+        load=(3, 4),
         store=(0, 1),
-        after=(out_other,),
+        after=(moved, crossed),
     )
     inner = lax.all_to_all(inner, "y", 0, 0, tiled=True)
 

time: 153 us -> 141 us (0.922)
  waiting for transfers between devices: 39.3 us -> 24.9 us
  starting transfers between devices: 83.5 us -> 90.9 us
  local copies, waits for them, and re-layouts: 9.82 us -> 6.35 us
  other arithmetic: 2.7 us -> 1.02 us
    ppermute x5 -> x7, waiting for transfers between devices: 21.7 us -> 10.5 us  [shift(): return lax.ppermute(value, axis, [(i, (i + k) % size) for i in range(size)])]
    ppermute x5 -> x7, starting transfers between devices: 20.1 us -> 27.2 us  [shift(): return lax.ppermute(value, axis, [(i, (i + k) % size) for i in range(size)])]
    ppermute x7, waiting for transfers between devices: 10.8 us -> 6.16 us  [swap(): lax.ppermute(value, axis, [(i, i ^ k) for i in range(lax.axis_size(axis))])]
    unnamed x32 -> x28, local copies, waits for them, and re-layouts: 9.01 us -> 5.47 us
    another operation x2, other arithmetic: 2.7 us -> 0.97 us  [on_device(): out_weights = gather(jnp.stack([out_pair, out_other]), 'x')]
    pallas_call x10 -> x13, Pallas kernels: 15.3 us -> 15 us  [kernel_call(): pl.pallas_call(kernel, out_shape=tuple(shapes), in_specs=[place(n, load)...]
  transfers between devices with their start and end apart: 16 -> 18, of which waited for: 7 -> 7; matrix products, arithmetic and copies ran while one was open for 2% -> 1% of each run, Pallas kernels for 6% -> 7%
where the time goes in v8:
time: 141 us; the launch traced here: 138 us
  starting transfers between devices  90.9 us (64%)
  waiting for transfers between devices  24.9 us (18%)
  Pallas kernels  15 us (11%)
  local copies, waits for them, and re-layouts  6.35 us (5%)
    ppermute x7, starting transfers between devices, shift(): return lax.ppermute(value, axis, [(i, (i + k) % size) for i in range(size)])  27.2 us
    ppermute x7, starting transfers between devices, swap(): lax.ppermute(value, axis, [(i, i ^ k) for i in range(lax.axis_size(axis))])  25.6 us
    pallas_call x13, Pallas kernels, kernel_call(): pl.pallas_call(kernel, out_shape=tuple(shapes), in_specs=[place(n, load)...  15 us
    all_to_all x1, starting transfers between devices, on_device(): named_rows = lax.all_to_all(send, EP, 0, 0, tiled=True)  15 us
    all_to_all x1, starting transfers between devices, on_device(): back = lax.all_to_all(back, EP, 0, 0, tiled=True)  12.1 us
    ppermute x7, waiting for transfers between devices, shift(): return lax.ppermute(value, axis, [(i, (i + k) % size) for i in range(size)])  10.5 us
    all_to_all x1, waiting for transfers between devices, on_device(): inner = lax.all_to_all(inner, 'y', 0, 0, tiled=True)  7.29 us
    all_to_all x1, starting transfers between devices, on_device(): inner = lax.all_to_all(inner, 'y', 0, 0, tiled=True)  7.05 us
  transfers between devices with their start and end apart: 18, of which 7 were waited for; matrix products, arithmetic and copies ran while one was open for 1% of the time, Pallas kernels for 7%

profile of v8, /device:TPU:1, one launch (start us, length us, event | category | flops | bytes accessed | tf_op | source)
XLA Modules:
  0.0 138.5 jit_solution(15375419951666038638)
XLA Ops:
  0.0 2.5 %shard_map.118 = (bf16[64,4,1408]{2,1,0:T(4,128)(2,1)}, f32[256,16]{1,0:T(8,128)}) custom-call(bf16[16,3584]{1,0:T(8,128)(2,1)} %refs_0_.2, bf16[3584]{0:T(1024)(128)(2,1)} %refs_1_.3, s32[8,16]{1,0:T(8,128)} %bitcast.19), custom_call_target="tpu_custom_call" | custom-call | bytes 122368 | tf_op jit(solution)/shard_map/pallas_call | solution.py:60
  2.6 15.0 %all-to-all-start = ((bf16[64,4,1408]{2,1,0:T(4,128)(2,1)}), bf16[64,4,1408]{2,1,0:T(4,128)(2,1)S(1)}, u32[]{:S(2)}, u32[]{:S(2)}) async-start(bf16[64,4,1408]{2,1,0:T(4,128)(2,1)} %get-tuple-element.18), calls=%async_computation | async-start | bytes 1441792 | tf_op jit(solution)/shard_map/all_to_all | solution.py:369
  17.6 2.4 %collective-permute-start.5 = (bf16[56,1024]{1,0:T(8,128)(2,1)S(1)}, bf16[56,1024]{1,0:T(8,128)(2,1)}, u32[]{:S(2)}, u32[]{:S(2)}) collective-permute-start(bf16[56,1024]{1,0:T(8,128)(2,1)S(1)} %bitcast.17), channel_id=1, source_target_pairs={{0,8},{8,0},{1,9},{9,1},{2,10},{10,2},{3,11},{11,3},{4,12},{12,4},... | collective-permute-start | bytes 344072 | tf_op jit(solution)/shard_map/ppermute | solution.py:314
  21.9 3.2 %collective-permute-start.2 = (bf16[128,896]{1,0:T(8,128)(2,1)}, bf16[128,896]{1,0:T(8,128)(2,1)S(1)}, u32[]{:S(2)}, u32[]{:S(2)}) collective-permute-start(bf16[128,896]{1,0:T(8,128)(2,1)} %get-tuple-element.22), channel_id=1, source_target_pairs={{0,1},{1,0},{2,3},{3,2},{4,5},{5,4},{6,7},{7,6},{8,9},{9,8},{10,11... | collective-permute-start | bytes 688136 | tf_op jit(solution)/shard_map/ppermute | solution.py:326
  25.1 4.2 %collective-permute-start.3 = (bf16[128,896]{1,0:T(8,128)(2,1)}, bf16[128,896]{1,0:T(8,128)(2,1)S(1)}, u32[]{:S(2)}, u32[]{:S(2)}) collective-permute-start(bf16[128,896]{1,0:T(8,128)(2,1)} %get-tuple-element.23), channel_id=1, source_target_pairs={{0,2},{1,3},{2,0},{3,1},{4,6},{5,7},{6,4},{7,5},{8,10},{9,11},{10,... | collective-permute-start | bytes 688136 | tf_op jit(solution)/shard_map/ppermute | solution.py:326
  29.3 1.9 %collective-permute-start.4 = (bf16[128,896]{1,0:T(8,128)(2,1)}, bf16[128,896]{1,0:T(8,128)(2,1)S(1)}, u32[]{:S(2)}, u32[]{:S(2)}) collective-permute-start(bf16[128,896]{1,0:T(8,128)(2,1)} %get-tuple-element.24), channel_id=1, source_target_pairs={{0,3},{1,2},{2,1},{3,0},{4,7},{5,6},{6,5},{7,4},{8,11},{9,10},{10,... | collective-permute-start | bytes 688136 | tf_op jit(solution)/shard_map/ppermute | solution.py:326
  35.4 7.1 %collective-permute-start.6 = (bf16[2,56,1024]{2,1,0:T(8,128)(2,1)S(1)}, bf16[2,56,1024]{2,1,0:T(8,128)(2,1)S(1)}, u32[]{:S(2)}, u32[]{:S(2)}) collective-permute-start(bf16[2,56,1024]{2,1,0:T(8,128)(2,1)S(1)} %get-tuple-element.32), channel_id=1, source_target_pairs={{0,64},{64,0},{1,65},{65,1},{2,66},{66,2},{3,67},{67,3},{4,68},{68... | collective-permute-start | bytes 688136 | tf_op jit(solution)/shard_map/ppermute | solution.py:314
  42.8 2.2 %collective-permute-start = (bf16[256,1152]{1,0:T(8,128)(2,1)S(1)}, bf16[256,1152]{1,0:T(8,128)(2,1)S(1)}, u32[]{:S(2)}, u32[]{:S(2)}) collective-permute-start(bf16[256,1152]{1,0:T(8,128)(2,1)S(1)} %get-tuple-element.20), channel_id=1, source_target_pairs={{0,1},{1,2},{2,3},{3,4},{4,5},{5,6},{6,7},{7,0},{8,9},{9,10},{10,1... | collective-permute-start | bytes 1769480 | tf_op jit(solution)/shard_map/ppermute | solution.py:314
  45.1 4.8 %collective-permute-start.1 = (bf16[256,1152]{1,0:T(8,128)(2,1)S(1)}, bf16[256,1152]{1,0:T(8,128)(2,1)S(1)}, u32[]{:S(2)}, u32[]{:S(2)}) collective-permute-start(bf16[256,1152]{1,0:T(8,128)(2,1)S(1)} %get-tuple-element.21), channel_id=1, source_target_pairs={{0,7},{1,0},{2,1},{3,2},{4,3},{5,4},{6,5},{7,6},{8,15},{9,8},{10,9... | collective-permute-start | bytes 1769480 | tf_op jit(solution)/shard_map/ppermute | solution.py:314
  50.8 9.4 %collective-permute-done.refs_1_ = bf16[256,1152]{1,0:T(8,128)(2,1)S(1)} collective-permute-done((bf16[256,1152]{1,0:T(8,128)(2,1)S(1)}, bf16[256,1152]{1,0:T(8,128)(2,1)S(1)}, u32[]{:S(2)}, u32[]{:S(2)}) %collective-permute-start) | collective-permute-done | bytes 589856 | tf_op jit(solution)/shard_map/ppermute | solution.py:314
  61.3 2.6 %shard_map.124 = (bf16[8,320,128]{2,1,0:T(8,128)(2,1)}, bf16[256,128]{1,0:T(8,128)(2,1)S(1)}) custom-call(bf16[256,1408]{1,0:T(8,128)(2,1)S(1)} %get-tuple-element.19.refs_0_, bf16[256,1152]{1,0:T(8,128)(2,1)S(1)} %collective-permute-done.refs_1_, bf16[256,1152]{1,0:T(8,128)(2,1)S(1)} %collective-permute-done.1.refs_2_, bf16[3584,128]{1,0:T(8,128)(2,1)S(1)} %bitcast.14, ...), custom_call_target="tpu_custom_call" | custom-call | bytes 3880960 | tf_op jit(solution)/shard_map/pallas_call | solution.py:60
  63.9 7.0 %all-to-all-start.1 = ((bf16[8,320,128]{2,1,0:T(8,128)(2,1)}), bf16[8,320,128]{2,1,0:T(8,128)(2,1)S(1)}, u32[]{:S(2)}, u32[]{:S(2)}) async-start(bf16[8,320,128]{2,1,0:T(8,128)(2,1)} %get-tuple-element.25), calls=%async_computation.1 | async-start | bytes 1310720 | tf_op jit(solution)/shard_map/all_to_all | solution.py:420
  71.0 3.1 %collective-permute-start.10 = (bf16[2,2,56,1024]{3,2,1,0:T(8,128)(2,1)S(1)}, bf16[2,2,56,1024]{3,2,1,0:T(8,128)(2,1)S(1)}, u32[]{:S(2)}, u32[]{:S(2)}) collective-permute-start(bf16[2,2,56,1024]{3,2,1,0:T(8,128)(2,1)S(1)} %pad_maximum_fusion.refs_4_), channel_id=1, source_target_pairs={{0,128},{128,256},{256,384},{384,0},{1,129},{129,257},{257,385},{3... | collective-permute-start | bytes 1376264 | tf_op jit(solution)/shard_map/ppermute | solution.py:314
  74.1 4.5 %collective-permute-start.11 = (bf16[2,2,56,1024]{3,2,1,0:T(8,128)(2,1)S(1)}, bf16[2,2,56,1024]{3,2,1,0:T(8,128)(2,1)S(1)}, u32[]{:S(2)}, u32[]{:S(2)}) collective-permute-start(bf16[2,2,56,1024]{3,2,1,0:T(8,128)(2,1)S(1)} %pad_maximum_fusion.refs_4_), channel_id=1, source_target_pairs={{0,256},{128,384},{256,0},{384,128},{1,257},{129,385},{257,1},{385... | collective-permute-start | bytes 1376264 | tf_op jit(solution)/shard_map/ppermute | solution.py:314
  78.6 3.0 %collective-permute-start.12 = (bf16[2,2,56,1024]{3,2,1,0:T(8,128)(2,1)S(1)}, bf16[2,2,56,1024]{3,2,1,0:T(8,128)(2,1)S(1)}, u32[]{:S(2)}, u32[]{:S(2)}) collective-permute-start(bf16[2,2,56,1024]{3,2,1,0:T(8,128)(2,1)S(1)} %pad_maximum_fusion.refs_4_), channel_id=1, source_target_pairs={{0,384},{128,0},{256,128},{384,256},{1,385},{129,1},{257,129},{385... | collective-permute-start | bytes 1376264 | tf_op jit(solution)/shard_map/ppermute | solution.py:314
  81.6 7.3 %all-to-all-done.1.refs_0_ = bf16[8,320,128]{2,1,0:T(8,128)(2,1)S(1)} async-done(((bf16[8,320,128]{2,1,0:T(8,128)(2,1)}), bf16[8,320,128]{2,1,0:T(8,128)(2,1)S(1)}, u32[]{:S(2)}, u32[]{:S(2)}) %all-to-all-start.1) | async-done | bytes 655392 | tf_op jit(solution)/shard_map/all_to_all | solution.py:420
  92.6 12.1 %all-to-all-start.3 = ((bf16[64,4,1024]{2,1,0:T(4,128)(2,1)}), bf16[64,4,1024]{2,1,0:T(4,128)(2,1)S(1)}, u32[]{:S(2)}, u32[]{:S(2)}) async-start(bf16[64,4,1024]{2,1,0:T(4,128)(2,1)} %shard_map.128), calls=%async_computation.3 | async-start | bytes 1048576 | tf_op jit(solution)/shard_map/all_to_all | solution.py:453
  107.5 3.3 %collective-permute-start.7 = (bf16[16,1024]{1,0:T(8,128)(2,1)S(1)}, bf16[16,1024]{1,0:T(8,128)(2,1)S(1)}, u32[]{:S(2)}, u32[]{:S(2)}) collective-permute-start(bf16[16,1024]{1,0:T(8,128)(2,1)S(1)} %shard_map.125.refs_0_), channel_id=1, source_target_pairs={{0,16},{16,0},{32,48},{48,32},{1,17},{17,1},{33,49},{49,33},{2,18}... | collective-permute-start | bytes 98312 | tf_op jit(solution)/shard_map/ppermute | solution.py:326
  110.8 4.0 %collective-permute-start.8 = (bf16[16,1024]{1,0:T(8,128)(2,1)S(1)}, bf16[16,1024]{1,0:T(8,128)(2,1)S(1)}, u32[]{:S(2)}, u32[]{:S(2)}) collective-permute-start(bf16[16,1024]{1,0:T(8,128)(2,1)S(1)} %shard_map.125.refs_0_), channel_id=1, source_target_pairs={{0,32},{16,48},{32,0},{48,16},{1,33},{17,49},{33,1},{49,17},{2,34}... | collective-permute-start | bytes 98312 | tf_op jit(solution)/shard_map/ppermute | solution.py:326
  114.8 2.0 %collective-permute-start.9 = (bf16[16,1024]{1,0:T(8,128)(2,1)S(1)}, bf16[16,1024]{1,0:T(8,128)(2,1)S(1)}, u32[]{:S(2)}, u32[]{:S(2)}) collective-permute-start(bf16[16,1024]{1,0:T(8,128)(2,1)S(1)} %shard_map.125.refs_0_), channel_id=1, source_target_pairs={{0,48},{16,32},{32,16},{48,0},{1,49},{17,33},{33,17},{49,1},{2,50}... | collective-permute-start | bytes 98312 | tf_op jit(solution)/shard_map/ppermute | solution.py:326
  116.9 2.3 %collective-permute-done.7.refs_1_ = bf16[16,1024]{1,0:T(8,128)(2,1)S(1)} collective-permute-done((bf16[16,1024]{1,0:T(8,128)(2,1)S(1)}, bf16[16,1024]{1,0:T(8,128)(2,1)S(1)}, u32[]{:S(2)}, u32[]{:S(2)}) %collective-permute-start.7) | collective-permute-done | bytes 32800 | tf_op jit(solution)/shard_map/ppermute | solution.py:326
  119.1 2.9 %collective-permute-done.9.refs_3_ = bf16[16,1024]{1,0:T(8,128)(2,1)S(1)} collective-permute-done((bf16[16,1024]{1,0:T(8,128)(2,1)S(1)}, bf16[16,1024]{1,0:T(8,128)(2,1)S(1)}, u32[]{:S(2)}, u32[]{:S(2)}) %collective-permute-start.9) | collective-permute-done | bytes 32800 | tf_op jit(solution)/shard_map/ppermute | solution.py:326
  123.4 4.0 %all-to-all-start.2 = ((bf16[32,16,128]{2,1,0:T(8,128)(2,1)}), bf16[32,16,128]{2,1,0:T(8,128)(2,1)S(1)}, u32[]{:S(2)}, u32[]{:S(2)}) async-start(bf16[32,16,128]{2,1,0:T(8,128)(2,1)} %shard_map.127), calls=%async_computation.2 | async-start | bytes 262144 | tf_op jit(solution)/shard_map/all_to_all | solution.py:443
  128.9 7.0 %collective-permute-start.13 = (f32[16,448]{1,0:T(8,128)S(1)}, f32[16,448]{1,0:T(8,128)S(1)}, u32[]{:S(2)}, u32[]{:S(2)}) collective-permute-start(f32[16,448]{1,0:T(8,128)S(1)} %get-tuple-element.30), channel_id=1, source_target_pairs={{0,4},{1,5},{2,6},{3,7},{4,0},{5,1},{6,2},{7,3},{8,12},{9,13},{10,... | collective-permute-start | bytes 86024 | tf_op jit(solution)/shard_map/ppermute | solution.py:326
  (58 shorter events, 20.3 us)
Async XLA Ops:
  0.0 19.9 %copy-start = (bf16[1,128,3584]{2,1,0:T(8,128)(2,1)S(1)}, bf16[1,128,3584]{2,1,0:T(8,128)(2,1)}, u32[]{:S(2)}) copy-start(bf16[1,128,3584]{2,1,0:T(8,128)(2,1)} %param.21) | copy-start | bytes 2752516
  0.0 17.5 %copy-start.12 = (bf16[1024,56]{0,1:T(8,128)(2,1)S(1)}, bf16[1024,56]{0,1:T(8,128)(2,1)}, u32[]{:S(2)}) copy-start(bf16[1024,56]{0,1:T(8,128)(2,1)} %param.23) | copy-start | bytes 344068
  2.5 28.8 %copy-start.3 = (bf16[2,384,576]{1,2,0:T(8,128)(2,1)S(1)}, bf16[2,384,576]{1,2,0:T(8,128)(2,1)}, u32[]{:S(2)}) copy-start(bf16[2,384,576]{1,2,0:T(8,128)(2,1)} %param.15) | copy-start | bytes 2654212
  2.6 40.0 %all-to-all-start = ((bf16[64,4,1408]{2,1,0:T(4,128)(2,1)}), bf16[64,4,1408]{2,1,0:T(4,128)(2,1)S(1)}, u32[]{:S(2)}, u32[]{:S(2)}) async-start(bf16[64,4,1408]{2,1,0:T(4,128)(2,1)} %get-tuple-element.18), calls=%async_computation | async-start | bytes 1441792 | tf_op jit(solution)/shard_map/all_to_all | solution.py:369
  17.6 17.0 %collective-permute-start.5 = (bf16[56,1024]{1,0:T(8,128)(2,1)S(1)}, bf16[56,1024]{1,0:T(8,128)(2,1)}, u32[]{:S(2)}, u32[]{:S(2)}) collective-permute-start(bf16[56,1024]{1,0:T(8,128)(2,1)S(1)} %bitcast.17), channel_id=1, source_target_pairs={{0,8},{8,0},{1,9},{9,1},{2,10},{10,2},{3,11},{11,3},{4,12},{12,4},... | collective-permute-start | bytes 344072 | tf_op jit(solution)/shard_map/ppermute | solution.py:314
  19.9 11.3 %copy-start.13 = (bf16[1,3584]{1,0:T(2,128)(2,1)S(1)}, bf16[1,3584]{1,0:T(2,128)(2,1)}, u32[]{:S(2)}) copy-start(bf16[1,3584]{1,0:T(2,128)(2,1)} %param.18) | copy-start | bytes 21508
  21.9 23.2 %collective-permute-start.2 = (bf16[128,896]{1,0:T(8,128)(2,1)}, bf16[128,896]{1,0:T(8,128)(2,1)S(1)}, u32[]{:S(2)}, u32[]{:S(2)}) collective-permute-start(bf16[128,896]{1,0:T(8,128)(2,1)} %get-tuple-element.22), channel_id=1, source_target_pairs={{0,1},{1,0},{2,3},{3,2},{4,5},{5,4},{6,7},{7,6},{8,9},{9,8},{10,11... | collective-permute-start | bytes 688136 | tf_op jit(solution)/shard_map/ppermute | solution.py:326
  25.1 24.9 %collective-permute-start.3 = (bf16[128,896]{1,0:T(8,128)(2,1)}, bf16[128,896]{1,0:T(8,128)(2,1)S(1)}, u32[]{:S(2)}, u32[]{:S(2)}) collective-permute-start(bf16[128,896]{1,0:T(8,128)(2,1)} %get-tuple-element.23), channel_id=1, source_target_pairs={{0,2},{1,3},{2,0},{3,1},{4,6},{5,7},{6,4},{7,5},{8,10},{9,11},{10,... | collective-permute-start | bytes 688136 | tf_op jit(solution)/shard_map/ppermute | solution.py:326
  29.3 20.7 %collective-permute-start.4 = (bf16[128,896]{1,0:T(8,128)(2,1)}, bf16[128,896]{1,0:T(8,128)(2,1)S(1)}, u32[]{:S(2)}, u32[]{:S(2)}) collective-permute-start(bf16[128,896]{1,0:T(8,128)(2,1)} %get-tuple-element.24), channel_id=1, source_target_pairs={{0,3},{1,2},{2,1},{3,0},{4,7},{5,6},{6,5},{7,4},{8,11},{9,10},{10,... | collective-permute-start | bytes 688136 | tf_op jit(solution)/shard_map/ppermute | solution.py:326
  35.4 15.3 %collective-permute-start.6 = (bf16[2,56,1024]{2,1,0:T(8,128)(2,1)S(1)}, bf16[2,56,1024]{2,1,0:T(8,128)(2,1)S(1)}, u32[]{:S(2)}, u32[]{:S(2)}) collective-permute-start(bf16[2,56,1024]{2,1,0:T(8,128)(2,1)S(1)} %get-tuple-element.32), channel_id=1, source_target_pairs={{0,64},{64,0},{1,65},{65,1},{2,66},{66,2},{3,67},{67,3},{4,68},{68... | collective-permute-start | bytes 688136 | tf_op jit(solution)/shard_map/ppermute | solution.py:314
  42.8 17.4 %collective-permute-start = (bf16[256,1152]{1,0:T(8,128)(2,1)S(1)}, bf16[256,1152]{1,0:T(8,128)(2,1)S(1)}, u32[]{:S(2)}, u32[]{:S(2)}) collective-permute-start(bf16[256,1152]{1,0:T(8,128)(2,1)S(1)} %get-tuple-element.20), channel_id=1, source_target_pairs={{0,1},{1,2},{2,3},{3,4},{4,5},{5,6},{6,7},{7,0},{8,9},{9,10},{10,1... | collective-permute-start | bytes 1769480 | tf_op jit(solution)/shard_map/ppermute | solution.py:314
  45.1 16.2 %copy-start.1 = (bf16[1,3584,128]{2,1,0:T(8,128)(2,1)S(1)}, bf16[1,3584,128]{2,1,0:T(8,128)(2,1)}, u32[]{:S(2)}) copy-start(bf16[1,3584,128]{2,1,0:T(8,128)(2,1)} %param.19) | copy-start | bytes 2752516
  45.1 16.2 %copy-start.2 = (bf16[1,3584,128]{2,1,0:T(8,128)(2,1)S(1)}, bf16[1,3584,128]{2,1,0:T(8,128)(2,1)}, u32[]{:S(2)}) copy-start(bf16[1,3584,128]{2,1,0:T(8,128)(2,1)} %param.20) | copy-start | bytes 2752516
  45.1 16.2 %collective-permute-start.1 = (bf16[256,1152]{1,0:T(8,128)(2,1)S(1)}, bf16[256,1152]{1,0:T(8,128)(2,1)S(1)}, u32[]{:S(2)}, u32[]{:S(2)}) collective-permute-start(bf16[256,1152]{1,0:T(8,128)(2,1)S(1)} %get-tuple-element.21), channel_id=1, source_target_pairs={{0,7},{1,0},{2,1},{3,2},{4,3},{5,4},{6,5},{7,6},{8,15},{9,8},{10,9... | collective-permute-start | bytes 1769480 | tf_op jit(solution)/shard_map/ppermute | solution.py:314
  63.9 25.0 %all-to-all-start.1 = ((bf16[8,320,128]{2,1,0:T(8,128)(2,1)}), bf16[8,320,128]{2,1,0:T(8,128)(2,1)S(1)}, u32[]{:S(2)}, u32[]{:S(2)}) async-start(bf16[8,320,128]{2,1,0:T(8,128)(2,1)} %get-tuple-element.25), calls=%async_computation.1 | async-start | bytes 1310720 | tf_op jit(solution)/shard_map/all_to_all | solution.py:420
  71.0 43.9 %collective-permute-start.10 = (bf16[2,2,56,1024]{3,2,1,0:T(8,128)(2,1)S(1)}, bf16[2,2,56,1024]{3,2,1,0:T(8,128)(2,1)S(1)}, u32[]{:S(2)}, u32[]{:S(2)}) collective-permute-start(bf16[2,2,56,1024]{3,2,1,0:T(8,128)(2,1)S(1)} %pad_maximum_fusion.refs_4_), channel_id=1, source_target_pairs={{0,128},{128,256},{256,384},{384,0},{1,129},{129,257},{257,385},{3... | collective-permute-start | bytes 1376264 | tf_op jit(solution)/shard_map/ppermute | solution.py:314
  74.1 42.7 %collective-permute-start.11 = (bf16[2,2,56,1024]{3,2,1,0:T(8,128)(2,1)S(1)}, bf16[2,2,56,1024]{3,2,1,0:T(8,128)(2,1)S(1)}, u32[]{:S(2)}, u32[]{:S(2)}) collective-permute-start(bf16[2,2,56,1024]{3,2,1,0:T(8,128)(2,1)S(1)} %pad_maximum_fusion.refs_4_), channel_id=1, source_target_pairs={{0,256},{128,384},{256,0},{384,128},{1,257},{129,385},{257,1},{385... | collective-permute-start | bytes 1376264 | tf_op jit(solution)/shard_map/ppermute | solution.py:314
  78.6 38.2 %collective-permute-start.12 = (bf16[2,2,56,1024]{3,2,1,0:T(8,128)(2,1)S(1)}, bf16[2,2,56,1024]{3,2,1,0:T(8,128)(2,1)S(1)}, u32[]{:S(2)}, u32[]{:S(2)}) collective-permute-start(bf16[2,2,56,1024]{3,2,1,0:T(8,128)(2,1)S(1)} %pad_maximum_fusion.refs_4_), channel_id=1, source_target_pairs={{0,384},{128,0},{256,128},{384,256},{1,385},{129,1},{257,129},{385... | collective-permute-start | bytes 1376264 | tf_op jit(solution)/shard_map/ppermute | solution.py:314
  92.6 30.8 %all-to-all-start.3 = ((bf16[64,4,1024]{2,1,0:T(4,128)(2,1)}), bf16[64,4,1024]{2,1,0:T(4,128)(2,1)S(1)}, u32[]{:S(2)}, u32[]{:S(2)}) async-start(bf16[64,4,1024]{2,1,0:T(4,128)(2,1)} %shard_map.128), calls=%async_computation.3 | async-start | bytes 1048576 | tf_op jit(solution)/shard_map/all_to_all | solution.py:453
  107.5 11.6 %collective-permute-start.7 = (bf16[16,1024]{1,0:T(8,128)(2,1)S(1)}, bf16[16,1024]{1,0:T(8,128)(2,1)S(1)}, u32[]{:S(2)}, u32[]{:S(2)}) collective-permute-start(bf16[16,1024]{1,0:T(8,128)(2,1)S(1)} %shard_map.125.refs_0_), channel_id=1, source_target_pairs={{0,16},{16,0},{32,48},{48,32},{1,17},{17,1},{33,49},{49,33},{2,18}... | collective-permute-start | bytes 98312 | tf_op jit(solution)/shard_map/ppermute | solution.py:326
  110.8 8.3 %collective-permute-start.8 = (bf16[16,1024]{1,0:T(8,128)(2,1)S(1)}, bf16[16,1024]{1,0:T(8,128)(2,1)S(1)}, u32[]{:S(2)}, u32[]{:S(2)}) collective-permute-start(bf16[16,1024]{1,0:T(8,128)(2,1)S(1)} %shard_map.125.refs_0_), channel_id=1, source_target_pairs={{0,32},{16,48},{32,0},{48,16},{1,33},{17,49},{33,1},{49,17},{2,34}... | collective-permute-start | bytes 98312 | tf_op jit(solution)/shard_map/ppermute | solution.py:326
  114.8 7.2 %collective-permute-start.9 = (bf16[16,1024]{1,0:T(8,128)(2,1)S(1)}, bf16[16,1024]{1,0:T(8,128)(2,1)S(1)}, u32[]{:S(2)}, u32[]{:S(2)}) collective-permute-start(bf16[16,1024]{1,0:T(8,128)(2,1)S(1)} %shard_map.125.refs_0_), channel_id=1, source_target_pairs={{0,48},{16,32},{32,16},{48,0},{1,49},{17,33},{33,17},{49,1},{2,50}... | collective-permute-start | bytes 98312 | tf_op jit(solution)/shard_map/ppermute | solution.py:326
  123.4 13.3 %all-to-all-start.2 = ((bf16[32,16,128]{2,1,0:T(8,128)(2,1)}), bf16[32,16,128]{2,1,0:T(8,128)(2,1)S(1)}, u32[]{:S(2)}, u32[]{:S(2)}) async-start(bf16[32,16,128]{2,1,0:T(8,128)(2,1)} %shard_map.127), calls=%async_computation.2 | async-start | bytes 262144 | tf_op jit(solution)/shard_map/all_to_all | solution.py:443
  128.9 8.9 %collective-permute-start.13 = (f32[16,448]{1,0:T(8,128)S(1)}, f32[16,448]{1,0:T(8,128)S(1)}, u32[]{:S(2)}, u32[]{:S(2)}) collective-permute-start(f32[16,448]{1,0:T(8,128)S(1)} %get-tuple-element.30), channel_id=1, source_target_pairs={{0,4},{1,5},{2,6},{3,7},{4,0},{5,1},{6,2},{7,3},{8,12},{9,13},{10,... | collective-permute-start | bytes 86024 | tf_op jit(solution)/shard_map/ppermute | solution.py:326
  (8 other events, 11.0 us)

commit v9 on v8

--- a/solution.py
+++ b/solution.py
@@ -126,19 +126,10 @@
     context_ref[...] = jnp.concatenate(found, axis=1).astype(BF16)
 
 
-def lift_heads(inner_ref, w_uv_ref, values_ref):
+def lift_heads(context_ref, w_uv_ref, values_ref):
     heads, latent, width = w_uv_ref.shape
     rows = values_ref.shape[0]
-    sources, depth, lanes = inner_ref.shape
-    share = rows * heads // sources
-    first = depth - share * latent // lanes
-    context = jnp.concatenate(
-        [
-            inner_ref[:, first + q * share : first + (q + 1) * share, :]
-            for q in range(latent // lanes)
-        ],
-        axis=2,
-    ).reshape(rows * heads, latent)
+    context = context_ref[...].reshape(rows * heads, latent)
     token, entry = iotas(rows, rows * heads)
     for h in range(heads):
         lifted = jnp.dot(context, w_uv_ref[h], preferred_element_type=F32).astype(BF16)
@@ -212,7 +203,6 @@
     w_gate_ref,
     w_up_ref,
     router_ref,
-    context_ref,
     inner_ref,
     score_ref,
 ):
@@ -251,15 +241,8 @@
         logits += lax.dot_general(rows, column, NT, preferred_element_type=F32)
     gate, lifted = lifted[:, :units], lifted[:, units:]
     inner = (gate / (1.0 + jnp.exp(-gate)) * lifted).astype(BF16)
-    copies, share, latent = context_ref.shape
-    lanes = inner_ref.shape[2]
-    for copy in range(copies):
-        inner_ref[copy, :slots] = inner
-        for q in range(latent // lanes):
-            first = slots + q * share
-            inner_ref[copy, first : first + share] = context_ref[
-                copy, :, q * lanes : (q + 1) * lanes
-            ]
+    for copy in range(inner_ref.shape[0]):
+        inner_ref[copy] = inner
     score_ref[...] = (1.0 / (1.0 + jnp.exp(-logits))).astype(BF16)
 
 
@@ -270,8 +253,8 @@
     width = parts[0].shape[1]
     total = jnp.zeros((slots, width), F32)
     for k in range(len(parts)):
-        source = lax.axis_index("y") ^ k
-        total += jnp.dot(inner_ref[source, :slots], parts[k][...], preferred_element_type=F32)
+        source = lax.axis_index("y") % len(parts) ^ k
+        total += jnp.dot(inner_ref[source], parts[k][...], preferred_element_type=F32)
     total = jnp.concatenate([total, score_ref[:, : padded - width].astype(F32)], axis=1)
     back_ref[...] = total.reshape(blocks, SLOTS, padded).astype(BF16)
 
@@ -385,11 +368,9 @@
         jnp.swapaxes(latent_cache, 1, 2),
         smem=(0,),
         load=(0, 1, 2),
-    )
-
-    out_pair = pair_up(w_out.T, "c")
-    out_other = shift(out_pair, "zh", 1)
-    (crossed,) = kernel_call(mark, [((8, 128), F32)], after=(out_other,))
+        after=(place,),
+    )
+
     (moved,) = kernel_call(mark, [((8, 128), F32)], after=down[1:], flops=20_000_000_000)
 
     held, up, below = kernel_call(
@@ -403,27 +384,33 @@
         after=(context,),
     )
 
+    contexts = lax.all_to_all(context, "y", 0, 0, tiled=True)
+    out_pair = pair_up(w_out.T, "c")
+    out_other = shift(out_pair, "zh", 1)
+
+    (crossed,) = kernel_call(mark, [((8, 128), F32)], after=(out_other,))
+
     inner, score = kernel_call(
         lift_experts,
-        [((tp_size, slots + 8 * heads, hidden_units), BF16), ((slots, 128), BF16)],
+        [((GROUP, slots, hidden_units), BF16), ((slots, 128), BF16)],
         held,
         shift(up, "y", 1),
         shift(below, "y", -1),
         w_gate[0],
         w_up[0],
         router_rows,
-        context,
         load=(3, 4),
         store=(0, 1),
         after=(moved, crossed),
     )
-    inner = lax.all_to_all(inner, "y", 0, 0, tiled=True)
+    groups = [list(range(i, i + GROUP)) for i in range(0, tp_size, GROUP)]
+    inner = lax.all_to_all(inner, "y", 0, 0, tiled=True, axis_index_groups=groups)
 
     out_weights = gather(jnp.stack([out_pair, out_other]), "x")
     (values,) = kernel_call(
         lift_heads,
         [((rows, depth), BF16)],
-        inner,
+        contexts,
         w_uv,
         load=(1,),
         flops=10_000_000_000,
@@ -431,7 +418,7 @@
 
     all_values = trade(values, "zl")
     (gathered,) = kernel_call(
-        mark, [((8, 128), F32)], after=out_weights[1:], flops=10_000_000_000
+        mark, [((8, 128), F32)], after=out_weights[1:], flops=15_000_000_000
     )
     (attn_parts,) = kernel_call(
         project,
@@ -449,6 +436,7 @@
         *down,
         score,
         load=(1, 1 + GROUP),
+        after=(contexts,),
     )
     back = lax.all_to_all(back, EP, 0, 0, tiled=True)
     own = lax.dynamic_slice_in_dim(hidden, tp * width, width, 1)

time: 141 us -> 134 us (0.950)
  waiting for transfers between devices: 24.9 us -> 13.2 us
  starting transfers between devices: 90.9 us -> 99.2 us
  local copies, waits for them, and re-layouts: 6.35 us -> 3.53 us
    ppermute x7, waiting for transfers between devices: 10.5 us -> 0.73 us  [shift(): return lax.ppermute(value, axis, [(i, (i + k) % size) for i in range(size)])]
    all_to_all x1 -> x2, waiting for transfers between devices: 7.29 us -> 0.01 us  [the longest x1 0.01 us: on_device(): lax.all_to_all(inner, 'y', 0, 0, tiled=True, axis_index_groups=groups)]
    all_to_all x1 -> x2, starting transfers between devices: 7.05 us -> 12.5 us  [the longest x1 6.76 us: on_device(): contexts = lax.all_to_all(context, 'y', 0, 0, tiled=True)]
    ppermute x7, waiting for transfers between devices: 6.16 us -> 9.75 us  [swap(): lax.ppermute(value, axis, [(i, i ^ k) for i in range(lax.axis_size(axis))])]
    all_to_all x1, starting transfers between devices: 3.98 us -> 7.52 us  [on_device(): attn_parts = lax.all_to_all(attn_parts, ('zl', 'y'), 0, 0, tiled=True)]
    unnamed x28 -> x32, local copies, waits for them, and re-layouts: 5.47 us -> 2.64 us
    all_to_all x1, waiting for transfers between devices: 0.01 us -> 1.85 us  [on_device(): back = lax.all_to_all(back, EP, 0, 0, tiled=True)]
  transfers between devices with their start and end apart: 18 -> 19, of which waited for: 7 -> 5; matrix products, arithmetic and copies ran while one was open for 1% -> 1% of each run, Pallas kernels for 7% -> 9%
where the time goes in v9:
time: 134 us; the launch traced here: 133 us
  starting transfers between devices  99.2 us (74%)
  Pallas kernels  15.5 us (12%)
  waiting for transfers between devices  13.2 us (10%)
  local copies, waits for them, and re-layouts  3.53 us (3%)
    ppermute x7, starting transfers between devices, shift(): return lax.ppermute(value, axis, [(i, (i + k) % size) for i in range(size)])  26.7 us
    ppermute x7, starting transfers between devices, swap(): lax.ppermute(value, axis, [(i, i ^ k) for i in range(lax.axis_size(axis))])  25.9 us
    pallas_call x13, Pallas kernels, kernel_call(): pl.pallas_call(kernel, out_shape=tuple(shapes), in_specs=[place(n, load)...  15.5 us
    all_to_all x1, starting transfers between devices, on_device(): named_rows = lax.all_to_all(send, EP, 0, 0, tiled=True)  15 us
    all_to_all x1, starting transfers between devices, on_device(): back = lax.all_to_all(back, EP, 0, 0, tiled=True)  11.5 us
    ppermute x7, waiting for transfers between devices, swap(): lax.ppermute(value, axis, [(i, i ^ k) for i in range(lax.axis_size(axis))])  9.75 us
    all_to_all x1, starting transfers between devices, on_device(): attn_parts = lax.all_to_all(attn_parts, ('zl', 'y'), 0, 0, tiled=True)  7.52 us
    all_to_all x1, starting transfers between devices, on_device(): contexts = lax.all_to_all(context, 'y', 0, 0, tiled=True)  6.76 us
  transfers between devices with their start and end apart: 19, of which 5 were waited for; matrix products, arithmetic and copies ran while one was open for 1% of the time, Pallas kernels for 9%

profile of v9, /device:TPU:1, one launch (start us, length us, event | category | flops | bytes accessed | tf_op | source)
XLA Modules:
  0.0 132.8 jit_solution(5088907673194141114)
XLA Ops:
  0.0 2.5 %shard_map.118 = (bf16[64,4,1408]{2,1,0:T(4,128)(2,1)}, f32[256,16]{1,0:T(8,128)}) custom-call(bf16[16,3584]{1,0:T(8,128)(2,1)} %refs_0_.2, bf16[3584]{0:T(1024)(128)(2,1)} %refs_1_.3, s32[8,16]{1,0:T(8,128)} %bitcast.19), custom_call_target="tpu_custom_call" | custom-call | bytes 122368 | tf_op jit(solution)/shard_map/pallas_call | solution.py:60
  2.6 15.0 %all-to-all-start.2 = ((bf16[64,4,1408]{2,1,0:T(4,128)(2,1)}), bf16[64,4,1408]{2,1,0:T(4,128)(2,1)S(1)}, u32[]{:S(2)}, u32[]{:S(2)}) async-start(bf16[64,4,1408]{2,1,0:T(4,128)(2,1)} %get-tuple-element.19), calls=%async_computation.2 | async-start | bytes 1441792 | tf_op jit(solution)/shard_map/all_to_all | solution.py:352
  17.6 2.4 %collective-permute-start.3 = (bf16[56,1024]{1,0:T(8,128)(2,1)S(1)}, bf16[56,1024]{1,0:T(8,128)(2,1)}, u32[]{:S(2)}, u32[]{:S(2)}) collective-permute-start(bf16[56,1024]{1,0:T(8,128)(2,1)S(1)} %bitcast.17), channel_id=1, source_target_pairs={{0,8},{8,0},{1,9},{9,1},{2,10},{10,2},{3,11},{11,3},{4,12},{12,4},... | collective-permute-start | bytes 344072 | tf_op jit(solution)/shard_map/ppermute | solution.py:297
  20.0 1.9 %shard_map.124 = (bf16[128,896]{1,0:T(8,128)(2,1)S(1)}, bf16[128,896]{1,0:T(8,128)(2,1)}, bf16[128,896]{1,0:T(8,128)(2,1)}, bf16[128,896]{1,0:T(8,128)(2,1)}) custom-call(bf16[128,3584]{1,0:T(8,128)(2,1)S(1)} %bitcast.15), custom_call_target="tpu_custom_call" | custom-call | bytes 917504 | tf_op jit(solution)/shard_map/pallas_call | solution.py:60
  21.9 3.2 %collective-permute-start.10 = (bf16[128,896]{1,0:T(8,128)(2,1)}, bf16[128,896]{1,0:T(8,128)(2,1)S(1)}, u32[]{:S(2)}, u32[]{:S(2)}) collective-permute-start(bf16[128,896]{1,0:T(8,128)(2,1)} %get-tuple-element.23), channel_id=1, source_target_pairs={{0,1},{1,0},{2,3},{3,2},{4,5},{5,4},{6,7},{7,6},{8,9},{9,8},{10,11... | collective-permute-start | bytes 688136 | tf_op jit(solution)/shard_map/ppermute | solution.py:309
  25.1 4.2 %collective-permute-start.11 = (bf16[128,896]{1,0:T(8,128)(2,1)}, bf16[128,896]{1,0:T(8,128)(2,1)S(1)}, u32[]{:S(2)}, u32[]{:S(2)}) collective-permute-start(bf16[128,896]{1,0:T(8,128)(2,1)} %get-tuple-element.24), channel_id=1, source_target_pairs={{0,2},{1,3},{2,0},{3,1},{4,6},{5,7},{6,4},{7,5},{8,10},{9,11},{10,... | collective-permute-start | bytes 688136 | tf_op jit(solution)/shard_map/ppermute | solution.py:309
  29.3 1.9 %collective-permute-start.12 = (bf16[128,896]{1,0:T(8,128)(2,1)}, bf16[128,896]{1,0:T(8,128)(2,1)S(1)}, u32[]{:S(2)}, u32[]{:S(2)}) collective-permute-start(bf16[128,896]{1,0:T(8,128)(2,1)} %get-tuple-element.25), channel_id=1, source_target_pairs={{0,3},{1,2},{2,1},{3,0},{4,7},{5,6},{6,5},{7,4},{8,11},{9,10},{10,... | collective-permute-start | bytes 688136 | tf_op jit(solution)/shard_map/ppermute | solution.py:309
  32.0 2.2 %shard_map.119.refs_1_ = bf16[8,16,512]{2,1,0:T(8,128)(2,1)} custom-call(s32[2]{0:T(128)S(1)} %copy-done.12, bf16[2,64,576]{2,1,0:T(8,128)(2,1)S(1)} %copy-done.11, bf16[2,576,384]{2,1,0:T(8,128)(2,1)S(1)} %bitcast.16, f32[256,16]{1,0:T(8,128)S(1)} %copy-done.4), custom_call_target="tpu_custom_call" | custom-call | bytes 1032200 | tf_op jit(solution)/shard_map/pallas_call | solution.py:60
  35.2 7.1 %collective-permute-start.4 = (bf16[2,56,1024]{2,1,0:T(8,128)(2,1)S(1)}, bf16[2,56,1024]{2,1,0:T(8,128)(2,1)S(1)}, u32[]{:S(2)}, u32[]{:S(2)}) collective-permute-start(bf16[2,56,1024]{2,1,0:T(8,128)(2,1)S(1)} %get-tuple-element.32), channel_id=1, source_target_pairs={{0,64},{64,0},{1,65},{65,1},{2,66},{66,2},{3,67},{67,3},{4,68},{68... | collective-permute-start | bytes 688136 | tf_op jit(solution)/shard_map/ppermute | solution.py:297
  42.3 6.8 %all-to-all-start = ((bf16[8,16,512]{2,1,0:T(8,128)(2,1)}), bf16[8,16,512]{2,1,0:T(8,128)(2,1)S(1)}, u32[]{:S(2)}, u32[]{:S(2)}) async-start(bf16[8,16,512]{2,1,0:T(8,128)(2,1)} %shard_map.119.refs_1_), calls=%async_computation | async-start | bytes 262144 | tf_op jit(solution)/shard_map/all_to_all | solution.py:387
  49.3 3.4 %collective-permute-start.8 = (bf16[256,1152]{1,0:T(8,128)(2,1)S(1)}, bf16[256,1152]{1,0:T(8,128)(2,1)S(1)}, u32[]{:S(2)}, u32[]{:S(2)}) collective-permute-start(bf16[256,1152]{1,0:T(8,128)(2,1)S(1)} %get-tuple-element.21), channel_id=1, source_target_pairs={{0,1},{1,2},{2,3},{3,4},{4,5},{5,6},{6,7},{7,0},{8,9},{9,10},{10,1... | collective-permute-start | bytes 1769480 | tf_op jit(solution)/shard_map/ppermute | solution.py:297
  52.7 3.1 %collective-permute-start.9 = (bf16[256,1152]{1,0:T(8,128)(2,1)S(1)}, bf16[256,1152]{1,0:T(8,128)(2,1)S(1)}, u32[]{:S(2)}, u32[]{:S(2)}) collective-permute-start(bf16[256,1152]{1,0:T(8,128)(2,1)S(1)} %get-tuple-element.22), channel_id=1, source_target_pairs={{0,7},{1,0},{2,1},{3,2},{4,3},{5,4},{6,5},{7,6},{8,15},{9,8},{10,9... | collective-permute-start | bytes 1769480 | tf_op jit(solution)/shard_map/ppermute | solution.py:297
  56.7 3.3 %collective-permute-start.5 = (bf16[2,2,56,1024]{3,2,1,0:T(8,128)(2,1)S(1)}, bf16[2,2,56,1024]{3,2,1,0:T(8,128)(2,1)S(1)}, u32[]{:S(2)}, u32[]{:S(2)}) collective-permute-start(bf16[2,2,56,1024]{3,2,1,0:T(8,128)(2,1)S(1)} %pad_maximum_fusion.refs_4_), channel_id=1, source_target_pairs={{0,128},{128,256},{256,384},{384,0},{1,129},{129,257},{257,385},{3... | collective-permute-start | bytes 1376264 | tf_op jit(solution)/shard_map/ppermute | solution.py:297
  60.0 4.5 %collective-permute-start.6 = (bf16[2,2,56,1024]{3,2,1,0:T(8,128)(2,1)S(1)}, bf16[2,2,56,1024]{3,2,1,0:T(8,128)(2,1)S(1)}, u32[]{:S(2)}, u32[]{:S(2)}) collective-permute-start(bf16[2,2,56,1024]{3,2,1,0:T(8,128)(2,1)S(1)} %pad_maximum_fusion.refs_4_), channel_id=1, source_target_pairs={{0,256},{128,384},{256,0},{384,128},{1,257},{129,385},{257,1},{385... | collective-permute-start | bytes 1376264 | tf_op jit(solution)/shard_map/ppermute | solution.py:297
  64.5 3.0 %collective-permute-start.7 = (bf16[2,2,56,1024]{3,2,1,0:T(8,128)(2,1)S(1)}, bf16[2,2,56,1024]{3,2,1,0:T(8,128)(2,1)S(1)}, u32[]{:S(2)}, u32[]{:S(2)}) collective-permute-start(bf16[2,2,56,1024]{3,2,1,0:T(8,128)(2,1)S(1)} %pad_maximum_fusion.refs_4_), channel_id=1, source_target_pairs={{0,384},{128,0},{256,128},{384,256},{1,385},{129,1},{257,129},{385... | collective-permute-start | bytes 1376264 | tf_op jit(solution)/shard_map/ppermute | solution.py:297
  68.2 2.4 %shard_map.127 = (bf16[4,256,128]{2,1,0:T(8,128)(2,1)}, bf16[256,128]{1,0:T(8,128)(2,1)S(1)}) custom-call(bf16[256,1408]{1,0:T(8,128)(2,1)S(1)} %get-tuple-element.20.refs_0_, bf16[256,1152]{1,0:T(8,128)(2,1)S(1)} %collective-permute-done.8.refs_1_, bf16[256,1152]{1,0:T(8,128)(2,1)S(1)} %collective-permute-done.9.refs_2_, bf16[3584,128]{1,0:T(8,128)(2,1)S(1)} %bitcast.12, ...), custom_call_target="tpu_custom_call" | custom-call | bytes 3749888 | tf_op jit(solution)/shard_map/pallas_call | solution.py:60
  70.7 5.8 %all-to-all-start.3 = ((bf16[4,256,128]{2,1,0:T(8,128)(2,1)}), bf16[4,256,128]{2,1,0:T(8,128)(2,1)S(1)}, u32[]{:S(2)}, u32[]{:S(2)}) async-start(bf16[4,256,128]{2,1,0:T(8,128)(2,1)} %get-tuple-element.26), calls=%async_computation.3 | async-start | bytes 524288 | tf_op jit(solution)/shard_map/all_to_all | solution.py:407
  79.2 2.2 %collective-permute-start = (bf16[16,1024]{1,0:T(8,128)(2,1)S(1)}, bf16[16,1024]{1,0:T(8,128)(2,1)S(1)}, u32[]{:S(2)}, u32[]{:S(2)}) collective-permute-start(bf16[16,1024]{1,0:T(8,128)(2,1)S(1)} %shard_map.120.refs_0_), channel_id=1, source_target_pairs={{0,16},{16,0},{32,48},{48,32},{1,17},{17,1},{33,49},{49,33},{2,18}... | collective-permute-start | bytes 98312 | tf_op jit(solution)/shard_map/ppermute | solution.py:309
  81.4 2.2 %collective-permute-start.1 = (bf16[16,1024]{1,0:T(8,128)(2,1)S(1)}, bf16[16,1024]{1,0:T(8,128)(2,1)S(1)}, u32[]{:S(2)}, u32[]{:S(2)}) collective-permute-start(bf16[16,1024]{1,0:T(8,128)(2,1)S(1)} %shard_map.120.refs_0_), channel_id=1, source_target_pairs={{0,32},{16,48},{32,0},{48,16},{1,33},{17,49},{33,1},{49,17},{2,34}... | collective-permute-start | bytes 98312 | tf_op jit(solution)/shard_map/ppermute | solution.py:309
  85.5 11.5 %all-to-all-start.4 = ((bf16[64,4,1024]{2,1,0:T(4,128)(2,1)}), bf16[64,4,1024]{2,1,0:T(4,128)(2,1)S(1)}, u32[]{:S(2)}, u32[]{:S(2)}) async-start(bf16[64,4,1024]{2,1,0:T(4,128)(2,1)} %shard_map.128), calls=%async_computation.4 | async-start | bytes 1048576 | tf_op jit(solution)/shard_map/all_to_all | solution.py:441
  97.1 5.1 %collective-permute-start.2 = (bf16[16,1024]{1,0:T(8,128)(2,1)S(1)}, bf16[16,1024]{1,0:T(8,128)(2,1)S(1)}, u32[]{:S(2)}, u32[]{:S(2)}) collective-permute-start(bf16[16,1024]{1,0:T(8,128)(2,1)S(1)} %shard_map.120.refs_0_), channel_id=1, source_target_pairs={{0,48},{16,32},{32,16},{48,0},{1,49},{17,33},{33,17},{49,1},{2,50}... | collective-permute-start | bytes 98312 | tf_op jit(solution)/shard_map/ppermute | solution.py:309
  102.3 8.8 %collective-permute-done.2.refs_3_ = bf16[16,1024]{1,0:T(8,128)(2,1)S(1)} collective-permute-done((bf16[16,1024]{1,0:T(8,128)(2,1)S(1)}, bf16[16,1024]{1,0:T(8,128)(2,1)S(1)}, u32[]{:S(2)}, u32[]{:S(2)}) %collective-permute-start.2) | collective-permute-done | bytes 32800 | tf_op jit(solution)/shard_map/ppermute | solution.py:309
  114.3 7.5 %all-to-all-start.1 = ((bf16[32,16,128]{2,1,0:T(8,128)(2,1)}), bf16[32,16,128]{2,1,0:T(8,128)(2,1)S(1)}, u32[]{:S(2)}, u32[]{:S(2)}) async-start(bf16[32,16,128]{2,1,0:T(8,128)(2,1)} %shard_map.122), calls=%async_computation.1 | async-start | bytes 262144 | tf_op jit(solution)/shard_map/all_to_all | solution.py:430
  123.3 7.0 %collective-permute-start.13 = (f32[16,448]{1,0:T(8,128)S(1)}, f32[16,448]{1,0:T(8,128)S(1)}, u32[]{:S(2)}, u32[]{:S(2)}) collective-permute-start(f32[16,448]{1,0:T(8,128)S(1)} %get-tuple-element.30), channel_id=1, source_target_pairs={{0,4},{1,5},{2,6},{3,7},{4,0},{5,1},{6,2},{7,3},{8,12},{9,13},{10,... | collective-permute-start | bytes 86024 | tf_op jit(solution)/shard_map/ppermute | solution.py:309
  (64 shorter events, 15.4 us)
Async XLA Ops:
  0.0 19.9 %copy-start.2 = (bf16[1,128,3584]{2,1,0:T(8,128)(2,1)S(1)}, bf16[1,128,3584]{2,1,0:T(8,128)(2,1)}, u32[]{:S(2)}) copy-start(bf16[1,128,3584]{2,1,0:T(8,128)(2,1)} %param.21) | copy-start | bytes 2752516
  0.0 17.5 %copy-start.14 = (bf16[1024,56]{0,1:T(8,128)(2,1)S(1)}, bf16[1024,56]{0,1:T(8,128)(2,1)}, u32[]{:S(2)}) copy-start(bf16[1024,56]{0,1:T(8,128)(2,1)} %param.23) | copy-start | bytes 344068
  2.6 28.8 %copy-start.3 = (bf16[2,384,576]{1,2,0:T(8,128)(2,1)S(1)}, bf16[2,384,576]{1,2,0:T(8,128)(2,1)}, u32[]{:S(2)}) copy-start(bf16[2,384,576]{1,2,0:T(8,128)(2,1)} %param.15) | copy-start | bytes 2654212
  2.6 39.7 %all-to-all-start.2 = ((bf16[64,4,1408]{2,1,0:T(4,128)(2,1)}), bf16[64,4,1408]{2,1,0:T(4,128)(2,1)S(1)}, u32[]{:S(2)}, u32[]{:S(2)}) async-start(bf16[64,4,1408]{2,1,0:T(4,128)(2,1)} %get-tuple-element.19), calls=%async_computation.2 | async-start | bytes 1441792 | tf_op jit(solution)/shard_map/all_to_all | solution.py:352
  17.6 16.7 %collective-permute-start.3 = (bf16[56,1024]{1,0:T(8,128)(2,1)S(1)}, bf16[56,1024]{1,0:T(8,128)(2,1)}, u32[]{:S(2)}, u32[]{:S(2)}) collective-permute-start(bf16[56,1024]{1,0:T(8,128)(2,1)S(1)} %bitcast.17), channel_id=1, source_target_pairs={{0,8},{8,0},{1,9},{9,1},{2,10},{10,2},{3,11},{11,3},{4,12},{12,4},... | collective-permute-start | bytes 344072 | tf_op jit(solution)/shard_map/ppermute | solution.py:297
  21.9 30.9 %collective-permute-start.10 = (bf16[128,896]{1,0:T(8,128)(2,1)}, bf16[128,896]{1,0:T(8,128)(2,1)S(1)}, u32[]{:S(2)}, u32[]{:S(2)}) collective-permute-start(bf16[128,896]{1,0:T(8,128)(2,1)} %get-tuple-element.23), channel_id=1, source_target_pairs={{0,1},{1,0},{2,3},{3,2},{4,5},{5,4},{6,7},{7,6},{8,9},{9,8},{10,11... | collective-permute-start | bytes 688136 | tf_op jit(solution)/shard_map/ppermute | solution.py:309
  25.1 30.8 %collective-permute-start.11 = (bf16[128,896]{1,0:T(8,128)(2,1)}, bf16[128,896]{1,0:T(8,128)(2,1)S(1)}, u32[]{:S(2)}, u32[]{:S(2)}) collective-permute-start(bf16[128,896]{1,0:T(8,128)(2,1)} %get-tuple-element.24), channel_id=1, source_target_pairs={{0,2},{1,3},{2,0},{3,1},{4,6},{5,7},{6,4},{7,5},{8,10},{9,11},{10,... | collective-permute-start | bytes 688136 | tf_op jit(solution)/shard_map/ppermute | solution.py:309
  29.3 26.6 %collective-permute-start.12 = (bf16[128,896]{1,0:T(8,128)(2,1)}, bf16[128,896]{1,0:T(8,128)(2,1)S(1)}, u32[]{:S(2)}, u32[]{:S(2)}) collective-permute-start(bf16[128,896]{1,0:T(8,128)(2,1)} %get-tuple-element.25), channel_id=1, source_target_pairs={{0,3},{1,2},{2,1},{3,0},{4,7},{5,6},{6,5},{7,4},{8,11},{9,10},{10,... | collective-permute-start | bytes 688136 | tf_op jit(solution)/shard_map/ppermute | solution.py:309
  35.2 21.5 %collective-permute-start.4 = (bf16[2,56,1024]{2,1,0:T(8,128)(2,1)S(1)}, bf16[2,56,1024]{2,1,0:T(8,128)(2,1)S(1)}, u32[]{:S(2)}, u32[]{:S(2)}) collective-permute-start(bf16[2,56,1024]{2,1,0:T(8,128)(2,1)S(1)} %get-tuple-element.32), channel_id=1, source_target_pairs={{0,64},{64,0},{1,65},{65,1},{2,66},{66,2},{3,67},{67,3},{4,68},{68... | collective-permute-start | bytes 688136 | tf_op jit(solution)/shard_map/ppermute | solution.py:297
  42.3 28.4 %all-to-all-start = ((bf16[8,16,512]{2,1,0:T(8,128)(2,1)}), bf16[8,16,512]{2,1,0:T(8,128)(2,1)S(1)}, u32[]{:S(2)}, u32[]{:S(2)}) async-start(bf16[8,16,512]{2,1,0:T(8,128)(2,1)} %shard_map.119.refs_1_), calls=%async_computation | async-start | bytes 262144 | tf_op jit(solution)/shard_map/all_to_all | solution.py:387
  49.3 18.9 %collective-permute-start.8 = (bf16[256,1152]{1,0:T(8,128)(2,1)S(1)}, bf16[256,1152]{1,0:T(8,128)(2,1)S(1)}, u32[]{:S(2)}, u32[]{:S(2)}) collective-permute-start(bf16[256,1152]{1,0:T(8,128)(2,1)S(1)} %get-tuple-element.21), channel_id=1, source_target_pairs={{0,1},{1,2},{2,3},{3,4},{4,5},{5,6},{6,7},{7,0},{8,9},{9,10},{10,1... | collective-permute-start | bytes 1769480 | tf_op jit(solution)/shard_map/ppermute | solution.py:297
  52.7 15.5 %collective-permute-start.9 = (bf16[256,1152]{1,0:T(8,128)(2,1)S(1)}, bf16[256,1152]{1,0:T(8,128)(2,1)S(1)}, u32[]{:S(2)}, u32[]{:S(2)}) collective-permute-start(bf16[256,1152]{1,0:T(8,128)(2,1)S(1)} %get-tuple-element.22), channel_id=1, source_target_pairs={{0,7},{1,0},{2,1},{3,2},{4,3},{5,4},{6,5},{7,6},{8,15},{9,8},{10,9... | collective-permute-start | bytes 1769480 | tf_op jit(solution)/shard_map/ppermute | solution.py:297
  55.9 12.3 %copy-start.1 = (bf16[1,3584,128]{2,1,0:T(8,128)(2,1)S(1)}, bf16[1,3584,128]{2,1,0:T(8,128)(2,1)}, u32[]{:S(2)}) copy-start(bf16[1,3584,128]{2,1,0:T(8,128)(2,1)} %param.20) | copy-start | bytes 2752516
  56.7 11.6 %copy-start = (bf16[1,3584,128]{2,1,0:T(8,128)(2,1)S(1)}, bf16[1,3584,128]{2,1,0:T(8,128)(2,1)}, u32[]{:S(2)}) copy-start(bf16[1,3584,128]{2,1,0:T(8,128)(2,1)} %param.19) | copy-start | bytes 2752516
  56.7 40.4 %collective-permute-start.5 = (bf16[2,2,56,1024]{3,2,1,0:T(8,128)(2,1)S(1)}, bf16[2,2,56,1024]{3,2,1,0:T(8,128)(2,1)S(1)}, u32[]{:S(2)}, u32[]{:S(2)}) collective-permute-start(bf16[2,2,56,1024]{3,2,1,0:T(8,128)(2,1)S(1)} %pad_maximum_fusion.refs_4_), channel_id=1, source_target_pairs={{0,128},{128,256},{256,384},{384,0},{1,129},{129,257},{257,385},{3... | collective-permute-start | bytes 1376264 | tf_op jit(solution)/shard_map/ppermute | solution.py:297
  60.0 42.2 %collective-permute-start.6 = (bf16[2,2,56,1024]{3,2,1,0:T(8,128)(2,1)S(1)}, bf16[2,2,56,1024]{3,2,1,0:T(8,128)(2,1)S(1)}, u32[]{:S(2)}, u32[]{:S(2)}) collective-permute-start(bf16[2,2,56,1024]{3,2,1,0:T(8,128)(2,1)S(1)} %pad_maximum_fusion.refs_4_), channel_id=1, source_target_pairs={{0,256},{128,384},{256,0},{384,128},{1,257},{129,385},{257,1},{385... | collective-permute-start | bytes 1376264 | tf_op jit(solution)/shard_map/ppermute | solution.py:297
  64.5 37.7 %collective-permute-start.7 = (bf16[2,2,56,1024]{3,2,1,0:T(8,128)(2,1)S(1)}, bf16[2,2,56,1024]{3,2,1,0:T(8,128)(2,1)S(1)}, u32[]{:S(2)}, u32[]{:S(2)}) collective-permute-start(bf16[2,2,56,1024]{3,2,1,0:T(8,128)(2,1)S(1)} %pad_maximum_fusion.refs_4_), channel_id=1, source_target_pairs={{0,384},{128,0},{256,128},{384,256},{1,385},{129,1},{257,129},{385... | collective-permute-start | bytes 1376264 | tf_op jit(solution)/shard_map/ppermute | solution.py:297
  70.7 13.0 %all-to-all-start.3 = ((bf16[4,256,128]{2,1,0:T(8,128)(2,1)}), bf16[4,256,128]{2,1,0:T(8,128)(2,1)S(1)}, u32[]{:S(2)}, u32[]{:S(2)}) async-start(bf16[4,256,128]{2,1,0:T(8,128)(2,1)} %get-tuple-element.26), calls=%async_computation.3 | async-start | bytes 524288 | tf_op jit(solution)/shard_map/all_to_all | solution.py:407
  79.2 23.0 %collective-permute-start = (bf16[16,1024]{1,0:T(8,128)(2,1)S(1)}, bf16[16,1024]{1,0:T(8,128)(2,1)S(1)}, u32[]{:S(2)}, u32[]{:S(2)}) collective-permute-start(bf16[16,1024]{1,0:T(8,128)(2,1)S(1)} %shard_map.120.refs_0_), channel_id=1, source_target_pairs={{0,16},{16,0},{32,48},{48,32},{1,17},{17,1},{33,49},{49,33},{2,18}... | collective-permute-start | bytes 98312 | tf_op jit(solution)/shard_map/ppermute | solution.py:309
  81.4 20.8 %collective-permute-start.1 = (bf16[16,1024]{1,0:T(8,128)(2,1)S(1)}, bf16[16,1024]{1,0:T(8,128)(2,1)S(1)}, u32[]{:S(2)}, u32[]{:S(2)}) collective-permute-start(bf16[16,1024]{1,0:T(8,128)(2,1)S(1)} %shard_map.120.refs_0_), channel_id=1, source_target_pairs={{0,32},{16,48},{32,0},{48,16},{1,33},{17,49},{33,1},{49,17},{2,34}... | collective-permute-start | bytes 98312 | tf_op jit(solution)/shard_map/ppermute | solution.py:309
  85.5 28.7 %all-to-all-start.4 = ((bf16[64,4,1024]{2,1,0:T(4,128)(2,1)}), bf16[64,4,1024]{2,1,0:T(4,128)(2,1)S(1)}, u32[]{:S(2)}, u32[]{:S(2)}) async-start(bf16[64,4,1024]{2,1,0:T(4,128)(2,1)} %shard_map.128), calls=%async_computation.4 | async-start | bytes 1048576 | tf_op jit(solution)/shard_map/all_to_all | solution.py:441
  97.1 13.9 %collective-permute-start.2 = (bf16[16,1024]{1,0:T(8,128)(2,1)S(1)}, bf16[16,1024]{1,0:T(8,128)(2,1)S(1)}, u32[]{:S(2)}, u32[]{:S(2)}) collective-permute-start(bf16[16,1024]{1,0:T(8,128)(2,1)S(1)} %shard_map.120.refs_0_), channel_id=1, source_target_pairs={{0,48},{16,32},{32,16},{48,0},{1,49},{17,33},{33,17},{49,1},{2,50}... | collective-permute-start | bytes 98312 | tf_op jit(solution)/shard_map/ppermute | solution.py:309
  114.3 16.9 %all-to-all-start.1 = ((bf16[32,16,128]{2,1,0:T(8,128)(2,1)}), bf16[32,16,128]{2,1,0:T(8,128)(2,1)S(1)}, u32[]{:S(2)}, u32[]{:S(2)}) async-start(bf16[32,16,128]{2,1,0:T(8,128)(2,1)} %shard_map.122), calls=%async_computation.1 | async-start | bytes 262144 | tf_op jit(solution)/shard_map/all_to_all | solution.py:430
  123.3 8.9 %collective-permute-start.13 = (f32[16,448]{1,0:T(8,128)S(1)}, f32[16,448]{1,0:T(8,128)S(1)}, u32[]{:S(2)}, u32[]{:S(2)}) collective-permute-start(f32[16,448]{1,0:T(8,128)S(1)} %get-tuple-element.30), channel_id=1, source_target_pairs={{0,4},{1,5},{2,6},{3,7},{4,0},{5,1},{6,2},{7,3},{8,12},{9,13},{10,... | collective-permute-start | bytes 86024 | tf_op jit(solution)/shard_map/ppermute | solution.py:309
  (11 other events, 58.6 us)

commit v10 on v9

--- a/solution.py
+++ b/solution.py
@@ -77,7 +77,7 @@
     return lax.broadcasted_iota(jnp.int32, shape, 0), lax.broadcasted_iota(jnp.int32, shape, 1)
 
 
-def prepare(hidden_ref, gain_ref, ids_ref, send_ref, place_ref):
+def prepare(hidden_ref, gain_ref, ids_ref, send_ref, place_ref, own_ref):
     values = hidden_ref[...].astype(F32)
     factor = lax.rsqrt(jnp.mean(values * values, axis=-1, keepdims=True) + EPSILON)
     gain = gain_ref[...].astype(F32).reshape(1, values.shape[1])
@@ -85,12 +85,16 @@
     width = values.shape[1] // 8
     pad = jnp.zeros((values.shape[0], send_ref.shape[2] - 3 * width), F32)
     sent = jnp.zeros((values.shape[0], send_ref.shape[2]), F32)
+    own = jnp.zeros((values.shape[0], width), F32)
     for s in range(8):
+        here = lax.axis_index("y") == s
+        own = jnp.where(here, values[:, s * width : (s + 1) * width], own)
         taken = [
             normalized[:, (s + k) % 8 * width : ((s + k) % 8 + 1) * width] for k in HELD
         ]
         taken = jnp.concatenate([*taken, pad], axis=1)
-        sent = jnp.where(lax.axis_index("y") == s, taken, sent)
+        sent = jnp.where(here, taken, sent)
+    own_ref[...] = own
     normalized = sent.astype(BF16)
     slots, rows = place_ref.shape
     slot = lax.broadcasted_iota(jnp.int32, (slots, rows), 0)
@@ -139,17 +143,15 @@
 
 
 def split_down(w_down_ref, *out_refs):
-    group = len(out_refs)
     width = out_refs[0].shape[1] // 2
-    for s in range(group):
-        for k in range(group):
-
-            @pl.when(lax.axis_index("y") % group ^ k == s)
-            def _(s=s, k=k):
-                for half in range(2):
-                    first = (half * group + s) * width
+    for d in range(8):
+        for k in range(len(out_refs)):
+
+            @pl.when(lax.axis_index("y") ^ k == d)
+            def _(d=d, k=k):
+                for half, s in enumerate((d, 7 - d)):
                     out_refs[k][:, half * width : (half + 1) * width] = w_down_ref[
-                        :, first : first + width
+                        :, s * width : (s + 1) * width
                     ]
 
 
@@ -270,24 +272,23 @@
     merged = lax.dot_general(upper, parts, TN, preferred_element_type=F32) + lax.dot_general(
         lower, parts, TN, preferred_element_type=F32
     )
-    first = lax.axis_index("y") < 4
-    near, far = merged[:, :width], merged[:, width:]
-    keep_ref[...] = own_ref[...].astype(F32) + jnp.where(first, near, far)
-    pass_ref[...] = jnp.where(first, far, near)
+    keep_ref[...] = own_ref[...] + merged[:, :width]
+    pass_ref[...] = merged[:, width:]
 
 
 def add_attention(parts_ref, keep_ref, passed_ref, out_ref):
     rows, width = out_ref.shape
     blocks = 4
     slices = parts_ref.shape[0] // blocks
-    attn = jnp.concatenate(
-        [
-            jnp.sum(parts_ref[b * slices : (b + 1) * slices].astype(F32), axis=0)[
-                :, : width // blocks
-            ]
-            for b in range(blocks)
-        ],
-        axis=1,
+    sums = [
+        jnp.sum(parts_ref[b * slices : (b + 1) * slices].astype(F32), axis=0)[
+            :, : width // blocks
+        ]
+        for b in range(blocks)
+    ]
+    straight = lax.axis_index("y") % 2 == lax.axis_index("zh")
+    attn = jnp.where(
+        straight, jnp.concatenate(sums, axis=1), jnp.concatenate(sums[::-1], axis=1)
     )
     out_ref[...] = (keep_ref[...] + passed_ref[...] + attn).astype(BF16)
 
@@ -307,6 +308,11 @@
 
 def swap(value, axis, k):
     return lax.ppermute(value, axis, [(i, i ^ k) for i in range(lax.axis_size(axis))])
+
+
+def mirror(value, axis):
+    size = lax.axis_size(axis)
+    return lax.ppermute(value, axis, [(i, size - 1 - i) for i in range(size)])
 
 
 def trade(value, axis):
@@ -335,18 +341,20 @@
     hidden_units = w_gate.shape[2]
     heads, latent, value_width = w_uv.shape
     out_cols, depth = w_out.shape[1], w_out.shape[0]
-    tp = lax.axis_index("y")
-
     router_rows = router.reshape(tp_size, width).astype(F32)
 
-    send, place = kernel_call(
+    send, place, own = kernel_call(
         prepare,
-        [((ep_size, SLOTS, 3 * width + 64), BF16), ((slots, rows), F32)],
+        [
+            ((ep_size, SLOTS, 3 * width + 64), BF16),
+            ((slots, rows), F32),
+            ((rows, width), F32),
+        ],
         hidden,
         norm_gain,
         expert_ids.T,
         load=(0, 1, 2),
-        store=(0, 1),
+        store=(0, 1, 2),
         vmem=60,
     )
     named_rows = lax.all_to_all(send, EP, 0, 0, tiled=True)
@@ -386,7 +394,7 @@
 
     contexts = lax.all_to_all(context, "y", 0, 0, tiled=True)
     out_pair = pair_up(w_out.T, "c")
-    out_other = shift(out_pair, "zh", 1)
+    out_other = mirror(out_pair, ("zh", "zl"))
 
     (crossed,) = kernel_call(mark, [((8, 128), F32)], after=(out_other,))
 
@@ -439,11 +447,10 @@
         after=(contexts,),
     )
     back = lax.all_to_all(back, EP, 0, 0, tiled=True)
-    own = lax.dynamic_slice_in_dim(hidden, tp * width, width, 1)
     keep, passed = kernel_call(
-        merge_experts, [((rows, width), F32)] * 2, back, place, own, load=(1,)
-    )
-    passed = swap(passed, "y", GROUP)
+        merge_experts, [((rows, width), F32)] * 2, back, place, own, load=(1, 2)
+    )
+    passed = mirror(passed, "y")
     (out,) = kernel_call(
         add_attention, [((rows, width), BF16)], attn_parts, keep, passed
     )

time: 134 us -> 131 us (0.978)
  starting transfers between devices: 99.2 us -> 94.5 us
  waiting for transfers between devices: 13.2 us -> 15.8 us
    ppermute x0 -> x2, starting transfers between devices: none -> 8.77 us  [mirror(): return lax.ppermute(value, axis, [(i, size - 1 - i) for i in range(size)])]
    ppermute x7 -> x6, starting transfers between devices: 26.7 us -> 19.7 us  [shift(): return lax.ppermute(value, axis, [(i, (i + k) % size) for i in range(size)])]
    ppermute x7 -> x6, starting transfers between devices: 25.9 us -> 21.5 us  [swap(): lax.ppermute(value, axis, [(i, i ^ k) for i in range(lax.axis_size(axis))])]
    all_to_all x1, waiting for transfers between devices: 0.82 us -> 4.29 us  [on_device(): attn_parts = lax.all_to_all(attn_parts, ('zl', 'y'), 0, 0, tiled=True)]
    all_to_all x1, starting transfers between devices: 11.5 us -> 9.78 us  [on_device(): back = lax.all_to_all(back, EP, 0, 0, tiled=True)]
    ppermute x7 -> x6, waiting for transfers between devices: 9.75 us -> 8.76 us  [swap(): lax.ppermute(value, axis, [(i, i ^ k) for i in range(lax.axis_size(axis))])]
  transfers between devices with their start and end apart: 19 -> 19, of which waited for: 5 -> 4; matrix products, arithmetic and copies ran while one was open for 1% -> 1% of each run, Pallas kernels for 9% -> 9%
where the time goes in v10:
time: 131 us; the launch traced here: 130 us
  starting transfers between devices  94.5 us (72%)
  waiting for transfers between devices  15.8 us (12%)
  Pallas kernels  15.6 us (12%)
  local copies, waits for them, and re-layouts  2.72 us (2%)
    ppermute x6, starting transfers between devices, swap(): lax.ppermute(value, axis, [(i, i ^ k) for i in range(lax.axis_size(axis))])  21.5 us
    ppermute x6, starting transfers between devices, shift(): return lax.ppermute(value, axis, [(i, (i + k) % size) for i in range(size)])  19.7 us
    pallas_call x13, Pallas kernels, kernel_call(): pl.pallas_call(kernel, out_shape=tuple(shapes), in_specs=[place(n, load)...  15.6 us
    all_to_all x1, starting transfers between devices, on_device(): named_rows = lax.all_to_all(send, EP, 0, 0, tiled=True)  15 us
    all_to_all x1, starting transfers between devices, on_device(): back = lax.all_to_all(back, EP, 0, 0, tiled=True)  9.78 us
    ppermute x2, starting transfers between devices, mirror(): return lax.ppermute(value, axis, [(i, size - 1 - i) for i in range(size)])  8.77 us
    ppermute x6, waiting for transfers between devices, swap(): lax.ppermute(value, axis, [(i, i ^ k) for i in range(lax.axis_size(axis))])  8.76 us
    all_to_all x1, starting transfers between devices, on_device(): attn_parts = lax.all_to_all(attn_parts, ('zl', 'y'), 0, 0, tiled=True)  7.52 us
  transfers between devices with their start and end apart: 19, of which 4 were waited for; matrix products, arithmetic and copies ran while one was open for 1% of the time, Pallas kernels for 9%

profile of v10, /device:TPU:1, one launch (start us, length us, event | category | flops | bytes accessed | tf_op | source)
XLA Modules:
  0.0 130.1 jit_solution(1523380665311034867)
XLA Ops:
  0.0 2.6 %shard_map.118 = (bf16[64,4,1408]{2,1,0:T(4,128)(2,1)}, f32[256,16]{1,0:T(8,128)}, f32[16,448]{1,0:T(8,128)}) custom-call(bf16[16,3584]{1,0:T(8,128)(2,1)} %refs_0_.2, bf16[3584]{0:T(1024)(128)(2,1)} %refs_1_.3, s32[8,16]{1,0:T(8,128)} %bitcast.19), custom_call_target="tpu_custom_call" | custom-call | bytes 122368 | tf_op jit(solution)/shard_map/pallas_call | solution.py:60
  2.6 15.0 %all-to-all-start.2 = ((bf16[64,4,1408]{2,1,0:T(4,128)(2,1)}), bf16[64,4,1408]{2,1,0:T(4,128)(2,1)S(1)}, u32[]{:S(2)}, u32[]{:S(2)}) async-start(bf16[64,4,1408]{2,1,0:T(4,128)(2,1)} %get-tuple-element.20), calls=%async_computation.2 | async-start | bytes 1441792 | tf_op jit(solution)/shard_map/all_to_all | solution.py:360
  17.6 2.4 %collective-permute-start.3 = (bf16[56,1024]{1,0:T(8,128)(2,1)S(1)}, bf16[56,1024]{1,0:T(8,128)(2,1)}, u32[]{:S(2)}, u32[]{:S(2)}) collective-permute-start(bf16[56,1024]{1,0:T(8,128)(2,1)S(1)} %bitcast.17), channel_id=1, source_target_pairs={{0,8},{8,0},{1,9},{9,1},{2,10},{10,2},{3,11},{11,3},{4,12},{12,4},... | collective-permute-start | bytes 344072 | tf_op jit(solution)/shard_map/ppermute | solution.py:298
  21.9 3.2 %collective-permute-start.10 = (bf16[128,896]{1,0:T(8,128)(2,1)}, bf16[128,896]{1,0:T(8,128)(2,1)S(1)}, u32[]{:S(2)}, u32[]{:S(2)}) collective-permute-start(bf16[128,896]{1,0:T(8,128)(2,1)} %get-tuple-element.24), channel_id=1, source_target_pairs={{0,1},{1,0},{2,3},{3,2},{4,5},{5,4},{6,7},{7,6},{8,9},{9,8},{10,11... | collective-permute-start | bytes 688136 | tf_op jit(solution)/shard_map/ppermute | solution.py:310
  25.1 4.2 %collective-permute-start.11 = (bf16[128,896]{1,0:T(8,128)(2,1)}, bf16[128,896]{1,0:T(8,128)(2,1)S(1)}, u32[]{:S(2)}, u32[]{:S(2)}) collective-permute-start(bf16[128,896]{1,0:T(8,128)(2,1)} %get-tuple-element.25), channel_id=1, source_target_pairs={{0,2},{1,3},{2,0},{3,1},{4,6},{5,7},{6,4},{7,5},{8,10},{9,11},{10,... | collective-permute-start | bytes 688136 | tf_op jit(solution)/shard_map/ppermute | solution.py:310
  29.3 1.9 %collective-permute-start.12 = (bf16[128,896]{1,0:T(8,128)(2,1)}, bf16[128,896]{1,0:T(8,128)(2,1)S(1)}, u32[]{:S(2)}, u32[]{:S(2)}) collective-permute-start(bf16[128,896]{1,0:T(8,128)(2,1)} %get-tuple-element.26), channel_id=1, source_target_pairs={{0,3},{1,2},{2,1},{3,0},{4,7},{5,6},{6,5},{7,4},{8,11},{9,10},{10,... | collective-permute-start | bytes 688136 | tf_op jit(solution)/shard_map/ppermute | solution.py:310
  32.1 2.2 %shard_map.119.refs_1_ = bf16[8,16,512]{2,1,0:T(8,128)(2,1)} custom-call(s32[2]{0:T(128)S(1)} %copy-done.13, bf16[2,64,576]{2,1,0:T(8,128)(2,1)S(1)} %copy-done.11, bf16[2,576,384]{2,1,0:T(8,128)(2,1)S(1)} %bitcast.16, f32[256,16]{1,0:T(8,128)S(1)} %copy-done.4), custom_call_target="tpu_custom_call" | custom-call | bytes 1032200 | tf_op jit(solution)/shard_map/pallas_call | solution.py:60
  35.2 4.4 %collective-permute-start.4 = (bf16[2,56,1024]{2,1,0:T(8,128)(2,1)S(1)}, bf16[2,56,1024]{2,1,0:T(8,128)(2,1)S(1)}, u32[]{:S(2)}, u32[]{:S(2)}) collective-permute-start(bf16[2,56,1024]{2,1,0:T(8,128)(2,1)S(1)} %get-tuple-element.34), channel_id=1, source_target_pairs={{0,112},{16,96},{32,80},{48,64},{64,48},{80,32},{96,16},{112,0},{1... | collective-permute-start | bytes 688136 | tf_op jit(solution)/shard_map/ppermute | solution.py:315
  39.7 6.8 %all-to-all-start = ((bf16[8,16,512]{2,1,0:T(8,128)(2,1)}), bf16[8,16,512]{2,1,0:T(8,128)(2,1)S(1)}, u32[]{:S(2)}, u32[]{:S(2)}) async-start(bf16[8,16,512]{2,1,0:T(8,128)(2,1)} %shard_map.119.refs_1_), calls=%async_computation | async-start | bytes 262144 | tf_op jit(solution)/shard_map/all_to_all | solution.py:395
  46.7 3.4 %collective-permute-start.8 = (bf16[256,1152]{1,0:T(8,128)(2,1)S(1)}, bf16[256,1152]{1,0:T(8,128)(2,1)S(1)}, u32[]{:S(2)}, u32[]{:S(2)}) collective-permute-start(bf16[256,1152]{1,0:T(8,128)(2,1)S(1)} %get-tuple-element.22), channel_id=1, source_target_pairs={{0,1},{1,2},{2,3},{3,4},{4,5},{5,6},{6,7},{7,0},{8,9},{9,10},{10,1... | collective-permute-start | bytes 1769480 | tf_op jit(solution)/shard_map/ppermute | solution.py:298
  50.1 3.1 %collective-permute-start.9 = (bf16[256,1152]{1,0:T(8,128)(2,1)S(1)}, bf16[256,1152]{1,0:T(8,128)(2,1)S(1)}, u32[]{:S(2)}, u32[]{:S(2)}) collective-permute-start(bf16[256,1152]{1,0:T(8,128)(2,1)S(1)} %get-tuple-element.23), channel_id=1, source_target_pairs={{0,7},{1,0},{2,1},{3,2},{4,3},{5,4},{6,5},{7,6},{8,15},{9,8},{10,9... | collective-permute-start | bytes 1769480 | tf_op jit(solution)/shard_map/ppermute | solution.py:298
  54.1 3.3 %collective-permute-start.5 = (bf16[2,2,56,1024]{3,2,1,0:T(8,128)(2,1)S(1)}, bf16[2,2,56,1024]{3,2,1,0:T(8,128)(2,1)S(1)}, u32[]{:S(2)}, u32[]{:S(2)}) collective-permute-start(bf16[2,2,56,1024]{3,2,1,0:T(8,128)(2,1)S(1)} %pad_maximum_fusion.refs_4_), channel_id=1, source_target_pairs={{0,128},{128,256},{256,384},{384,0},{1,129},{129,257},{257,385},{3... | collective-permute-start | bytes 1376264 | tf_op jit(solution)/shard_map/ppermute | solution.py:298
  57.4 4.5 %collective-permute-start.6 = (bf16[2,2,56,1024]{3,2,1,0:T(8,128)(2,1)S(1)}, bf16[2,2,56,1024]{3,2,1,0:T(8,128)(2,1)S(1)}, u32[]{:S(2)}, u32[]{:S(2)}) collective-permute-start(bf16[2,2,56,1024]{3,2,1,0:T(8,128)(2,1)S(1)} %pad_maximum_fusion.refs_4_), channel_id=1, source_target_pairs={{0,256},{128,384},{256,0},{384,128},{1,257},{129,385},{257,1},{385... | collective-permute-start | bytes 1376264 | tf_op jit(solution)/shard_map/ppermute | solution.py:298
  61.9 3.0 %collective-permute-start.7 = (bf16[2,2,56,1024]{3,2,1,0:T(8,128)(2,1)S(1)}, bf16[2,2,56,1024]{3,2,1,0:T(8,128)(2,1)S(1)}, u32[]{:S(2)}, u32[]{:S(2)}) collective-permute-start(bf16[2,2,56,1024]{3,2,1,0:T(8,128)(2,1)S(1)} %pad_maximum_fusion.refs_4_), channel_id=1, source_target_pairs={{0,384},{128,0},{256,128},{384,256},{1,385},{129,1},{257,129},{385... | collective-permute-start | bytes 1376264 | tf_op jit(solution)/shard_map/ppermute | solution.py:298
  65.8 2.4 %shard_map.127 = (bf16[4,256,128]{2,1,0:T(8,128)(2,1)}, bf16[256,128]{1,0:T(8,128)(2,1)S(1)}) custom-call(bf16[256,1408]{1,0:T(8,128)(2,1)S(1)} %get-tuple-element.21.refs_0_, bf16[256,1152]{1,0:T(8,128)(2,1)S(1)} %collective-permute-done.8.refs_1_, bf16[256,1152]{1,0:T(8,128)(2,1)S(1)} %collective-permute-done.9.refs_2_, bf16[3584,128]{1,0:T(8,128)(2,1)S(1)} %bitcast.12, ...), custom_call_target="tpu_custom_call" | custom-call | bytes 3749888 | tf_op jit(solution)/shard_map/pallas_call | solution.py:60
  68.3 5.5 %all-to-all-start.3 = ((bf16[4,256,128]{2,1,0:T(8,128)(2,1)}), bf16[4,256,128]{2,1,0:T(8,128)(2,1)S(1)}, u32[]{:S(2)}, u32[]{:S(2)}) async-start(bf16[4,256,128]{2,1,0:T(8,128)(2,1)} %get-tuple-element.27), calls=%async_computation.3 | async-start | bytes 524288 | tf_op jit(solution)/shard_map/all_to_all | solution.py:415
  76.6 4.0 %collective-permute-start = (bf16[16,1024]{1,0:T(8,128)(2,1)S(1)}, bf16[16,1024]{1,0:T(8,128)(2,1)S(1)}, u32[]{:S(2)}, u32[]{:S(2)}) collective-permute-start(bf16[16,1024]{1,0:T(8,128)(2,1)S(1)} %shard_map.120.refs_0_), channel_id=1, source_target_pairs={{0,16},{16,0},{32,48},{48,32},{1,17},{17,1},{33,49},{49,33},{2,18}... | collective-permute-start | bytes 98312 | tf_op jit(solution)/shard_map/ppermute | solution.py:310
  80.6 3.1 %collective-permute-start.1 = (bf16[16,1024]{1,0:T(8,128)(2,1)S(1)}, bf16[16,1024]{1,0:T(8,128)(2,1)S(1)}, u32[]{:S(2)}, u32[]{:S(2)}) collective-permute-start(bf16[16,1024]{1,0:T(8,128)(2,1)S(1)} %shard_map.120.refs_0_), channel_id=1, source_target_pairs={{0,32},{16,48},{32,0},{48,16},{1,33},{17,49},{33,1},{49,17},{2,34}... | collective-permute-start | bytes 98312 | tf_op jit(solution)/shard_map/ppermute | solution.py:310
  85.6 9.8 %all-to-all-start.4 = ((bf16[64,4,1024]{2,1,0:T(4,128)(2,1)}), bf16[64,4,1024]{2,1,0:T(4,128)(2,1)S(1)}, u32[]{:S(2)}, u32[]{:S(2)}) async-start(bf16[64,4,1024]{2,1,0:T(4,128)(2,1)} %shard_map.128), calls=%async_computation.4 | async-start | bytes 1048576 | tf_op jit(solution)/shard_map/all_to_all | solution.py:449
  95.4 5.1 %collective-permute-start.2 = (bf16[16,1024]{1,0:T(8,128)(2,1)S(1)}, bf16[16,1024]{1,0:T(8,128)(2,1)S(1)}, u32[]{:S(2)}, u32[]{:S(2)}) collective-permute-start(bf16[16,1024]{1,0:T(8,128)(2,1)S(1)} %shard_map.120.refs_0_), channel_id=1, source_target_pairs={{0,48},{16,32},{32,16},{48,0},{1,49},{17,33},{33,17},{49,1},{2,50}... | collective-permute-start | bytes 98312 | tf_op jit(solution)/shard_map/ppermute | solution.py:310
  100.5 8.8 %collective-permute-done.2.refs_3_ = bf16[16,1024]{1,0:T(8,128)(2,1)S(1)} collective-permute-done((bf16[16,1024]{1,0:T(8,128)(2,1)S(1)}, bf16[16,1024]{1,0:T(8,128)(2,1)S(1)}, u32[]{:S(2)}, u32[]{:S(2)}) %collective-permute-start.2) | collective-permute-done | bytes 32800 | tf_op jit(solution)/shard_map/ppermute | solution.py:310
  112.5 7.5 %all-to-all-start.1 = ((bf16[32,16,128]{2,1,0:T(8,128)(2,1)}), bf16[32,16,128]{2,1,0:T(8,128)(2,1)S(1)}, u32[]{:S(2)}, u32[]{:S(2)}) async-start(bf16[32,16,128]{2,1,0:T(8,128)(2,1)} %shard_map.122), calls=%async_computation.1 | async-start | bytes 262144 | tf_op jit(solution)/shard_map/all_to_all | solution.py:438
  120.8 4.4 %collective-permute-start.13 = (f32[16,448]{1,0:T(8,128)S(1)}, f32[16,448]{1,0:T(8,128)S(1)}, u32[]{:S(2)}, u32[]{:S(2)}) collective-permute-start(f32[16,448]{1,0:T(8,128)S(1)} %get-tuple-element.32), channel_id=1, source_target_pairs={{0,7},{1,6},{2,5},{3,4},{4,3},{5,2},{6,1},{7,0},{8,15},{9,14},{10,... | collective-permute-start | bytes 86024 | tf_op jit(solution)/shard_map/ppermute | solution.py:315
  125.2 4.3 %all-to-all-done.1.refs_0_ = bf16[32,16,128]{2,1,0:T(8,128)(2,1)S(1)} async-done(((bf16[32,16,128]{2,1,0:T(8,128)(2,1)}), bf16[32,16,128]{2,1,0:T(8,128)(2,1)S(1)}, u32[]{:S(2)}, u32[]{:S(2)}) %all-to-all-start.1) | async-done | bytes 131104 | tf_op jit(solution)/shard_map/all_to_all | solution.py:438
  (65 shorter events, 14.9 us)
Async XLA Ops:
  0.0 20.0 %copy-start.2 = (bf16[1,128,3584]{2,1,0:T(8,128)(2,1)S(1)}, bf16[1,128,3584]{2,1,0:T(8,128)(2,1)}, u32[]{:S(2)}) copy-start(bf16[1,128,3584]{2,1,0:T(8,128)(2,1)} %param.21) | copy-start | bytes 2752516
  0.0 17.6 %copy-start.15 = (bf16[1024,56]{0,1:T(8,128)(2,1)S(1)}, bf16[1024,56]{0,1:T(8,128)(2,1)}, u32[]{:S(2)}) copy-start(bf16[1024,56]{0,1:T(8,128)(2,1)} %param.23) | copy-start | bytes 344068
  2.6 28.8 %copy-start.3 = (bf16[2,384,576]{1,2,0:T(8,128)(2,1)S(1)}, bf16[2,384,576]{1,2,0:T(8,128)(2,1)}, u32[]{:S(2)}) copy-start(bf16[2,384,576]{1,2,0:T(8,128)(2,1)} %param.15) | copy-start | bytes 2654212
  2.6 37.0 %all-to-all-start.2 = ((bf16[64,4,1408]{2,1,0:T(4,128)(2,1)}), bf16[64,4,1408]{2,1,0:T(4,128)(2,1)S(1)}, u32[]{:S(2)}, u32[]{:S(2)}) async-start(bf16[64,4,1408]{2,1,0:T(4,128)(2,1)} %get-tuple-element.20), calls=%async_computation.2 | async-start | bytes 1441792 | tf_op jit(solution)/shard_map/all_to_all | solution.py:360
  17.6 16.7 %collective-permute-start.3 = (bf16[56,1024]{1,0:T(8,128)(2,1)S(1)}, bf16[56,1024]{1,0:T(8,128)(2,1)}, u32[]{:S(2)}, u32[]{:S(2)}) collective-permute-start(bf16[56,1024]{1,0:T(8,128)(2,1)S(1)} %bitcast.17), channel_id=1, source_target_pairs={{0,8},{8,0},{1,9},{9,1},{2,10},{10,2},{3,11},{11,3},{4,12},{12,4},... | collective-permute-start | bytes 344072 | tf_op jit(solution)/shard_map/ppermute | solution.py:298
  21.9 28.2 %collective-permute-start.10 = (bf16[128,896]{1,0:T(8,128)(2,1)}, bf16[128,896]{1,0:T(8,128)(2,1)S(1)}, u32[]{:S(2)}, u32[]{:S(2)}) collective-permute-start(bf16[128,896]{1,0:T(8,128)(2,1)} %get-tuple-element.24), channel_id=1, source_target_pairs={{0,1},{1,0},{2,3},{3,2},{4,5},{5,4},{6,7},{7,6},{8,9},{9,8},{10,11... | collective-permute-start | bytes 688136 | tf_op jit(solution)/shard_map/ppermute | solution.py:310
  25.1 28.1 %collective-permute-start.11 = (bf16[128,896]{1,0:T(8,128)(2,1)}, bf16[128,896]{1,0:T(8,128)(2,1)S(1)}, u32[]{:S(2)}, u32[]{:S(2)}) collective-permute-start(bf16[128,896]{1,0:T(8,128)(2,1)} %get-tuple-element.25), channel_id=1, source_target_pairs={{0,2},{1,3},{2,0},{3,1},{4,6},{5,7},{6,4},{7,5},{8,10},{9,11},{10,... | collective-permute-start | bytes 688136 | tf_op jit(solution)/shard_map/ppermute | solution.py:310
  29.3 23.9 %collective-permute-start.12 = (bf16[128,896]{1,0:T(8,128)(2,1)}, bf16[128,896]{1,0:T(8,128)(2,1)S(1)}, u32[]{:S(2)}, u32[]{:S(2)}) collective-permute-start(bf16[128,896]{1,0:T(8,128)(2,1)} %get-tuple-element.26), channel_id=1, source_target_pairs={{0,3},{1,2},{2,1},{3,0},{4,7},{5,6},{6,5},{7,4},{8,11},{9,10},{10,... | collective-permute-start | bytes 688136 | tf_op jit(solution)/shard_map/ppermute | solution.py:310
  35.2 18.8 %collective-permute-start.4 = (bf16[2,56,1024]{2,1,0:T(8,128)(2,1)S(1)}, bf16[2,56,1024]{2,1,0:T(8,128)(2,1)S(1)}, u32[]{:S(2)}, u32[]{:S(2)}) collective-permute-start(bf16[2,56,1024]{2,1,0:T(8,128)(2,1)S(1)} %get-tuple-element.34), channel_id=1, source_target_pairs={{0,112},{16,96},{32,80},{48,64},{64,48},{80,32},{96,16},{112,0},{1... | collective-permute-start | bytes 688136 | tf_op jit(solution)/shard_map/ppermute | solution.py:315
  39.7 28.6 %all-to-all-start = ((bf16[8,16,512]{2,1,0:T(8,128)(2,1)}), bf16[8,16,512]{2,1,0:T(8,128)(2,1)S(1)}, u32[]{:S(2)}, u32[]{:S(2)}) async-start(bf16[8,16,512]{2,1,0:T(8,128)(2,1)} %shard_map.119.refs_1_), calls=%async_computation | async-start | bytes 262144 | tf_op jit(solution)/shard_map/all_to_all | solution.py:395
  46.7 19.1 %collective-permute-start.8 = (bf16[256,1152]{1,0:T(8,128)(2,1)S(1)}, bf16[256,1152]{1,0:T(8,128)(2,1)S(1)}, u32[]{:S(2)}, u32[]{:S(2)}) collective-permute-start(bf16[256,1152]{1,0:T(8,128)(2,1)S(1)} %get-tuple-element.22), channel_id=1, source_target_pairs={{0,1},{1,2},{2,3},{3,4},{4,5},{5,6},{6,7},{7,0},{8,9},{9,10},{10,1... | collective-permute-start | bytes 1769480 | tf_op jit(solution)/shard_map/ppermute | solution.py:298
  50.1 15.7 %collective-permute-start.9 = (bf16[256,1152]{1,0:T(8,128)(2,1)S(1)}, bf16[256,1152]{1,0:T(8,128)(2,1)S(1)}, u32[]{:S(2)}, u32[]{:S(2)}) collective-permute-start(bf16[256,1152]{1,0:T(8,128)(2,1)S(1)} %get-tuple-element.23), channel_id=1, source_target_pairs={{0,7},{1,0},{2,1},{3,2},{4,3},{5,4},{6,5},{7,6},{8,15},{9,8},{10,9... | collective-permute-start | bytes 1769480 | tf_op jit(solution)/shard_map/ppermute | solution.py:298
  53.3 12.6 %copy-start.1 = (bf16[1,3584,128]{2,1,0:T(8,128)(2,1)S(1)}, bf16[1,3584,128]{2,1,0:T(8,128)(2,1)}, u32[]{:S(2)}) copy-start(bf16[1,3584,128]{2,1,0:T(8,128)(2,1)} %param.20) | copy-start | bytes 2752516
  54.0 11.8 %copy-start = (bf16[1,3584,128]{2,1,0:T(8,128)(2,1)S(1)}, bf16[1,3584,128]{2,1,0:T(8,128)(2,1)}, u32[]{:S(2)}) copy-start(bf16[1,3584,128]{2,1,0:T(8,128)(2,1)} %param.19) | copy-start | bytes 2752516
  54.1 41.3 %collective-permute-start.5 = (bf16[2,2,56,1024]{3,2,1,0:T(8,128)(2,1)S(1)}, bf16[2,2,56,1024]{3,2,1,0:T(8,128)(2,1)S(1)}, u32[]{:S(2)}, u32[]{:S(2)}) collective-permute-start(bf16[2,2,56,1024]{3,2,1,0:T(8,128)(2,1)S(1)} %pad_maximum_fusion.refs_4_), channel_id=1, source_target_pairs={{0,128},{128,256},{256,384},{384,0},{1,129},{129,257},{257,385},{3... | collective-permute-start | bytes 1376264 | tf_op jit(solution)/shard_map/ppermute | solution.py:298
  57.4 43.1 %collective-permute-start.6 = (bf16[2,2,56,1024]{3,2,1,0:T(8,128)(2,1)S(1)}, bf16[2,2,56,1024]{3,2,1,0:T(8,128)(2,1)S(1)}, u32[]{:S(2)}, u32[]{:S(2)}) collective-permute-start(bf16[2,2,56,1024]{3,2,1,0:T(8,128)(2,1)S(1)} %pad_maximum_fusion.refs_4_), channel_id=1, source_target_pairs={{0,256},{128,384},{256,0},{384,128},{1,257},{129,385},{257,1},{385... | collective-permute-start | bytes 1376264 | tf_op jit(solution)/shard_map/ppermute | solution.py:298
  61.9 38.6 %collective-permute-start.7 = (bf16[2,2,56,1024]{3,2,1,0:T(8,128)(2,1)S(1)}, bf16[2,2,56,1024]{3,2,1,0:T(8,128)(2,1)S(1)}, u32[]{:S(2)}, u32[]{:S(2)}) collective-permute-start(bf16[2,2,56,1024]{3,2,1,0:T(8,128)(2,1)S(1)} %pad_maximum_fusion.refs_4_), channel_id=1, source_target_pairs={{0,384},{128,0},{256,128},{384,256},{1,385},{129,1},{257,129},{385... | collective-permute-start | bytes 1376264 | tf_op jit(solution)/shard_map/ppermute | solution.py:298
  68.3 15.4 %all-to-all-start.3 = ((bf16[4,256,128]{2,1,0:T(8,128)(2,1)}), bf16[4,256,128]{2,1,0:T(8,128)(2,1)S(1)}, u32[]{:S(2)}, u32[]{:S(2)}) async-start(bf16[4,256,128]{2,1,0:T(8,128)(2,1)} %get-tuple-element.27), calls=%async_computation.3 | async-start | bytes 524288 | tf_op jit(solution)/shard_map/all_to_all | solution.py:415
  76.6 23.9 %collective-permute-start = (bf16[16,1024]{1,0:T(8,128)(2,1)S(1)}, bf16[16,1024]{1,0:T(8,128)(2,1)S(1)}, u32[]{:S(2)}, u32[]{:S(2)}) collective-permute-start(bf16[16,1024]{1,0:T(8,128)(2,1)S(1)} %shard_map.120.refs_0_), channel_id=1, source_target_pairs={{0,16},{16,0},{32,48},{48,32},{1,17},{17,1},{33,49},{49,33},{2,18}... | collective-permute-start | bytes 98312 | tf_op jit(solution)/shard_map/ppermute | solution.py:310
  80.6 20.0 %collective-permute-start.1 = (bf16[16,1024]{1,0:T(8,128)(2,1)S(1)}, bf16[16,1024]{1,0:T(8,128)(2,1)S(1)}, u32[]{:S(2)}, u32[]{:S(2)}) collective-permute-start(bf16[16,1024]{1,0:T(8,128)(2,1)S(1)} %shard_map.120.refs_0_), channel_id=1, source_target_pairs={{0,32},{16,48},{32,0},{48,16},{1,33},{17,49},{33,1},{49,17},{2,34}... | collective-permute-start | bytes 98312 | tf_op jit(solution)/shard_map/ppermute | solution.py:310
  85.6 27.0 %all-to-all-start.4 = ((bf16[64,4,1024]{2,1,0:T(4,128)(2,1)}), bf16[64,4,1024]{2,1,0:T(4,128)(2,1)S(1)}, u32[]{:S(2)}, u32[]{:S(2)}) async-start(bf16[64,4,1024]{2,1,0:T(4,128)(2,1)} %shard_map.128), calls=%async_computation.4 | async-start | bytes 1048576 | tf_op jit(solution)/shard_map/all_to_all | solution.py:449
  95.4 13.9 %collective-permute-start.2 = (bf16[16,1024]{1,0:T(8,128)(2,1)S(1)}, bf16[16,1024]{1,0:T(8,128)(2,1)S(1)}, u32[]{:S(2)}, u32[]{:S(2)}) collective-permute-start(bf16[16,1024]{1,0:T(8,128)(2,1)S(1)} %shard_map.120.refs_0_), channel_id=1, source_target_pairs={{0,48},{16,32},{32,16},{48,0},{1,49},{17,33},{33,17},{49,1},{2,50}... | collective-permute-start | bytes 98312 | tf_op jit(solution)/shard_map/ppermute | solution.py:310
  112.5 16.9 %all-to-all-start.1 = ((bf16[32,16,128]{2,1,0:T(8,128)(2,1)}), bf16[32,16,128]{2,1,0:T(8,128)(2,1)S(1)}, u32[]{:S(2)}, u32[]{:S(2)}) async-start(bf16[32,16,128]{2,1,0:T(8,128)(2,1)} %shard_map.122), calls=%async_computation.1 | async-start | bytes 262144 | tf_op jit(solution)/shard_map/all_to_all | solution.py:438
  120.8 8.7 %collective-permute-start.13 = (f32[16,448]{1,0:T(8,128)S(1)}, f32[16,448]{1,0:T(8,128)S(1)}, u32[]{:S(2)}, u32[]{:S(2)}) collective-permute-start(f32[16,448]{1,0:T(8,128)S(1)} %get-tuple-element.32), channel_id=1, source_target_pairs={{0,7},{1,6},{2,5},{3,4},{4,3},{5,2},{6,1},{7,0},{8,15},{9,14},{10,... | collective-permute-start | bytes 86024 | tf_op jit(solution)/shard_map/ppermute | solution.py:315
  (12 other events, 76.0 us)

commit v11 on v10

--- a/solution.py
+++ b/solution.py
@@ -142,6 +142,10 @@
         values_ref[:, h * width : (h + 1) * width] = mine
 
 
+def repeat(value_ref, out_ref):
+    out_ref[...] = value_ref[...]
+
+
 def split_down(w_down_ref, *out_refs):
     width = out_refs[0].shape[1] // 2
     for d in range(8):
@@ -424,19 +428,9 @@
         flops=10_000_000_000,
     )
 
-    all_values = trade(values, "zl")
     (gathered,) = kernel_call(
         mark, [((8, 128), F32)], after=out_weights[1:], flops=15_000_000_000
     )
-    (attn_parts,) = kernel_call(
-        project,
-        [((4 * tp_size, rows, 128), BF16)],
-        *all_values,
-        *out_weights,
-        after=(gathered,),
-    )
-    attn_parts = lax.all_to_all(attn_parts, ("zl", "y"), 0, 0, tiled=True)
-
     (back,) = kernel_call(
         lower_experts,
         [((ep_size, SLOTS, PADDED), BF16)],
@@ -446,6 +440,18 @@
         load=(1, 1 + GROUP),
         after=(contexts,),
     )
+    (again,) = kernel_call(repeat, [((rows, depth), BF16)], values, after=(back,))
+    all_values = [values, swap(values, "zl", 1)]
+    all_values += [swap(again, "zl", k) for k in (2, 3)]
+    (attn_parts,) = kernel_call(
+        project,
+        [((4 * tp_size, rows, 128), BF16)],
+        *all_values,
+        *out_weights,
+        after=(gathered,),
+    )
+    attn_parts = lax.all_to_all(attn_parts, ("zl", "y"), 0, 0, tiled=True)
+
     back = lax.all_to_all(back, EP, 0, 0, tiled=True)
     keep, passed = kernel_call(
         merge_experts, [((rows, width), F32)] * 2, back, place, own, load=(1, 2)

time: 131 us -> 128 us (0.977)
  starting transfers between devices: 94.5 us -> 93 us
    ppermute x6, starting transfers between devices: 21.5 us -> 19.5 us  [swap(): lax.ppermute(value, axis, [(i, i ^ k) for i in range(lax.axis_size(axis))])]
    all_to_all x1, starting transfers between devices: 7.52 us -> 6.15 us  [on_device(): attn_parts = lax.all_to_all(attn_parts, ('zl', 'y'), 0, 0, tiled=True)]
    pallas_call x13 -> x14, Pallas kernels: 15.6 us -> 15.6 us  [kernel_call(): pl.pallas_call(kernel, out_shape=tuple(shapes), in_specs=[place(n, load)...]
  transfers between devices with their start and end apart: 19 -> 19, of which waited for: 4 -> 7; matrix products, arithmetic and copies ran while one was open for 1% -> 0% of each run, Pallas kernels for 9% -> 10%
where the time goes in v11:
time: 128 us; the launch traced here: 127 us
  starting transfers between devices  93 us (73%)
  Pallas kernels  15.6 us (12%)
  waiting for transfers between devices  15.1 us (12%)
  local copies, waits for them, and re-layouts  2.72 us (2%)
    ppermute x6, starting transfers between devices, shift(): return lax.ppermute(value, axis, [(i, (i + k) % size) for i in range(size)])  19.5 us
    ppermute x6, starting transfers between devices, swap(): lax.ppermute(value, axis, [(i, i ^ k) for i in range(lax.axis_size(axis))])  19.5 us
    pallas_call x14, Pallas kernels, kernel_call(): pl.pallas_call(kernel, out_shape=tuple(shapes), in_specs=[place(n, load)...  15.6 us
    all_to_all x1, starting transfers between devices, on_device(): named_rows = lax.all_to_all(send, EP, 0, 0, tiled=True)  15 us
    all_to_all x1, starting transfers between devices, on_device(): back = lax.all_to_all(back, EP, 0, 0, tiled=True)  11 us
    ppermute x2, starting transfers between devices, mirror(): return lax.ppermute(value, axis, [(i, size - 1 - i) for i in range(size)])  8.77 us
    ppermute x6, waiting for transfers between devices, swap(): lax.ppermute(value, axis, [(i, i ^ k) for i in range(lax.axis_size(axis))])  8.02 us
    all_to_all x1, starting transfers between devices, on_device(): contexts = lax.all_to_all(context, 'y', 0, 0, tiled=True)  6.82 us
  transfers between devices with their start and end apart: 19, of which 7 were waited for; matrix products, arithmetic and copies ran while one was open for 0% of the time, Pallas kernels for 10%

profile of v11, /device:TPU:1, one launch (start us, length us, event | category | flops | bytes accessed | tf_op | source)
XLA Modules:
  0.0 126.9 jit_solution(2397322990505104855)
XLA Ops:
  0.0 2.6 %shard_map.118 = (bf16[64,4,1408]{2,1,0:T(4,128)(2,1)}, f32[256,16]{1,0:T(8,128)}, f32[16,448]{1,0:T(8,128)}) custom-call(bf16[16,3584]{1,0:T(8,128)(2,1)} %refs_0_.2, bf16[3584]{0:T(1024)(128)(2,1)} %refs_1_.3, s32[8,16]{1,0:T(8,128)} %bitcast.20), custom_call_target="tpu_custom_call" | custom-call | bytes 122368 | tf_op jit(solution)/shard_map/pallas_call | solution.py:60
  2.6 15.0 %all-to-all-start.1 = ((bf16[64,4,1408]{2,1,0:T(4,128)(2,1)}), bf16[64,4,1408]{2,1,0:T(4,128)(2,1)S(1)}, u32[]{:S(2)}, u32[]{:S(2)}) async-start(bf16[64,4,1408]{2,1,0:T(4,128)(2,1)} %get-tuple-element.20), calls=%async_computation.1 | async-start | bytes 1441792 | tf_op jit(solution)/shard_map/all_to_all | solution.py:364
  17.6 2.4 %collective-permute-start.6 = (bf16[56,1024]{1,0:T(8,128)(2,1)S(1)}, bf16[56,1024]{1,0:T(8,128)(2,1)S(1)}, u32[]{:S(2)}, u32[]{:S(2)}) collective-permute-start(bf16[56,1024]{1,0:T(8,128)(2,1)S(1)} %bitcast.17), channel_id=1, source_target_pairs={{0,8},{8,0},{1,9},{9,1},{2,10},{10,2},{3,11},{11,3},{4,12},{12,4},... | collective-permute-start | bytes 344072 | tf_op jit(solution)/shard_map/ppermute | solution.py:302
  21.9 3.2 %collective-permute-start.3 = (bf16[128,896]{1,0:T(8,128)(2,1)}, bf16[128,896]{1,0:T(8,128)(2,1)S(1)}, u32[]{:S(2)}, u32[]{:S(2)}) collective-permute-start(bf16[128,896]{1,0:T(8,128)(2,1)} %get-tuple-element.24), channel_id=1, source_target_pairs={{0,1},{1,0},{2,3},{3,2},{4,5},{5,4},{6,7},{7,6},{8,9},{9,8},{10,11... | collective-permute-start | bytes 688136 | tf_op jit(solution)/shard_map/ppermute | solution.py:314
  25.1 4.2 %collective-permute-start.4 = (bf16[128,896]{1,0:T(8,128)(2,1)}, bf16[128,896]{1,0:T(8,128)(2,1)S(1)}, u32[]{:S(2)}, u32[]{:S(2)}) collective-permute-start(bf16[128,896]{1,0:T(8,128)(2,1)} %get-tuple-element.25), channel_id=1, source_target_pairs={{0,2},{1,3},{2,0},{3,1},{4,6},{5,7},{6,4},{7,5},{8,10},{9,11},{10,... | collective-permute-start | bytes 688136 | tf_op jit(solution)/shard_map/ppermute | solution.py:314
  29.3 1.9 %collective-permute-start.5 = (bf16[128,896]{1,0:T(8,128)(2,1)}, bf16[128,896]{1,0:T(8,128)(2,1)S(1)}, u32[]{:S(2)}, u32[]{:S(2)}) collective-permute-start(bf16[128,896]{1,0:T(8,128)(2,1)} %get-tuple-element.26), channel_id=1, source_target_pairs={{0,3},{1,2},{2,1},{3,0},{4,7},{5,6},{6,5},{7,4},{8,11},{9,10},{10,... | collective-permute-start | bytes 688136 | tf_op jit(solution)/shard_map/ppermute | solution.py:314
  32.1 2.2 %shard_map.119.refs_1_ = bf16[8,16,512]{2,1,0:T(8,128)(2,1)} custom-call(s32[2]{0:T(128)S(1)} %copy-done.13, bf16[2,64,576]{2,1,0:T(8,128)(2,1)S(1)} %copy-done.11, bf16[2,576,384]{2,1,0:T(8,128)(2,1)S(1)} %bitcast.16, f32[256,16]{1,0:T(8,128)S(1)} %copy-done.4), custom_call_target="tpu_custom_call" | custom-call | bytes 1032200 | tf_op jit(solution)/shard_map/pallas_call | solution.py:60
  34.3 4.4 %collective-permute-start.7 = (bf16[2,56,1024]{2,1,0:T(8,128)(2,1)S(1)}, bf16[2,56,1024]{2,1,0:T(8,128)(2,1)S(1)}, u32[]{:S(2)}, u32[]{:S(2)}) collective-permute-start(bf16[2,56,1024]{2,1,0:T(8,128)(2,1)S(1)} %get-tuple-element.34), channel_id=1, source_target_pairs={{0,112},{16,96},{32,80},{48,64},{64,48},{80,32},{96,16},{112,0},{1... | collective-permute-start | bytes 688136 | tf_op jit(solution)/shard_map/ppermute | solution.py:319
  39.3 6.8 %all-to-all-start = ((bf16[8,16,512]{2,1,0:T(8,128)(2,1)}), bf16[8,16,512]{2,1,0:T(8,128)(2,1)S(1)}, u32[]{:S(2)}, u32[]{:S(2)}) async-start(bf16[8,16,512]{2,1,0:T(8,128)(2,1)} %shard_map.119.refs_1_), calls=%async_computation | async-start | bytes 262144 | tf_op jit(solution)/shard_map/all_to_all | solution.py:399
  46.3 3.4 %collective-permute-start.1 = (bf16[256,1152]{1,0:T(8,128)(2,1)S(1)}, bf16[256,1152]{1,0:T(8,128)(2,1)S(1)}, u32[]{:S(2)}, u32[]{:S(2)}) collective-permute-start(bf16[256,1152]{1,0:T(8,128)(2,1)S(1)} %get-tuple-element.22), channel_id=1, source_target_pairs={{0,1},{1,2},{2,3},{3,4},{4,5},{5,6},{6,7},{7,0},{8,9},{9,10},{10,1... | collective-permute-start | bytes 1769480 | tf_op jit(solution)/shard_map/ppermute | solution.py:302
  49.7 3.1 %collective-permute-start.2 = (bf16[256,1152]{1,0:T(8,128)(2,1)S(1)}, bf16[256,1152]{1,0:T(8,128)(2,1)S(1)}, u32[]{:S(2)}, u32[]{:S(2)}) collective-permute-start(bf16[256,1152]{1,0:T(8,128)(2,1)S(1)} %get-tuple-element.23), channel_id=1, source_target_pairs={{0,7},{1,0},{2,1},{3,2},{4,3},{5,4},{6,5},{7,6},{8,15},{9,8},{10,9... | collective-permute-start | bytes 1769480 | tf_op jit(solution)/shard_map/ppermute | solution.py:302
  53.7 3.2 %collective-permute-start.10 = (bf16[2,2,56,1024]{3,2,1,0:T(8,128)(2,1)S(1)}, bf16[2,2,56,1024]{3,2,1,0:T(8,128)(2,1)S(1)}, u32[]{:S(2)}, u32[]{:S(2)}) collective-permute-start(bf16[2,2,56,1024]{3,2,1,0:T(8,128)(2,1)S(1)} %pad_maximum_fusion.refs_4_), channel_id=1, source_target_pairs={{0,128},{128,256},{256,384},{384,0},{1,129},{129,257},{257,385},{3... | collective-permute-start | bytes 1376264 | tf_op jit(solution)/shard_map/ppermute | solution.py:302
  56.9 4.5 %collective-permute-start.11 = (bf16[2,2,56,1024]{3,2,1,0:T(8,128)(2,1)S(1)}, bf16[2,2,56,1024]{3,2,1,0:T(8,128)(2,1)S(1)}, u32[]{:S(2)}, u32[]{:S(2)}) collective-permute-start(bf16[2,2,56,1024]{3,2,1,0:T(8,128)(2,1)S(1)} %pad_maximum_fusion.refs_4_), channel_id=1, source_target_pairs={{0,256},{128,384},{256,0},{384,128},{1,257},{129,385},{257,1},{385... | collective-permute-start | bytes 1376264 | tf_op jit(solution)/shard_map/ppermute | solution.py:302
  61.4 3.0 %collective-permute-start.12 = (bf16[2,2,56,1024]{3,2,1,0:T(8,128)(2,1)S(1)}, bf16[2,2,56,1024]{3,2,1,0:T(8,128)(2,1)S(1)}, u32[]{:S(2)}, u32[]{:S(2)}) collective-permute-start(bf16[2,2,56,1024]{3,2,1,0:T(8,128)(2,1)S(1)} %pad_maximum_fusion.refs_4_), channel_id=1, source_target_pairs={{0,384},{128,0},{256,128},{384,256},{1,385},{129,1},{257,129},{385... | collective-permute-start | bytes 1376264 | tf_op jit(solution)/shard_map/ppermute | solution.py:302
  65.4 2.4 %shard_map.125 = (bf16[4,256,128]{2,1,0:T(8,128)(2,1)}, bf16[256,128]{1,0:T(8,128)(2,1)S(1)}) custom-call(bf16[256,1408]{1,0:T(8,128)(2,1)S(1)} %get-tuple-element.21.refs_0_, bf16[256,1152]{1,0:T(8,128)(2,1)S(1)} %collective-permute-done.1.refs_1_, bf16[256,1152]{1,0:T(8,128)(2,1)S(1)} %collective-permute-done.2.refs_2_, bf16[3584,128]{1,0:T(8,128)(2,1)S(1)} %bitcast.12, ...), custom_call_target="tpu_custom_call" | custom-call | bytes 3749888 | tf_op jit(solution)/shard_map/pallas_call | solution.py:60
  67.8 6.2 %all-to-all-start.2 = ((bf16[4,256,128]{2,1,0:T(8,128)(2,1)}), bf16[4,256,128]{2,1,0:T(8,128)(2,1)S(1)}, u32[]{:S(2)}, u32[]{:S(2)}) async-start(bf16[4,256,128]{2,1,0:T(8,128)(2,1)} %get-tuple-element.27), calls=%async_computation.2 | async-start | bytes 524288 | tf_op jit(solution)/shard_map/all_to_all | solution.py:419
  76.8 2.9 %collective-permute-start = (bf16[16,1024]{1,0:T(8,128)(2,1)S(1)}, bf16[16,1024]{1,0:T(8,128)(2,1)S(1)}, u32[]{:S(2)}, u32[]{:S(2)}) collective-permute-start(bf16[16,1024]{1,0:T(8,128)(2,1)S(1)} %shard_map.120.refs_0_), channel_id=1, source_target_pairs={{0,16},{16,0},{32,48},{48,32},{1,17},{17,1},{33,49},{49,33},{2,18}... | collective-permute-start | bytes 98312 | tf_op jit(solution)/shard_map/ppermute | solution.py:314
  81.8 11.0 %all-to-all-start.4 = ((bf16[64,4,1024]{2,1,0:T(4,128)(2,1)}), bf16[64,4,1024]{2,1,0:T(4,128)(2,1)S(1)}, u32[]{:S(2)}, u32[]{:S(2)}) async-start(bf16[64,4,1024]{2,1,0:T(4,128)(2,1)} %shard_map.126.refs_1_), calls=%async_computation.4 | async-start | bytes 1048576 | tf_op jit(solution)/shard_map/all_to_all | solution.py:455
  92.8 4.2 %collective-permute-start.8 = (bf16[16,1024]{1,0:T(8,128)(2,1)S(1)}, bf16[16,1024]{1,0:T(8,128)(2,1)S(1)}, u32[]{:S(2)}, u32[]{:S(2)}) collective-permute-start(bf16[16,1024]{1,0:T(8,128)(2,1)S(1)} %shard_map.127), channel_id=1, source_target_pairs={{0,32},{16,48},{32,0},{48,16},{1,33},{17,49},{33,1},{49,17},{2,34}... | collective-permute-start | bytes 98312 | tf_op jit(solution)/shard_map/ppermute | solution.py:314
  97.0 3.1 %collective-permute-start.9 = (bf16[16,1024]{1,0:T(8,128)(2,1)S(1)}, bf16[16,1024]{1,0:T(8,128)(2,1)S(1)}, u32[]{:S(2)}, u32[]{:S(2)}) collective-permute-start(bf16[16,1024]{1,0:T(8,128)(2,1)S(1)} %shard_map.127), channel_id=1, source_target_pairs={{0,48},{16,32},{32,16},{48,0},{1,49},{17,33},{33,17},{49,1},{2,50}... | collective-permute-start | bytes 98312 | tf_op jit(solution)/shard_map/ppermute | solution.py:314
  100.1 7.6 %collective-permute-done.8.refs_2_ = bf16[16,1024]{1,0:T(8,128)(2,1)S(1)} collective-permute-done((bf16[16,1024]{1,0:T(8,128)(2,1)S(1)}, bf16[16,1024]{1,0:T(8,128)(2,1)S(1)}, u32[]{:S(2)}, u32[]{:S(2)}) %collective-permute-start.8) | collective-permute-done | bytes 32800 | tf_op jit(solution)/shard_map/ppermute | solution.py:314
  110.7 6.1 %all-to-all-start.3 = ((bf16[32,16,128]{2,1,0:T(8,128)(2,1)}), bf16[32,16,128]{2,1,0:T(8,128)(2,1)S(1)}, u32[]{:S(2)}, u32[]{:S(2)}) async-start(bf16[32,16,128]{2,1,0:T(8,128)(2,1)} %shard_map.129), calls=%async_computation.3 | async-start | bytes 262144 | tf_op jit(solution)/shard_map/all_to_all | solution.py:453
  117.6 4.4 %collective-permute-start.13 = (f32[16,448]{1,0:T(8,128)S(1)}, f32[16,448]{1,0:T(8,128)S(1)}, u32[]{:S(2)}, u32[]{:S(2)}) collective-permute-start(f32[16,448]{1,0:T(8,128)S(1)} %get-tuple-element.32), channel_id=1, source_target_pairs={{0,7},{1,6},{2,5},{3,4},{4,3},{5,2},{6,1},{7,0},{8,15},{9,14},{10,... | collective-permute-start | bytes 86024 | tf_op jit(solution)/shard_map/ppermute | solution.py:319
  121.9 4.3 %all-to-all-done.3.refs_0_ = bf16[32,16,128]{2,1,0:T(8,128)(2,1)S(1)} async-done(((bf16[32,16,128]{2,1,0:T(8,128)(2,1)}), bf16[32,16,128]{2,1,0:T(8,128)(2,1)S(1)}, u32[]{:S(2)}, u32[]{:S(2)}) %all-to-all-start.3) | async-done | bytes 131104 | tf_op jit(solution)/shard_map/all_to_all | solution.py:453
  (66 shorter events, 14.4 us)
Async XLA Ops:
  0.0 20.0 %copy-start.2 = (bf16[1,128,3584]{2,1,0:T(8,128)(2,1)S(1)}, bf16[1,128,3584]{2,1,0:T(8,128)(2,1)}, u32[]{:S(2)}) copy-start(bf16[1,128,3584]{2,1,0:T(8,128)(2,1)} %param.21) | copy-start | bytes 2752516
  0.0 17.6 %copy-start.15 = (bf16[1024,56]{0,1:T(8,128)(2,1)S(1)}, bf16[1024,56]{0,1:T(8,128)(2,1)}, u32[]{:S(2)}) copy-start(bf16[1024,56]{0,1:T(8,128)(2,1)} %param.23) | copy-start | bytes 344068
  2.6 28.8 %copy-start.3 = (bf16[2,384,576]{1,2,0:T(8,128)(2,1)S(1)}, bf16[2,384,576]{1,2,0:T(8,128)(2,1)}, u32[]{:S(2)}) copy-start(bf16[2,384,576]{1,2,0:T(8,128)(2,1)} %param.15) | copy-start | bytes 2654212
  2.6 36.6 %all-to-all-start.1 = ((bf16[64,4,1408]{2,1,0:T(4,128)(2,1)}), bf16[64,4,1408]{2,1,0:T(4,128)(2,1)S(1)}, u32[]{:S(2)}, u32[]{:S(2)}) async-start(bf16[64,4,1408]{2,1,0:T(4,128)(2,1)} %get-tuple-element.20), calls=%async_computation.1 | async-start | bytes 1441792 | tf_op jit(solution)/shard_map/all_to_all | solution.py:364
  17.6 16.7 %collective-permute-start.6 = (bf16[56,1024]{1,0:T(8,128)(2,1)S(1)}, bf16[56,1024]{1,0:T(8,128)(2,1)S(1)}, u32[]{:S(2)}, u32[]{:S(2)}) collective-permute-start(bf16[56,1024]{1,0:T(8,128)(2,1)S(1)} %bitcast.17), channel_id=1, source_target_pairs={{0,8},{8,0},{1,9},{9,1},{2,10},{10,2},{3,11},{11,3},{4,12},{12,4},... | collective-permute-start | bytes 344072 | tf_op jit(solution)/shard_map/ppermute | solution.py:302
  21.9 27.8 %collective-permute-start.3 = (bf16[128,896]{1,0:T(8,128)(2,1)}, bf16[128,896]{1,0:T(8,128)(2,1)S(1)}, u32[]{:S(2)}, u32[]{:S(2)}) collective-permute-start(bf16[128,896]{1,0:T(8,128)(2,1)} %get-tuple-element.24), channel_id=1, source_target_pairs={{0,1},{1,0},{2,3},{3,2},{4,5},{5,4},{6,7},{7,6},{8,9},{9,8},{10,11... | collective-permute-start | bytes 688136 | tf_op jit(solution)/shard_map/ppermute | solution.py:314
  25.1 27.8 %collective-permute-start.4 = (bf16[128,896]{1,0:T(8,128)(2,1)}, bf16[128,896]{1,0:T(8,128)(2,1)S(1)}, u32[]{:S(2)}, u32[]{:S(2)}) collective-permute-start(bf16[128,896]{1,0:T(8,128)(2,1)} %get-tuple-element.25), channel_id=1, source_target_pairs={{0,2},{1,3},{2,0},{3,1},{4,6},{5,7},{6,4},{7,5},{8,10},{9,11},{10,... | collective-permute-start | bytes 688136 | tf_op jit(solution)/shard_map/ppermute | solution.py:314
  29.3 23.6 %collective-permute-start.5 = (bf16[128,896]{1,0:T(8,128)(2,1)}, bf16[128,896]{1,0:T(8,128)(2,1)S(1)}, u32[]{:S(2)}, u32[]{:S(2)}) collective-permute-start(bf16[128,896]{1,0:T(8,128)(2,1)} %get-tuple-element.26), channel_id=1, source_target_pairs={{0,3},{1,2},{2,1},{3,0},{4,7},{5,6},{6,5},{7,4},{8,11},{9,10},{10,... | collective-permute-start | bytes 688136 | tf_op jit(solution)/shard_map/ppermute | solution.py:314
  34.3 19.3 %collective-permute-start.7 = (bf16[2,56,1024]{2,1,0:T(8,128)(2,1)S(1)}, bf16[2,56,1024]{2,1,0:T(8,128)(2,1)S(1)}, u32[]{:S(2)}, u32[]{:S(2)}) collective-permute-start(bf16[2,56,1024]{2,1,0:T(8,128)(2,1)S(1)} %get-tuple-element.34), channel_id=1, source_target_pairs={{0,112},{16,96},{32,80},{48,64},{64,48},{80,32},{96,16},{112,0},{1... | collective-permute-start | bytes 688136 | tf_op jit(solution)/shard_map/ppermute | solution.py:319
  39.3 28.5 %all-to-all-start = ((bf16[8,16,512]{2,1,0:T(8,128)(2,1)}), bf16[8,16,512]{2,1,0:T(8,128)(2,1)S(1)}, u32[]{:S(2)}, u32[]{:S(2)}) async-start(bf16[8,16,512]{2,1,0:T(8,128)(2,1)} %shard_map.119.refs_1_), calls=%async_computation | async-start | bytes 262144 | tf_op jit(solution)/shard_map/all_to_all | solution.py:399
  46.3 19.0 %collective-permute-start.1 = (bf16[256,1152]{1,0:T(8,128)(2,1)S(1)}, bf16[256,1152]{1,0:T(8,128)(2,1)S(1)}, u32[]{:S(2)}, u32[]{:S(2)}) collective-permute-start(bf16[256,1152]{1,0:T(8,128)(2,1)S(1)} %get-tuple-element.22), channel_id=1, source_target_pairs={{0,1},{1,2},{2,3},{3,4},{4,5},{5,6},{6,7},{7,0},{8,9},{9,10},{10,1... | collective-permute-start | bytes 1769480 | tf_op jit(solution)/shard_map/ppermute | solution.py:302
  49.7 15.6 %collective-permute-start.2 = (bf16[256,1152]{1,0:T(8,128)(2,1)S(1)}, bf16[256,1152]{1,0:T(8,128)(2,1)S(1)}, u32[]{:S(2)}, u32[]{:S(2)}) collective-permute-start(bf16[256,1152]{1,0:T(8,128)(2,1)S(1)} %get-tuple-element.23), channel_id=1, source_target_pairs={{0,7},{1,0},{2,1},{3,2},{4,3},{5,4},{6,5},{7,6},{8,15},{9,8},{10,9... | collective-permute-start | bytes 1769480 | tf_op jit(solution)/shard_map/ppermute | solution.py:302
  52.9 12.4 %copy-start.1 = (bf16[1,3584,128]{2,1,0:T(8,128)(2,1)S(1)}, bf16[1,3584,128]{2,1,0:T(8,128)(2,1)}, u32[]{:S(2)}) copy-start(bf16[1,3584,128]{2,1,0:T(8,128)(2,1)} %param.20) | copy-start | bytes 2752516
  53.7 11.7 %copy-start = (bf16[1,3584,128]{2,1,0:T(8,128)(2,1)S(1)}, bf16[1,3584,128]{2,1,0:T(8,128)(2,1)}, u32[]{:S(2)}) copy-start(bf16[1,3584,128]{2,1,0:T(8,128)(2,1)} %param.19) | copy-start | bytes 2752516
  53.7 43.3 %collective-permute-start.10 = (bf16[2,2,56,1024]{3,2,1,0:T(8,128)(2,1)S(1)}, bf16[2,2,56,1024]{3,2,1,0:T(8,128)(2,1)S(1)}, u32[]{:S(2)}, u32[]{:S(2)}) collective-permute-start(bf16[2,2,56,1024]{3,2,1,0:T(8,128)(2,1)S(1)} %pad_maximum_fusion.refs_4_), channel_id=1, source_target_pairs={{0,128},{128,256},{256,384},{384,0},{1,129},{129,257},{257,385},{3... | collective-permute-start | bytes 1376264 | tf_op jit(solution)/shard_map/ppermute | solution.py:302
  56.9 43.2 %collective-permute-start.11 = (bf16[2,2,56,1024]{3,2,1,0:T(8,128)(2,1)S(1)}, bf16[2,2,56,1024]{3,2,1,0:T(8,128)(2,1)S(1)}, u32[]{:S(2)}, u32[]{:S(2)}) collective-permute-start(bf16[2,2,56,1024]{3,2,1,0:T(8,128)(2,1)S(1)} %pad_maximum_fusion.refs_4_), channel_id=1, source_target_pairs={{0,256},{128,384},{256,0},{384,128},{1,257},{129,385},{257,1},{385... | collective-permute-start | bytes 1376264 | tf_op jit(solution)/shard_map/ppermute | solution.py:302
  61.4 38.7 %collective-permute-start.12 = (bf16[2,2,56,1024]{3,2,1,0:T(8,128)(2,1)S(1)}, bf16[2,2,56,1024]{3,2,1,0:T(8,128)(2,1)S(1)}, u32[]{:S(2)}, u32[]{:S(2)}) collective-permute-start(bf16[2,2,56,1024]{3,2,1,0:T(8,128)(2,1)S(1)} %pad_maximum_fusion.refs_4_), channel_id=1, source_target_pairs={{0,384},{128,0},{256,128},{384,256},{1,385},{129,1},{257,129},{385... | collective-permute-start | bytes 1376264 | tf_op jit(solution)/shard_map/ppermute | solution.py:302
  67.8 12.1 %all-to-all-start.2 = ((bf16[4,256,128]{2,1,0:T(8,128)(2,1)}), bf16[4,256,128]{2,1,0:T(8,128)(2,1)S(1)}, u32[]{:S(2)}, u32[]{:S(2)}) async-start(bf16[4,256,128]{2,1,0:T(8,128)(2,1)} %get-tuple-element.27), calls=%async_computation.2 | async-start | bytes 524288 | tf_op jit(solution)/shard_map/all_to_all | solution.py:419
  76.8 23.4 %collective-permute-start = (bf16[16,1024]{1,0:T(8,128)(2,1)S(1)}, bf16[16,1024]{1,0:T(8,128)(2,1)S(1)}, u32[]{:S(2)}, u32[]{:S(2)}) collective-permute-start(bf16[16,1024]{1,0:T(8,128)(2,1)S(1)} %shard_map.120.refs_0_), channel_id=1, source_target_pairs={{0,16},{16,0},{32,48},{48,32},{1,17},{17,1},{33,49},{49,33},{2,18}... | collective-permute-start | bytes 98312 | tf_op jit(solution)/shard_map/ppermute | solution.py:314
  81.8 28.9 %all-to-all-start.4 = ((bf16[64,4,1024]{2,1,0:T(4,128)(2,1)}), bf16[64,4,1024]{2,1,0:T(4,128)(2,1)S(1)}, u32[]{:S(2)}, u32[]{:S(2)}) async-start(bf16[64,4,1024]{2,1,0:T(4,128)(2,1)} %shard_map.126.refs_1_), calls=%async_computation.4 | async-start | bytes 1048576 | tf_op jit(solution)/shard_map/all_to_all | solution.py:455
  92.8 15.0 %collective-permute-start.8 = (bf16[16,1024]{1,0:T(8,128)(2,1)S(1)}, bf16[16,1024]{1,0:T(8,128)(2,1)S(1)}, u32[]{:S(2)}, u32[]{:S(2)}) collective-permute-start(bf16[16,1024]{1,0:T(8,128)(2,1)S(1)} %shard_map.127), channel_id=1, source_target_pairs={{0,32},{16,48},{32,0},{48,16},{1,33},{17,49},{33,1},{49,17},{2,34}... | collective-permute-start | bytes 98312 | tf_op jit(solution)/shard_map/ppermute | solution.py:314
  97.0 11.1 %collective-permute-start.9 = (bf16[16,1024]{1,0:T(8,128)(2,1)S(1)}, bf16[16,1024]{1,0:T(8,128)(2,1)S(1)}, u32[]{:S(2)}, u32[]{:S(2)}) collective-permute-start(bf16[16,1024]{1,0:T(8,128)(2,1)S(1)} %shard_map.127), channel_id=1, source_target_pairs={{0,48},{16,32},{32,16},{48,0},{1,49},{17,33},{33,17},{49,1},{2,50}... | collective-permute-start | bytes 98312 | tf_op jit(solution)/shard_map/ppermute | solution.py:314
  110.7 15.5 %all-to-all-start.3 = ((bf16[32,16,128]{2,1,0:T(8,128)(2,1)}), bf16[32,16,128]{2,1,0:T(8,128)(2,1)S(1)}, u32[]{:S(2)}, u32[]{:S(2)}) async-start(bf16[32,16,128]{2,1,0:T(8,128)(2,1)} %shard_map.129), calls=%async_computation.3 | async-start | bytes 262144 | tf_op jit(solution)/shard_map/all_to_all | solution.py:453
  117.6 8.7 %collective-permute-start.13 = (f32[16,448]{1,0:T(8,128)S(1)}, f32[16,448]{1,0:T(8,128)S(1)}, u32[]{:S(2)}, u32[]{:S(2)}) collective-permute-start(f32[16,448]{1,0:T(8,128)S(1)} %get-tuple-element.32), channel_id=1, source_target_pairs={{0,7},{1,6},{2,5},{3,4},{4,3},{5,2},{6,1},{7,0},{8,15},{9,14},{10,... | collective-permute-start | bytes 86024 | tf_op jit(solution)/shard_map/ppermute | solution.py:319
  (12 other events, 61.9 us)

commit v12 on v11

--- a/solution.py
+++ b/solution.py
@@ -424,7 +424,6 @@
         [((rows, depth), BF16)],
         contexts,
         w_uv,
-        load=(1,),
         flops=10_000_000_000,
     )
 
@@ -441,8 +440,7 @@
         after=(contexts,),
     )
     (again,) = kernel_call(repeat, [((rows, depth), BF16)], values, after=(back,))
-    all_values = [values, swap(values, "zl", 1)]
-    all_values += [swap(again, "zl", k) for k in (2, 3)]
+    all_values = [values, swap(again, "zl", 1), swap(values, "zl", 2), swap(again, "zl", 3)]
     (attn_parts,) = kernel_call(
         project,
         [((4 * tp_size, rows, 128), BF16)],

time: 128 us -> 128 us (level)
  transfers between devices with their start and end apart: 19 -> 19, of which waited for: 7 -> 6; matrix products, arithmetic and copies ran while one was open for 0% -> 0% of each run, Pallas kernels for 10% -> 10%
where the time goes in v12:
time: 128 us; the launch traced here: 127 us
  starting transfers between devices  93.5 us (73%)
  Pallas kernels  15.5 us (12%)
  waiting for transfers between devices  14.6 us (11%)
  local copies, waits for them, and re-layouts  2.72 us (2%)
    ppermute x6, starting transfers between devices, swap(): lax.ppermute(value, axis, [(i, i ^ k) for i in range(lax.axis_size(axis))])  20.4 us
    ppermute x6, starting transfers between devices, shift(): return lax.ppermute(value, axis, [(i, (i + k) % size) for i in range(size)])  19.5 us
    pallas_call x14, Pallas kernels, kernel_call(): pl.pallas_call(kernel, out_shape=tuple(shapes), in_specs=[place(n, load)...  15.5 us
    all_to_all x1, starting transfers between devices, on_device(): named_rows = lax.all_to_all(send, EP, 0, 0, tiled=True)  15 us
    all_to_all x1, starting transfers between devices, on_device(): back = lax.all_to_all(back, EP, 0, 0, tiled=True)  10.4 us
    ppermute x2, starting transfers between devices, mirror(): return lax.ppermute(value, axis, [(i, size - 1 - i) for i in range(size)])  8.77 us
    ppermute x6, waiting for transfers between devices, swap(): lax.ppermute(value, axis, [(i, i ^ k) for i in range(lax.axis_size(axis))])  8.02 us
    all_to_all x1, starting transfers between devices, on_device(): contexts = lax.all_to_all(context, 'y', 0, 0, tiled=True)  6.82 us
  transfers between devices with their start and end apart: 19, of which 6 were waited for; matrix products, arithmetic and copies ran while one was open for 0% of the time, Pallas kernels for 10%

profile of v12, /device:TPU:1, one launch (start us, length us, event | category | flops | bytes accessed | tf_op | source)
XLA Modules:
  0.0 126.9 jit_solution(16759977837587820245)
XLA Ops:
  0.0 2.6 %shard_map.118 = (bf16[64,4,1408]{2,1,0:T(4,128)(2,1)}, f32[256,16]{1,0:T(8,128)}, f32[16,448]{1,0:T(8,128)}) custom-call(bf16[16,3584]{1,0:T(8,128)(2,1)} %refs_0_.2, bf16[3584]{0:T(1024)(128)(2,1)} %refs_1_.3, s32[8,16]{1,0:T(8,128)} %bitcast.20), custom_call_target="tpu_custom_call" | custom-call | bytes 122368 | tf_op jit(solution)/shard_map/pallas_call | solution.py:60
  2.6 15.0 %all-to-all-start.1 = ((bf16[64,4,1408]{2,1,0:T(4,128)(2,1)}), bf16[64,4,1408]{2,1,0:T(4,128)(2,1)S(1)}, u32[]{:S(2)}, u32[]{:S(2)}) async-start(bf16[64,4,1408]{2,1,0:T(4,128)(2,1)} %get-tuple-element.20), calls=%async_computation.1 | async-start | bytes 1441792 | tf_op jit(solution)/shard_map/all_to_all | solution.py:364
  17.6 2.4 %collective-permute-start.5 = (bf16[56,1024]{1,0:T(8,128)(2,1)S(1)}, bf16[56,1024]{1,0:T(8,128)(2,1)S(1)}, u32[]{:S(2)}, u32[]{:S(2)}) collective-permute-start(bf16[56,1024]{1,0:T(8,128)(2,1)S(1)} %bitcast.17), channel_id=1, source_target_pairs={{0,8},{8,0},{1,9},{9,1},{2,10},{10,2},{3,11},{11,3},{4,12},{12,4},... | collective-permute-start | bytes 344072 | tf_op jit(solution)/shard_map/ppermute | solution.py:302
  21.9 3.2 %collective-permute-start.2 = (bf16[128,896]{1,0:T(8,128)(2,1)}, bf16[128,896]{1,0:T(8,128)(2,1)S(1)}, u32[]{:S(2)}, u32[]{:S(2)}) collective-permute-start(bf16[128,896]{1,0:T(8,128)(2,1)} %get-tuple-element.24), channel_id=1, source_target_pairs={{0,1},{1,0},{2,3},{3,2},{4,5},{5,4},{6,7},{7,6},{8,9},{9,8},{10,11... | collective-permute-start | bytes 688136 | tf_op jit(solution)/shard_map/ppermute | solution.py:314
  25.1 4.2 %collective-permute-start.3 = (bf16[128,896]{1,0:T(8,128)(2,1)}, bf16[128,896]{1,0:T(8,128)(2,1)S(1)}, u32[]{:S(2)}, u32[]{:S(2)}) collective-permute-start(bf16[128,896]{1,0:T(8,128)(2,1)} %get-tuple-element.25), channel_id=1, source_target_pairs={{0,2},{1,3},{2,0},{3,1},{4,6},{5,7},{6,4},{7,5},{8,10},{9,11},{10,... | collective-permute-start | bytes 688136 | tf_op jit(solution)/shard_map/ppermute | solution.py:314
  29.3 1.9 %collective-permute-start.4 = (bf16[128,896]{1,0:T(8,128)(2,1)}, bf16[128,896]{1,0:T(8,128)(2,1)S(1)}, u32[]{:S(2)}, u32[]{:S(2)}) collective-permute-start(bf16[128,896]{1,0:T(8,128)(2,1)} %get-tuple-element.26), channel_id=1, source_target_pairs={{0,3},{1,2},{2,1},{3,0},{4,7},{5,6},{6,5},{7,4},{8,11},{9,10},{10,... | collective-permute-start | bytes 688136 | tf_op jit(solution)/shard_map/ppermute | solution.py:314
  32.1 2.2 %shard_map.119.refs_1_ = bf16[8,16,512]{2,1,0:T(8,128)(2,1)} custom-call(s32[2]{0:T(128)S(1)} %copy-done.13, bf16[2,64,576]{2,1,0:T(8,128)(2,1)S(1)} %copy-done.11, bf16[2,576,384]{2,1,0:T(8,128)(2,1)S(1)} %bitcast.16, f32[256,16]{1,0:T(8,128)S(1)} %copy-done.4), custom_call_target="tpu_custom_call" | custom-call | bytes 1032200 | tf_op jit(solution)/shard_map/pallas_call | solution.py:60
  34.3 4.4 %collective-permute-start.6 = (bf16[2,56,1024]{2,1,0:T(8,128)(2,1)S(1)}, bf16[2,56,1024]{2,1,0:T(8,128)(2,1)S(1)}, u32[]{:S(2)}, u32[]{:S(2)}) collective-permute-start(bf16[2,56,1024]{2,1,0:T(8,128)(2,1)S(1)} %get-tuple-element.34), channel_id=1, source_target_pairs={{0,112},{16,96},{32,80},{48,64},{64,48},{80,32},{96,16},{112,0},{1... | collective-permute-start | bytes 688136 | tf_op jit(solution)/shard_map/ppermute | solution.py:319
  39.3 6.8 %all-to-all-start = ((bf16[8,16,512]{2,1,0:T(8,128)(2,1)}), bf16[8,16,512]{2,1,0:T(8,128)(2,1)S(1)}, u32[]{:S(2)}, u32[]{:S(2)}) async-start(bf16[8,16,512]{2,1,0:T(8,128)(2,1)} %shard_map.119.refs_1_), calls=%async_computation | async-start | bytes 262144 | tf_op jit(solution)/shard_map/all_to_all | solution.py:399
  46.3 3.4 %collective-permute-start = (bf16[256,1152]{1,0:T(8,128)(2,1)S(1)}, bf16[256,1152]{1,0:T(8,128)(2,1)S(1)}, u32[]{:S(2)}, u32[]{:S(2)}) collective-permute-start(bf16[256,1152]{1,0:T(8,128)(2,1)S(1)} %get-tuple-element.22), channel_id=1, source_target_pairs={{0,1},{1,2},{2,3},{3,4},{4,5},{5,6},{6,7},{7,0},{8,9},{9,10},{10,1... | collective-permute-start | bytes 1769480 | tf_op jit(solution)/shard_map/ppermute | solution.py:302
  49.7 3.1 %collective-permute-start.1 = (bf16[256,1152]{1,0:T(8,128)(2,1)S(1)}, bf16[256,1152]{1,0:T(8,128)(2,1)S(1)}, u32[]{:S(2)}, u32[]{:S(2)}) collective-permute-start(bf16[256,1152]{1,0:T(8,128)(2,1)S(1)} %get-tuple-element.23), channel_id=1, source_target_pairs={{0,7},{1,0},{2,1},{3,2},{4,3},{5,4},{6,5},{7,6},{8,15},{9,8},{10,9... | collective-permute-start | bytes 1769480 | tf_op jit(solution)/shard_map/ppermute | solution.py:302
  53.7 3.2 %collective-permute-start.10 = (bf16[2,2,56,1024]{3,2,1,0:T(8,128)(2,1)S(1)}, bf16[2,2,56,1024]{3,2,1,0:T(8,128)(2,1)S(1)}, u32[]{:S(2)}, u32[]{:S(2)}) collective-permute-start(bf16[2,2,56,1024]{3,2,1,0:T(8,128)(2,1)S(1)} %pad_maximum_fusion.refs_4_), channel_id=1, source_target_pairs={{0,128},{128,256},{256,384},{384,0},{1,129},{129,257},{257,385},{3... | collective-permute-start | bytes 1376264 | tf_op jit(solution)/shard_map/ppermute | solution.py:302
  56.9 4.5 %collective-permute-start.11 = (bf16[2,2,56,1024]{3,2,1,0:T(8,128)(2,1)S(1)}, bf16[2,2,56,1024]{3,2,1,0:T(8,128)(2,1)S(1)}, u32[]{:S(2)}, u32[]{:S(2)}) collective-permute-start(bf16[2,2,56,1024]{3,2,1,0:T(8,128)(2,1)S(1)} %pad_maximum_fusion.refs_4_), channel_id=1, source_target_pairs={{0,256},{128,384},{256,0},{384,128},{1,257},{129,385},{257,1},{385... | collective-permute-start | bytes 1376264 | tf_op jit(solution)/shard_map/ppermute | solution.py:302
  61.4 3.0 %collective-permute-start.12 = (bf16[2,2,56,1024]{3,2,1,0:T(8,128)(2,1)S(1)}, bf16[2,2,56,1024]{3,2,1,0:T(8,128)(2,1)S(1)}, u32[]{:S(2)}, u32[]{:S(2)}) collective-permute-start(bf16[2,2,56,1024]{3,2,1,0:T(8,128)(2,1)S(1)} %pad_maximum_fusion.refs_4_), channel_id=1, source_target_pairs={{0,384},{128,0},{256,128},{384,256},{1,385},{129,1},{257,129},{385... | collective-permute-start | bytes 1376264 | tf_op jit(solution)/shard_map/ppermute | solution.py:302
  65.4 2.4 %shard_map.125 = (bf16[4,256,128]{2,1,0:T(8,128)(2,1)}, bf16[256,128]{1,0:T(8,128)(2,1)S(1)}) custom-call(bf16[256,1408]{1,0:T(8,128)(2,1)S(1)} %get-tuple-element.21.refs_0_, bf16[256,1152]{1,0:T(8,128)(2,1)S(1)} %collective-permute-done.refs_1_, bf16[256,1152]{1,0:T(8,128)(2,1)S(1)} %collective-permute-done.1.refs_2_, bf16[3584,128]{1,0:T(8,128)(2,1)S(1)} %bitcast.12, ...), custom_call_target="tpu_custom_call" | custom-call | bytes 3749888 | tf_op jit(solution)/shard_map/pallas_call | solution.py:60
  67.8 6.2 %all-to-all-start.2 = ((bf16[4,256,128]{2,1,0:T(8,128)(2,1)}), bf16[4,256,128]{2,1,0:T(8,128)(2,1)S(1)}, u32[]{:S(2)}, u32[]{:S(2)}) async-start(bf16[4,256,128]{2,1,0:T(8,128)(2,1)} %get-tuple-element.27), calls=%async_computation.2 | async-start | bytes 524288 | tf_op jit(solution)/shard_map/all_to_all | solution.py:419
  76.7 3.8 %collective-permute-start.8 = (bf16[16,1024]{1,0:T(8,128)(2,1)S(1)}, bf16[16,1024]{1,0:T(8,128)(2,1)S(1)}, u32[]{:S(2)}, u32[]{:S(2)}) collective-permute-start(bf16[16,1024]{1,0:T(8,128)(2,1)S(1)} %shard_map.120.refs_0_), channel_id=1, source_target_pairs={{0,32},{16,48},{32,0},{48,16},{1,33},{17,49},{33,1},{49,17},{2,34}... | collective-permute-start | bytes 98312 | tf_op jit(solution)/shard_map/ppermute | solution.py:314
  82.4 10.4 %all-to-all-start.4 = ((bf16[64,4,1024]{2,1,0:T(4,128)(2,1)}), bf16[64,4,1024]{2,1,0:T(4,128)(2,1)S(1)}, u32[]{:S(2)}, u32[]{:S(2)}) async-start(bf16[64,4,1024]{2,1,0:T(4,128)(2,1)} %shard_map.126.refs_1_), calls=%async_computation.4 | async-start | bytes 1048576 | tf_op jit(solution)/shard_map/all_to_all | solution.py:453
  92.8 3.3 %collective-permute-start.7 = (bf16[16,1024]{1,0:T(8,128)(2,1)S(1)}, bf16[16,1024]{1,0:T(8,128)(2,1)S(1)}, u32[]{:S(2)}, u32[]{:S(2)}) collective-permute-start(bf16[16,1024]{1,0:T(8,128)(2,1)S(1)} %shard_map.127), channel_id=1, source_target_pairs={{0,16},{16,0},{32,48},{48,32},{1,17},{17,1},{33,49},{49,33},{2,18}... | collective-permute-start | bytes 98312 | tf_op jit(solution)/shard_map/ppermute | solution.py:314
  96.1 4.0 %collective-permute-start.9 = (bf16[16,1024]{1,0:T(8,128)(2,1)S(1)}, bf16[16,1024]{1,0:T(8,128)(2,1)S(1)}, u32[]{:S(2)}, u32[]{:S(2)}) collective-permute-start(bf16[16,1024]{1,0:T(8,128)(2,1)S(1)} %shard_map.127), channel_id=1, source_target_pairs={{0,48},{16,32},{32,16},{48,0},{1,49},{17,33},{33,17},{49,1},{2,50}... | collective-permute-start | bytes 98312 | tf_op jit(solution)/shard_map/ppermute | solution.py:314
  100.1 6.5 %collective-permute-done.7.refs_1_ = bf16[16,1024]{1,0:T(8,128)(2,1)S(1)} collective-permute-done((bf16[16,1024]{1,0:T(8,128)(2,1)S(1)}, bf16[16,1024]{1,0:T(8,128)(2,1)S(1)}, u32[]{:S(2)}, u32[]{:S(2)}) %collective-permute-start.7) | collective-permute-done | bytes 32800 | tf_op jit(solution)/shard_map/ppermute | solution.py:314
  110.3 6.4 %all-to-all-start.3 = ((bf16[32,16,128]{2,1,0:T(8,128)(2,1)}), bf16[32,16,128]{2,1,0:T(8,128)(2,1)S(1)}, u32[]{:S(2)}, u32[]{:S(2)}) async-start(bf16[32,16,128]{2,1,0:T(8,128)(2,1)} %shard_map.129), calls=%async_computation.3 | async-start | bytes 262144 | tf_op jit(solution)/shard_map/all_to_all | solution.py:451
  117.5 4.4 %collective-permute-start.13 = (f32[16,448]{1,0:T(8,128)S(1)}, f32[16,448]{1,0:T(8,128)S(1)}, u32[]{:S(2)}, u32[]{:S(2)}) collective-permute-start(f32[16,448]{1,0:T(8,128)S(1)} %get-tuple-element.32), channel_id=1, source_target_pairs={{0,7},{1,6},{2,5},{3,4},{4,3},{5,2},{6,1},{7,0},{8,15},{9,14},{10,... | collective-permute-start | bytes 86024 | tf_op jit(solution)/shard_map/ppermute | solution.py:319
  121.8 4.4 %all-to-all-done.3.refs_0_ = bf16[32,16,128]{2,1,0:T(8,128)(2,1)S(1)} async-done(((bf16[32,16,128]{2,1,0:T(8,128)(2,1)}), bf16[32,16,128]{2,1,0:T(8,128)(2,1)S(1)}, u32[]{:S(2)}, u32[]{:S(2)}) %all-to-all-start.3) | async-done | bytes 131104 | tf_op jit(solution)/shard_map/all_to_all | solution.py:451
  (66 shorter events, 14.8 us)
Async XLA Ops:
  0.0 20.0 %copy-start.2 = (bf16[1,128,3584]{2,1,0:T(8,128)(2,1)S(1)}, bf16[1,128,3584]{2,1,0:T(8,128)(2,1)}, u32[]{:S(2)}) copy-start(bf16[1,128,3584]{2,1,0:T(8,128)(2,1)} %param.21) | copy-start | bytes 2752516
  0.0 17.6 %copy-start.15 = (bf16[1024,56]{0,1:T(8,128)(2,1)S(1)}, bf16[1024,56]{0,1:T(8,128)(2,1)}, u32[]{:S(2)}) copy-start(bf16[1024,56]{0,1:T(8,128)(2,1)} %param.23) | copy-start | bytes 344068
  2.6 28.8 %copy-start.3 = (bf16[2,384,576]{1,2,0:T(8,128)(2,1)S(1)}, bf16[2,384,576]{1,2,0:T(8,128)(2,1)}, u32[]{:S(2)}) copy-start(bf16[2,384,576]{1,2,0:T(8,128)(2,1)} %param.15) | copy-start | bytes 2654212
  2.6 36.6 %all-to-all-start.1 = ((bf16[64,4,1408]{2,1,0:T(4,128)(2,1)}), bf16[64,4,1408]{2,1,0:T(4,128)(2,1)S(1)}, u32[]{:S(2)}, u32[]{:S(2)}) async-start(bf16[64,4,1408]{2,1,0:T(4,128)(2,1)} %get-tuple-element.20), calls=%async_computation.1 | async-start | bytes 1441792 | tf_op jit(solution)/shard_map/all_to_all | solution.py:364
  17.6 16.7 %collective-permute-start.5 = (bf16[56,1024]{1,0:T(8,128)(2,1)S(1)}, bf16[56,1024]{1,0:T(8,128)(2,1)S(1)}, u32[]{:S(2)}, u32[]{:S(2)}) collective-permute-start(bf16[56,1024]{1,0:T(8,128)(2,1)S(1)} %bitcast.17), channel_id=1, source_target_pairs={{0,8},{8,0},{1,9},{9,1},{2,10},{10,2},{3,11},{11,3},{4,12},{12,4},... | collective-permute-start | bytes 344072 | tf_op jit(solution)/shard_map/ppermute | solution.py:302
  21.9 27.8 %collective-permute-start.2 = (bf16[128,896]{1,0:T(8,128)(2,1)}, bf16[128,896]{1,0:T(8,128)(2,1)S(1)}, u32[]{:S(2)}, u32[]{:S(2)}) collective-permute-start(bf16[128,896]{1,0:T(8,128)(2,1)} %get-tuple-element.24), channel_id=1, source_target_pairs={{0,1},{1,0},{2,3},{3,2},{4,5},{5,4},{6,7},{7,6},{8,9},{9,8},{10,11... | collective-permute-start | bytes 688136 | tf_op jit(solution)/shard_map/ppermute | solution.py:314
  25.1 27.8 %collective-permute-start.3 = (bf16[128,896]{1,0:T(8,128)(2,1)}, bf16[128,896]{1,0:T(8,128)(2,1)S(1)}, u32[]{:S(2)}, u32[]{:S(2)}) collective-permute-start(bf16[128,896]{1,0:T(8,128)(2,1)} %get-tuple-element.25), channel_id=1, source_target_pairs={{0,2},{1,3},{2,0},{3,1},{4,6},{5,7},{6,4},{7,5},{8,10},{9,11},{10,... | collective-permute-start | bytes 688136 | tf_op jit(solution)/shard_map/ppermute | solution.py:314
  29.3 23.6 %collective-permute-start.4 = (bf16[128,896]{1,0:T(8,128)(2,1)}, bf16[128,896]{1,0:T(8,128)(2,1)S(1)}, u32[]{:S(2)}, u32[]{:S(2)}) collective-permute-start(bf16[128,896]{1,0:T(8,128)(2,1)} %get-tuple-element.26), channel_id=1, source_target_pairs={{0,3},{1,2},{2,1},{3,0},{4,7},{5,6},{6,5},{7,4},{8,11},{9,10},{10,... | collective-permute-start | bytes 688136 | tf_op jit(solution)/shard_map/ppermute | solution.py:314
  34.3 19.3 %collective-permute-start.6 = (bf16[2,56,1024]{2,1,0:T(8,128)(2,1)S(1)}, bf16[2,56,1024]{2,1,0:T(8,128)(2,1)S(1)}, u32[]{:S(2)}, u32[]{:S(2)}) collective-permute-start(bf16[2,56,1024]{2,1,0:T(8,128)(2,1)S(1)} %get-tuple-element.34), channel_id=1, source_target_pairs={{0,112},{16,96},{32,80},{48,64},{64,48},{80,32},{96,16},{112,0},{1... | collective-permute-start | bytes 688136 | tf_op jit(solution)/shard_map/ppermute | solution.py:319
  39.3 28.5 %all-to-all-start = ((bf16[8,16,512]{2,1,0:T(8,128)(2,1)}), bf16[8,16,512]{2,1,0:T(8,128)(2,1)S(1)}, u32[]{:S(2)}, u32[]{:S(2)}) async-start(bf16[8,16,512]{2,1,0:T(8,128)(2,1)} %shard_map.119.refs_1_), calls=%async_computation | async-start | bytes 262144 | tf_op jit(solution)/shard_map/all_to_all | solution.py:399
  46.3 19.0 %collective-permute-start = (bf16[256,1152]{1,0:T(8,128)(2,1)S(1)}, bf16[256,1152]{1,0:T(8,128)(2,1)S(1)}, u32[]{:S(2)}, u32[]{:S(2)}) collective-permute-start(bf16[256,1152]{1,0:T(8,128)(2,1)S(1)} %get-tuple-element.22), channel_id=1, source_target_pairs={{0,1},{1,2},{2,3},{3,4},{4,5},{5,6},{6,7},{7,0},{8,9},{9,10},{10,1... | collective-permute-start | bytes 1769480 | tf_op jit(solution)/shard_map/ppermute | solution.py:302
  49.7 15.6 %collective-permute-start.1 = (bf16[256,1152]{1,0:T(8,128)(2,1)S(1)}, bf16[256,1152]{1,0:T(8,128)(2,1)S(1)}, u32[]{:S(2)}, u32[]{:S(2)}) collective-permute-start(bf16[256,1152]{1,0:T(8,128)(2,1)S(1)} %get-tuple-element.23), channel_id=1, source_target_pairs={{0,7},{1,0},{2,1},{3,2},{4,3},{5,4},{6,5},{7,6},{8,15},{9,8},{10,9... | collective-permute-start | bytes 1769480 | tf_op jit(solution)/shard_map/ppermute | solution.py:302
  52.9 12.4 %copy-start.1 = (bf16[1,3584,128]{2,1,0:T(8,128)(2,1)S(1)}, bf16[1,3584,128]{2,1,0:T(8,128)(2,1)}, u32[]{:S(2)}) copy-start(bf16[1,3584,128]{2,1,0:T(8,128)(2,1)} %param.20) | copy-start | bytes 2752516
  53.7 11.7 %copy-start = (bf16[1,3584,128]{2,1,0:T(8,128)(2,1)S(1)}, bf16[1,3584,128]{2,1,0:T(8,128)(2,1)}, u32[]{:S(2)}) copy-start(bf16[1,3584,128]{2,1,0:T(8,128)(2,1)} %param.19) | copy-start | bytes 2752516
  53.7 42.4 %collective-permute-start.10 = (bf16[2,2,56,1024]{3,2,1,0:T(8,128)(2,1)S(1)}, bf16[2,2,56,1024]{3,2,1,0:T(8,128)(2,1)S(1)}, u32[]{:S(2)}, u32[]{:S(2)}) collective-permute-start(bf16[2,2,56,1024]{3,2,1,0:T(8,128)(2,1)S(1)} %pad_maximum_fusion.refs_4_), channel_id=1, source_target_pairs={{0,128},{128,256},{256,384},{384,0},{1,129},{129,257},{257,385},{3... | collective-permute-start | bytes 1376264 | tf_op jit(solution)/shard_map/ppermute | solution.py:302
  56.9 43.2 %collective-permute-start.11 = (bf16[2,2,56,1024]{3,2,1,0:T(8,128)(2,1)S(1)}, bf16[2,2,56,1024]{3,2,1,0:T(8,128)(2,1)S(1)}, u32[]{:S(2)}, u32[]{:S(2)}) collective-permute-start(bf16[2,2,56,1024]{3,2,1,0:T(8,128)(2,1)S(1)} %pad_maximum_fusion.refs_4_), channel_id=1, source_target_pairs={{0,256},{128,384},{256,0},{384,128},{1,257},{129,385},{257,1},{385... | collective-permute-start | bytes 1376264 | tf_op jit(solution)/shard_map/ppermute | solution.py:302
  61.4 38.7 %collective-permute-start.12 = (bf16[2,2,56,1024]{3,2,1,0:T(8,128)(2,1)S(1)}, bf16[2,2,56,1024]{3,2,1,0:T(8,128)(2,1)S(1)}, u32[]{:S(2)}, u32[]{:S(2)}) collective-permute-start(bf16[2,2,56,1024]{3,2,1,0:T(8,128)(2,1)S(1)} %pad_maximum_fusion.refs_4_), channel_id=1, source_target_pairs={{0,384},{128,0},{256,128},{384,256},{1,385},{129,1},{257,129},{385... | collective-permute-start | bytes 1376264 | tf_op jit(solution)/shard_map/ppermute | solution.py:302
  67.8 12.7 %all-to-all-start.2 = ((bf16[4,256,128]{2,1,0:T(8,128)(2,1)}), bf16[4,256,128]{2,1,0:T(8,128)(2,1)S(1)}, u32[]{:S(2)}, u32[]{:S(2)}) async-start(bf16[4,256,128]{2,1,0:T(8,128)(2,1)} %get-tuple-element.27), calls=%async_computation.2 | async-start | bytes 524288 | tf_op jit(solution)/shard_map/all_to_all | solution.py:419
  76.7 23.5 %collective-permute-start.8 = (bf16[16,1024]{1,0:T(8,128)(2,1)S(1)}, bf16[16,1024]{1,0:T(8,128)(2,1)S(1)}, u32[]{:S(2)}, u32[]{:S(2)}) collective-permute-start(bf16[16,1024]{1,0:T(8,128)(2,1)S(1)} %shard_map.120.refs_0_), channel_id=1, source_target_pairs={{0,32},{16,48},{32,0},{48,16},{1,33},{17,49},{33,1},{49,17},{2,34}... | collective-permute-start | bytes 98312 | tf_op jit(solution)/shard_map/ppermute | solution.py:314
  82.4 27.9 %all-to-all-start.4 = ((bf16[64,4,1024]{2,1,0:T(4,128)(2,1)}), bf16[64,4,1024]{2,1,0:T(4,128)(2,1)S(1)}, u32[]{:S(2)}, u32[]{:S(2)}) async-start(bf16[64,4,1024]{2,1,0:T(4,128)(2,1)} %shard_map.126.refs_1_), calls=%async_computation.4 | async-start | bytes 1048576 | tf_op jit(solution)/shard_map/all_to_all | solution.py:453
  92.8 13.8 %collective-permute-start.7 = (bf16[16,1024]{1,0:T(8,128)(2,1)S(1)}, bf16[16,1024]{1,0:T(8,128)(2,1)S(1)}, u32[]{:S(2)}, u32[]{:S(2)}) collective-permute-start(bf16[16,1024]{1,0:T(8,128)(2,1)S(1)} %shard_map.127), channel_id=1, source_target_pairs={{0,16},{16,0},{32,48},{48,32},{1,17},{17,1},{33,49},{49,33},{2,18}... | collective-permute-start | bytes 98312 | tf_op jit(solution)/shard_map/ppermute | solution.py:314
  96.1 12.0 %collective-permute-start.9 = (bf16[16,1024]{1,0:T(8,128)(2,1)S(1)}, bf16[16,1024]{1,0:T(8,128)(2,1)S(1)}, u32[]{:S(2)}, u32[]{:S(2)}) collective-permute-start(bf16[16,1024]{1,0:T(8,128)(2,1)S(1)} %shard_map.127), channel_id=1, source_target_pairs={{0,48},{16,32},{32,16},{48,0},{1,49},{17,33},{33,17},{49,1},{2,50}... | collective-permute-start | bytes 98312 | tf_op jit(solution)/shard_map/ppermute | solution.py:314
  110.3 15.9 %all-to-all-start.3 = ((bf16[32,16,128]{2,1,0:T(8,128)(2,1)}), bf16[32,16,128]{2,1,0:T(8,128)(2,1)S(1)}, u32[]{:S(2)}, u32[]{:S(2)}) async-start(bf16[32,16,128]{2,1,0:T(8,128)(2,1)} %shard_map.129), calls=%async_computation.3 | async-start | bytes 262144 | tf_op jit(solution)/shard_map/all_to_all | solution.py:451
  117.5 8.7 %collective-permute-start.13 = (f32[16,448]{1,0:T(8,128)S(1)}, f32[16,448]{1,0:T(8,128)S(1)}, u32[]{:S(2)}, u32[]{:S(2)}) collective-permute-start(f32[16,448]{1,0:T(8,128)S(1)} %get-tuple-element.32), channel_id=1, source_target_pairs={{0,7},{1,6},{2,5},{3,4},{4,3},{5,2},{6,1},{7,0},{8,15},{9,14},{10,... | collective-permute-start | bytes 86024 | tf_op jit(solution)/shard_map/ppermute | solution.py:319
  (12 other events, 63.6 us)

commit v13 on v11

--- a/solution.py
+++ b/solution.py
@@ -367,7 +367,6 @@
         split_down,
         [((hidden_units, 2 * width), BF16)] * GROUP,
         w_down[0],
-        load=(0,),
         store=(0,),
     )
     down = [down[0]] + [swap(down[k], "y", k) for k in range(1, GROUP)]
@@ -379,7 +378,6 @@
         queries,
         jnp.swapaxes(latent_cache, 1, 2),
         smem=(0,),
-        load=(0, 1, 2),
         after=(place,),
     )
 
@@ -411,7 +409,6 @@
         w_gate[0],
         w_up[0],
         router_rows,
-        load=(3, 4),
         store=(0, 1),
         after=(moved, crossed),
     )
@@ -424,7 +421,6 @@
         [((rows, depth), BF16)],
         contexts,
         w_uv,
-        load=(1,),
         flops=10_000_000_000,
     )
 

time: 128 us -> 127 us (level)
  waiting for transfers between devices: 15.1 us -> 17.1 us
  starting transfers between devices: 93 us -> 91.4 us
  Pallas kernels: 15.6 us -> 14.2 us
    pallas_call x14, Pallas kernels: 15.6 us -> 14.2 us  [kernel_call(): pl.pallas_call(kernel, out_shape=tuple(shapes), in_specs=[place(n, load)...]
  transfers between devices with their start and end apart: 19 -> 19, of which waited for: 7 -> 7; matrix products, arithmetic and copies ran while one was open for 0% -> 0% of each run, Pallas kernels for 10% -> 9%
where the time goes in v13:
time: 127 us; the launch traced here: 126 us
  starting transfers between devices  91.4 us (72%)
  waiting for transfers between devices  17.1 us (13%)
  Pallas kernels  14.2 us (11%)
  local copies, waits for them, and re-layouts  2.72 us (2%)
    ppermute x6, starting transfers between devices, shift(): return lax.ppermute(value, axis, [(i, (i + k) % size) for i in range(size)])  19.5 us
    ppermute x6, starting transfers between devices, swap(): lax.ppermute(value, axis, [(i, i ^ k) for i in range(lax.axis_size(axis))])  18.5 us
    all_to_all x1, starting transfers between devices, on_device(): named_rows = lax.all_to_all(send, EP, 0, 0, tiled=True)  15 us
    pallas_call x14, Pallas kernels, kernel_call(): pl.pallas_call(kernel, out_shape=tuple(shapes), in_specs=[place(n, load)...  14.2 us
    all_to_all x1, starting transfers between devices, on_device(): back = lax.all_to_all(back, EP, 0, 0, tiled=True)  9.91 us
    ppermute x2, starting transfers between devices, mirror(): return lax.ppermute(value, axis, [(i, size - 1 - i) for i in range(size)])  8.77 us
    ppermute x6, waiting for transfers between devices, swap(): lax.ppermute(value, axis, [(i, i ^ k) for i in range(lax.axis_size(axis))])  8.02 us
    all_to_all x1, starting transfers between devices, on_device(): contexts = lax.all_to_all(context, 'y', 0, 0, tiled=True)  6.83 us
  transfers between devices with their start and end apart: 19, of which 7 were waited for; matrix products, arithmetic and copies ran while one was open for 0% of the time, Pallas kernels for 9%

profile of v13, /device:TPU:1, one launch (start us, length us, event | category | flops | bytes accessed | tf_op | source)
XLA Modules:
  0.0 126.0 jit_solution(8949220835979743262)
XLA Ops:
  0.0 2.6 %shard_map.118 = (bf16[64,4,1408]{2,1,0:T(4,128)(2,1)}, f32[256,16]{1,0:T(8,128)}, f32[16,448]{1,0:T(8,128)}) custom-call(bf16[16,3584]{1,0:T(8,128)(2,1)} %refs_0_.2, bf16[3584]{0:T(1024)(128)(2,1)} %refs_1_.3, s32[8,16]{1,0:T(8,128)} %bitcast.20), custom_call_target="tpu_custom_call" | custom-call | bytes 122368 | tf_op jit(solution)/shard_map/pallas_call | solution.py:60
  2.6 15.0 %all-to-all-start.1 = ((bf16[64,4,1408]{2,1,0:T(4,128)(2,1)}), bf16[64,4,1408]{2,1,0:T(4,128)(2,1)S(1)}, u32[]{:S(2)}, u32[]{:S(2)}) async-start(bf16[64,4,1408]{2,1,0:T(4,128)(2,1)} %get-tuple-element.20), calls=%async_computation.1 | async-start | bytes 1441792 | tf_op jit(solution)/shard_map/all_to_all | solution.py:364
  17.6 2.4 %collective-permute-start.6 = (bf16[56,1024]{1,0:T(8,128)(2,1)S(1)}, bf16[56,1024]{1,0:T(8,128)(2,1)S(1)}, u32[]{:S(2)}, u32[]{:S(2)}) collective-permute-start(bf16[56,1024]{1,0:T(8,128)(2,1)S(1)} %bitcast.17), channel_id=1, source_target_pairs={{0,8},{8,0},{1,9},{9,1},{2,10},{10,2},{3,11},{11,3},{4,12},{12,4},... | collective-permute-start | bytes 344072 | tf_op jit(solution)/shard_map/ppermute | solution.py:302
  21.7 3.2 %collective-permute-start.3 = (bf16[128,896]{1,0:T(8,128)(2,1)}, bf16[128,896]{1,0:T(8,128)(2,1)S(1)}, u32[]{:S(2)}, u32[]{:S(2)}) collective-permute-start(bf16[128,896]{1,0:T(8,128)(2,1)} %get-tuple-element.24), channel_id=1, source_target_pairs={{0,1},{1,0},{2,3},{3,2},{4,5},{5,4},{6,7},{7,6},{8,9},{9,8},{10,11... | collective-permute-start | bytes 688136 | tf_op jit(solution)/shard_map/ppermute | solution.py:314
  24.9 4.2 %collective-permute-start.4 = (bf16[128,896]{1,0:T(8,128)(2,1)}, bf16[128,896]{1,0:T(8,128)(2,1)S(1)}, u32[]{:S(2)}, u32[]{:S(2)}) collective-permute-start(bf16[128,896]{1,0:T(8,128)(2,1)} %get-tuple-element.25), channel_id=1, source_target_pairs={{0,2},{1,3},{2,0},{3,1},{4,6},{5,7},{6,4},{7,5},{8,10},{9,11},{10,... | collective-permute-start | bytes 688136 | tf_op jit(solution)/shard_map/ppermute | solution.py:314
  29.1 1.9 %collective-permute-start.5 = (bf16[128,896]{1,0:T(8,128)(2,1)}, bf16[128,896]{1,0:T(8,128)(2,1)S(1)}, u32[]{:S(2)}, u32[]{:S(2)}) collective-permute-start(bf16[128,896]{1,0:T(8,128)(2,1)} %get-tuple-element.26), channel_id=1, source_target_pairs={{0,3},{1,2},{2,1},{3,0},{4,7},{5,6},{6,5},{7,4},{8,11},{9,10},{10,... | collective-permute-start | bytes 688136 | tf_op jit(solution)/shard_map/ppermute | solution.py:314
  33.5 4.4 %collective-permute-start.7 = (bf16[2,56,1024]{2,1,0:T(8,128)(2,1)S(1)}, bf16[2,56,1024]{2,1,0:T(8,128)(2,1)S(1)}, u32[]{:S(2)}, u32[]{:S(2)}) collective-permute-start(bf16[2,56,1024]{2,1,0:T(8,128)(2,1)S(1)} %get-tuple-element.34), channel_id=1, source_target_pairs={{0,112},{16,96},{32,80},{48,64},{64,48},{80,32},{96,16},{112,0},{1... | collective-permute-start | bytes 688136 | tf_op jit(solution)/shard_map/ppermute | solution.py:319
  39.3 6.8 %all-to-all-start = ((bf16[8,16,512]{2,1,0:T(8,128)(2,1)}), bf16[8,16,512]{2,1,0:T(8,128)(2,1)S(1)}, u32[]{:S(2)}, u32[]{:S(2)}) async-start(bf16[8,16,512]{2,1,0:T(8,128)(2,1)} %shard_map.119.refs_1_), calls=%async_computation | async-start | bytes 262144 | tf_op jit(solution)/shard_map/all_to_all | solution.py:397
  46.3 3.4 %collective-permute-start.1 = (bf16[256,1152]{1,0:T(8,128)(2,1)S(1)}, bf16[256,1152]{1,0:T(8,128)(2,1)S(1)}, u32[]{:S(2)}, u32[]{:S(2)}) collective-permute-start(bf16[256,1152]{1,0:T(8,128)(2,1)S(1)} %get-tuple-element.22), channel_id=1, source_target_pairs={{0,1},{1,2},{2,3},{3,4},{4,5},{5,6},{6,7},{7,0},{8,9},{9,10},{10,1... | collective-permute-start | bytes 1769480 | tf_op jit(solution)/shard_map/ppermute | solution.py:302
  49.7 3.1 %collective-permute-start.2 = (bf16[256,1152]{1,0:T(8,128)(2,1)S(1)}, bf16[256,1152]{1,0:T(8,128)(2,1)S(1)}, u32[]{:S(2)}, u32[]{:S(2)}) collective-permute-start(bf16[256,1152]{1,0:T(8,128)(2,1)S(1)} %get-tuple-element.23), channel_id=1, source_target_pairs={{0,7},{1,0},{2,1},{3,2},{4,3},{5,4},{6,5},{7,6},{8,15},{9,8},{10,9... | collective-permute-start | bytes 1769480 | tf_op jit(solution)/shard_map/ppermute | solution.py:302
  53.7 3.2 %collective-permute-start.10 = (bf16[2,2,56,1024]{3,2,1,0:T(8,128)(2,1)S(1)}, bf16[2,2,56,1024]{3,2,1,0:T(8,128)(2,1)S(1)}, u32[]{:S(2)}, u32[]{:S(2)}) collective-permute-start(bf16[2,2,56,1024]{3,2,1,0:T(8,128)(2,1)S(1)} %pad_maximum_fusion.refs_4_), channel_id=1, source_target_pairs={{0,128},{128,256},{256,384},{384,0},{1,129},{129,257},{257,385},{3... | collective-permute-start | bytes 1376264 | tf_op jit(solution)/shard_map/ppermute | solution.py:302
  56.9 4.5 %collective-permute-start.11 = (bf16[2,2,56,1024]{3,2,1,0:T(8,128)(2,1)S(1)}, bf16[2,2,56,1024]{3,2,1,0:T(8,128)(2,1)S(1)}, u32[]{:S(2)}, u32[]{:S(2)}) collective-permute-start(bf16[2,2,56,1024]{3,2,1,0:T(8,128)(2,1)S(1)} %pad_maximum_fusion.refs_4_), channel_id=1, source_target_pairs={{0,256},{128,384},{256,0},{384,128},{1,257},{129,385},{257,1},{385... | collective-permute-start | bytes 1376264 | tf_op jit(solution)/shard_map/ppermute | solution.py:302
  61.4 3.0 %collective-permute-start.12 = (bf16[2,2,56,1024]{3,2,1,0:T(8,128)(2,1)S(1)}, bf16[2,2,56,1024]{3,2,1,0:T(8,128)(2,1)S(1)}, u32[]{:S(2)}, u32[]{:S(2)}) collective-permute-start(bf16[2,2,56,1024]{3,2,1,0:T(8,128)(2,1)S(1)} %pad_maximum_fusion.refs_4_), channel_id=1, source_target_pairs={{0,384},{128,0},{256,128},{384,256},{1,385},{129,1},{257,129},{385... | collective-permute-start | bytes 1376264 | tf_op jit(solution)/shard_map/ppermute | solution.py:302
  65.5 1.9 %shard_map.125 = (bf16[4,256,128]{2,1,0:T(8,128)(2,1)}, bf16[256,128]{1,0:T(8,128)(2,1)S(1)}) custom-call(bf16[256,1408]{1,0:T(8,128)(2,1)S(1)} %get-tuple-element.21.refs_0_, bf16[256,1152]{1,0:T(8,128)(2,1)S(1)} %collective-permute-done.1.refs_1_, bf16[256,1152]{1,0:T(8,128)(2,1)S(1)} %collective-permute-done.2.refs_2_, bf16[3584,128]{1,0:T(8,128)(2,1)S(1)} %bitcast.12, ...), custom_call_target="tpu_custom_call" | custom-call | bytes 3749888 | tf_op jit(solution)/shard_map/pallas_call | solution.py:60
  67.5 6.4 %all-to-all-start.2 = ((bf16[4,256,128]{2,1,0:T(8,128)(2,1)}), bf16[4,256,128]{2,1,0:T(8,128)(2,1)S(1)}, u32[]{:S(2)}, u32[]{:S(2)}) async-start(bf16[4,256,128]{2,1,0:T(8,128)(2,1)} %get-tuple-element.27), calls=%async_computation.2 | async-start | bytes 524288 | tf_op jit(solution)/shard_map/all_to_all | solution.py:416
  76.6 1.9 %collective-permute-start = (bf16[16,1024]{1,0:T(8,128)(2,1)S(1)}, bf16[16,1024]{1,0:T(8,128)(2,1)S(1)}, u32[]{:S(2)}, u32[]{:S(2)}) collective-permute-start(bf16[16,1024]{1,0:T(8,128)(2,1)S(1)} %shard_map.120.refs_0_), channel_id=1, source_target_pairs={{0,16},{16,0},{32,48},{48,32},{1,17},{17,1},{33,49},{49,33},{2,18}... | collective-permute-start | bytes 98312 | tf_op jit(solution)/shard_map/ppermute | solution.py:314
  79.8 1.9 %shard_map.126.refs_1_ = bf16[64,4,1024]{2,1,0:T(4,128)(2,1)} custom-call(bf16[4,256,128]{2,1,0:T(8,128)(2,1)S(1)} %all-to-all-done.2.refs_0_, bf16[128,896]{1,0:T(8,128)(2,1)S(1)} %get-tuple-element.28.refs_1_, bf16[128,896]{1,0:T(8,128)(2,1)S(1)} %copy-done.6, bf16[128,896]{1,0:T(8,128)(2,1)S(1)} %copy-done.8, bf16[128,896]{1,0:T(8,128)(2,1)S(1)} %copy-done.10, ...), custom_call_target="tpu_custom_call" | custom-call | bytes 1245184 | tf_op jit(solution)/shard_map/pallas_call | solution.py:60
  81.7 9.9 %all-to-all-start.4 = ((bf16[64,4,1024]{2,1,0:T(4,128)(2,1)}), bf16[64,4,1024]{2,1,0:T(4,128)(2,1)S(1)}, u32[]{:S(2)}, u32[]{:S(2)}) async-start(bf16[64,4,1024]{2,1,0:T(4,128)(2,1)} %shard_map.126.refs_1_), calls=%async_computation.4 | async-start | bytes 1048576 | tf_op jit(solution)/shard_map/all_to_all | solution.py:451
  91.6 4.2 %collective-permute-start.8 = (bf16[16,1024]{1,0:T(8,128)(2,1)S(1)}, bf16[16,1024]{1,0:T(8,128)(2,1)S(1)}, u32[]{:S(2)}, u32[]{:S(2)}) collective-permute-start(bf16[16,1024]{1,0:T(8,128)(2,1)S(1)} %shard_map.127), channel_id=1, source_target_pairs={{0,32},{16,48},{32,0},{48,16},{1,33},{17,49},{33,1},{49,17},{2,34}... | collective-permute-start | bytes 98312 | tf_op jit(solution)/shard_map/ppermute | solution.py:314
  95.8 3.1 %collective-permute-start.9 = (bf16[16,1024]{1,0:T(8,128)(2,1)S(1)}, bf16[16,1024]{1,0:T(8,128)(2,1)S(1)}, u32[]{:S(2)}, u32[]{:S(2)}) collective-permute-start(bf16[16,1024]{1,0:T(8,128)(2,1)S(1)} %shard_map.127), channel_id=1, source_target_pairs={{0,48},{16,32},{32,16},{48,0},{1,49},{17,33},{33,17},{49,1},{2,50}... | collective-permute-start | bytes 98312 | tf_op jit(solution)/shard_map/ppermute | solution.py:314
  99.0 7.6 %collective-permute-done.8.refs_2_ = bf16[16,1024]{1,0:T(8,128)(2,1)S(1)} collective-permute-done((bf16[16,1024]{1,0:T(8,128)(2,1)S(1)}, bf16[16,1024]{1,0:T(8,128)(2,1)S(1)}, u32[]{:S(2)}, u32[]{:S(2)}) %collective-permute-start.8) | collective-permute-done | bytes 32800 | tf_op jit(solution)/shard_map/ppermute | solution.py:314
  109.5 6.4 %all-to-all-start.3 = ((bf16[32,16,128]{2,1,0:T(8,128)(2,1)}), bf16[32,16,128]{2,1,0:T(8,128)(2,1)S(1)}, u32[]{:S(2)}, u32[]{:S(2)}) async-start(bf16[32,16,128]{2,1,0:T(8,128)(2,1)} %shard_map.129), calls=%async_computation.3 | async-start | bytes 262144 | tf_op jit(solution)/shard_map/all_to_all | solution.py:449
  116.7 4.4 %collective-permute-start.13 = (f32[16,448]{1,0:T(8,128)S(1)}, f32[16,448]{1,0:T(8,128)S(1)}, u32[]{:S(2)}, u32[]{:S(2)}) collective-permute-start(f32[16,448]{1,0:T(8,128)S(1)} %get-tuple-element.32), channel_id=1, source_target_pairs={{0,7},{1,6},{2,5},{3,4},{4,3},{5,2},{6,1},{7,0},{8,15},{9,14},{10,... | collective-permute-start | bytes 86024 | tf_op jit(solution)/shard_map/ppermute | solution.py:319
  121.0 4.3 %all-to-all-done.3.refs_0_ = bf16[32,16,128]{2,1,0:T(8,128)(2,1)S(1)} async-done(((bf16[32,16,128]{2,1,0:T(8,128)(2,1)}), bf16[32,16,128]{2,1,0:T(8,128)(2,1)S(1)}, u32[]{:S(2)}, u32[]{:S(2)}) %all-to-all-start.3) | async-done | bytes 131104 | tf_op jit(solution)/shard_map/all_to_all | solution.py:449
  (66 shorter events, 15.9 us)
Async XLA Ops:
  0.0 20.0 %copy-start.2 = (bf16[1,128,3584]{2,1,0:T(8,128)(2,1)S(1)}, bf16[1,128,3584]{2,1,0:T(8,128)(2,1)}, u32[]{:S(2)}) copy-start(bf16[1,128,3584]{2,1,0:T(8,128)(2,1)} %param.21) | copy-start | bytes 2752516
  0.0 17.6 %copy-start.15 = (bf16[1024,56]{0,1:T(8,128)(2,1)S(1)}, bf16[1024,56]{0,1:T(8,128)(2,1)}, u32[]{:S(2)}) copy-start(bf16[1024,56]{0,1:T(8,128)(2,1)} %param.23) | copy-start | bytes 344068
  2.6 28.5 %copy-start.3 = (bf16[2,384,576]{1,2,0:T(8,128)(2,1)S(1)}, bf16[2,384,576]{1,2,0:T(8,128)(2,1)}, u32[]{:S(2)}) copy-start(bf16[2,384,576]{1,2,0:T(8,128)(2,1)} %param.15) | copy-start | bytes 2654212
  2.6 36.6 %all-to-all-start.1 = ((bf16[64,4,1408]{2,1,0:T(4,128)(2,1)}), bf16[64,4,1408]{2,1,0:T(4,128)(2,1)S(1)}, u32[]{:S(2)}, u32[]{:S(2)}) async-start(bf16[64,4,1408]{2,1,0:T(4,128)(2,1)} %get-tuple-element.20), calls=%async_computation.1 | async-start | bytes 1441792 | tf_op jit(solution)/shard_map/all_to_all | solution.py:364
  17.6 15.9 %collective-permute-start.6 = (bf16[56,1024]{1,0:T(8,128)(2,1)S(1)}, bf16[56,1024]{1,0:T(8,128)(2,1)S(1)}, u32[]{:S(2)}, u32[]{:S(2)}) collective-permute-start(bf16[56,1024]{1,0:T(8,128)(2,1)S(1)} %bitcast.17), channel_id=1, source_target_pairs={{0,8},{8,0},{1,9},{9,1},{2,10},{10,2},{3,11},{11,3},{4,12},{12,4},... | collective-permute-start | bytes 344072 | tf_op jit(solution)/shard_map/ppermute | solution.py:302
  21.7 28.1 %collective-permute-start.3 = (bf16[128,896]{1,0:T(8,128)(2,1)}, bf16[128,896]{1,0:T(8,128)(2,1)S(1)}, u32[]{:S(2)}, u32[]{:S(2)}) collective-permute-start(bf16[128,896]{1,0:T(8,128)(2,1)} %get-tuple-element.24), channel_id=1, source_target_pairs={{0,1},{1,0},{2,3},{3,2},{4,5},{5,4},{6,7},{7,6},{8,9},{9,8},{10,11... | collective-permute-start | bytes 688136 | tf_op jit(solution)/shard_map/ppermute | solution.py:314
  24.9 28.0 %collective-permute-start.4 = (bf16[128,896]{1,0:T(8,128)(2,1)}, bf16[128,896]{1,0:T(8,128)(2,1)S(1)}, u32[]{:S(2)}, u32[]{:S(2)}) collective-permute-start(bf16[128,896]{1,0:T(8,128)(2,1)} %get-tuple-element.25), channel_id=1, source_target_pairs={{0,2},{1,3},{2,0},{3,1},{4,6},{5,7},{6,4},{7,5},{8,10},{9,11},{10,... | collective-permute-start | bytes 688136 | tf_op jit(solution)/shard_map/ppermute | solution.py:314
  29.1 23.8 %collective-permute-start.5 = (bf16[128,896]{1,0:T(8,128)(2,1)}, bf16[128,896]{1,0:T(8,128)(2,1)S(1)}, u32[]{:S(2)}, u32[]{:S(2)}) collective-permute-start(bf16[128,896]{1,0:T(8,128)(2,1)} %get-tuple-element.26), channel_id=1, source_target_pairs={{0,3},{1,2},{2,1},{3,0},{4,7},{5,6},{6,5},{7,4},{8,11},{9,10},{10,... | collective-permute-start | bytes 688136 | tf_op jit(solution)/shard_map/ppermute | solution.py:314
  33.5 20.2 %collective-permute-start.7 = (bf16[2,56,1024]{2,1,0:T(8,128)(2,1)S(1)}, bf16[2,56,1024]{2,1,0:T(8,128)(2,1)S(1)}, u32[]{:S(2)}, u32[]{:S(2)}) collective-permute-start(bf16[2,56,1024]{2,1,0:T(8,128)(2,1)S(1)} %get-tuple-element.34), channel_id=1, source_target_pairs={{0,112},{16,96},{32,80},{48,64},{64,48},{80,32},{96,16},{112,0},{1... | collective-permute-start | bytes 688136 | tf_op jit(solution)/shard_map/ppermute | solution.py:319
  39.3 28.2 %all-to-all-start = ((bf16[8,16,512]{2,1,0:T(8,128)(2,1)}), bf16[8,16,512]{2,1,0:T(8,128)(2,1)S(1)}, u32[]{:S(2)}, u32[]{:S(2)}) async-start(bf16[8,16,512]{2,1,0:T(8,128)(2,1)} %shard_map.119.refs_1_), calls=%async_computation | async-start | bytes 262144 | tf_op jit(solution)/shard_map/all_to_all | solution.py:397
  46.3 19.2 %collective-permute-start.1 = (bf16[256,1152]{1,0:T(8,128)(2,1)S(1)}, bf16[256,1152]{1,0:T(8,128)(2,1)S(1)}, u32[]{:S(2)}, u32[]{:S(2)}) collective-permute-start(bf16[256,1152]{1,0:T(8,128)(2,1)S(1)} %get-tuple-element.22), channel_id=1, source_target_pairs={{0,1},{1,2},{2,3},{3,4},{4,5},{5,6},{6,7},{7,0},{8,9},{9,10},{10,1... | collective-permute-start | bytes 1769480 | tf_op jit(solution)/shard_map/ppermute | solution.py:302
  49.7 15.8 %collective-permute-start.2 = (bf16[256,1152]{1,0:T(8,128)(2,1)S(1)}, bf16[256,1152]{1,0:T(8,128)(2,1)S(1)}, u32[]{:S(2)}, u32[]{:S(2)}) collective-permute-start(bf16[256,1152]{1,0:T(8,128)(2,1)S(1)} %get-tuple-element.23), channel_id=1, source_target_pairs={{0,7},{1,0},{2,1},{3,2},{4,3},{5,4},{6,5},{7,6},{8,15},{9,8},{10,9... | collective-permute-start | bytes 1769480 | tf_op jit(solution)/shard_map/ppermute | solution.py:302
  52.9 12.6 %copy-start.1 = (bf16[1,3584,128]{2,1,0:T(8,128)(2,1)S(1)}, bf16[1,3584,128]{2,1,0:T(8,128)(2,1)}, u32[]{:S(2)}) copy-start(bf16[1,3584,128]{2,1,0:T(8,128)(2,1)} %param.20) | copy-start | bytes 2752516
  53.7 11.8 %copy-start = (bf16[1,3584,128]{2,1,0:T(8,128)(2,1)S(1)}, bf16[1,3584,128]{2,1,0:T(8,128)(2,1)}, u32[]{:S(2)}) copy-start(bf16[1,3584,128]{2,1,0:T(8,128)(2,1)} %param.19) | copy-start | bytes 2752516
  53.7 42.1 %collective-permute-start.10 = (bf16[2,2,56,1024]{3,2,1,0:T(8,128)(2,1)S(1)}, bf16[2,2,56,1024]{3,2,1,0:T(8,128)(2,1)S(1)}, u32[]{:S(2)}, u32[]{:S(2)}) collective-permute-start(bf16[2,2,56,1024]{3,2,1,0:T(8,128)(2,1)S(1)} %pad_maximum_fusion.refs_4_), channel_id=1, source_target_pairs={{0,128},{128,256},{256,384},{384,0},{1,129},{129,257},{257,385},{3... | collective-permute-start | bytes 1376264 | tf_op jit(solution)/shard_map/ppermute | solution.py:302
  56.9 42.0 %collective-permute-start.11 = (bf16[2,2,56,1024]{3,2,1,0:T(8,128)(2,1)S(1)}, bf16[2,2,56,1024]{3,2,1,0:T(8,128)(2,1)S(1)}, u32[]{:S(2)}, u32[]{:S(2)}) collective-permute-start(bf16[2,2,56,1024]{3,2,1,0:T(8,128)(2,1)S(1)} %pad_maximum_fusion.refs_4_), channel_id=1, source_target_pairs={{0,256},{128,384},{256,0},{384,128},{1,257},{129,385},{257,1},{385... | collective-permute-start | bytes 1376264 | tf_op jit(solution)/shard_map/ppermute | solution.py:302
  61.4 37.5 %collective-permute-start.12 = (bf16[2,2,56,1024]{3,2,1,0:T(8,128)(2,1)S(1)}, bf16[2,2,56,1024]{3,2,1,0:T(8,128)(2,1)S(1)}, u32[]{:S(2)}, u32[]{:S(2)}) collective-permute-start(bf16[2,2,56,1024]{3,2,1,0:T(8,128)(2,1)S(1)} %pad_maximum_fusion.refs_4_), channel_id=1, source_target_pairs={{0,384},{128,0},{256,128},{384,256},{1,385},{129,1},{257,129},{385... | collective-permute-start | bytes 1376264 | tf_op jit(solution)/shard_map/ppermute | solution.py:302
  67.5 12.3 %all-to-all-start.2 = ((bf16[4,256,128]{2,1,0:T(8,128)(2,1)}), bf16[4,256,128]{2,1,0:T(8,128)(2,1)S(1)}, u32[]{:S(2)}, u32[]{:S(2)}) async-start(bf16[4,256,128]{2,1,0:T(8,128)(2,1)} %get-tuple-element.27), calls=%async_computation.2 | async-start | bytes 524288 | tf_op jit(solution)/shard_map/all_to_all | solution.py:416
  76.6 22.4 %collective-permute-start = (bf16[16,1024]{1,0:T(8,128)(2,1)S(1)}, bf16[16,1024]{1,0:T(8,128)(2,1)S(1)}, u32[]{:S(2)}, u32[]{:S(2)}) collective-permute-start(bf16[16,1024]{1,0:T(8,128)(2,1)S(1)} %shard_map.120.refs_0_), channel_id=1, source_target_pairs={{0,16},{16,0},{32,48},{48,32},{1,17},{17,1},{33,49},{49,33},{2,18}... | collective-permute-start | bytes 98312 | tf_op jit(solution)/shard_map/ppermute | solution.py:314
  81.7 27.8 %all-to-all-start.4 = ((bf16[64,4,1024]{2,1,0:T(4,128)(2,1)}), bf16[64,4,1024]{2,1,0:T(4,128)(2,1)S(1)}, u32[]{:S(2)}, u32[]{:S(2)}) async-start(bf16[64,4,1024]{2,1,0:T(4,128)(2,1)} %shard_map.126.refs_1_), calls=%async_computation.4 | async-start | bytes 1048576 | tf_op jit(solution)/shard_map/all_to_all | solution.py:451
  91.6 15.0 %collective-permute-start.8 = (bf16[16,1024]{1,0:T(8,128)(2,1)S(1)}, bf16[16,1024]{1,0:T(8,128)(2,1)S(1)}, u32[]{:S(2)}, u32[]{:S(2)}) collective-permute-start(bf16[16,1024]{1,0:T(8,128)(2,1)S(1)} %shard_map.127), channel_id=1, source_target_pairs={{0,32},{16,48},{32,0},{48,16},{1,33},{17,49},{33,1},{49,17},{2,34}... | collective-permute-start | bytes 98312 | tf_op jit(solution)/shard_map/ppermute | solution.py:314
  95.8 11.1 %collective-permute-start.9 = (bf16[16,1024]{1,0:T(8,128)(2,1)S(1)}, bf16[16,1024]{1,0:T(8,128)(2,1)S(1)}, u32[]{:S(2)}, u32[]{:S(2)}) collective-permute-start(bf16[16,1024]{1,0:T(8,128)(2,1)S(1)} %shard_map.127), channel_id=1, source_target_pairs={{0,48},{16,32},{32,16},{48,0},{1,49},{17,33},{33,17},{49,1},{2,50}... | collective-permute-start | bytes 98312 | tf_op jit(solution)/shard_map/ppermute | solution.py:314
  109.5 15.8 %all-to-all-start.3 = ((bf16[32,16,128]{2,1,0:T(8,128)(2,1)}), bf16[32,16,128]{2,1,0:T(8,128)(2,1)S(1)}, u32[]{:S(2)}, u32[]{:S(2)}) async-start(bf16[32,16,128]{2,1,0:T(8,128)(2,1)} %shard_map.129), calls=%async_computation.3 | async-start | bytes 262144 | tf_op jit(solution)/shard_map/all_to_all | solution.py:449
  116.7 8.7 %collective-permute-start.13 = (f32[16,448]{1,0:T(8,128)S(1)}, f32[16,448]{1,0:T(8,128)S(1)}, u32[]{:S(2)}, u32[]{:S(2)}) collective-permute-start(f32[16,448]{1,0:T(8,128)S(1)} %get-tuple-element.32), channel_id=1, source_target_pairs={{0,7},{1,6},{2,5},{3,4},{4,3},{5,2},{6,1},{7,0},{8,15},{9,14},{10,... | collective-permute-start | bytes 86024 | tf_op jit(solution)/shard_map/ppermute | solution.py:319
  (12 other events, 61.5 us)
